TPU v7x, 32 devices: a whole 2x2x4 slice. The times are simulated.
32 devices in a mesh: tp: 4 (over x, core), dp: 8 (over z, y).
Axes of the slice: x: 2, y: 2, z: 4, core: 2. Of those that a mesh axis runs over, the one named last changes fastest.
Arguments:
- tokens: bfloat16 [16384, 768], P('dp'), may hold values from -6 to 6
- memory: bfloat16 [16384, 768], P('dp'), may hold values from -6 to 6
- cotangent: bfloat16 [16384, 768], P('dp'), may hold values from -6 to 6
- tgt_len: int32 [16], P('dp'), may hold values from 1 to 1024, 10240 in all
- src_len: int32 [16], P('dp'), may hold values from 1 to 1024, 12288 in all
- self_query: bfloat16 [768, 768], P(None, 'tp'), may hold values from -0.21875 to 0.21875
- self_key: bfloat16 [768, 768], P(None, 'tp'), may hold values from -0.21875 to 0.21875
- self_value: bfloat16 [768, 768], P(None, 'tp'), may hold values from -0.21875 to 0.21875
- self_out: bfloat16 [768, 768], P('tp'), may hold values from -1.25 to 1.25
- cross_query: bfloat16 [768, 768], P(None, 'tp'), may hold values from -0.21875 to 0.21875
- cross_key: bfloat16 [768, 768], P(None, 'tp'), may hold values from -0.21875 to 0.21875
- cross_value: bfloat16 [768, 768], P(None, 'tp'), may hold values from -0.21875 to 0.21875
- cross_out: bfloat16 [768, 768], P('tp'), may hold values from -1.25 to 1.25
- ffn_up: bfloat16 [768, 3072], P(None, 'tp'), may hold values from -0.21875 to 0.21875
- ffn_down: bfloat16 [3072, 768], P('tp'), may hold values from -0.109375 to 0.109375
- gain_one: float32 [768], replicated, may hold values from 0.5 to 1.5
- shift_one: float32 [768], replicated, may hold values from -1.8 to 1.8
- gain_two: float32 [768], replicated, may hold values from 0.5 to 1.5
- shift_two: float32 [768], replicated, may hold values from -1.8 to 1.8
- gain_three: float32 [768], replicated, may hold values from 0.5 to 1.5
- shift_three: float32 [768], replicated, may hold values from -1.8 to 1.8
Outputs:
- layer_out: bfloat16 [16384, 768], P('dp')
- tokens_grad: bfloat16 [16384, 768], P('dp')
- memory_grad: bfloat16 [16384, 768], P('dp')
- self_query_grad: float32 [768, 768], P(None, 'tp')
- self_key_grad: float32 [768, 768], P(None, 'tp')
- self_value_grad: float32 [768, 768], P(None, 'tp')
- self_out_grad: float32 [768, 768], P('tp')
- cross_query_grad: float32 [768, 768], P(None, 'tp')
- cross_key_grad: float32 [768, 768], P(None, 'tp')
- cross_value_grad: float32 [768, 768], P(None, 'tp')
- cross_out_grad: float32 [768, 768], P('tp')
- ffn_up_grad: float32 [768, 3072], P(None, 'tp')
- ffn_down_grad: float32 [3072, 768], P('tp')
- gain_one_grad: float32 [768], replicated
- shift_one_grad: float32 [768], replicated
- gain_two_grad: float32 [768], replicated
- shift_two_grad: float32 [768], replicated
- gain_three_grad: float32 [768], replicated
- shift_three_grad: float32 [768], replicated
Inputs may be any that keep to these rules, and one draw needn't show every extreme that they name: `tgt_len`: one row has all 1024 slots live. `src_len`: one row has all 1024 memory slots live.
All inputs are finite; a program needn't handle non-finite values. No bound on the sum of `tgt_len` or of `src_len` on one device may be relied on, other than what follows from the above.
Results may differ from a plain program's by a relative error of at most 0.04.
Values may be sent and summed in bfloat16 or wider, within the bound.
No kernel may reach another device: no remote copies, remote signals or barrier semaphores. Data moves between devices by JAX's collectives and lax.ppermute only.
A program may use at most 192 MiB of HBM per device.

v0:
```python
import jax
import jax.numpy as jnp
from jax import lax
from jax.sharding import PartitionSpec as P

HEAD_DIM = 64


eps_norm = 1e-05
masked = -1e30


def layer_norm(resid, gain, shift):
    center = resid - jnp.mean(resid, -1, keepdims=True)
    spread = jnp.mean(center * center, -1, keepdims=True)
    return center * lax.rsqrt(spread + eps_norm) * gain + shift


def matmul(left, right):
    return jnp.dot(left, right, preferred_element_type=jnp.float32)


def matmul_left(left, right):
    return lax.dot_general(
        left, right, (((0,), (0,)), ((), ())), preferred_element_type=jnp.float32
    )


def matmul_right(left, right):
    return lax.dot_general(
        left, right, (((1,), (1,)), ((), ())), preferred_element_type=jnp.float32
    )


def exact_gelu(value):
    return jax.nn.gelu(value, approximate=False)


def visible(offset, span, key_count, key_limit, causal):
    key_index = jnp.arange(key_count)
    allowed = jnp.broadcast_to((key_index < key_limit)[None, :], (span, key_count))
    if causal:
        query_index = offset + jnp.arange(span)
        allowed = allowed & (key_index[None, :] <= query_index[:, None])
    return allowed


def split_heads(matrix):
    return matrix.reshape(matrix.shape[0], -1, HEAD_DIM)


def attend_forward(queries, keys, values, key_limit, causal):
    length = queries.shape[0]
    span = min(512, length)
    key_heads = split_heads(keys)
    value_heads = split_heads(values)
    head_count = key_heads.shape[1]
    query_blocks = split_heads(queries).reshape(length // span, span, head_count, HEAD_DIM)
    offsets = jnp.arange(length // span) * span

    def one_block(element):
        query_block, offset = element
        scores = jnp.einsum(
            "qhd,khd->hqk", query_block, key_heads, preferred_element_type=jnp.float32
        )
        scores = jnp.where(
            visible(offset, span, key_heads.shape[0], key_limit, causal)[None], scores, masked
        )
        row_peak = jnp.max(scores, -1, keepdims=True)
        lifted = jnp.exp(scores - row_peak)
        row_total = jnp.sum(lifted, -1, keepdims=True)
        attn_weights = (lifted / row_total).astype(jnp.bfloat16)
        mixed = jnp.einsum(
            "hqk,khd->qhd", attn_weights, value_heads, preferred_element_type=jnp.float32
        )
        return (mixed.astype(jnp.bfloat16), (row_peak + jnp.log(row_total))[..., 0])

    mixed, log_sums = lax.map(one_block, (query_blocks, offsets))
    return (mixed.reshape(length, head_count * HEAD_DIM), log_sums)


def attend_backward(queries, keys, values, grad_mixed, log_sums, key_limit, causal):
    length = queries.shape[0]
    span = min(512, length)
    key_heads = split_heads(keys)
    value_heads = split_heads(values)
    head_count = key_heads.shape[1]
    query_blocks = split_heads(queries).reshape(length // span, span, head_count, HEAD_DIM)
    grad_blocks = split_heads(grad_mixed).reshape(length // span, span, head_count, HEAD_DIM)
    offsets = jnp.arange(length // span) * span

    def one_block(running, element):
        grad_keys, grad_values = running
        query_block, grad_block, log_sum, offset = element
        scores = jnp.einsum(
            "qhd,khd->hqk", query_block, key_heads, preferred_element_type=jnp.float32
        )
        scores = jnp.where(
            visible(offset, span, key_heads.shape[0], key_limit, causal)[None], scores, masked
        )
        attn_weights = jnp.exp(scores - log_sum[..., None])
        grad_weights = jnp.einsum(
            "qhd,khd->hqk", grad_block, value_heads, preferred_element_type=jnp.float32
        )
        inner = jnp.sum(attn_weights * grad_weights, -1, keepdims=True)
        grad_scores = (attn_weights * (grad_weights - inner)).astype(jnp.bfloat16)
        grad_query = jnp.einsum(
            "hqk,khd->qhd", grad_scores, key_heads, preferred_element_type=jnp.float32
        )
        grad_keys = grad_keys + jnp.einsum(
            "hqk,qhd->khd", grad_scores, query_block, preferred_element_type=jnp.float32
        )
        grad_values = grad_values + jnp.einsum(
            "hqk,qhd->khd",
            attn_weights.astype(jnp.bfloat16),
            grad_block,
            preferred_element_type=jnp.float32,
        )
        return ((grad_keys, grad_values), grad_query.astype(jnp.bfloat16))

    zero_keys = jnp.zeros(key_heads.shape, jnp.float32)
    (grad_keys, grad_values), grad_queries = lax.scan(
        one_block, (zero_keys, zero_keys), (query_blocks, grad_blocks, log_sums, offsets)
    )
    key_count = key_heads.shape[0]
    return (
        grad_queries.reshape(length, head_count * HEAD_DIM),
        grad_keys.reshape(key_count, head_count * HEAD_DIM).astype(jnp.bfloat16),
        grad_values.reshape(key_count, head_count * HEAD_DIM).astype(jnp.bfloat16),
    )


def local(
    tokens,
    memory,
    cotangent,
    tgt_len,
    src_len,
    self_query,
    self_key,
    self_value,
    self_out,
    cross_query,
    cross_key,
    cross_value,
    cross_out,
    ffn_up,
    ffn_down,
    gain_one,
    shift_one,
    gain_two,
    shift_two,
    gain_three,
    shift_three,
):
    row_count = tgt_len.shape[0]
    length = tokens.shape[0] // row_count
    source = memory.shape[0] // row_count
    scaling = HEAD_DIM ** (-0.5)

    def forward_rows(queries, keys, values, limits, causal, key_len):
        mixed_rows, log_rows = ([], [])
        for row_index in range(row_count):
            mixed, log_sums = attend_forward(
                queries[row_index * length : (row_index + 1) * length],
                keys[row_index * key_len : (row_index + 1) * key_len],
                values[row_index * key_len : (row_index + 1) * key_len],
                limits[row_index],
                causal,
            )
            mixed_rows.append(mixed)
            log_rows.append(log_sums)
        return (jnp.concatenate(mixed_rows, 0), log_rows)

    def backward_rows(queries, keys, values, grad_mixed, log_rows, limits, causal, key_len):
        query_rows, key_rows, value_rows = ([], [], [])
        for row_index in range(row_count):
            grad_query, grad_key, grad_value = attend_backward(
                queries[row_index * length : (row_index + 1) * length],
                keys[row_index * key_len : (row_index + 1) * key_len],
                values[row_index * key_len : (row_index + 1) * key_len],
                grad_mixed[row_index * length : (row_index + 1) * length],
                log_rows[row_index],
                limits[row_index],
                causal,
            )
            query_rows.append(grad_query)
            key_rows.append(grad_key)
            value_rows.append(grad_value)
        return (
            jnp.concatenate(query_rows, 0),
            jnp.concatenate(key_rows, 0),
            jnp.concatenate(value_rows, 0),
        )

    self_queries = (matmul(tokens, self_query) * scaling).astype(jnp.bfloat16)
    self_keys = matmul(tokens, self_key).astype(jnp.bfloat16)
    self_values = matmul(tokens, self_value).astype(jnp.bfloat16)
    self_mixed, self_logs = forward_rows(
        self_queries, self_keys, self_values, tgt_len, True, length
    )
    self_branch = lax.psum(matmul(self_mixed, self_out).astype(jnp.bfloat16), "tp").astype(
        jnp.float32
    )
    resid_one = tokens.astype(jnp.float32) + self_branch
    h_one = layer_norm(resid_one, gain_one, shift_one)
    h_one_low = h_one.astype(jnp.bfloat16)
    cross_queries = (matmul(h_one_low, cross_query) * scaling).astype(jnp.bfloat16)
    cross_keys = matmul(memory, cross_key).astype(jnp.bfloat16)
    cross_values = matmul(memory, cross_value).astype(jnp.bfloat16)
    cross_mixed, cross_logs = forward_rows(
        cross_queries, cross_keys, cross_values, src_len, False, source
    )
    cross_branch = lax.psum(matmul(cross_mixed, cross_out).astype(jnp.bfloat16), "tp").astype(
        jnp.float32
    )
    resid_two = h_one + cross_branch
    h_two = layer_norm(resid_two, gain_two, shift_two)
    h_two_low = h_two.astype(jnp.bfloat16)
    pre_act = matmul(h_two_low, ffn_up)
    activated = exact_gelu(pre_act).astype(jnp.bfloat16)
    ffn_branch = lax.psum(matmul(activated, ffn_down).astype(jnp.bfloat16), "tp").astype(
        jnp.float32
    )
    resid_three = h_two + ffn_branch
    layer_out = layer_norm(resid_three, gain_three, shift_three).astype(jnp.bfloat16)
    live_mask = (
        (jnp.arange(length)[None, :] < tgt_len[:, None])
        .astype(jnp.float32)
        .reshape(row_count * length, 1)
    )
    grad_out = cotangent.astype(jnp.float32) * live_mask
    _, norm_pull = jax.vjp(layer_norm, resid_three, gain_three, shift_three)
    d_three, grad_gain_three, grad_shift_three = norm_pull(grad_out)
    e_three = d_three.astype(jnp.bfloat16)
    grad_down = matmul_left(activated, e_three)
    _, gelu_pull = jax.vjp(exact_gelu, pre_act)
    d_pre = gelu_pull(matmul_right(e_three, ffn_down))[0].astype(jnp.bfloat16)
    grad_up = matmul_left(h_two_low, d_pre)
    d_htwo = d_three + lax.psum(matmul_right(d_pre, ffn_up).astype(jnp.bfloat16), "tp").astype(
        jnp.float32
    )
    _, norm_pull = jax.vjp(layer_norm, resid_two, gain_two, shift_two)
    d_two, grad_gain_two, grad_shift_two = norm_pull(d_htwo)
    e_two = d_two.astype(jnp.bfloat16)
    grad_cross_out = matmul_left(cross_mixed, e_two)
    d_cross_mixed = matmul_right(e_two, cross_out).astype(jnp.bfloat16)
    d_cross_q, d_cross_k, d_cross_v = backward_rows(
        cross_queries, cross_keys, cross_values, d_cross_mixed, cross_logs, src_len, False, source
    )
    d_cross_q = d_cross_q * jnp.asarray(scaling, jnp.bfloat16)
    grad_cross_query = matmul_left(h_one_low, d_cross_q)
    grad_cross_key = matmul_left(memory, d_cross_k)
    grad_cross_value = matmul_left(memory, d_cross_v)
    part_hone = matmul_right(d_cross_q, cross_query)
    part_memory = matmul_right(d_cross_k, cross_key) + matmul_right(d_cross_v, cross_value)
    sum_hone, sum_memory = (
        lax.psum(part_hone.astype(jnp.bfloat16), "tp").astype(jnp.float32),
        lax.psum(part_memory.astype(jnp.bfloat16), "tp").astype(jnp.float32),
    )
    d_hone = d_two + sum_hone
    memory_grad = sum_memory.astype(jnp.bfloat16)
    _, norm_pull = jax.vjp(layer_norm, resid_one, gain_one, shift_one)
    d_one, grad_gain_one, grad_shift_one = norm_pull(d_hone)
    e_one = d_one.astype(jnp.bfloat16)
    grad_self_out = matmul_left(self_mixed, e_one)
    d_self_mixed = matmul_right(e_one, self_out).astype(jnp.bfloat16)
    d_self_q, d_self_k, d_self_v = backward_rows(
        self_queries, self_keys, self_values, d_self_mixed, self_logs, tgt_len, True, length
    )
    d_self_q = d_self_q * jnp.asarray(scaling, jnp.bfloat16)
    grad_self_query = matmul_left(tokens, d_self_q)
    grad_self_key = matmul_left(tokens, d_self_k)
    grad_self_value = matmul_left(tokens, d_self_v)
    part_tokens = (
        matmul_right(d_self_q, self_query)
        + matmul_right(d_self_k, self_key)
        + matmul_right(d_self_v, self_value)
    )
    tokens_grad = (
        d_one + lax.psum(part_tokens.astype(jnp.bfloat16), "tp").astype(jnp.float32)
    ).astype(jnp.bfloat16)
    summed = lax.psum(
        (
            grad_self_query,
            grad_self_key,
            grad_self_value,
            grad_self_out,
            grad_cross_query,
            grad_cross_key,
            grad_cross_value,
            grad_cross_out,
            grad_up,
            grad_down,
            grad_gain_one,
            grad_shift_one,
            grad_gain_two,
            grad_shift_two,
            grad_gain_three,
            grad_shift_three,
        ),
        "dp",
    )
    return (
        layer_out,
        tokens_grad,
        memory_grad,
        summed[0],
        summed[1],
        summed[2],
        summed[3],
        summed[4],
        summed[5],
        summed[6],
        summed[7],
        summed[8],
        summed[9],
        summed[10],
        summed[11],
        summed[12],
        summed[13],
        summed[14],
        summed[15],
    )


def solution(mesh):
    return jax.shard_map(
        local,
        mesh=mesh,
        in_specs=(
            P("dp", None),
            P("dp", None),
            P("dp", None),
            P("dp"),
            P("dp"),
            P(None, "tp"),
            P(None, "tp"),
            P(None, "tp"),
            P("tp", None),
            P(None, "tp"),
            P(None, "tp"),
            P(None, "tp"),
            P("tp", None),
            P(None, "tp"),
            P("tp", None),
            P(),
            P(),
            P(),
            P(),
            P(),
            P(),
        ),
        out_specs=(
            P("dp", None),
            P("dp", None),
            P("dp", None),
            P(None, "tp"),
            P(None, "tp"),
            P(None, "tp"),
            P("tp", None),
            P(None, "tp"),
            P(None, "tp"),
            P(None, "tp"),
            P("tp", None),
            P(None, "tp"),
            P("tp", None),
            P(),
            P(),
            P(),
            P(),
            P(),
            P(),
        ),
        check_vma=False,
    )
```

profile of v0, /device:TPU:0, one launch (start us, length us, event | category | flops | bytes accessed | tf_op | source)
XLA Modules:
  0.0 1230.6 jit_solution(10704373058153287561)
XLA Ops:
  22.0 19.5 %while.108 = (s32[]{:T(128)}, bf16[2,512,3,64]{1,3,2,0:T(8,128)(2,1)}, f32[2,3,512]{2,1,0:T(4,128)S(1)}, s32[]{:T(128)}, s32[2]{0:T(128)}, /*index=5*/bf16[2,512...) while((s32[]{:T(128)}, bf16[2,512,3,64]{1,3,2,0:T(8,128)(2,1)}, ...), condition=%wide.region_3.4_spmd, body=%wide.region_0.3_spmd.sunk | while | flops 417955840 | bytes 23786640 | solution.py:78
  49.0 20.4 %while.109 = (s32[]{:T(128)}, bf16[2,512,3,64]{1,3,2,0:T(8,128)(2,1)}, f32[2,3,512]{2,1,0:T(4,128)}, s32[]{:T(128)}, s32[2]{0:T(128)}, /*index=5*/bf16[2,512,3,6...) while((s32[]{:T(128)}, bf16[2,512,3,64]{1,3,2,0:T(8,128)(2,1)}, ...), condition=%wide.region_7.8_spmd, body=%wide.region_4.7_spmd.sunk | while | flops 417955840 | bytes 23783052 | solution.py:78
  71.9 3.9 convolution_convert_fusion.8
  82.1 65.1 %all-reduce.11.cloned.1.call-done = bf16[2048,768]{1,0:T(8,128)(2,1)} async-done(((bf16[2048,768]{1,0:T(8,128)(2,1)}), bf16[2048,768]{1,0:T(8,128)(2,1)}) %all-reduce.11.cloned.1.call-update) | async-done | bytes 3145744 | tf_op jit(solution)/shard_map/psum | solution.py:202
  147.2 3.9 fusion.173
  164.6 14.6 %while.110 = (s32[]{:T(128)}, bf16[2,512,3,64]{1,3,2,0:T(8,128)(2,1)}, f32[2,3,512]{2,1,0:T(4,128)}, s32[]{:T(128)}, bf16[2,512,3,64]{1,3,2,0:T(8,128)(2,1)}, /*...) while((s32[]{:T(128)}, bf16[2,512,3,64]{1,3,2,0:T(8,128)(2,1)}, ...), condition=%wide.region_14.15_spmd, body=%wide.region_11.14_spmd.sunk | while | flops 416906752 | bytes 21683828 | solution.py:78
  186.7 14.3 %while.111 = (s32[]{:T(128)}, bf16[2,512,3,64]{1,3,2,0:T(8,128)(2,1)}, f32[2,3,512]{2,1,0:T(4,128)}, s32[]{:T(128)}, bf16[2,512,3,64]{1,3,2,0:T(8,128)(2,1)}, /*...) while((s32[]{:T(128)}, bf16[2,512,3,64]{1,3,2,0:T(8,128)(2,1)}, ...), condition=%wide.region_18.19_spmd, body=%wide.region_15.18_spmd.sunk | while | flops 416906752 | bytes 21683828 | solution.py:78
  203.3 3.9 convolution_convert_fusion.7
  207.3 68.6 %all-reduce.13.cloned.1.call-done = bf16[2048,768]{1,0:T(8,128)(2,1)} async-done(((bf16[2048,768]{1,0:T(8,128)(2,1)}), bf16[2048,768]{1,0:T(8,128)(2,1)}) %all-reduce.13.cloned.1.call-update) | async-done | bytes 3145744 | tf_op jit(solution)/shard_map/psum | solution.py:214
  275.9 5.3 fusion.217
  284.3 18.2 %multiply_convert_fusion.4 = (bf16[2048,768]{1,0:T(8,128)(2,1)S(1)}, f32[2048,768]{1,0:T(8,128)}, f32[2048,768]{1,0:T(8,128)}) fusion(bf16[2048,768]{1,0:T(8,128)(2,1)S(1)} %fusion.175, bf16[768,768]{1,0:T(8,128)(2,1)S(1)} %copy-done.126), kind=kOutput, calls=%fused_computation.223 | convolution fusion | flops 2518155264 | bytes 20054016 | tf_op jit(solution)/shard_map/dot_general | solution.py:20
  304.1 3.9 convolution_convert_fusion.5
  308.2 68.6 %all-reduce.15.cloned.1.call-done = bf16[2048,768]{1,0:T(8,128)(2,1)} async-done(((bf16[2048,768]{1,0:T(8,128)(2,1)}), bf16[2048,768]{1,0:T(8,128)(2,1)}) %all-reduce.15.cloned.1.call-update) | async-done | bytes 3145744 | tf_op jit(solution)/shard_map/psum | solution.py:222
  376.8 4.8 fusion.215
  387.1 4.7 fusion.214
  391.9 8.4 add_convert_fusion.3
  402.1 4.0 convolution_convert_fusion.4
  406.2 68.6 %all-reduce.17.cloned.1.call-done = bf16[2048,768]{1,0:T(8,128)(2,1)} async-done(((bf16[2048,768]{1,0:T(8,128)(2,1)}), bf16[2048,768]{1,0:T(8,128)(2,1)}) %all-reduce.17.cloned.1.call-update) | async-done | bytes 3145744 | tf_op jit(solution)/shard_map/psum | solution.py:240
  474.8 8.3 multiply_reduce_fusion.5
  483.1 6.2 fusion.213
  497.1 37.3 %while.112 = (s32[]{:T(128)}, f32[1024,3,64]{0,2,1:T(8,128)}, f32[1024,3,64]{0,2,1:T(8,128)}, bf16[2,512,3,64]{1,3,2,0:T(8,128)(2,1)}, bf16[2,512,3,64]{1,3,2,0:...) while((s32[]{:T(128)}, f32[1024,3,64]{0,2,1:T(8,128)}, ...), condition=%wide.region_32.33_spmd.clone, body=%wide.region_30.32_spmd.clone.sunk | while | flops 1026391552 | bytes 107597592 | solution.py:122
  505.4 3.7 fusion.399
  509.2 3.7 fusion.401
  523.4 3.9 fusion.399
  527.3 3.7 fusion.401
  541.2 36.9 %while.113 = (s32[]{:T(128)}, f32[1024,3,64]{0,2,1:T(8,128)}, f32[1024,3,64]{0,2,1:T(8,128)}, bf16[2,512,3,64]{1,3,2,0:T(8,128)(2,1)}, bf16[2,512,3,64]{1,3,2,0:...) while((s32[]{:T(128)}, f32[1024,3,64]{0,2,1:T(8,128)}, ...), condition=%wide.region_35.36_spmd.clone, body=%wide.region_33.35_spmd.clone.sunk | while | flops 1026391552 | bytes 107597592 | solution.py:122
  549.5 3.7 fusion.412
  567.2 3.9 fusion.412
  580.3 3.8 convolution_convert_fusion.6
  584.2 8.0 fusion.206
  599.5 53.3 %all-reduce.19.cloned.1.call-done = bf16[2048,768]{1,0:T(8,128)(2,1)} async-done(((bf16[2048,768]{1,0:T(8,128)(2,1)}), bf16[2048,768]{1,0:T(8,128)(2,1)}) %all-reduce.19.cloned.1.call-update) | async-done | bytes 3145744 | tf_op jit(solution)/shard_map/psum | solution.py:258
  652.9 8.3 multiply_reduce_fusion.6
  661.2 5.9 fusion.212
  675.0 41.4 %while.114 = (s32[]{:T(128)}, f32[1024,3,64]{0,2,1:T(8,128)}, f32[1024,3,64]{0,2,1:T(8,128)}, bf16[2,512,3,64]{1,3,2,0:T(8,128)(2,1)}, bf16[2,512,3,64]{1,3,2,0:...) while((s32[]{:T(128)}, f32[1024,3,64]{0,2,1:T(8,128)}, ...), condition=%wide.region_41.42_spmd.clone, body=%wide.region_39.41_spmd.clone.sunk | while | flops 1027440640 | bytes 113940368 | solution.py:122
  684.9 3.7 fusion.426
  688.7 3.7 fusion.428
  705.0 3.9 fusion.426
  708.9 3.7 fusion.428
  712.6 3.8 fusion.427
  723.0 42.7 %while.115 = (s32[]{:T(128)}, f32[1024,3,64]{0,2,1:T(8,128)}, f32[1024,3,64]{0,2,1:T(8,128)}, bf16[2,512,3,64]{1,3,2,0:T(8,128)(2,1)}, bf16[2,512,3,64]{1,3,2,0:...) while((s32[]{:T(128)}, f32[1024,3,64]{0,2,1:T(8,128)}, ...), condition=%wide.region_44.45_spmd.clone, body=%wide.region_42.44_spmd.clone.sunk | while | flops 1027440640 | bytes 113891184 | solution.py:122
  754.4 3.9 fusion.440
  761.9 3.8 fusion.441
  778.0 7.0 fusion.228
  799.5 37.7 %all-reduce = (f32[768]{0:T(1024)}, f32[768]{0:T(1024)}, f32[768]{0:T(1024)}, f32[768]{0:T(1024)}, f32[768]{0:T(1024)}, /*index=5*/f32[768]{0:T(1024)}) all-reduce(f32[768]{0:T(1024)S(1)} %copy-done.118, f32[768]{0:T(1024)S(1)} %copy-done.119, f32[768]{0:T(1024)S(1)} %copy-done.116, ...), channel_id=1, replica_groups=mesh['tp'=4,'dp'=8] {'dp'}, use_global_device_ids=true, to_apply=%region_58.59 | all-reduce | flops 4608 | bytes 36864 | tf_op jit(solution)/shard_map/psum | solution.py:283
  837.2 60.6 %all-reduce.23.cloned.1.call-done = (bf16[2048,768]{1,0:T(8,128)(2,1)}, bf16[2048,768]{1,0:T(8,128)(2,1)}) async-done(((bf16[2048,768]{1,0:T(8,128)(2,1)}, bf16[2048,768]{1,0:T(8,128)(2,1)}), (bf16[2048,768]{1,0:T(8,128)(2,1)}, bf16[2048,768]{1,0:T(8,128)(2,1)})) %all-reduce.23.cloned.1.call-update) | async-done | bytes 6291472 | tf_op jit(solution)/shard_map/psum | solution.py:281
  897.8 6.2 add_convert_fusion.1
  904.0 306.3 %all-reduce.21.cloned.1.call-done = (f32[768,192]{0,1:T(8,128)}, f32[768,192]{0,1:T(8,128)}, f32[768,192]{0,1:T(8,128)}, f32[192,768]{1,0:T(8,128)}, f32[768,192...) async-done(((f32[768,192]{0,1:T(8,128)}, f32[768,192]{0,1:T(8,128)}, ...) | async-done | bytes 9437200 | tf_op jit(solution)/shard_map/psum | solution.py:283
  1210.3 3.9 copy.198
  (592 shorter events, 316.9 us)
Async XLA Ops:
  7.2 69.8 %copy-start = (bf16[2048,768]{1,0:T(8,128)(2,1)S(1)}, bf16[2048,768]{1,0:T(8,128)(2,1)}, u32[]{:S(2)}) copy-start(bf16[2048,768]{1,0:T(8,128)(2,1)} %param.38) | copy-start | bytes 9437188
  7.2 139.9 %all-reduce.11.cloned.1.call-start = ((), (), s32[]{:S(2)}) async-start(), calls=%async_computation | async-start | bytes 6291456 | tf_op jit(solution)/shard_map/psum | solution.py:202
  75.9 200.0 %all-reduce.13.cloned.1.call-start = ((), (), s32[]{:S(2)}) async-start(), calls=%async_computation.1 | async-start | bytes 6291456 | tf_op jit(solution)/shard_map/psum | solution.py:214
  151.8 124.1 %copy-start.93 = (f32[2048]{0:T(1024)}, f32[2048]{0:T(1024)S(1)}, u32[]{:S(2)}) copy-start(f32[2048]{0:T(1024)S(1)} %broadcast_multiply_fusion.2) | copy-start | bytes 24580
  154.0 121.9 %copy-start.95 = (f32[2048]{0:T(1024)}, f32[2048]{0:T(1024)S(1)}, u32[]{:S(2)}) copy-start(f32[2048]{0:T(1024)S(1)} %fusion.187) | copy-start | bytes 24580
  207.2 169.6 %all-reduce.15.cloned.1.call-start = ((), (), s32[]{:S(2)}) async-start(), calls=%async_computation.2 | async-start | bytes 6291456 | tf_op jit(solution)/shard_map/psum | solution.py:222
  284.3 18.2 %copy-start.52 = (bf16[2048,768]{1,0:T(8,128)(2,1)}, bf16[2048,768]{1,0:T(8,128)(2,1)S(1)}, u32[]{:S(2)}) copy-start(bf16[2048,768]{1,0:T(8,128)(2,1)S(1)} %fusion.175) | copy-start | bytes 9437188
  284.3 19.8 %copy-start.124 = (bf16[768,768]{1,0:T(8,128)(2,1)S(1)}, bf16[768,768]{1,0:T(8,128)(2,1)}, u32[]{:S(2)}) copy-start(bf16[768,768]{1,0:T(8,128)(2,1)} %param.51) | copy-start | bytes 3538948
  308.1 166.7 %all-reduce.17.cloned.1.call-start = ((), (), s32[]{:S(2)}) async-start(), calls=%async_computation.3 | async-start | bytes 6291456 | tf_op jit(solution)/shard_map/psum | solution.py:240
  383.5 8.4 slice-start.4
  391.9 8.5 copy-start.26
  391.9 91.2 %copy-start.104 = (f32[2048]{0:T(1024)}, f32[2048]{0:T(1024)S(1)}, u32[]{:S(2)}) copy-start(f32[2048]{0:T(1024)S(1)} %negate_multiply_fusion.3) | copy-start | bytes 24580
  391.9 10.2 copy-start.127
  406.1 246.8 %all-reduce.19.cloned.1.call-start = ((), (), s32[]{:S(2)}) async-start(), calls=%async_computation.4 | async-start | bytes 6291456 | tf_op jit(solution)/shard_map/psum | solution.py:258
  474.8 8.3 copy-start.47
  483.1 8.9 copy-start.73
  497.1 44.1 %copy-start.25 = (bf16[1024,3,64]{0,2,1:T(8,128)(2,1)S(1)}, bf16[1024,3,64]{0,2,1:T(8,128)(2,1)}, u32[]{:S(2)}) copy-start(bf16[1024,3,64]{0,2,1:T(8,128)(2,1)} %copy-done.24) | copy-start | bytes 1179652
  523.4 7.6 copy-start.6
  523.4 7.6 copy-start.42
  567.2 7.6 copy-start.8
  567.2 7.6 copy-start.44
  584.1 11.6 copy-start.86
  584.1 313.7 %all-reduce.23.cloned.1.call-start = ((), (), s32[]{:S(2)}) async-start(), calls=%async_computation.6 | async-start | bytes 12582912 | tf_op jit(solution)/shard_map/psum | solution.py:281
  584.2 10.6 copy-start.28
  584.2 10.7 copy-start.27
  596.7 56.1 %copy-start.94 = (f32[2048]{0:T(1024)S(1)}, f32[2048]{0:T(1024)}, u32[]{:S(2)}) copy-start(f32[2048]{0:T(1024)} %copy-done.93) | copy-start | bytes 24580
  596.8 56.1 %copy-start.96 = (f32[2048]{0:T(1024)S(1)}, f32[2048]{0:T(1024)}, u32[]{:S(2)}) copy-start(f32[2048]{0:T(1024)} %copy-done.95) | copy-start | bytes 24580
  596.8 56.1 %copy-start.98 = (f32[2048]{0:T(1024)S(1)}, f32[2048]{0:T(1024)}, u32[]{:S(2)}) copy-start(f32[2048]{0:T(1024)} %copy-done.97) | copy-start | bytes 24580
  596.8 56.1 %copy-start.110 = (f32[768]{0:T(1024)S(1)}, f32[768]{0:T(1024)}, u32[]{:S(2)}) copy-start(f32[768]{0:T(1024)} %param.52) | copy-start | bytes 9220
  599.5 61.6 %copy-start.107 = (f32[2048]{0:T(1024)S(1)}, f32[2048]{0:T(1024)}, u32[]{:S(2)}) copy-start(f32[2048]{0:T(1024)} %copy-done.106) | copy-start | bytes 24580
  652.8 8.3 copy-start.17
  652.8 8.3 copy-start.20
  652.9 8.3 copy-start.46
  661.2 8.7 copy-start.74
  667.2 7.8 copy-start.129
  675.0 48.0 %copy-start.23 = (bf16[1024,3,64]{0,2,1:T(8,128)(2,1)S(1)}, bf16[1024,3,64]{0,2,1:T(8,128)(2,1)}, u32[]{:S(2)}) copy-start(bf16[1024,3,64]{0,2,1:T(8,128)(2,1)} %copy-done.22) | copy-start | bytes 1179652
  705.0 7.6 copy-start.2
  705.0 7.6 copy-start.11
  705.0 7.6 copy-start.40
  754.4 7.5 copy-start.38
  767.0 8.0 copy-start.71
  777.8 432.5 %all-reduce.21.cloned.1.call-start = ((), (), s32[]{:S(2)}) async-start(), calls=%async_computation.5 | async-start | bytes 18874368 | tf_op jit(solution)/shard_map/psum | solution.py:283
  778.0 8.7 copy-start.62
  778.0 8.7 copy-start.64
  1210.3 8.0 copy-start.77
  1210.3 8.8 copy-start.76
  1210.3 9.7 copy-start.75
  1210.3 10.5 copy-start.54
  (126 other events, 517.6 us)
Sparse Core Ops, SparseCore 0:
  76.0 71.1 all-reduce.10
  207.3 68.5 all-reduce.12
  308.2 68.5 all-reduce.14
  406.2 68.5 all-reduce.16
  584.2 68.5 all-reduce.18
  777.9 119.8 all-reduce.22
  905.2 305.0 all-reduce.20
where the time goes:
time: 1240 us; the launch traced here: 1230 us
  waiting for transfers between devices  691 us (56%)
  matrix products  255 us (21%)
  other arithmetic  129 us (10%)
  local copies, waits for them, and re-layouts  99.8 us (8%)
  blocking collectives  37.7 us (3%)
  between operations  15.7 us (1%)
    psum x1, waiting for transfers between devices, local(): lax.psum((grad_self_query, grad_self_key, grad_self_value, grad_self_out,...  306 us
    psum x1, waiting for transfers between devices, local(): lax.psum(matmul(cross_mixed, cross_out).astype(jnp.bfloat16), 'tp')  68.6 us
    psum x1, waiting for transfers between devices, local(): lax.psum(matmul_right(d_pre, ffn_up).astype(jnp.bfloat16), 'tp')  68.6 us
    psum x1, waiting for transfers between devices, local(): lax.psum(matmul(activated, ffn_down).astype(jnp.bfloat16), 'tp')  68.6 us
    psum x1, waiting for transfers between devices, local(): lax.psum(matmul(self_mixed, self_out).astype(jnp.bfloat16), 'tp')  65.1 us
    psum x1, waiting for transfers between devices, local(): lax.psum(part_tokens.astype(jnp.bfloat16), 'tp').astype(jnp.float32)  60.6 us
    psum x1, waiting for transfers between devices, local(): lax.psum(part_hone.astype(jnp.bfloat16), 'tp').astype(jnp.float32)  53.3 us
    dot_general x10, matrix products, matmul(): return jnp.dot(left, right, preferred_element_type=jnp.float32)  42.4 us
  transfers between devices with their start and end apart: 7, of which 7 were waited for; matrix products, arithmetic and copies ran while one was open for 4% of the time, Pallas kernels for 0%

commit v1 on v0

v1 whole, which is shorter than its diff:
```python
import functools

import jax
import jax.numpy as jnp
from jax import lax
from jax.experimental import pallas as pl
from jax.experimental.pallas import tpu as pltpu
from jax.sharding import PartitionSpec as P

HEAD_DIM = 64
WIDE = 2 * HEAD_DIM
EPS = 1e-05
MASKED = -1e30
LOG2E = 1.4426950408889634
LN2 = 0.6931471805599453
f32 = jnp.float32
bf16 = jnp.bfloat16

CORE = [(0, 1), (1, 0), (2, 3), (3, 2)]
ACROSS = [(0, 2), (2, 0), (1, 3), (3, 1)]
MIB = 1 << 20


def nn(left, right):
    return lax.dot_general(left, right, (((1,), (0,)), ((), ())), preferred_element_type=f32)


def nt(left, right):
    return lax.dot_general(left, right, (((1,), (1,)), ((), ())), preferred_element_type=f32)


def tn(left, right):
    return lax.dot_general(left, right, (((0,), (0,)), ((), ())), preferred_element_type=f32)


def lanes(rows):
    return lax.broadcasted_iota(jnp.int32, (rows, HEAD_DIM), 1)


def three_parts(value):
    high = value.astype(bf16).astype(f32)
    rest = value - high
    middle = rest.astype(bf16).astype(f32)
    return high, middle, rest - middle


def fill_queries(q_ref, rows, count, acc, heads):
    tail = jnp.where(lanes(count) == 0, 1.0, 0.0)
    for h in range(heads):
        part = acc[:, h * HEAD_DIM : (h + 1) * HEAD_DIM]
        q_ref[h, rows, :] = jnp.concatenate([part, tail], 1).astype(bf16)


def fill_keys(k_ref, v_ref, rows, start, count, acc, heads, limit):
    lane = lanes(count)
    index = start + lax.broadcasted_iota(jnp.int32, (count, HEAD_DIM), 0)
    tail = jnp.where(lane == 0, jnp.where(index < limit, 0.0, MASKED), jnp.where(lane < 4, 1.0, 0.0))
    ones = jnp.ones((count, HEAD_DIM), f32)
    for h in range(heads):
        k = acc[:, h * HEAD_DIM : (h + 1) * HEAD_DIM]
        v = acc[:, (heads + h) * HEAD_DIM : (heads + h + 1) * HEAD_DIM]
        k_ref[h, rows, :] = jnp.concatenate([k, tail], 1).astype(bf16)
        v_ref[h, rows, :] = jnp.concatenate([v, ones], 1).astype(bf16)


def attend_block(q_ref, k_ref, v_ref, att_ref, h, column, rows, count, key_end, causal):
    s = nt(q_ref[h, rows, :], k_ref[h, :key_end, :])
    if causal:
        r = lax.broadcasted_iota(jnp.int32, (count, count), 0)
        c = lax.broadcasted_iota(jnp.int32, (count, count), 1)
        diagonal = jnp.where(c <= r, s[:, key_end - count :], MASKED)
        s = diagonal if key_end == count else jnp.concatenate([s[:, : key_end - count], diagonal], 1)
    peak = jnp.max(s, 1, keepdims=True)
    p = jnp.exp2(s - peak).astype(bf16)
    o = nn(p, v_ref[h, :key_end, :])
    total = o[:, HEAD_DIM : HEAD_DIM + 1]
    att_ref[rows, column : column + HEAD_DIM] = (o[:, :HEAD_DIM] / total).astype(bf16)
    high, middle, low = three_parts(-(peak + jnp.log2(total)))
    lane = lanes(count)
    tail = jnp.where(
        lane == 0, 1.0, jnp.where(lane == 1, high, jnp.where(lane == 2, middle, jnp.where(lane == 3, low, 0.0)))
    )
    q_ref[h, rows, HEAD_DIM:] = tail.astype(bf16)


def fill_grads(do_ref, rows, count, grad, att, heads):
    lane = lanes(count)
    for h in range(heads):
        part = grad[:, h * HEAD_DIM : (h + 1) * HEAD_DIM].astype(bf16)
        mixed = att[:, h * HEAD_DIM : (h + 1) * HEAD_DIM].astype(f32)
        inner = jnp.sum(part.astype(f32) * mixed, 1, keepdims=True)
        high, middle, low = three_parts(-inner)
        tail = jnp.where(lane == 0, high, jnp.where(lane == 1, middle, jnp.where(lane == 2, low, 0.0)))
        do_ref[h, rows, :] = jnp.concatenate([part, tail.astype(bf16)], 1)


def back_block(q_ref, k_ref, v_ref, do_ref, dq_ref, dk_ref, dv_ref, h, rows, count, key_end, causal, first):
    q = q_ref[h, rows, :]
    d = do_ref[h, rows, :]
    k = k_ref[h, :key_end, :]
    v = v_ref[h, :key_end, :]
    p = jnp.exp2(nt(k, q))
    if causal:
        r = lax.broadcasted_iota(jnp.int32, (count, count), 0)
        c = lax.broadcasted_iota(jnp.int32, (count, count), 1)
        diagonal = jnp.where(r <= c, p[key_end - count :], 0.0)
        p = diagonal if key_end == count else jnp.concatenate([p[: key_end - count], diagonal], 0)
    ds = (p * nt(v, d)).astype(bf16)
    dv = nn(p.astype(bf16), d)
    dk = nn(ds, q)
    if first:
        dv_ref[h, :key_end, :] = dv
        dk_ref[h, :key_end, :] = dk
    else:
        dv_ref[h, :key_end, :] += dv
        dk_ref[h, :key_end, :] += dk
    dq_ref[h, rows, :] = tn(k, ds).T


def pack_heads(source, rows, heads, factor):
    return jnp.concatenate([source[h, rows, :HEAD_DIM] * factor for h in range(heads)], 1).astype(bf16)


def norm(resid):
    center = resid - jnp.mean(resid, -1, keepdims=True)
    scale = lax.rsqrt(jnp.mean(center * center, -1, keepdims=True) + EPS)
    return center * scale, scale


def norm_back(grad, gain, unit, scale):
    lifted = grad * gain
    first = jnp.mean(lifted, -1, keepdims=True)
    second = jnp.mean(lifted * unit, -1, keepdims=True)
    return scale * (lifted - first - unit * second)


def gelu_pair(value):
    scaled = value * 0.7071067811865476
    density = jnp.exp(-scaled * scaled) * 0.3989422804014327
    below = 0.5 * (1.0 + lax.erf(scaled))
    return value * below, below + value * density


BLOCK = 512


def self_forward_kernel(s_ref, x_ref, w_ref, *rest, heads, second):
    if second:
        att_own_ref, out_own_ref, out_ref, part_ref, q_ref, k_ref, v_ref, att_ref = rest
    else:
        m_ref, ckv_ref, ck_ref, cv_ref, q_ref, k_ref, v_ref, att_ref = rest
    row = s_ref[0]
    limit = s_ref[1 + row]
    length = x_ref.shape[0]
    each = heads * HEAD_DIM

    @pl.loop(0, length, step=BLOCK)
    def _(start):
        rows = pl.ds(pl.multiple_of(start, BLOCK), BLOCK)
        acc = nn(x_ref[rows, :], w_ref[...])
        fill_queries(q_ref, rows, BLOCK, acc[:, :each] * (HEAD_DIM ** (-0.5) * LOG2E), heads)
        fill_keys(k_ref, v_ref, rows, start, BLOCK, acc[:, each:], heads, limit)

    for block in range(length // BLOCK):
        for h in range(heads):
            attend_block(
                q_ref, k_ref, v_ref, att_ref, h, h * HEAD_DIM, pl.ds(block * BLOCK, BLOCK), BLOCK, (block + 1) * BLOCK, True
            )
    if second:

        @pl.loop(0, length, step=BLOCK)
        def _(start):
            rows = pl.ds(pl.multiple_of(start, BLOCK), BLOCK)
            part = nn(att_own_ref[rows, :], out_own_ref[...]) + nn(att_ref[rows, :], out_ref[...])
            part_ref[rows, :] = part.astype(bf16)
    else:
        source = m_ref.shape[0]

        @pl.loop(0, source, step=BLOCK)
        def _(start):
            rows = pl.ds(pl.multiple_of(start, BLOCK), BLOCK)
            acc = nn(m_ref[rows, :], ckv_ref[...])
            fill_keys(ck_ref, cv_ref, rows, start, BLOCK, acc, heads, s_ref[3 + row])


def memory_keys_kernel(s_ref, m_ref, w_ref, k_ref, v_ref, *, heads):
    row = s_ref[0]

    @pl.loop(0, m_ref.shape[0], step=BLOCK)
    def _(start):
        rows = pl.ds(pl.multiple_of(start, BLOCK), BLOCK)
        fill_keys(k_ref, v_ref, rows, start, BLOCK, nn(m_ref[rows, :], w_ref[...]), heads, s_ref[3 + row])


def cross_forward_kernel(
    s_ref, x_ref, pa_ref, pb_ref, gain_ref, shift_ref, wqa_ref, wqb_ref, ka_ref, va_ref, kb_ref, vb_ref, oa_ref, ob_ref,
    part_ref, h_ref, hl_ref, unit_ref, scale_ref, qa_ref, qb_ref, atta_ref, attb_ref, *, heads,
):
    row = s_ref[0]
    limit = s_ref[3 + row]
    length = x_ref.shape[0]
    source = ka_ref.shape[1]

    @pl.loop(0, length, step=BLOCK)
    def _(start):
        rows = pl.ds(pl.multiple_of(start, BLOCK), BLOCK)
        resid = x_ref[rows, :].astype(f32) + (pa_ref[rows, :].astype(f32) + pb_ref[rows, :].astype(f32))
        unit, scale = norm(resid)
        h = unit * gain_ref[...] + shift_ref[...]
        h_ref[rows, :] = h
        unit_ref[rows, :] = unit.astype(bf16)
        scale_ref[rows, :] = scale
        low = h.astype(bf16)
        hl_ref[rows, :] = low
        factor = HEAD_DIM ** (-0.5) * LOG2E
        fill_queries(qa_ref, rows, BLOCK, nn(low, wqa_ref[...]) * factor, heads)
        fill_queries(qb_ref, rows, BLOCK, nn(low, wqb_ref[...]) * factor, heads)

    step = 256
    live = (limit + step - 1) // step
    for count in range(1, source // step + 1):

        @pl.when(live == count)
        def _():
            for q_ref, k_ref, v_ref, att_ref in ((qa_ref, ka_ref, va_ref, atta_ref), (qb_ref, kb_ref, vb_ref, attb_ref)):

                @pl.loop(0, length, step=BLOCK)
                def _(start):
                    rows = pl.ds(pl.multiple_of(start, BLOCK), BLOCK)
                    for h in range(heads):
                        attend_block(q_ref, k_ref, v_ref, att_ref, h, h * HEAD_DIM, rows, BLOCK, count * step, False)

    @pl.loop(0, length, step=BLOCK)
    def _(start):
        rows = pl.ds(pl.multiple_of(start, BLOCK), BLOCK)
        part_ref[rows, :] = (nn(atta_ref[rows, :], oa_ref[...]) + nn(attb_ref[rows, :], ob_ref[...])).astype(bf16)


def ffn_forward_kernel(
    h_in_ref, pa_ref, pb_ref, gain_ref, shift_ref, upa_ref, upb_ref, downa_ref, downb_ref,
    part_ref, h_ref, hl_ref, unit_ref, scale_ref, acta_ref, actb_ref, slopea_ref, slopeb_ref,
):
    length = h_in_ref.shape[0]
    span = 256

    @pl.loop(0, length, step=span)
    def _(start):
        rows = pl.ds(pl.multiple_of(start, span), span)
        resid = h_in_ref[rows, :] + (pa_ref[rows, :].astype(f32) + pb_ref[rows, :].astype(f32))
        unit, scale = norm(resid)
        h = unit * gain_ref[...] + shift_ref[...]
        h_ref[rows, :] = h
        unit_ref[rows, :] = unit.astype(bf16)
        scale_ref[rows, :] = scale
        low = h.astype(bf16)
        hl_ref[rows, :] = low
        part = None
        for up_ref, down_ref, act_ref, slope_ref in (
            (upa_ref, downa_ref, acta_ref, slopea_ref),
            (upb_ref, downb_ref, actb_ref, slopeb_ref),
        ):
            act, slope = gelu_pair(nn(low, up_ref[...]))
            act = act.astype(bf16)
            act_ref[rows, :] = act
            slope_ref[rows, :] = slope.astype(bf16)
            term = nn(act, down_ref[...])
            part = term if part is None else part + term
        part_ref[rows, :] = part.astype(bf16)


def ffn_back_kernel(
    s_ref, h_ref, pa_ref, pb_ref, cot_ref, gain_ref, shift_ref, upa_ref, upb_ref, downa_ref, downb_ref, slopea_ref, slopeb_ref,
    part_ref, out_ref, d_ref, e_ref, prea_ref, preb_ref, sums_ref,
):
    row = s_ref[0]
    limit = s_ref[1 + row]
    length = h_ref.shape[0]
    span = 256
    sums_ref[...] = jnp.zeros_like(sums_ref)

    @pl.loop(0, length, step=span)
    def _(start):
        rows = pl.ds(pl.multiple_of(start, span), span)
        resid = h_ref[rows, :] + (pa_ref[rows, :].astype(f32) + pb_ref[rows, :].astype(f32))
        unit, scale = norm(resid)
        out_ref[rows, :] = (unit * gain_ref[...] + shift_ref[...]).astype(bf16)
        index = start + lax.broadcasted_iota(jnp.int32, (span, 1), 0)
        grad = jnp.where(index < limit, cot_ref[rows, :].astype(f32), 0.0)
        sums_ref[0:1, :] += jnp.sum(grad * unit, 0, keepdims=True)
        sums_ref[1:2, :] += jnp.sum(grad, 0, keepdims=True)
        d = norm_back(grad, gain_ref[...], unit, scale)
        d_ref[rows, :] = d
        e = d.astype(bf16)
        e_ref[rows, :] = e
        part = None
        for up_ref, down_ref, slope_ref, pre_ref in (
            (upa_ref, downa_ref, slopea_ref, prea_ref),
            (upb_ref, downb_ref, slopeb_ref, preb_ref),
        ):
            pre = (nt(e, down_ref[...]) * slope_ref[rows, :].astype(f32)).astype(bf16)
            pre_ref[rows, :] = pre
            term = nt(pre, up_ref[...])
            part = term if part is None else part + term
        part_ref[rows, :] = part.astype(bf16)


def ffn_grad_kernel(h_ref, act_ref, e_ref, pre_ref, grad_ref):
    step = 256
    for start in range(0, grad_ref.shape[1], step):
        columns = slice(start, start + step)
        grad_ref[0, columns, :] = tn(h_ref[:, columns], pre_ref[...]).astype(bf16)
        grad_ref[1, columns, :] = tn(act_ref[:, columns], e_ref[...]).astype(bf16)


def norm_attention_back(
    d_in_ref, pa_ref, pb_ref, gain_ref, unit_ref, scale_ref, groups, d_ref, e_ref, sums_ref, do_ref, heads
):
    length = d_in_ref.shape[0]
    sums_ref[...] = jnp.zeros_like(sums_ref)

    @pl.loop(0, length, step=BLOCK)
    def _(start):
        rows = pl.ds(pl.multiple_of(start, BLOCK), BLOCK)
        grad = d_in_ref[rows, :] + (pa_ref[rows, :].astype(f32) + pb_ref[rows, :].astype(f32))
        unit = unit_ref[rows, :].astype(f32)
        sums_ref[0:1, :] += jnp.sum(grad * unit, 0, keepdims=True)
        sums_ref[1:2, :] += jnp.sum(grad, 0, keepdims=True)
        d = norm_back(grad, gain_ref[...], unit, scale_ref[rows, :])
        d_ref[rows, :] = d
        e = d.astype(bf16)
        e_ref[rows, :] = e
        for g, (out_ref, att_ref) in enumerate(groups):
            fill_grads(do_ref.at[g], rows, BLOCK, nt(e, out_ref[...]), att_ref[rows, :], heads)


def cross_back_kernel(
    s_ref, d_in_ref, pa_ref, pb_ref, gain_ref, unit_ref, scale_ref, oa_ref, ob_ref, atta_ref, attb_ref,
    qa_ref, qb_ref, ka_ref, va_ref, kb_ref, vb_ref, wqa_ref, wqb_ref,
    part_ref, d_ref, e_ref, sums_ref, dqa_ref, dqb_ref, dkva_ref, dkvb_ref, do_ref, dq_ref, dk_ref, dv_ref, *, heads,
):
    row = s_ref[0]
    limit = s_ref[3 + row]
    length = d_in_ref.shape[0]
    source = ka_ref.shape[1]
    norm_attention_back(
        d_in_ref, pa_ref, pb_ref, gain_ref, unit_ref, scale_ref, ((oa_ref, atta_ref), (ob_ref, attb_ref)),
        d_ref, e_ref, sums_ref, do_ref, heads,
    )
    step = 256
    live = (limit + step - 1) // step
    for g, (q_ref, k_ref, v_ref, dqo_ref, dkv_ref) in enumerate(
        ((qa_ref, ka_ref, va_ref, dqa_ref, dkva_ref), (qb_ref, kb_ref, vb_ref, dqb_ref, dkvb_ref))
    ):
        for count in range(1, source // step + 1):

            @pl.when(live == count)
            def _():
                key_end = count * step

                @pl.loop(0, heads)
                def _(h):
                    for block in range(length // BLOCK):
                        back_block(
                            q_ref, k_ref, v_ref, do_ref.at[g], dq_ref, dk_ref, dv_ref, h,
                            pl.ds(block * BLOCK, BLOCK), BLOCK, key_end, False, block == 0,
                        )
                    if key_end < source:
                        dk_ref[h, key_end:, :] = jnp.zeros((source - key_end, WIDE), f32)
                        dv_ref[h, key_end:, :] = jnp.zeros((source - key_end, WIDE), f32)

        @pl.loop(0, length, step=BLOCK)
        def _(start):
            rows = pl.ds(pl.multiple_of(start, BLOCK), BLOCK)
            dqo_ref[rows, :] = pack_heads(dq_ref, rows, heads, HEAD_DIM ** (-0.5))

        @pl.loop(0, source, step=BLOCK)
        def _(start):
            rows = pl.ds(pl.multiple_of(start, BLOCK), BLOCK)
            dkv_ref[rows, :] = jnp.concatenate([pack_heads(dk_ref, rows, heads, LN2), pack_heads(dv_ref, rows, heads, 1.0)], 1)

    @pl.loop(0, length, step=BLOCK)
    def _(start):
        rows = pl.ds(pl.multiple_of(start, BLOCK), BLOCK)
        part_ref[rows, :] = (nt(dqa_ref[rows, :], wqa_ref[...]) + nt(dqb_ref[rows, :], wqb_ref[...])).astype(bf16)


def cross_grad_kernel(s_ref, h_ref, m_ref, att_ref, e_ref, dq_ref, dkv_ref, gq_ref, gkv_ref, go_ref):
    gq_ref[...] = tn(h_ref[...], dq_ref[...]).astype(bf16)
    gkv_ref[...] = tn(m_ref[...], dkv_ref[...]).astype(bf16)
    go_ref[...] = tn(att_ref[...], e_ref[...]).astype(bf16)


def pair_kernel(a_ref, b_ref, wa_ref, wb_ref, part_ref):
    @pl.loop(0, a_ref.shape[0], step=BLOCK)
    def _(start):
        rows = pl.ds(pl.multiple_of(start, BLOCK), BLOCK)
        part_ref[rows, :] = (nt(a_ref[rows, :], wa_ref[...]) + nt(b_ref[rows, :], wb_ref[...])).astype(bf16)


def self_back_heads(q_ref, k_ref, v_ref, do_ref, dq_ref, dk_ref, dv_ref, dqkv_ref, length, heads):
    block = 256

    @pl.loop(0, heads)
    def _(h):
        for at in reversed(range(length // block)):
            back_block(
                q_ref, k_ref, v_ref, do_ref, dq_ref, dk_ref, dv_ref, h,
                pl.ds(at * block, block), block, (at + 1) * block, True, at == length // block - 1,
            )

    @pl.loop(0, length, step=BLOCK)
    def _(start):
        rows = pl.ds(pl.multiple_of(start, BLOCK), BLOCK)
        dqkv_ref[rows, :] = jnp.concatenate(
            [
                pack_heads(dq_ref, rows, heads, HEAD_DIM ** (-0.5)),
                pack_heads(dk_ref, rows, heads, LN2),
                pack_heads(dv_ref, rows, heads, 1.0),
            ],
            1,
        )


def self_back_first_kernel(
    s_ref, x_ref, d_in_ref, pa_ref, pb_ref, gain_ref, unit_ref, scale_ref, oa_ref, ob_ref, atta_ref, attb_ref,
    q_ref, k_ref, v_ref,
    d_ref, e_ref, sums_ref, do_out_ref, dqkv_ref, gw_ref, go_ref, do_ref, dq_ref, dk_ref, dv_ref, *, heads,
):
    length = d_in_ref.shape[0]
    norm_attention_back(
        d_in_ref, pa_ref, pb_ref, gain_ref, unit_ref, scale_ref, ((oa_ref, atta_ref), (ob_ref, attb_ref)),
        d_ref, e_ref, sums_ref, do_ref, heads,
    )
    do_out_ref[...] = do_ref[0]
    self_back_heads(q_ref, k_ref, v_ref, do_ref.at[1], dq_ref, dk_ref, dv_ref, dqkv_ref, length, heads)
    gw_ref[...] = tn(x_ref[...], dqkv_ref[...]).astype(bf16)
    go_ref[...] = tn(attb_ref[...], e_ref[...]).astype(bf16)


def self_back_second_kernel(
    s_ref, x_ref, e_ref, att_ref, q_ref, k_ref, v_ref, do_ref, dqkv_ref, gw_ref, go_ref, dq_ref, dk_ref, dv_ref, *, heads
):
    self_back_heads(q_ref, k_ref, v_ref, do_ref, dq_ref, dk_ref, dv_ref, dqkv_ref, x_ref.shape[0], heads)
    gw_ref[...] = tn(x_ref[...], dqkv_ref[...]).astype(bf16)
    go_ref[...] = tn(att_ref[...], e_ref[...]).astype(bf16)


class Row:
    def __init__(self, array, length):
        self.array = array
        self.length = length


def call(kernel, name, inputs, outputs, scalars=None, scratch=(), micros=5.0, limit=48):
    specs, arrays = [], []
    for item in inputs:
        if isinstance(item, Row):
            specs.append(pl.BlockSpec((item.length, item.array.shape[1]), lambda i, s: (s[0], 0)))
            arrays.append(item.array)
        else:
            rank = item.ndim
            specs.append(pl.BlockSpec(item.shape, functools.partial(lambda rank, *a: (0,) * rank, rank)))
            arrays.append(item)
    shapes = [jax.ShapeDtypeStruct(shape, dtype) for shape, dtype in outputs]
    out_specs = [
        pl.BlockSpec(shape, functools.partial(lambda rank, *a: (0,) * rank, len(shape))) for shape, _ in outputs
    ]
    moved = sum(a.size * a.dtype.itemsize for a in arrays) + sum(s.size * s.dtype.itemsize for s in shapes)
    settings = dict(
        out_shape=shapes,
        compiler_params=pltpu.CompilerParams(vmem_limit_bytes=limit * MIB, dimension_semantics=("arbitrary",)),
        cost_estimate=pl.CostEstimate(flops=int(micros * 1.0e9), bytes_accessed=int(moved), transcendentals=0),
        name=name,
    )
    if scalars is None:
        return pl.pallas_call(
            kernel, grid=(1,), in_specs=specs, out_specs=out_specs, scratch_shapes=list(scratch), **settings
        )(*arrays)
    grid_spec = pltpu.PrefetchScalarGridSpec(
        num_scalar_prefetch=1, grid=(1,), in_specs=specs, out_specs=out_specs, scratch_shapes=list(scratch)
    )
    return pl.pallas_call(kernel, grid_spec=grid_spec, **settings)(scalars, *arrays)


def sum_over_dp(buffer, order, size):
    index = lax.axis_index("dp")
    pieces = buffer
    for bit in order:
        take = (index // (1 << bit)) % 2 == 1
        half = pieces.shape[0] // 2
        low, high = pieces[:half], pieces[half:]
        partner = [(i, i ^ (1 << bit)) for i in range(size)]
        got = lax.ppermute(jnp.where(take, low, high), "dp", partner)
        pieces = (jnp.where(take, high, low).astype(f32) + got.astype(f32)).astype(bf16)
    for bit in reversed(order):
        take = (index // (1 << bit)) % 2 == 1
        partner = [(i, i ^ (1 << bit)) for i in range(size)]
        got = lax.ppermute(pieces, "dp", partner)
        pieces = jnp.concatenate([jnp.where(take, got, pieces), jnp.where(take, pieces, got)], 0)
    return pieces


def local(
    size, tokens, memory, cotangent, tgt_len, src_len, self_query, self_key, self_value, self_out,
    cross_query, cross_key, cross_value, cross_out, ffn_up, ffn_down,
    gain_one, shift_one, gain_two, shift_two, gain_three, shift_three,
):
    width = tokens.shape[1]
    length = tokens.shape[0] // 2
    source = memory.shape[0] // 2
    each = self_query.shape[1]
    heads = each // HEAD_DIM
    hidden = ffn_up.shape[1]
    place = lax.axis_index("tp")
    row = place // 2
    core = place % 2
    scalars = jnp.concatenate([row.astype(jnp.int32).reshape(1), tgt_len, src_len])
    gain_one, shift_one, gain_two, shift_two, gain_three, shift_three = (
        v.reshape(1, width) for v in (gain_one, shift_one, gain_two, shift_two, gain_three, shift_three)
    )
    x = Row(tokens, length)
    mem = Row(memory, source)

    def across(value):
        return lax.ppermute(value, "tp", ACROSS)

    def sibling(value):
        return lax.ppermute(value, "tp", CORE)

    w_a = jnp.concatenate([self_query, self_key, self_value], 1)
    w_b = across(w_a)
    ckv_a = jnp.concatenate([cross_key, cross_value], 1)
    so_a, cq_a, co_a, up_a, down_a = self_out, cross_query, cross_out, ffn_up, ffn_down
    so_b = across(so_a)
    ckv_b = across(ckv_a)
    cq_b = across(cq_a)
    co_b = across(co_a)
    up_b = across(up_a)
    down_b = across(down_a)

    head_shape = ((heads, length, WIDE), bf16)
    key_shape = ((heads, source, WIDE), bf16)
    low = ((length, width), bf16)
    full = ((length, width), f32)
    column = ((length, 1), f32)
    att_shape = ((length, each), bf16)
    sums = ((8, width), f32)

    ck_a, cv_a, q_a, k_a, v_a, att_a = call(
        functools.partial(self_forward_kernel, heads=heads, second=False), "self_forward_own",
        [x, w_a, mem, ckv_a], [key_shape, key_shape, head_shape, head_shape, head_shape, att_shape], scalars, micros=10,
    )
    part, q_b, k_b, v_b, att_b = call(
        functools.partial(self_forward_kernel, heads=heads, second=True), "self_forward_other",
        [x, w_b, att_a, so_a, so_b], [low, head_shape, head_shape, head_shape, att_shape], scalars, micros=9,
    )
    part_other = sibling(part)
    ck_b, cv_b = call(
        functools.partial(memory_keys_kernel, heads=heads), "memory_keys_other", [mem, ckv_b], [key_shape, key_shape], scalars,
        micros=3,
    )
    part, h_one, h_one_low, unit_one, scale_one, cq_rows_a, cq_rows_b, catt_a, catt_b = call(
        functools.partial(cross_forward_kernel, heads=heads), "cross_forward",
        [x, part, part_other, gain_one, shift_one, cq_a, cq_b, ck_a, cv_a, ck_b, cv_b, co_a, co_b],
        [low, full, low, low, column, head_shape, head_shape, att_shape, att_shape], scalars, micros=18,
    )
    part_other = sibling(part)
    hid = ((length, hidden), bf16)
    part, h_two, h_two_low, unit_two, scale_two, act_a, act_b, slope_a, slope_b = call(
        ffn_forward_kernel, "ffn_forward",
        [h_one, part, part_other, gain_two, shift_two, up_a, up_b, down_a, down_b],
        [low, full, low, low, column, hid, hid, hid, hid], micros=12,
    )
    part_other = sibling(part)
    part, out_row, d_three, e_three, pre_a, pre_b, sums_three = call(
        ffn_back_kernel, "ffn_back",
        [h_two, part, part_other, Row(cotangent, length), gain_three, shift_three, up_a, up_b, down_a, down_b, slope_a, slope_b],
        [low, low, full, low, hid, hid, sums], scalars, micros=12,
    )
    part_other = sibling(part)
    ffn_shape = ((2, width, hidden), bf16)
    (gf_b,) = call(ffn_grad_kernel, "ffn_grad_other", [h_two_low, act_b, e_three, pre_b], [ffn_shape], micros=4)
    gf_b_got = across(gf_b)
    (gf_a,) = call(ffn_grad_kernel, "ffn_grad_own", [h_two_low, act_a, e_three, pre_a], [ffn_shape], micros=4)

    back_scratch = [
        pltpu.VMEM((2, heads, length, WIDE), bf16),
        pltpu.VMEM((heads, length, WIDE), f32),
        pltpu.VMEM((heads, source, WIDE), f32),
        pltpu.VMEM((heads, source, WIDE), f32),
    ]
    dkv_shape = ((source, 2 * each), bf16)
    part, d_two, e_two, sums_two, dcq_a, dcq_b, dckv_a, dckv_b = call(
        functools.partial(cross_back_kernel, heads=heads), "cross_back",
        [
            d_three, part, part_other, gain_two, unit_two, scale_two, co_a, co_b, catt_a, catt_b,
            cq_rows_a, cq_rows_b, ck_a, cv_a, ck_b, cv_b, cq_a, cq_b,
        ],
        [low, full, low, sums, att_shape, att_shape, dkv_shape, dkv_shape], scalars, scratch=back_scratch, micros=25,
    )
    part_other = sibling(part)
    cross_shapes = [((width, each), bf16), ((width, 2 * each), bf16), ((each, width), bf16)]
    grads_cross_b = call(
        cross_grad_kernel, "cross_grad_other", [h_one_low, mem, catt_b, e_two, dcq_b, dckv_b], cross_shapes, scalars, micros=3
    )
    grads_cross_got = [across(g) for g in grads_cross_b]
    grads_cross_a = call(
        cross_grad_kernel, "cross_grad_own", [h_one_low, mem, catt_a, e_two, dcq_a, dckv_a], cross_shapes, scalars, micros=3
    )
    (part_memory,) = call(pair_kernel, "memory_grad", [dckv_a, dckv_b, ckv_a, ckv_b], [((source, width), bf16)], micros=3)

    w_shape = ((width, 3 * each), bf16)
    o_shape = ((each, width), bf16)
    qkv_shape = ((length, 3 * each), bf16)
    d_one, e_one, sums_one, do_a, dqkv_b, gw_b, go_b = call(
        functools.partial(self_back_first_kernel, heads=heads), "self_back_other",
        [
            x, d_two, part, part_other, gain_one, unit_one, scale_one, so_a, so_b, att_a, att_b, q_b, k_b, v_b,
        ],
        [full, low, sums, head_shape, qkv_shape, w_shape, o_shape], scalars, scratch=back_scratch, micros=16,
    )
    gw_got = across(gw_b)
    go_got = across(go_b)
    dqkv_a, gw_a, go_a = call(
        functools.partial(self_back_second_kernel, heads=heads), "self_back_own",
        [x, e_one, att_a, q_a, k_a, v_a, do_a], [qkv_shape, w_shape, o_shape], scalars, scratch=back_scratch[1:], micros=11,
    )
    (part_tokens,) = call(pair_kernel, "tokens_grad", [dqkv_a, dqkv_b, w_a, w_b], [low], micros=4)

    def own_half(value, which):
        half = value.shape[0] // 2
        return jnp.where(which == 0, value[:half], value[half:])

    def whole(half):
        far = across(half)
        pair = jnp.stack([half, far])
        other = sibling(pair)
        first = jnp.where(core == 0, pair, other)
        second = jnp.where(core == 0, other, pair)
        mine = [first[0], second[0]]
        theirs = [first[1], second[1]]
        top = [jnp.where(row == 0, m, t) for m, t in zip(mine, theirs)]
        bottom = [jnp.where(row == 0, t, m) for m, t in zip(mine, theirs)]
        return jnp.concatenate(top + bottom, 0)

    layer_out = whole(own_half(out_row, core))
    memory_half = own_half(part_memory, core).astype(f32) + sibling(own_half(part_memory, 1 - core)).astype(f32)
    memory_grad = whole(memory_half.astype(bf16))
    tokens_half = own_half(d_one, core) + (
        own_half(part_tokens, core).astype(f32) + sibling(own_half(part_tokens, 1 - core)).astype(f32)
    )
    tokens_grad = whole(tokens_half.astype(bf16))

    bits = [b for b in range(size.bit_length() - 1)]
    turned = bits[1:] + bits[:1]

    def total(mine, got, order):
        return sum_over_dp((mine.astype(f32) + got.astype(f32)).astype(bf16), order, size)

    gf_sum = [total(gf_a[i], gf_b_got[i], order) for i, order in ((0, bits), (1, turned))]
    cross_sum = [total(a, b, order) for a, b, order in zip(grads_cross_a, grads_cross_got, (turned, bits, turned))]
    go_sum = total(go_a, go_got, turned)
    half = width // 2
    gw_sum = jnp.concatenate(
        [total(gw_a[:half], gw_got[:half], bits), total(gw_a[half:], gw_got[half:], turned)], 0
    )

    small = jnp.concatenate([sums_one[:2], sums_two[:2], sums_three[:2], sums_three[2:4]], 0)
    small = small + across(small)
    for bit in bits:
        small = small + lax.ppermute(small, "dp", [(i, i ^ (1 << bit)) for i in range(size)])

    gw_sum = gw_sum.astype(f32)
    ckv_sum = cross_sum[1].astype(f32)
    return (
        layer_out, tokens_grad, memory_grad,
        gw_sum[:, :each], gw_sum[:, each : 2 * each], gw_sum[:, 2 * each :], go_sum.astype(f32),
        cross_sum[0].astype(f32), ckv_sum[:, :each], ckv_sum[:, each:], cross_sum[2].astype(f32),
        gf_sum[0].astype(f32), gf_sum[1].astype(f32),
        small[0], small[1], small[2], small[3], small[4], small[5],
    )


def solution(mesh):
    rows, columns, down = P("dp", None), P(None, "tp"), P("tp", None)
    return jax.shard_map(
        functools.partial(local, mesh.shape["dp"]),
        mesh=mesh,
        in_specs=(rows, rows, rows, P("dp"), P("dp"))
        + (columns, columns, columns, down) * 2
        + (columns, down)
        + (P(),) * 6,
        out_specs=(rows, rows, rows) + (columns, columns, columns, down) * 2 + (columns, down) + (P(),) * 6,
        check_vma=False,
    )
```

time: 1240 us -> 623 us (0.50)
  waiting for transfers between devices: 691 us -> 248 us
  matrix products: 255 us -> 0 us
  Pallas kernels: 0 us -> 168 us
  starting transfers between devices: 0.93 us -> 89.7 us
  other arithmetic: 129 us -> 54.1 us
  local copies, waits for them, and re-layouts: 99.8 us -> 52.4 us
  blocking collectives: 37.7 us -> 0 us
  between operations: 15.7 us -> 2.58 us
    psum x7 -> x0, waiting for transfers between devices: 691 us -> none  [the longest x1 306 us: local(): lax.psum((grad_self_query, grad_self_key, grad_self_value, grad_self_out,...]
    dot_general x86 -> x0, matrix products: 255 us -> none  [the longest x10 42.4 us: matmul(): return jnp.dot(left, right, preferred_element_type=jnp.float32)]
    ppermute x0 -> x78, waiting for transfers between devices: none -> 248 us  [the longest x17 109 us: across(): return lax.ppermute(value, 'tp', ACROSS)]
    pallas_call x0 -> x15, Pallas kernels: none -> 168 us  [the longest x10 136 us: call(): pl.pallas_call(kernel, grid_spec=grid_spec, **settings)(scalars, *arrays)]
    ppermute x0 -> x78, starting transfers between devices: none -> 89.7 us  [the longest x24 34.1 us: sum_over_dp(): got = lax.ppermute(jnp.where(take, low, high), 'dp', partner)]
    reduce_sum x20 -> x0, other arithmetic: 66.2 us -> none  [the longest x6 30.8 us: layer_norm(): center = resid - jnp.mean(resid, -1, keepdims=True)]
    psum x1 -> x0, blocking collectives: 37.7 us -> none  [local(): lax.psum((grad_self_query, grad_self_key, grad_self_value, grad_self_out,...]
    another operation x20 -> x0, local copies, waits for them, and re-layouts: 22.1 us -> none
  transfers between devices with their start and end apart: 7 -> 78, of which waited for: 7 -> 43; matrix products, arithmetic and copies ran while one was open for 4% -> 12% of each run, Pallas kernels for 0% -> 17%
where the time goes in v1:
time: 623 us; the launch traced here: 616 us
  waiting for transfers between devices  248 us (40%)
  Pallas kernels  168 us (27%)
  starting transfers between devices  89.7 us (14%)
  other arithmetic  54.1 us (9%)
  local copies, waits for them, and re-layouts  52.4 us (8%)
    pallas_call x10, Pallas kernels, call(): pl.pallas_call(kernel, grid_spec=grid_spec, **settings)(scalars, *arrays)  136 us
    ppermute x17, waiting for transfers between devices, across(): return lax.ppermute(value, 'tp', ACROSS)  109 us
    ppermute x24, waiting for transfers between devices, sum_over_dp(): got = lax.ppermute(jnp.where(take, low, high), 'dp', partner)  94 us
    unnamed x210, local copies, waits for them, and re-layouts  42.6 us
    ppermute x24, waiting for transfers between devices, sum_over_dp(): got = lax.ppermute(pieces, 'dp', partner)  41 us
    ppermute x24, starting transfers between devices, sum_over_dp(): got = lax.ppermute(jnp.where(take, low, high), 'dp', partner)  34.1 us
    pallas_call x5, Pallas kernels, call(): pl.pallas_call(kernel, grid=(1,), in_specs=specs, out_specs=out_specs, sc...  32.5 us
    ppermute x24, starting transfers between devices, sum_over_dp(): got = lax.ppermute(pieces, 'dp', partner)  29.7 us
  transfers between devices with their start and end apart: 78, of which 43 were waited for; matrix products, arithmetic and copies ran while one was open for 12% of the time, Pallas kernels for 17%

profile of v1, /device:TPU:0, one launch (start us, length us, event | category | flops | bytes accessed | tf_op | source)
XLA Modules:
  0.0 615.5 jit_solution(4009344769588157811)
XLA Ops:
  4.8 2.9 collective-permute-start
  8.5 10.6 %self_forward_own.1 = (bf16[3,1024,128]{2,1,0:T(8,128)(2,1)S(1)}, bf16[3,1024,128]{2,1,0:T(8,128)(2,1)S(1)}, bf16[3,1024,128]{2,1,0:T(8,128)(2,1)S(1)}, bf16[3,1...) custom-call(s32[5]{0:T(128)S(1)} %pad_add_fusion.s_ref, ...), custom_call_target="tpu_custom_call" | custom-call | flops 10000000000 | bytes 12091392 | tf_op jit(solution)/shard_map/self_forward_own/pallas_call | solution.py:482
  24.4 4.1 collective-permute-done
  30.1 3.8 collective-permute-done.1.rest_2_.ob_ref
  35.1 11.3 %self_forward_other.1 = (bf16[1024,768]{1,0:T(8,128)(2,1)}, bf16[3,1024,128]{2,1,0:T(8,128)(2,1)S(1)}, bf16[3,1024,128]{2,1,0:T(8,128)(2,1)S(1)}, bf16[3,1024,128]{2,1,0:T(8,128)(2,1)S(1)}, bf16[1024,192]{1,0:T(8,128)(2,1)S(1)}) custom-call(s32[5]{0:T(128)S(1)} %pad_add_fusion.s_ref, bf16[2048,768]{1,0:T(8,128)(2,1)} %x_ref.9, ...), custom_call_target="tpu_custom_call" | custom-call | flops 8999999488 | bytes 9338880 | tf_op jit(solution)/shard_map/self_forward_other/pallas_call | solution.py:482
  54.1 12.2 %collective-permute-done.4.w_ref.wb_ref = bf16[768,384]{1,0:T(8,128)(2,1)} collective-permute-done((bf16[768,384]{1,0:T(8,128)(2,1)S(1)}, bf16[768,384]{1,0:T(8,128)(2,1)}, u32[]{:S(2)}, u32[]{:S(2)}) %collective-permute-start.4) | collective-permute-done | bytes 589856 | tf_op jit(solution)/shard_map/ppermute | solution.py:525
  68.1 2.9 memory_keys_other.1
  74.6 5.9 collective-permute-done.5.ob_ref
  80.6 22.6 %cross_forward.1 = (bf16[1024,768]{1,0:T(8,128)(2,1)}, f32[1024,768]{1,0:T(8,128)}, bf16[1024,768]{1,0:T(8,128)(2,1)}, bf16[1024,768]{1,0:T(8,128)(2,1)}, f32[10...) custom-call(s32[5]{0:T(128)S(1)} %pad_add_fusion.s_ref, ...), custom_call_target="tpu_custom_call" | custom-call | flops 17999998976 | bytes 20850688 | tf_op jit(solution)/shard_map/cross_forward/pallas_call | solution.py:482
  107.1 26.7 %collective-permute-done.7.upb_ref = bf16[768,768]{1,0:T(8,128)(2,1)S(1)} collective-permute-done((bf16[768,768]{1,0:T(8,128)(2,1)S(1)}, bf16[768,768]{1,0:T(8,128)(2,1)S(1)}, u32[]{:S(2)}, u32[]{:S(2)}) %collective-permute-start.7) | collective-permute-done | bytes 1179680 | tf_op jit(solution)/shard_map/ppermute | solution.py:525
  133.9 24.8 %collective-permute-done.8.downb_ref = bf16[768,768]{1,0:T(8,128)(2,1)S(1)} collective-permute-done((bf16[768,768]{1,0:T(8,128)(2,1)S(1)}, bf16[768,768]{1,0:T(8,128)(2,1)S(1)}, u32[]{:S(2)}, u32[]{:S(2)}) %collective-permute-start.8) | collective-permute-done | bytes 1179680 | tf_op jit(solution)/shard_map/ppermute | solution.py:525
  159.8 15.6 %ffn_forward.1 = (bf16[1024,768]{1,0:T(8,128)(2,1)}, f32[1024,768]{1,0:T(8,128)}, bf16[1024,768]{1,0:T(8,128)(2,1)}, bf16[1024,768]{1,0:T(8,128)(2,1)}, f32[1024...) custom-call(f32[1024,768]{1,0:T(8,128)} %get-tuple-element.87.h_in_r, ...), custom_call_target="tpu_custom_call" | custom-call | flops 12000000000 | bytes 25176064 | tf_op jit(solution)/shard_map/ffn_forward/pallas_call | solution.py:476
  176.3 3.6 collective-permute-done.9.pb_ref
  181.0 16.9 %ffn_back.1 = (bf16[1024,768]{1,0:T(8,128)(2,1)}, bf16[1024,768]{1,0:T(8,128)(2,1)}, f32[1024,768]{1,0:T(8,128)}, bf16[1024,768]{1,0:T(8,128)(2,1)}, bf16[1024,7...) custom-call(s32[5]{0:T(128)S(1)} %pad_add_fusion.s_ref, f32[1024,768]{1,0:T(8,128)} %get-tuple-element.89.h_ref, ...), custom_call_target="tpu_custom_call" | custom-call | flops 12000000000 | bytes 28342272 | tf_op jit(solution)/shard_map/ffn_back/pallas_call | solution.py:482
  203.5 5.6 ffn_grad_other.1
  210.5 5.5 ffn_grad_own.1
  216.0 4.1 collective-permute-done.10
  222.2 31.2 %cross_back.1 = (bf16[1024,768]{1,0:T(8,128)(2,1)}, f32[1024,768]{1,0:T(8,128)}, bf16[1024,768]{1,0:T(8,128)(2,1)}, f32[8,768]{1,0:T(8,128)S(1)}, bf16[1024,192]...) custom-call(s32[5]{0:T(128)S(1)} %pad_add_fusion.s_ref, ...), custom_call_target="tpu_custom_call" | custom-call | flops 24999999488 | bytes 23231488 | tf_op jit(solution)/shard_map/cross_back/pallas_call | solution.py:482
  253.4 4.2 cross_grad_other.1
  257.5 4.8 collective-permute-start.54
  262.5 3.0 memory_grad.1
  266.5 4.2 cross_grad_own.1
  270.7 6.3 %collective-permute-done.54 = bf16[192,768]{1,0:T(8,128)(2,1)S(1)} collective-permute-done((bf16[192,768]{1,0:T(8,128)(2,1)S(1)}, bf16[192,768]{1,0:T(8,128)(2,1)S(1)}, u32[]{:S(2)}, u32[]{:S(2)}) %collective-permute-start.54) | collective-permute-done | bytes 294944 | tf_op jit(solution)/shard_map/ppermute | solution.py:525
  278.0 19.4 %collective-permute-done.40 = bf16[768,192]{1,0:T(8,128)(2,1)S(1)} collective-permute-done((bf16[768,192]{1,0:T(8,128)(2,1)S(1)}, bf16[768,192]{1,0:T(8,128)(2,1)S(1)}, u32[]{:S(2)}, u32[]{:S(2)}) %collective-permute-start.40) | collective-permute-done | bytes 294944 | tf_op jit(solution)/shard_map/ppermute | solution.py:525
  298.7 4.1 collective-permute-done.55
  303.9 4.5 collective-permute-done.41
  319.2 7.9 %collective-permute-start.57 = (bf16[24,768]{1,0:T(8,128)(2,1)S(1)}, bf16[24,768]{1,0:T(8,128)(2,1)S(1)}, u32[]{:S(2)}, u32[]{:S(2)}) collective-permute-start(bf16[24,768]{1,0:T(8,128)(2,1)S(1)} %broadcast_select_fusion.74), channel_id=1, source_target_pairs={{0,1},{1,0},{2,3},{3,2},{4,5},{5,4},{6,7},{7,6},{8,9},{9,8},{10,11... | collective-permute-start | bytes 110600 | tf_op jit(solution)/shard_map/ppermute | solution.py:493
  341.6 2.9 collective-permute-start.59
  349.9 3.5 collective-permute-done.45
  367.1 13.2 %collective-permute-done.49 = bf16[192,384]{1,0:T(8,128)(2,1)S(1)} collective-permute-done((bf16[192,384]{1,0:T(8,128)(2,1)S(1)}, bf16[192,384]{1,0:T(8,128)(2,1)S(1)}, u32[]{:S(2)}, u32[]{:S(2)}) %collective-permute-start.49) | collective-permute-done | bytes 147488 | tf_op jit(solution)/shard_map/ppermute | solution.py:493
  381.0 5.6 collective-permute-done.50
  387.5 4.5 collective-permute-done.51
  409.5 21.4 %self_back_other.1 = (f32[1024,768]{1,0:T(8,128)}, bf16[1024,768]{1,0:T(8,128)(2,1)}, f32[8,768]{1,0:T(8,128)S(1)}, bf16[3,1024,128]{2,1,0:T(8,128)(2,1)S(1)}, b...) custom-call(s32[5]{0:T(128)S(1)} %pad_add_fusion.s_ref, bf16[2048,768]{1,0:T(8,128)(2,1)} %x_ref.9, ...), custom_call_target="tpu_custom_call" | custom-call | flops 16000000000 | bytes 22641664 | tf_op jit(solution)/shard_map/self_back_other/pallas_call | solution.py:482
  433.5 10.4 %self_back_own.1 = (bf16[1024,576]{1,0:T(8,128)(2,1)}, bf16[768,576]{1,0:T(8,128)(2,1)S(1)}, bf16[192,768]{1,0:T(8,128)(2,1)S(1)}) custom-call(s32[5]{0:T(128)S(1)} %pad_add_fusion.s_ref, bf16[2048,768]{1,0:T(8,128)(2,1)} %x_ref.9, bf16[1024,768]{1,0:T(8,128)(2,1)} %get-tuple-element.111.e_ref, bf16[1024,192]{1,0:T(8,128)(2,1)S(1)} %copy-done.48, ...), custom_call_target="tpu_custom_call" | custom-call | flops 11000000512 | bytes 10616832 | tf_op jit(solution)/shard_map/self_back_own/pallas_call | solution.py:482
  473.3 3.2 collective-permute-done.70
  479.8 6.0 collective-permute-done.64
  485.8 5.1 collective-permute-done.34
  494.0 7.4 %collective-permute-done.35 = bf16[48,768]{1,0:T(8,128)(2,1)S(1)} collective-permute-done((bf16[48,768]{1,0:T(8,128)(2,1)S(1)}, bf16[48,768]{1,0:T(8,128)(2,1)S(1)}, u32[]{:S(2)}, u32[]{:S(2)}) %collective-permute-start.35) | collective-permute-done | bytes 73760 | tf_op jit(solution)/shard_map/ppermute | solution.py:493
  509.6 3.0 collective-permute-start.38
  512.6 10.4 %collective-permute-done.38 = bf16[48,768]{1,0:T(8,128)(2,1)S(1)} collective-permute-done((bf16[48,768]{1,0:T(8,128)(2,1)S(1)}, bf16[48,768]{1,0:T(8,128)(2,1)S(1)}, u32[]{:S(2)}, u32[]{:S(2)}) %collective-permute-start.38) | collective-permute-done | bytes 73760 | tf_op jit(solution)/shard_map/ppermute | solution.py:498
  526.1 6.7 %collective-permute-done.66 = bf16[192,768]{1,0:T(8,128)(2,1)S(1)} collective-permute-done((bf16[192,768]{1,0:T(8,128)(2,1)S(1)}, bf16[192,768]{1,0:T(8,128)(2,1)S(1)}, u32[]{:S(2)}, u32[]{:S(2)}) %collective-permute-start.66) | collective-permute-done | bytes 294944 | tf_op jit(solution)/shard_map/ppermute | solution.py:498
  545.8 7.4 %collective-permute-done.21 = bf16[192,576]{1,0:T(8,128)(2,1)S(1)} collective-permute-done((bf16[192,576]{1,0:T(8,128)(2,1)S(1)}, bf16[192,576]{1,0:T(8,128)(2,1)S(1)}, u32[]{:S(2)}, u32[]{:S(2)}) %collective-permute-start.21) | collective-permute-done | bytes 221216 | tf_op jit(solution)/shard_map/ppermute | solution.py:493
  554.7 5.5 collective-permute-done.27
  562.1 4.2 collective-permute-done.22
  567.8 6.2 %collective-permute-done.28 = bf16[96,576]{1,0:T(8,128)(2,1)S(1)} collective-permute-done((bf16[96,576]{1,0:T(8,128)(2,1)S(1)}, bf16[96,576]{1,0:T(8,128)(2,1)S(1)}, u32[]{:S(2)}, u32[]{:S(2)}) %collective-permute-start.28) | collective-permute-done | bytes 110624 | tf_op jit(solution)/shard_map/ppermute | solution.py:493
  574.1 5.7 collective-permute-done.23
  580.2 3.8 collective-permute-done.29
  593.6 3.0 collective-permute-done.25
  (476 shorter events, 204.9 us)
Async XLA Ops:
  4.8 23.7 %collective-permute-start = (bf16[768,576]{0,1:T(8,128)(2,1)}, bf16[768,576]{0,1:T(8,128)(2,1)}, u32[]{:S(2)}, u32[]{:S(2)}) collective-permute-start(bf16[768,576]{0,1:T(8,128)(2,1)} %copy.57), channel_id=1, source_target_pairs={{0,16},{16,0},{8,24},{24,8},{1,17},{17,1},{9,25},{25,9},{2,18},{18... | collective-permute-start | bytes 2654216 | tf_op jit(solution)/shard_map/ppermute | solution.py:525
  7.8 26.2 %collective-permute-start.1 = (bf16[192,768]{1,0:T(8,128)(2,1)S(1)}, bf16[192,768]{1,0:T(8,128)(2,1)S(1)}, u32[]{:S(2)}, u32[]{:S(2)}) collective-permute-start(bf16[192,768]{1,0:T(8,128)(2,1)S(1)} %copy-done.9), channel_id=1, source_target_pairs={{0,16},{16,0},{8,24},{24,8},{1,17},{17,1},{9,25},{25,9},{2,18},{18... | collective-permute-start | bytes 884744 | tf_op jit(solution)/shard_map/ppermute | solution.py:525
  50.0 30.5 %collective-permute-start.2 = (bf16[1024,768]{1,0:T(8,128)(2,1)}, bf16[1024,768]{1,0:T(8,128)(2,1)}, u32[]{:S(2)}, u32[]{:S(2)}) collective-permute-start(bf16[1024,768]{1,0:T(8,128)(2,1)} %get-tuple-element.82.pa_ref), channel_id=1, source_target_pairs={{0,8},{8,0},{16,24},{24,16},{1,9},{9,1},{17,25},{25,17},{2,10},{10... | collective-permute-start | bytes 4718600 | tf_op jit(solution)/shard_map/ppermute | solution.py:528
  50.0 16.2 %collective-permute-start.4 = (bf16[768,384]{1,0:T(8,128)(2,1)S(1)}, bf16[768,384]{1,0:T(8,128)(2,1)}, u32[]{:S(2)}, u32[]{:S(2)}) collective-permute-start(bf16[768,384]{1,0:T(8,128)(2,1)S(1)} %pad_maximum_fusion.7.rest_1_.wa_ref), channel_id=1, source_target_pairs={{0,16},{16,0},{8,24},{24,8},{1,17},{17,1},{9,25},{25,9},{2,18},{18... | collective-permute-start | bytes 1769480 | tf_op jit(solution)/shard_map/ppermute | solution.py:525
  51.9 22.6 %collective-permute-start.3 = (bf16[768,192]{1,0:T(8,128)(2,1)S(1)}, bf16[768,192]{1,0:T(8,128)(2,1)S(1)}, u32[]{:S(2)}, u32[]{:S(2)}) collective-permute-start(bf16[768,192]{1,0:T(8,128)(2,1)S(1)} %copy.62.wqa_ref), channel_id=1, source_target_pairs={{0,16},{16,0},{8,24},{24,8},{1,17},{17,1},{9,25},{25,9},{2,18},{18... | collective-permute-start | bytes 884744 | tf_op jit(solution)/shard_map/ppermute | solution.py:525
  52.3 28.2 %collective-permute-start.5 = (bf16[192,768]{1,0:T(8,128)(2,1)}, bf16[192,768]{1,0:T(8,128)(2,1)S(1)}, u32[]{:S(2)}, u32[]{:S(2)}) collective-permute-start(bf16[192,768]{1,0:T(8,128)(2,1)} %oa_ref.4), channel_id=1, source_target_pairs={{0,16},{16,0},{8,24},{24,8},{1,17},{17,1},{9,25},{25,9},{2,18},{18... | collective-permute-start | bytes 884744 | tf_op jit(solution)/shard_map/ppermute | solution.py:525
  105.0 53.7 %collective-permute-start.6 = (bf16[1024,768]{1,0:T(8,128)(2,1)}, bf16[1024,768]{1,0:T(8,128)(2,1)S(1)}, u32[]{:S(2)}, u32[]{:S(2)}) collective-permute-start(bf16[1024,768]{1,0:T(8,128)(2,1)} %get-tuple-element.88.pa_ref), channel_id=1, source_target_pairs={{0,8},{8,0},{16,24},{24,16},{1,9},{9,1},{17,25},{25,17},{2,10},{10... | collective-permute-start | bytes 4718600 | tf_op jit(solution)/shard_map/ppermute | solution.py:528
  105.0 28.8 %collective-permute-start.7 = (bf16[768,768]{1,0:T(8,128)(2,1)S(1)}, bf16[768,768]{1,0:T(8,128)(2,1)S(1)}, u32[]{:S(2)}, u32[]{:S(2)}) collective-permute-start(bf16[768,768]{1,0:T(8,128)(2,1)S(1)} %copy-done.5), channel_id=1, source_target_pairs={{0,16},{16,0},{8,24},{24,8},{1,17},{17,1},{9,25},{25,9},{2,18},{18... | collective-permute-start | bytes 3538952 | tf_op jit(solution)/shard_map/ppermute | solution.py:525
  106.1 52.6 %collective-permute-start.8 = (bf16[768,768]{1,0:T(8,128)(2,1)S(1)}, bf16[768,768]{1,0:T(8,128)(2,1)S(1)}, u32[]{:S(2)}, u32[]{:S(2)}) collective-permute-start(bf16[768,768]{1,0:T(8,128)(2,1)S(1)} %copy-done.6), channel_id=1, source_target_pairs={{0,16},{16,0},{8,24},{24,8},{1,17},{17,1},{9,25},{25,9},{2,18},{18... | collective-permute-start | bytes 3538952 | tf_op jit(solution)/shard_map/ppermute | solution.py:525
  197.9 23.5 %collective-permute-start.12 = (bf16[1024,768]{1,0:T(8,128)(2,1)}, bf16[1024,768]{1,0:T(8,128)(2,1)}, u32[]{:S(2)}, u32[]{:S(2)}) collective-permute-start(bf16[1024,768]{1,0:T(8,128)(2,1)} %get-tuple-element.95.pa_ref), channel_id=1, source_target_pairs={{0,8},{8,0},{16,24},{24,16},{1,9},{9,1},{17,25},{25,17},{2,10},{10... | collective-permute-start | bytes 4718600 | tf_op jit(solution)/shard_map/ppermute | solution.py:528
  199.6 20.4 %collective-permute-start.10 = (bf16[512,768]{1,0:T(8,128)(2,1)S(1)}, bf16[512,768]{1,0:T(8,128)(2,1)S(1)}, u32[]{:S(2)}, u32[]{:S(2)}) collective-permute-start(bf16[512,768]{1,0:T(8,128)(2,1)S(1)} %slice_select_fusion), channel_id=1, source_target_pairs={{0,16},{16,0},{8,24},{24,8},{1,17},{17,1},{9,25},{25,9},{2,18},{18... | collective-permute-start | bytes 2359304 | tf_op jit(solution)/shard_map/ppermute | solution.py:525
  209.1 146.1 %collective-permute-start.61 = (bf16[2,768,768]{2,1,0:T(8,128)(2,1)}, bf16[2,768,768]{2,1,0:T(8,128)(2,1)S(1)}, u32[]{:S(2)}, u32[]{:S(2)}) collective-permute-start(bf16[2,768,768]{2,1,0:T(8,128)(2,1)} %ffn_grad_other.1), channel_id=1, source_target_pairs={{0,16},{16,0},{8,24},{24,8},{1,17},{17,1},{9,25},{25,9},{2,18},{18... | collective-permute-start | bytes 7077896 | tf_op jit(solution)/shard_map/ppermute | solution.py:525
  221.4 135.4 %collective-permute-start.11 = (bf16[2,512,768]{2,1,0:T(8,128)(2,1)}, bf16[2,512,768]{2,1,0:T(8,128)(2,1)}, u32[]{:S(2)}, u32[]{:S(2)}) collective-permute-start(bf16[2,512,768]{2,1,0:T(8,128)(2,1)} %pad_maximum_fusion.3), channel_id=1, source_target_pairs={{0,8},{8,0},{16,24},{24,16},{1,9},{9,1},{17,25},{25,17},{2,10},{10... | collective-permute-start | bytes 4718600 | tf_op jit(solution)/shard_map/ppermute | solution.py:528
  253.4 156.0 %collective-permute-start.13 = (bf16[1024,768]{1,0:T(8,128)(2,1)}, bf16[1024,768]{1,0:T(8,128)(2,1)}, u32[]{:S(2)}, u32[]{:S(2)}) collective-permute-start(bf16[1024,768]{1,0:T(8,128)(2,1)} %get-tuple-element.103.pa_ref), channel_id=1, source_target_pairs={{0,8},{8,0},{16,24},{24,16},{1,9},{9,1},{17,25},{25,17},{2,10},{10... | collective-permute-start | bytes 4718600 | tf_op jit(solution)/shard_map/ppermute | solution.py:528
  257.5 19.4 %collective-permute-start.54 = (bf16[192,768]{1,0:T(8,128)(2,1)S(1)}, bf16[192,768]{1,0:T(8,128)(2,1)S(1)}, u32[]{:S(2)}, u32[]{:S(2)}) collective-permute-start(bf16[192,768]{1,0:T(8,128)(2,1)S(1)} %get-tuple-element.133), channel_id=1, source_target_pairs={{0,16},{16,0},{8,24},{24,8},{1,17},{17,1},{9,25},{25,9},{2,18},{18... | collective-permute-start | bytes 884744 | tf_op jit(solution)/shard_map/ppermute | solution.py:525
  262.4 74.7 %collective-permute-start.47 = (bf16[768,384]{1,0:T(8,128)(2,1)S(1)}, bf16[768,384]{1,0:T(8,128)(2,1)S(1)}, u32[]{:S(2)}, u32[]{:S(2)}) collective-permute-start(bf16[768,384]{1,0:T(8,128)(2,1)S(1)} %get-tuple-element.131), channel_id=1, source_target_pairs={{0,16},{16,0},{8,24},{24,8},{1,17},{17,1},{9,25},{25,9},{2,18},{18... | collective-permute-start | bytes 1769480 | tf_op jit(solution)/shard_map/ppermute | solution.py:525
  276.9 20.5 %collective-permute-start.40 = (bf16[768,192]{1,0:T(8,128)(2,1)S(1)}, bf16[768,192]{1,0:T(8,128)(2,1)S(1)}, u32[]{:S(2)}, u32[]{:S(2)}) collective-permute-start(bf16[768,192]{1,0:T(8,128)(2,1)S(1)} %get-tuple-element.129), channel_id=1, source_target_pairs={{0,16},{16,0},{8,24},{24,8},{1,17},{17,1},{9,25},{25,9},{2,18},{18... | collective-permute-start | bytes 884744 | tf_op jit(solution)/shard_map/ppermute | solution.py:525
  319.2 9.8 %collective-permute-start.57 = (bf16[24,768]{1,0:T(8,128)(2,1)S(1)}, bf16[24,768]{1,0:T(8,128)(2,1)S(1)}, u32[]{:S(2)}, u32[]{:S(2)}) collective-permute-start(bf16[24,768]{1,0:T(8,128)(2,1)S(1)} %broadcast_select_fusion.74), channel_id=1, source_target_pairs={{0,1},{1,0},{2,3},{3,2},{4,5},{5,4},{6,7},{7,6},{8,9},{9,8},{10,11... | collective-permute-start | bytes 110600 | tf_op jit(solution)/shard_map/ppermute | solution.py:493
  337.1 23.8 %collective-permute-start.17 = (bf16[512,768]{1,0:T(8,128)(2,1)}, bf16[512,768]{1,0:T(8,128)(2,1)S(1)}, u32[]{:S(2)}, u32[]{:S(2)}) collective-permute-start(bf16[512,768]{1,0:T(8,128)(2,1)} %broadcast_select_fusion.6), channel_id=1, source_target_pairs={{0,8},{8,0},{16,24},{24,16},{1,9},{9,1},{17,25},{25,17},{2,10},{10... | collective-permute-start | bytes 2359304 | tf_op jit(solution)/shard_map/ppermute | solution.py:528
  353.3 10.7 %collective-permute-start.48 = (bf16[384,384]{1,0:T(8,128)(2,1)S(1)}, bf16[384,384]{1,0:T(8,128)(2,1)S(1)}, u32[]{:S(2)}, u32[]{:S(2)}) collective-permute-start(bf16[384,384]{1,0:T(8,128)(2,1)S(1)} %broadcast_select_fusion.20), channel_id=1, source_target_pairs={{0,1},{1,0},{2,3},{3,2},{4,5},{5,4},{6,7},{7,6},{8,9},{9,8},{10,11... | collective-permute-start | bytes 884744 | tf_op jit(solution)/shard_map/ppermute | solution.py:493
  355.2 31.5 %collective-permute-start.60 = (bf16[96,768]{1,0:T(8,128)(2,1)S(1)}, bf16[96,768]{1,0:T(8,128)(2,1)S(1)}, u32[]{:S(2)}, u32[]{:S(2)}) collective-permute-start(bf16[96,768]{1,0:T(8,128)(2,1)S(1)} %pad_maximum_fusion.18), channel_id=1, source_target_pairs={{0,2},{1,3},{2,0},{3,1},{4,6},{5,7},{6,4},{7,5},{8,10},{9,11},{10,... | collective-permute-start | bytes 442376 | tf_op jit(solution)/shard_map/ppermute | solution.py:498
  356.8 23.9 %collective-permute-start.46 = (bf16[384,192]{1,0:T(8,128)(2,1)S(1)}, bf16[384,192]{1,0:T(8,128)(2,1)S(1)}, u32[]{:S(2)}, u32[]{:S(2)}) collective-permute-start(bf16[384,192]{1,0:T(8,128)(2,1)S(1)} %pad_maximum_fusion.15), channel_id=1, source_target_pairs={{0,2},{1,3},{2,0},{3,1},{4,6},{5,7},{6,4},{7,5},{8,10},{9,11},{10,... | collective-permute-start | bytes 442376 | tf_op jit(solution)/shard_map/ppermute | solution.py:498
  360.9 42.7 %collective-permute-start.68 = (bf16[384,768]{1,0:T(8,128)(2,1)}, bf16[384,768]{1,0:T(8,128)(2,1)}, u32[]{:S(2)}, u32[]{:S(2)}) collective-permute-start(bf16[384,768]{1,0:T(8,128)(2,1)} %select_bitcast_fusion.12), channel_id=1, source_target_pairs={{0,2},{1,3},{2,0},{3,1},{4,6},{5,7},{6,4},{7,5},{8,10},{9,11},{10,... | collective-permute-start | bytes 1769480 | tf_op jit(solution)/shard_map/ppermute | solution.py:493
  364.2 16.2 %collective-permute-start.49 = (bf16[192,384]{1,0:T(8,128)(2,1)S(1)}, bf16[192,384]{1,0:T(8,128)(2,1)S(1)}, u32[]{:S(2)}, u32[]{:S(2)}) collective-permute-start(bf16[192,384]{1,0:T(8,128)(2,1)S(1)} %broadcast_select_fusion.38), channel_id=1, source_target_pairs={{0,2},{1,3},{2,0},{3,1},{4,6},{5,7},{6,4},{7,5},{8,10},{9,11},{10,... | collective-permute-start | bytes 442376 | tf_op jit(solution)/shard_map/ppermute | solution.py:493
  380.3 26.3 %collective-permute-start.62 = (bf16[384,768]{1,0:T(8,128)(2,1)}, bf16[384,768]{1,0:T(8,128)(2,1)}, u32[]{:S(2)}, u32[]{:S(2)}) collective-permute-start(bf16[384,768]{1,0:T(8,128)(2,1)} %select_bitcast_fusion.13), channel_id=1, source_target_pairs={{0,1},{1,0},{2,3},{3,2},{4,5},{5,4},{6,7},{7,6},{8,9},{9,8},{10,11... | collective-permute-start | bytes 1769480 | tf_op jit(solution)/shard_map/ppermute | solution.py:493
  386.5 66.6 %collective-permute-start.18 = (bf16[512,768]{1,0:T(8,128)(2,1)}, bf16[512,768]{1,0:T(8,128)(2,1)}, u32[]{:S(2)}, u32[]{:S(2)}) collective-permute-start(bf16[512,768]{1,0:T(8,128)(2,1)} %add_convert_fusion.2), channel_id=1, source_target_pairs={{0,16},{16,0},{8,24},{24,8},{1,17},{17,1},{9,25},{25,9},{2,18},{18... | collective-permute-start | bytes 2359304 | tf_op jit(solution)/shard_map/ppermute | solution.py:525
  402.0 56.9 %collective-permute-start.53 = (bf16[384,384]{1,0:T(8,128)(2,1)}, bf16[384,384]{1,0:T(8,128)(2,1)}, u32[]{:S(2)}, u32[]{:S(2)}) collective-permute-start(bf16[384,384]{1,0:T(8,128)(2,1)} %pad_maximum_fusion.10), channel_id=1, source_target_pairs={{0,1},{1,0},{2,3},{3,2},{4,5},{5,4},{6,7},{7,6},{8,9},{9,8},{10,11... | collective-permute-start | bytes 884744 | tf_op jit(solution)/shard_map/ppermute | solution.py:498
  406.5 60.9 %collective-permute-start.69 = (bf16[192,768]{1,0:T(8,128)(2,1)}, bf16[192,768]{1,0:T(8,128)(2,1)}, u32[]{:S(2)}, u32[]{:S(2)}) collective-permute-start(bf16[192,768]{1,0:T(8,128)(2,1)} %broadcast_select_fusion.14), channel_id=1, source_target_pairs={{0,4},{1,5},{2,6},{3,7},{4,0},{5,1},{6,2},{7,3},{8,12},{9,13},{10,... | collective-permute-start | bytes 884744 | tf_op jit(solution)/shard_map/ppermute | solution.py:493
  408.9 61.5 %collective-permute-start.63 = (bf16[192,768]{1,0:T(8,128)(2,1)}, bf16[192,768]{1,0:T(8,128)(2,1)}, u32[]{:S(2)}, u32[]{:S(2)}) collective-permute-start(bf16[192,768]{1,0:T(8,128)(2,1)} %broadcast_select_fusion.17), channel_id=1, source_target_pairs={{0,2},{1,3},{2,0},{3,1},{4,6},{5,7},{6,4},{7,5},{8,10},{9,11},{10,... | collective-permute-start | bytes 884744 | tf_op jit(solution)/shard_map/ppermute | solution.py:493
  431.6 20.5 %collective-permute-start.74 = (f32[8,768]{1,0:T(8,128)}, f32[8,768]{1,0:T(8,128)}, u32[]{:S(2)}, u32[]{:S(2)}) collective-permute-start(f32[8,768]{1,0:T(8,128)} %pad_maximum_fusion.24), channel_id=1, source_target_pairs={{0,16},{16,0},{8,24},{24,8},{1,17},{17,1},{9,25},{25,9},{2,18},{18... | collective-permute-start | bytes 73736 | tf_op jit(solution)/shard_map/ppermute | solution.py:525
  452.1 25.6 %collective-permute-start.33 = (bf16[192,768]{1,0:T(8,128)(2,1)S(1)}, bf16[192,768]{1,0:T(8,128)(2,1)}, u32[]{:S(2)}, u32[]{:S(2)}) collective-permute-start(bf16[192,768]{1,0:T(8,128)(2,1)S(1)} %copy-done.16), channel_id=1, source_target_pairs={{0,16},{16,0},{8,24},{24,8},{1,17},{17,1},{9,25},{25,9},{2,18},{18... | collective-permute-start | bytes 884744 | tf_op jit(solution)/shard_map/ppermute | solution.py:525
  457.1 80.7 %collective-permute-start.20 = (bf16[768,576]{0,1:T(8,128)(2,1)}, bf16[768,576]{0,1:T(8,128)(2,1)}, u32[]{:S(2)}, u32[]{:S(2)}) collective-permute-start(bf16[768,576]{0,1:T(8,128)(2,1)} %copy.65), channel_id=1, source_target_pairs={{0,16},{16,0},{8,24},{24,8},{1,17},{17,1},{9,25},{25,9},{2,18},{18... | collective-permute-start | bytes 2654216 | tf_op jit(solution)/shard_map/ppermute | solution.py:525
  467.5 66.4 %collective-permute-start.14 = (bf16[512,768]{1,0:T(8,128)(2,1)}, bf16[512,768]{1,0:T(8,128)(2,1)S(1)}, u32[]{:S(2)}, u32[]{:S(2)}) collective-permute-start(bf16[512,768]{1,0:T(8,128)(2,1)} %broadcast_select_fusion.7), channel_id=1, source_target_pairs={{0,8},{8,0},{16,24},{24,16},{1,9},{9,1},{17,25},{25,17},{2,10},{10... | collective-permute-start | bytes 2359304 | tf_op jit(solution)/shard_map/ppermute | solution.py:528
  472.6 129.1 %collective-permute-start.19 = (bf16[2,512,768]{2,1,0:T(8,128)(2,1)}, bf16[2,512,768]{2,1,0:T(8,128)(2,1)}, u32[]{:S(2)}, u32[]{:S(2)}) collective-permute-start(bf16[2,512,768]{2,1,0:T(8,128)(2,1)} %pad_maximum_fusion.5), channel_id=1, source_target_pairs={{0,8},{8,0},{16,24},{24,16},{1,9},{9,1},{17,25},{25,17},{2,10},{10... | collective-permute-start | bytes 4718600 | tf_op jit(solution)/shard_map/ppermute | solution.py:528
  476.5 9.2 %collective-permute-start.64 = (bf16[96,768]{1,0:T(8,128)(2,1)S(1)}, bf16[96,768]{1,0:T(8,128)(2,1)S(1)}, u32[]{:S(2)}, u32[]{:S(2)}) collective-permute-start(bf16[96,768]{1,0:T(8,128)(2,1)S(1)} %broadcast_select_fusion.35), channel_id=1, source_target_pairs={{0,4},{1,5},{2,6},{3,7},{4,0},{5,1},{6,2},{7,3},{8,12},{9,13},{10,... | collective-permute-start | bytes 442376 | tf_op jit(solution)/shard_map/ppermute | solution.py:493
  477.7 13.7 %collective-permute-start.71 = (bf16[96,768]{1,0:T(8,128)(2,1)S(1)}, bf16[96,768]{1,0:T(8,128)(2,1)S(1)}, u32[]{:S(2)}, u32[]{:S(2)}) collective-permute-start(bf16[96,768]{1,0:T(8,128)(2,1)S(1)} %add_convert_fusion.16), channel_id=1, source_target_pairs={{0,1},{1,0},{2,3},{3,2},{4,5},{5,4},{6,7},{7,6},{8,9},{9,8},{10,11... | collective-permute-start | bytes 442376 | tf_op jit(solution)/shard_map/ppermute | solution.py:498
  490.9 14.6 %collective-permute-start.65 = (bf16[96,768]{1,0:T(8,128)(2,1)S(1)}, bf16[96,768]{1,0:T(8,128)(2,1)S(1)}, u32[]{:S(2)}, u32[]{:S(2)}) collective-permute-start(bf16[96,768]{1,0:T(8,128)(2,1)S(1)} %add_convert_fusion.17), channel_id=1, source_target_pairs={{0,4},{1,5},{2,6},{3,7},{4,0},{5,1},{6,2},{7,3},{8,12},{9,13},{10,... | collective-permute-start | bytes 442376 | tf_op jit(solution)/shard_map/ppermute | solution.py:498
  491.4 10.0 %collective-permute-start.35 = (bf16[48,768]{1,0:T(8,128)(2,1)S(1)}, bf16[48,768]{1,0:T(8,128)(2,1)S(1)}, u32[]{:S(2)}, u32[]{:S(2)}) collective-permute-start(bf16[48,768]{1,0:T(8,128)(2,1)S(1)} %broadcast_select_fusion.62), channel_id=1, source_target_pairs={{0,4},{1,5},{2,6},{3,7},{4,0},{5,1},{6,2},{7,3},{8,12},{9,13},{10,... | collective-permute-start | bytes 221192 | tf_op jit(solution)/shard_map/ppermute | solution.py:493
  505.5 17.5 %collective-permute-start.72 = (bf16[192,768]{1,0:T(8,128)(2,1)S(1)}, bf16[192,768]{1,0:T(8,128)(2,1)S(1)}, u32[]{:S(2)}, u32[]{:S(2)}) collective-permute-start(bf16[192,768]{1,0:T(8,128)(2,1)S(1)} %pad_maximum_fusion.12), channel_id=1, source_target_pairs={{0,4},{1,5},{2,6},{3,7},{4,0},{5,1},{6,2},{7,3},{8,12},{9,13},{10,... | collective-permute-start | bytes 884744 | tf_op jit(solution)/shard_map/ppermute | solution.py:498
  509.6 13.4 %collective-permute-start.38 = (bf16[48,768]{1,0:T(8,128)(2,1)S(1)}, bf16[48,768]{1,0:T(8,128)(2,1)S(1)}, u32[]{:S(2)}, u32[]{:S(2)}) collective-permute-start(bf16[48,768]{1,0:T(8,128)(2,1)S(1)} %pad_maximum_fusion.22), channel_id=1, source_target_pairs={{0,4},{1,5},{2,6},{3,7},{4,0},{5,1},{6,2},{7,3},{8,12},{9,13},{10,... | collective-permute-start | bytes 221192 | tf_op jit(solution)/shard_map/ppermute | solution.py:498
  522.9 9.9 %collective-permute-start.66 = (bf16[192,768]{1,0:T(8,128)(2,1)S(1)}, bf16[192,768]{1,0:T(8,128)(2,1)S(1)}, u32[]{:S(2)}, u32[]{:S(2)}) collective-permute-start(bf16[192,768]{1,0:T(8,128)(2,1)S(1)} %pad_maximum_fusion.11), channel_id=1, source_target_pairs={{0,2},{1,3},{2,0},{3,1},{4,6},{5,7},{6,4},{7,5},{8,10},{9,11},{10,... | collective-permute-start | bytes 884744 | tf_op jit(solution)/shard_map/ppermute | solution.py:498
  523.0 13.0 %collective-permute-start.39 = (bf16[96,768]{1,0:T(8,128)(2,1)S(1)}, bf16[96,768]{1,0:T(8,128)(2,1)S(1)}, u32[]{:S(2)}, u32[]{:S(2)}) collective-permute-start(bf16[96,768]{1,0:T(8,128)(2,1)S(1)} %pad_maximum_fusion.16), channel_id=1, source_target_pairs={{0,2},{1,3},{2,0},{3,1},{4,6},{5,7},{6,4},{7,5},{8,10},{9,11},{10,... | collective-permute-start | bytes 442376 | tf_op jit(solution)/shard_map/ppermute | solution.py:498
  532.8 51.3 %collective-permute-start.73 = (bf16[384,768]{1,0:T(8,128)(2,1)}, bf16[384,768]{1,0:T(8,128)(2,1)}, u32[]{:S(2)}, u32[]{:S(2)}) collective-permute-start(bf16[384,768]{1,0:T(8,128)(2,1)} %pad_maximum_fusion.9), channel_id=1, source_target_pairs={{0,2},{1,3},{2,0},{3,1},{4,6},{5,7},{6,4},{7,5},{8,10},{9,11},{10,... | collective-permute-start | bytes 1769480 | tf_op jit(solution)/shard_map/ppermute | solution.py:498
  533.9 54.1 %collective-permute-start.67 = (bf16[384,768]{1,0:T(8,128)(2,1)}, bf16[384,768]{1,0:T(8,128)(2,1)}, u32[]{:S(2)}, u32[]{:S(2)}) collective-permute-start(bf16[384,768]{1,0:T(8,128)(2,1)} %pad_maximum_fusion.8), channel_id=1, source_target_pairs={{0,1},{1,0},{2,3},{3,2},{4,5},{5,4},{6,7},{7,6},{8,9},{9,8},{10,11... | collective-permute-start | bytes 1769480 | tf_op jit(solution)/shard_map/ppermute | solution.py:498
  536.0 64.4 %collective-permute-start.15 = (bf16[512,768]{1,0:T(8,128)(2,1)S(1)}, bf16[512,768]{1,0:T(8,128)(2,1)S(1)}, u32[]{:S(2)}, u32[]{:S(2)}) collective-permute-start(bf16[512,768]{1,0:T(8,128)(2,1)S(1)} %add_convert_fusion.3), channel_id=1, source_target_pairs={{0,16},{16,0},{8,24},{24,8},{1,17},{17,1},{9,25},{25,9},{2,18},{18... | collective-permute-start | bytes 2359304 | tf_op jit(solution)/shard_map/ppermute | solution.py:525
  584.1 9.4 %collective-permute-start.30 = (bf16[48,576]{1,0:T(8,128)(2,1)S(1)}, bf16[48,576]{1,0:T(8,128)(2,1)S(1)}, u32[]{:S(2)}, u32[]{:S(2)}) collective-permute-start(bf16[48,576]{1,0:T(8,128)(2,1)S(1)} %add_convert_fusion.27), channel_id=1, source_target_pairs={{0,1},{1,0},{2,3},{3,2},{4,5},{5,4},{6,7},{7,6},{8,9},{9,8},{10,11... | collective-permute-start | bytes 165896 | tf_op jit(solution)/shard_map/ppermute | solution.py:498
  596.6 9.2 %collective-permute-start.26 = (bf16[192,576]{1,0:T(8,128)(2,1)S(1)}, bf16[192,576]{1,0:T(8,128)(2,1)S(1)}, u32[]{:S(2)}, u32[]{:S(2)}) collective-permute-start(bf16[192,576]{1,0:T(8,128)(2,1)S(1)} %pad_maximum_fusion.13), channel_id=1, source_target_pairs={{0,1},{1,0},{2,3},{3,2},{4,5},{5,4},{6,7},{7,6},{8,9},{9,8},{10,11... | collective-permute-start | bytes 663560 | tf_op jit(solution)/shard_map/ppermute | solution.py:498
  601.7 9.6 %collective-permute-start.16 = (bf16[2,512,768]{2,1,0:T(8,128)(2,1)}, bf16[2,512,768]{2,1,0:T(8,128)(2,1)}, u32[]{:S(2)}, u32[]{:S(2)}) collective-permute-start(bf16[2,512,768]{2,1,0:T(8,128)(2,1)} %pad_maximum_fusion.4), channel_id=1, source_target_pairs={{0,8},{8,0},{16,24},{24,16},{1,9},{9,1},{17,25},{25,17},{2,10},{10... | collective-permute-start | bytes 4718600 | tf_op jit(solution)/shard_map/ppermute | solution.py:528
  (128 other events, 1255.3 us)

commit v2 on v1

v2 whole, which is shorter than its diff:
```python
import functools

import jax
import jax.numpy as jnp
from jax import lax
from jax.experimental import pallas as pl
from jax.experimental.pallas import tpu as pltpu
from jax.sharding import PartitionSpec as P

HEAD_DIM = 64
WIDE = 2 * HEAD_DIM
EPS = 1e-05
MASKED = -1e30
LOG2E = 1.4426950408889634
LN2 = 0.6931471805599453
f32 = jnp.float32
bf16 = jnp.bfloat16

CORE = [(0, 1), (1, 0), (2, 3), (3, 2)]
ACROSS = [(0, 2), (2, 0), (1, 3), (3, 1)]
MIB = 1 << 20
LIMIT = 56


def nn(left, right):
    return lax.dot_general(left, right, (((1,), (0,)), ((), ())), preferred_element_type=f32)


def nt(left, right):
    return lax.dot_general(left, right, (((1,), (1,)), ((), ())), preferred_element_type=f32)


def tn(left, right):
    return lax.dot_general(left, right, (((0,), (0,)), ((), ())), preferred_element_type=f32)


def lanes(rows):
    return lax.broadcasted_iota(jnp.int32, (rows, HEAD_DIM), 1)


def three_parts(value):
    high = value.astype(bf16).astype(f32)
    rest = value - high
    middle = rest.astype(bf16).astype(f32)
    return high, middle, rest - middle


def fill_queries(q_ref, rows, count, acc, heads):
    tail = jnp.where(lanes(count) == 0, 1.0, 0.0)
    for h in range(heads):
        part = acc[:, h * HEAD_DIM : (h + 1) * HEAD_DIM]
        q_ref[h, rows, :] = jnp.concatenate([part, tail], 1).astype(bf16)


def fill_keys(k_ref, v_ref, rows, start, count, acc, heads, limit):
    lane = lanes(count)
    index = start + lax.broadcasted_iota(jnp.int32, (count, HEAD_DIM), 0)
    tail = jnp.where(lane == 0, jnp.where(index < limit, 0.0, MASKED), jnp.where(lane < 4, 1.0, 0.0))
    ones = jnp.ones((count, HEAD_DIM), f32)
    for h in range(heads):
        k = acc[:, h * HEAD_DIM : (h + 1) * HEAD_DIM]
        v = acc[:, (heads + h) * HEAD_DIM : (heads + h + 1) * HEAD_DIM]
        k_ref[h, rows, :] = jnp.concatenate([k, tail], 1).astype(bf16)
        v_ref[h, rows, :] = jnp.concatenate([v, ones], 1).astype(bf16)


def attend_block(q_ref, k_ref, v_ref, att_ref, h, column, rows, count, key_end, causal):
    s = nt(q_ref[h, rows, :], k_ref[h, :key_end, :])
    if causal:
        r = lax.broadcasted_iota(jnp.int32, (count, count), 0)
        c = lax.broadcasted_iota(jnp.int32, (count, count), 1)
        diagonal = jnp.where(c <= r, s[:, key_end - count :], MASKED)
        s = diagonal if key_end == count else jnp.concatenate([s[:, : key_end - count], diagonal], 1)
    peak = jnp.max(s, 1, keepdims=True)
    p = jnp.exp2(s - peak).astype(bf16)
    o = nn(p, v_ref[h, :key_end, :])
    total = o[:, HEAD_DIM : HEAD_DIM + 1]
    att_ref[rows, column : column + HEAD_DIM] = (o[:, :HEAD_DIM] / total).astype(bf16)
    high, middle, low = three_parts(-(peak + jnp.log2(total)))
    lane = lanes(count)
    tail = jnp.where(
        lane == 0, 1.0, jnp.where(lane == 1, high, jnp.where(lane == 2, middle, jnp.where(lane == 3, low, 0.0)))
    )
    q_ref[h, rows, HEAD_DIM:] = tail.astype(bf16)


def fill_grads(do_ref, rows, count, grad, att, heads):
    lane = lanes(count)
    for h in range(heads):
        part = grad[:, h * HEAD_DIM : (h + 1) * HEAD_DIM].astype(bf16)
        mixed = att[:, h * HEAD_DIM : (h + 1) * HEAD_DIM].astype(f32)
        inner = jnp.sum(part.astype(f32) * mixed, 1, keepdims=True)
        high, middle, low = three_parts(-inner)
        tail = jnp.where(lane == 0, high, jnp.where(lane == 1, middle, jnp.where(lane == 2, low, 0.0)))
        do_ref[h, rows, :] = jnp.concatenate([part, tail.astype(bf16)], 1)


def back_block(q_ref, k_ref, v_ref, do_ref, dq_ref, dk_ref, dv_ref, h, rows, count, key_end, causal, first):
    q = q_ref[h, rows, :]
    d = do_ref[h, rows, :]
    k = k_ref[h, :key_end, :]
    v = v_ref[h, :key_end, :]
    p = jnp.exp2(nt(k, q))
    if causal:
        r = lax.broadcasted_iota(jnp.int32, (count, count), 0)
        c = lax.broadcasted_iota(jnp.int32, (count, count), 1)
        diagonal = jnp.where(r <= c, p[key_end - count :], 0.0)
        p = diagonal if key_end == count else jnp.concatenate([p[: key_end - count], diagonal], 0)
    ds = (p * nt(v, d)).astype(bf16)
    dv = nn(p.astype(bf16), d)
    dk = nn(ds, q)
    if first:
        dv_ref[h, :key_end, :] = dv
        dk_ref[h, :key_end, :] = dk
    else:
        dv_ref[h, :key_end, :] += dv
        dk_ref[h, :key_end, :] += dk
    dq_ref[h, rows, :] = tn(k, ds).T


def pack_heads(source, rows, heads, factor):
    return jnp.concatenate([source[h, rows, :HEAD_DIM] * factor for h in range(heads)], 1).astype(bf16)


def norm(resid):
    center = resid - jnp.mean(resid, -1, keepdims=True)
    scale = lax.rsqrt(jnp.mean(center * center, -1, keepdims=True) + EPS)
    return center * scale, scale


def norm_back(grad, gain, unit, scale):
    lifted = grad * gain
    first = jnp.mean(lifted, -1, keepdims=True)
    second = jnp.mean(lifted * unit, -1, keepdims=True)
    return scale * (lifted - first - unit * second)


def gelu_pair(value):
    scaled = value * 0.7071067811865476
    density = jnp.exp(-scaled * scaled) * 0.3989422804014327
    below = 0.5 * (1.0 + lax.erf(scaled))
    return value * below, below + value * density


BLOCK = 512
SPAN = 256


def both_halves(first_ref, second_ref, blocks):
    return jnp.where(pl.program_id(0) < blocks // 2, first_ref[...], second_ref[...]).astype(f32)


def self_forward_kernel(s_ref, x_ref, w_ref, *rest, heads, second):
    if second:
        att_own_ref, out_own_ref, out_ref, part_ref, q_ref, k_ref, v_ref, att_ref = rest
    else:
        m_ref, wq_ref, wk_ref, wv_ref, so_ref, co_ref, cw_ref, o_ref, ck_ref, cv_ref, q_ref, k_ref, v_ref, att_ref = rest

        @pl.when(pl.program_id(0) == 0)
        def _():
            for at, ref in enumerate((wq_ref, wk_ref, wv_ref)):
                cw_ref[at * ref.shape[0] : (at + 1) * ref.shape[0], :] = ref[...]
            for at, ref in enumerate((so_ref, co_ref)):
                o_ref[at * ref.shape[0] : (at + 1) * ref.shape[0], :] = ref[...]

    row = s_ref[0]
    limit = s_ref[1 + row]
    each = heads * HEAD_DIM
    at = pl.program_id(0)
    start = pl.multiple_of(at * BLOCK, BLOCK)
    acc = nt(x_ref[...], w_ref[...])
    everything = pl.ds(0, BLOCK)
    fill_queries(q_ref, everything, BLOCK, acc[:, :each] * (HEAD_DIM ** (-0.5) * LOG2E), heads)
    fill_keys(k_ref, v_ref, pl.ds(start, BLOCK), start, BLOCK, acc[:, each:], heads, limit)
    for block in range(k_ref.shape[1] // BLOCK):

        @pl.when(at == block)
        def _():
            for h in range(heads):
                attend_block(
                    q_ref, k_ref, v_ref, att_ref, h, h * HEAD_DIM, everything, BLOCK, (block + 1) * BLOCK, True
                )

    if second:
        part = nn(att_own_ref[...], out_own_ref[:each, :]) + nn(att_ref[...], out_ref[:each, :])
        part_ref[...] = part.astype(bf16)
    else:
        acc = nt(m_ref[...], cw_ref[each:, :])
        fill_keys(ck_ref, cv_ref, everything, start, BLOCK, acc, heads, s_ref[3 + row])


def memory_keys_kernel(s_ref, m_ref, w_ref, k_ref, v_ref, *, heads):
    row = s_ref[0]
    acc = nt(m_ref[...], w_ref[heads * HEAD_DIM :, :])
    fill_keys(k_ref, v_ref, pl.ds(0, BLOCK), pl.program_id(0) * BLOCK, BLOCK, acc, heads, s_ref[3 + row])


def cross_forward_kernel(
    s_ref, x_ref, pa_ref, pb_first_ref, pb_second_ref, gain_ref, shift_ref, cwa_ref, cwb_ref,
    ka_ref, va_ref, kb_ref, vb_ref, oa_ref, ob_ref,
    part_ref, h_ref, hl_ref, unit_ref, scale_ref, qa_ref, qb_ref, atta_ref, attb_ref, *, heads, blocks,
):
    row = s_ref[0]
    limit = s_ref[3 + row]
    source = ka_ref.shape[1]
    each = heads * HEAD_DIM
    everything = pl.ds(0, BLOCK)
    other = both_halves(pb_first_ref, pb_second_ref, blocks)
    unit, scale = norm(x_ref[...].astype(f32) + (pa_ref[...].astype(f32) + other))
    h = unit * gain_ref[...] + shift_ref[...]
    h_ref[...] = h
    unit_ref[...] = unit.astype(bf16)
    scale_ref[...] = scale
    low = h.astype(bf16)
    hl_ref[...] = low
    factor = HEAD_DIM ** (-0.5) * LOG2E
    fill_queries(qa_ref, everything, BLOCK, nt(low, cwa_ref[:each, :]) * factor, heads)
    fill_queries(qb_ref, everything, BLOCK, nt(low, cwb_ref[:each, :]) * factor, heads)

    step = 256
    live = (limit + step - 1) // step
    for count in range(1, source // step + 1):

        @pl.when(live == count)
        def _():
            for q_ref, k_ref, v_ref, att_ref in ((qa_ref, ka_ref, va_ref, atta_ref), (qb_ref, kb_ref, vb_ref, attb_ref)):
                for h in range(heads):
                    attend_block(q_ref, k_ref, v_ref, att_ref, h, h * HEAD_DIM, everything, BLOCK, count * step, False)

    part_ref[...] = (nn(atta_ref[...], oa_ref[each:, :]) + nn(attb_ref[...], ob_ref[each:, :])).astype(bf16)


def ffn_forward_kernel(
    h_in_ref, pa_ref, pb_first_ref, pb_second_ref, gain_ref, shift_ref, upa_ref, upb_ref, downa_ref, downb_ref,
    part_ref, h_ref, hl_ref, unit_ref, scale_ref, acta_ref, actb_ref, slopea_ref, slopeb_ref, *, blocks,
):
    other = both_halves(pb_first_ref, pb_second_ref, blocks)
    unit, scale = norm(h_in_ref[...] + (pa_ref[...].astype(f32) + other))
    h = unit * gain_ref[...] + shift_ref[...]
    h_ref[...] = h
    unit_ref[...] = unit.astype(bf16)
    scale_ref[...] = scale
    low = h.astype(bf16)
    hl_ref[...] = low
    part = None
    for up_ref, down_ref, act_ref, slope_ref in (
        (upa_ref, downa_ref, acta_ref, slopea_ref),
        (upb_ref, downb_ref, actb_ref, slopeb_ref),
    ):
        act, slope = gelu_pair(nn(low, up_ref[...]))
        act = act.astype(bf16)
        act_ref[...] = act
        slope_ref[...] = slope.astype(bf16)
        term = nn(act, down_ref[...])
        part = term if part is None else part + term
    part_ref[...] = part.astype(bf16)


def ffn_back_kernel(
    s_ref, h_ref, pa_ref, pb_first_ref, pb_second_ref, cot_ref, gain_ref, shift_ref, upa_ref, upb_ref, downa_ref, downb_ref,
    slopea_ref, slopeb_ref,
    part_ref, out_ref, half_ref, d_ref, e_ref, prea_ref, preb_ref, sums_ref, *, blocks,
):
    row = s_ref[0]
    limit = s_ref[1 + row]
    at = pl.program_id(0)

    @pl.when(at == 0)
    def _():
        sums_ref[...] = jnp.zeros_like(sums_ref)

    other = both_halves(pb_first_ref, pb_second_ref, blocks)
    unit, scale = norm(h_ref[...] + (pa_ref[...].astype(f32) + other))
    out = (unit * gain_ref[...] + shift_ref[...]).astype(bf16)
    out_ref[...] = out

    @pl.when(at // (blocks // 2) == s_ref[5])
    def _():
        half_ref[...] = out

    index = at * SPAN + lax.broadcasted_iota(jnp.int32, (SPAN, 1), 0)
    grad = jnp.where(index < limit, cot_ref[...].astype(f32), 0.0)
    sums_ref[0:1, :] += jnp.sum(grad * unit, 0, keepdims=True)
    sums_ref[1:2, :] += jnp.sum(grad, 0, keepdims=True)
    d = norm_back(grad, gain_ref[...], unit, scale)
    d_ref[...] = d
    e = d.astype(bf16)
    e_ref[...] = e
    part = None
    for up_ref, down_ref, slope_ref, pre_ref in (
        (upa_ref, downa_ref, slopea_ref, prea_ref),
        (upb_ref, downb_ref, slopeb_ref, preb_ref),
    ):
        pre = (nt(e, down_ref[...]) * slope_ref[...].astype(f32)).astype(bf16)
        pre_ref[...] = pre
        term = nt(pre, up_ref[...])
        part = term if part is None else part + term
    part_ref[...] = part.astype(bf16)


def ffn_grad_kernel(h_ref, act_ref, e_ref, pre_ref, up_ref, down_ref):
    up_ref[...] = tn(h_ref[...], pre_ref[...]).astype(bf16)
    down_ref[...] = tn(act_ref[...], e_ref[...]).astype(bf16)


def norm_attention_back(
    d_in_ref, pa_ref, pb_first_ref, pb_second_ref, gain_ref, unit_ref, scale_ref, groups, d_ref, e_ref, sums_ref, do_ref,
    heads, count, blocks,
):
    @pl.when(pl.program_id(0) == 0)
    def _():
        sums_ref[...] = jnp.zeros_like(sums_ref)

    other = both_halves(pb_first_ref, pb_second_ref, blocks)
    grad = d_in_ref[...] + (pa_ref[...].astype(f32) + other)
    unit = unit_ref[...].astype(f32)
    sums_ref[0:1, :] += jnp.sum(grad * unit, 0, keepdims=True)
    sums_ref[1:2, :] += jnp.sum(grad, 0, keepdims=True)
    d = norm_back(grad, gain_ref[...], unit, scale_ref[...])
    d_ref[...] = d
    e = d.astype(bf16)
    e_ref[...] = e
    for g, (out, att_ref) in enumerate(groups):
        fill_grads(do_ref.at[g], pl.ds(0, count), count, nt(e, out), att_ref[...], heads)


def cross_back_kernel(
    s_ref, d_in_ref, pa_ref, pb_first_ref, pb_second_ref, gain_ref, unit_ref, scale_ref, oa_ref, ob_ref, atta_ref, attb_ref,
    qa_ref, qb_ref, ka_ref, va_ref, kb_ref, vb_ref, cwa_ref, cwb_ref,
    part_ref, d_ref, e_ref, sums_ref, dqa_ref, dqb_ref, dkva_ref, dkvb_ref, do_ref, dq_ref, dk_ref, dv_ref, *, heads, blocks,
):
    row = s_ref[0]
    limit = s_ref[3 + row]
    source = ka_ref.shape[1]
    each = heads * HEAD_DIM
    at = pl.program_id(0)
    norm_attention_back(
        d_in_ref, pa_ref, pb_first_ref, pb_second_ref, gain_ref, unit_ref, scale_ref,
        ((oa_ref[each:, :], atta_ref), (ob_ref[each:, :], attb_ref)),
        d_ref, e_ref, sums_ref, do_ref, heads, BLOCK, blocks,
    )

    @pl.when(at == 0)
    def _():
        dk_ref[...] = jnp.zeros_like(dk_ref)
        dv_ref[...] = jnp.zeros_like(dv_ref)

    step = 256
    live = (limit + step - 1) // step
    everything = pl.ds(0, BLOCK)
    for count in range(1, source // step + 1):

        @pl.when(live == count)
        def _():
            for g, (q_ref, k_ref, v_ref) in enumerate(((qa_ref, ka_ref, va_ref), (qb_ref, kb_ref, vb_ref))):

                @pl.loop(0, heads)
                def _(h):
                    back_block(
                        q_ref, k_ref, v_ref, do_ref.at[g], dq_ref.at[g], dk_ref.at[g], dv_ref.at[g], h,
                        everything, BLOCK, count * step, False, False,
                    )

    for g, dqo_ref in enumerate((dqa_ref, dqb_ref)):
        dqo_ref[...] = pack_heads(dq_ref.at[g], everything, heads, HEAD_DIM ** (-0.5))
    part_ref[...] = (nn(dqa_ref[...], cwa_ref[:each, :]) + nn(dqb_ref[...], cwb_ref[:each, :])).astype(bf16)

    @pl.when(at == blocks - 1)
    def _():
        for g, dkv_ref in enumerate((dkva_ref, dkvb_ref)):

            @pl.loop(0, source, step=BLOCK)
            def _(start):
                rows = pl.ds(pl.multiple_of(start, BLOCK), BLOCK)
                dkv_ref[rows, :] = jnp.concatenate(
                    [pack_heads(dk_ref.at[g], rows, heads, LN2), pack_heads(dv_ref.at[g], rows, heads, 1.0)], 1
                )


def cross_grad_kernel(s_ref, h_ref, m_ref, att_ref, e_ref, dq_ref, dkv_ref, g_ref):
    each = dq_ref.shape[1]
    g_ref[:each, :] = tn(dq_ref[...], h_ref[...]).astype(bf16)
    g_ref[each : 3 * each, :] = tn(dkv_ref[...], m_ref[...]).astype(bf16)
    g_ref[3 * each :, :] = tn(att_ref[...], e_ref[...]).astype(bf16)


def memory_grad_kernel(s_ref, a_ref, b_ref, wa_ref, wb_ref, send_ref, keep_ref, *, skip):
    part = (nn(a_ref[...], wa_ref[skip:, :]) + nn(b_ref[...], wb_ref[skip:, :])).astype(bf16)
    mine = pl.program_id(0) == s_ref[5]

    @pl.when(mine)
    def _():
        keep_ref[...] = part

    @pl.when(jnp.logical_not(mine))
    def _():
        send_ref[...] = part


def tokens_grad_kernel(s_ref, d_ref, a_ref, b_ref, wa_ref, wb_ref, send_ref, keep_ref):
    part = nn(a_ref[...], wa_ref[...]) + nn(b_ref[...], wb_ref[...])
    mine = pl.program_id(0) == s_ref[5]

    @pl.when(mine)
    def _():
        keep_ref[...] = d_ref[...] + part

    @pl.when(jnp.logical_not(mine))
    def _():
        send_ref[...] = part.astype(bf16)


def finish_kernel(keep_ref, got_ref, out_ref):
    out_ref[...] = (keep_ref[...].astype(f32) + got_ref[...].astype(f32)).astype(bf16)


def place_kernel(s_ref, *refs, shift):
    out_ref = refs[-1]
    pieces = refs[:-1]
    half = out_ref.shape[0]
    row, core, at = s_ref[0], s_ref[5], pl.program_id(0)
    if shift:
        sources = [
            (pieces[0].at[:half, :], 2 * row), (pieces[0].at[half:, :], 2 * row + 1),
            (pieces[1], 2 * (1 - row) + core), (pieces[2], 2 * (1 - row) + 1 - core),
        ]
    else:
        sources = [
            (pieces[0], 2 * row + core), (pieces[1], 2 * row + 1 - core),
            (pieces[2], 2 * (1 - row) + core), (pieces[3], 2 * (1 - row) + 1 - core),
        ]
    for ref, place in sources:

        @pl.when(at == place)
        def _():
            out_ref[...] = ref[...]


def hop_kernel(s_ref, *refs, plans, slots):
    at = 0
    scratch = refs[-1]
    inputs = sum(own + got for own, got, _ in plans)
    outs = list(refs[inputs:-1])
    for own, got, chains in plans:
        mine, theirs = refs[at : at + own], refs[at + own : at + own + got]
        at += own + got
        row = 0
        for a_ref, b_ref in zip(mine, theirs):
            count = a_ref.shape[0]
            scratch[row : row + count, :] = (a_ref[...].astype(f32) + b_ref[...].astype(f32)).astype(bf16)
            row += count
        end = max(first + rows for first, rows, _ in chains)
        if row < end:
            scratch[row:end, :] = jnp.zeros((end - row, scratch.shape[1]), bf16)
        for first, rows, bit in chains:
            if bit is None:
                outs.pop(0)[...] = scratch[first : first + rows, :]
            else:
                half = rows // 2
                high = s_ref[6 + bit]
                outs.pop(0)[...] = scratch[pl.ds(pl.multiple_of(first + (1 - high) * half, 16), half), :]
                outs.pop(0)[...] = scratch[pl.ds(pl.multiple_of(first + high * half, 16), half), :]


def gather_kernel(s_ref, *refs, chains, cuts):
    scratch = refs[-1]
    at = 0
    for first, rows, order in chains:
        piece = rows // 8
        for turn in range(8):
            place = first
            for level, bit in enumerate(order):
                flip = (turn >> (2 - level)) & 1
                value = s_ref[6 + bit] if flip == 0 else 1 - s_ref[6 + bit]
                place = place + value * (rows >> (level + 1))
            scratch[pl.ds(pl.multiple_of(place, 16), piece), :] = refs[at][...]
            at += 1
    for out_ref, (first, count) in zip(refs[at:-1], cuts):
        out_ref[...] = scratch[first : first + count, :].astype(f32)


def add_kernel(*refs):
    count = len(refs) // 3
    for a_ref, b_ref, out_ref in zip(refs[:count], refs[count : 2 * count], refs[2 * count :]):
        out_ref[...] = (a_ref[...].astype(f32) + b_ref[...].astype(f32)).astype(bf16)


def self_back_heads(q_ref, k_ref, v_ref, do_ref, dq_ref, dk_ref, dv_ref, dqkv_ref, length, heads, at):
    each = heads * HEAD_DIM

    @pl.when(at == 0)
    def _():
        dk_ref[...] = jnp.zeros_like(dk_ref)
        dv_ref[...] = jnp.zeros_like(dv_ref)

    everything = pl.ds(0, SPAN)
    for block in range(length // SPAN):

        @pl.when(at == block)
        def _():
            @pl.loop(0, heads)
            def _(h):
                back_block(
                    q_ref, k_ref, v_ref, do_ref, dq_ref, dk_ref, dv_ref, h,
                    everything, SPAN, (block + 1) * SPAN, True, False,
                )

    dqkv_ref[pl.ds(pl.multiple_of(at * SPAN, SPAN), SPAN), :each] = pack_heads(dq_ref, everything, heads, HEAD_DIM ** (-0.5))

    @pl.when(at == length // SPAN - 1)
    def _():
        @pl.loop(0, length, step=BLOCK)
        def _(start):
            rows = pl.ds(pl.multiple_of(start, BLOCK), BLOCK)
            dqkv_ref[rows, each:] = jnp.concatenate(
                [pack_heads(dk_ref, rows, heads, LN2), pack_heads(dv_ref, rows, heads, 1.0)], 1
            )


def self_back_first_kernel(
    s_ref, x_ref, d_in_ref, pa_ref, pb_first_ref, pb_second_ref, gain_ref, unit_ref, scale_ref, oa_ref, ob_ref,
    atta_ref, attb_ref, q_ref, k_ref, v_ref, sums_two_ref, sums_three_ref,
    d_ref, do_out_ref, dqkv_ref, gw_ref, ra_ref, rb_ref, e_ref, sums_ref, do_ref, dq_ref, dk_ref, dv_ref, *, heads, blocks,
):
    at = pl.program_id(0)
    each = heads * HEAD_DIM
    rows = pl.ds(pl.multiple_of(at * SPAN, SPAN), SPAN)
    norm_attention_back(
        d_in_ref, pa_ref, pb_first_ref, pb_second_ref, gain_ref, unit_ref, scale_ref,
        ((oa_ref[:each, :], atta_ref.at[rows, :]), (ob_ref[:each, :], attb_ref.at[rows, :])),
        d_ref, e_ref.at[rows, :], sums_ref, do_ref, heads, SPAN, blocks,
    )
    do_out_ref[...] = do_ref[0]
    self_back_heads(q_ref, k_ref, v_ref, do_ref.at[1], dq_ref, dk_ref, dv_ref, dqkv_ref, k_ref.shape[1], heads, at)

    @pl.when(at == blocks - 1)
    def _():
        gw_ref[...] = tn(dqkv_ref[...], x_ref[...]).astype(bf16)
        norms = jnp.concatenate(
            [sums_ref[:2, :], sums_two_ref[:2, :], sums_three_ref[:2, :], jnp.zeros((10, x_ref.shape[1]), f32)], 0
        ).astype(bf16)
        for att_ref, r_ref in ((atta_ref, ra_ref), (attb_ref, rb_ref)):
            r_ref[:each, :] = tn(att_ref[...], e_ref[...]).astype(bf16)
            r_ref[each:, :] = norms


def self_back_second_kernel(s_ref, x_ref, q_ref, k_ref, v_ref, do_ref, dqkv_ref, gw_ref, dq_ref, dk_ref, dv_ref, *, heads, blocks):
    at = pl.program_id(0)
    self_back_heads(q_ref, k_ref, v_ref, do_ref, dq_ref, dk_ref, dv_ref, dqkv_ref, k_ref.shape[1], heads, at)

    @pl.when(at == blocks - 1)
    def _():
        gw_ref[...] = tn(dqkv_ref[...], x_ref[...]).astype(bf16)


class Row:
    def __init__(self, array, length, how="whole"):
        self.array, self.length, self.how = array, length, how


class Part:
    def __init__(self, array, how="rows", pick=None):
        self.array, self.how, self.pick = array, how, pick


def block_of(shape, how, blocks, pick=None):
    rank = len(shape)
    if how == "whole":
        return pl.BlockSpec(shape, lambda *a: (0,) * rank)
    if how == "own half":
        return pl.BlockSpec(
            (2 * shape[0] // blocks,) + shape[1:], lambda i, s: (jnp.clip(i - s[5] * (blocks // 2), 0, blocks // 2 - 1), 0)
        )
    dim = rank - 2 if how == "rows" else rank - 1
    pick = pick or (lambda i: i)
    parts = blocks if how != "half" else blocks // 2
    if how == "half":
        dim = rank - 2
    block = tuple(n // parts if d == dim else n for d, n in enumerate(shape))
    return pl.BlockSpec(block, lambda i, *a: tuple(pick(i) if d == dim else 0 for d in range(rank)))


def row_of(item, blocks):
    width = item.array.shape[1]
    if item.how == "whole":
        return pl.BlockSpec((item.length, width), lambda i, s: (s[0], 0))
    if item.how == "rows":
        return pl.BlockSpec((item.length // blocks, width), lambda i, s: (s[0] * blocks + i, 0))
    return pl.BlockSpec((item.length, width // blocks), lambda i, s: (s[0], i))


def call(kernel, name, blocks, inputs, outputs, scalars=None, scratch=(), micros=5.0, limit=LIMIT, after=()):
    specs, arrays = [], []
    for item in inputs:
        if isinstance(item, Row):
            specs.append(row_of(item, blocks))
            arrays.append(item.array)
        elif isinstance(item, Part):
            specs.append(block_of(item.array.shape, item.how, blocks, item.pick))
            arrays.append(item.array)
        else:
            specs.append(block_of(item.shape, "whole", blocks))
            arrays.append(item)
    count = len(arrays)
    for item in after:
        specs.append(pl.BlockSpec(memory_space=pl.ANY))
        arrays.append(item)
    shapes = [jax.ShapeDtypeStruct(shape, dtype) for shape, dtype, _ in outputs]
    out_specs = [block_of(shape, how, blocks) for shape, _, how in outputs]
    lead = 0 if scalars is None else 1
    if after:
        inner = kernel

        def kernel(*refs):
            return inner(*refs[: lead + count], *refs[lead + count + len(after) :])

    settings = dict(
        out_shape=shapes,
        compiler_params=pltpu.CompilerParams(vmem_limit_bytes=limit * MIB, dimension_semantics=("arbitrary",)),
        cost_estimate=pl.CostEstimate(flops=int(micros * 1.0e9), bytes_accessed=0, transcendentals=0),
        name=name,
    )
    if scalars is None:
        return pl.pallas_call(
            kernel, grid=(blocks,), in_specs=specs, out_specs=out_specs, scratch_shapes=list(scratch), **settings
        )(*arrays)
    grid_spec = pltpu.PrefetchScalarGridSpec(
        num_scalar_prefetch=1, grid=(blocks,), in_specs=specs, out_specs=out_specs, scratch_shapes=list(scratch)
    )
    return pl.pallas_call(kernel, grid_spec=grid_spec, **settings)(scalars, *arrays)


def local(
    size, tokens, memory, cotangent, tgt_len, src_len, self_query, self_key, self_value, self_out,
    cross_query, cross_key, cross_value, cross_out, ffn_up, ffn_down,
    gain_one, shift_one, gain_two, shift_two, gain_three, shift_three,
):
    width = tokens.shape[1]
    length = tokens.shape[0] // 2
    source = memory.shape[0] // 2
    each = self_query.shape[1]
    heads = each // HEAD_DIM
    hidden = ffn_up.shape[1]
    place = lax.axis_index("tp").astype(jnp.int32)
    group = lax.axis_index("dp").astype(jnp.int32)
    scalars = jnp.concatenate(
        [jnp.stack([place // 2]), tgt_len, src_len, jnp.stack([place % 2] + [(group >> b) & 1 for b in range(3)])]
    )
    gain_one, shift_one, gain_two, shift_two, gain_three, shift_three = (
        v.reshape(1, width) for v in (gain_one, shift_one, gain_two, shift_two, gain_three, shift_three)
    )
    big, small = length // BLOCK, length // SPAN

    def across(value):
        return lax.ppermute(value, "tp", ACROSS)

    def sibling(value):
        return lax.ppermute(value, "tp", CORE)

    def exchange(part):
        half = length // 2
        return sibling(part[:half]), sibling(part[half:])

    def shares(part, halves, blocks):
        per = blocks // 2
        first = Part(halves[0], "half", lambda i: jnp.minimum(i, per - 1))
        second = Part(halves[1], "half", lambda i: jnp.maximum(i - per, 0))
        return [Part(part), first, second]

    w_a = jnp.concatenate([self_query.T, self_key.T, self_value.T], 0)
    w_b = across(w_a)
    up_a, down_a = ffn_up, ffn_down
    up_b = across(up_a)
    down_b = across(down_a)

    head_shape = ((heads, length, WIDE), bf16, "rows")
    key_shape = ((heads, source, WIDE), bf16, "rows")
    kept_shape = ((heads, length, WIDE), bf16, "whole")
    low = ((length, width), bf16, "rows")
    full = ((length, width), f32, "rows")
    column = ((length, 1), f32, "rows")
    att_shape = ((length, each), bf16, "rows")
    sums = ((8, width), f32, "whole")

    cw_a, o_a, ck_a, cv_a, q_a, k_a, v_a, att_a = call(
        functools.partial(self_forward_kernel, heads=heads, second=False), "self_forward_own", big,
        [
            Row(tokens, length, "rows"), w_a, Row(memory, source, "rows"), cross_query.T, cross_key.T, cross_value.T,
            self_out, cross_out,
        ],
        [
            ((3 * each, width), bf16, "whole"), ((2 * each, width), bf16, "whole"),
            key_shape, key_shape, head_shape, kept_shape, kept_shape, att_shape,
        ],
        scalars, micros=13,
    )
    o_b = across(o_a)
    cw_b = across(cw_a)
    part, q_b, k_b, v_b, att_b = call(
        functools.partial(self_forward_kernel, heads=heads, second=True), "self_forward_other", big,
        [Row(tokens, length, "rows"), w_b, Part(att_a), o_a, o_b],
        [low, head_shape, kept_shape, kept_shape, att_shape], scalars, micros=13,
    )
    halves = exchange(part)
    ck_b, cv_b = call(
        functools.partial(memory_keys_kernel, heads=heads), "memory_keys_other", big, [Row(memory, source, "rows"), cw_b],
        [key_shape, key_shape], scalars, micros=4,
    )
    part, h_one, h_one_low, unit_one, scale_one, cq_rows_a, cq_rows_b, catt_a, catt_b = call(
        functools.partial(cross_forward_kernel, heads=heads, blocks=big), "cross_forward", big,
        [Row(tokens, length, "rows"), *shares(part, halves, big), gain_one, shift_one, cw_a, cw_b, ck_a, cv_a, ck_b, cv_b, o_a, o_b],
        [low, full, low, low, column, head_shape, head_shape, att_shape, att_shape], scalars, micros=20,
    )
    halves = exchange(part)
    hid = ((length, hidden), bf16, "rows")
    part, h_two, h_two_low, unit_two, scale_two, act_a, act_b, slope_a, slope_b = call(
        functools.partial(ffn_forward_kernel, blocks=small), "ffn_forward", small,
        [Part(h_one), *shares(part, halves, small), gain_two, shift_two, up_a, up_b, down_a, down_b],
        [low, full, low, low, column, hid, hid, hid, hid], micros=13,
    )
    halves = exchange(part)
    part, out_row, out_half, d_three, e_three, pre_a, pre_b, sums_three = call(
        functools.partial(ffn_back_kernel, blocks=small), "ffn_back", small,
        [
            Part(h_two), *shares(part, halves, small), Row(cotangent, length, "rows"), gain_three, shift_three,
            up_a, up_b, down_a, down_b, Part(slope_a), Part(slope_b),
        ],
        [low, low, ((length // 2, width), bf16, "own half"), full, low, hid, hid, sums], scalars, micros=15,
    )
    halves = exchange(part)
    third = width // SPAN
    square = ((width, hidden), bf16, "rows")
    gu_b, gd_b = call(
        ffn_grad_kernel, "ffn_grad_other", third, [Part(h_two_low, "columns"), Part(act_b, "columns"), e_three, pre_b],
        [square, square], micros=6,
    )
    gu_got, gd_got = across(gu_b), across(gd_b)
    gu_a, gd_a = call(
        ffn_grad_kernel, "ffn_grad_own", third, [Part(h_two_low, "columns"), Part(act_a, "columns"), e_three, pre_a],
        [square, square], micros=6,
    )

    dkv_shape = ((source, 2 * each), bf16, "whole")
    part, d_two, e_two, sums_two, dcq_a, dcq_b, dckv_a, dckv_b = call(
        functools.partial(cross_back_kernel, heads=heads, blocks=big), "cross_back", big,
        [
            Part(d_three), *shares(part, halves, big), gain_two, Part(unit_two), Part(scale_two), o_a, o_b,
            Part(catt_a), Part(catt_b), Part(cq_rows_a), Part(cq_rows_b), ck_a, cv_a, ck_b, cv_b, cw_a, cw_b,
        ],
        [low, full, low, sums, att_shape, att_shape, dkv_shape, dkv_shape], scalars,
        scratch=[
            pltpu.VMEM((2, heads, BLOCK, WIDE), bf16),
            pltpu.VMEM((2, heads, BLOCK, WIDE), f32),
            pltpu.VMEM((2, heads, source, WIDE), f32),
            pltpu.VMEM((2, heads, source, WIDE), f32),
        ],
        micros=36,
    )
    halves = exchange(part)

    def cross_grads(name, att, dq, dkv, after=()):
        return call(
            cross_grad_kernel, name, third,
            [Part(h_one_low, "columns"), Row(memory, source, "columns"), att, Part(e_two, "columns"), dq, dkv],
            [((4 * each, width), bf16, "columns")], scalars, micros=6, after=after,
        )[0]

    gc_b = cross_grads("cross_grad_other", catt_b, dcq_b, dckv_b)
    gc_got = across(gc_b)
    gc_a = cross_grads("cross_grad_own", catt_a, dcq_a, dckv_a)
    whole_square = ((width, hidden), bf16, "rows")
    gu_one, gd_one = call(
        add_kernel, "ffn_grad_join", third, [Part(gu_a), Part(gd_a), Part(gu_got), Part(gd_got)], [whole_square] * 2, micros=3,
        after=[gc_a],
    )
    gu_sum, gd_sum = lax.psum((gu_one, gd_one), "dp")
    half_low = ((length // 2, width), bf16, "whole")
    memory_send, memory_keep = call(
        functools.partial(memory_grad_kernel, skip=each), "memory_grad", 2, [Part(dckv_a), Part(dckv_b), cw_a, cw_b],
        [half_low, half_low], scalars, micros=4, after=[gu_one],
    )

    kept_w = ((3 * each, width), bf16, "whole")
    rest_shape = ((each + 16, width), bf16, "whole")
    qkv_shape = ((length, 3 * each), bf16, "whole")
    back_scratch = [
        pltpu.VMEM((heads, SPAN, WIDE), f32),
        pltpu.VMEM((heads, length, WIDE), f32),
        pltpu.VMEM((heads, length, WIDE), f32),
    ]
    d_one, do_a, dqkv_b, gw_b, rest_a, rest_b = call(
        functools.partial(self_back_first_kernel, heads=heads, blocks=small), "self_back_other", small,
        [
            Row(tokens, length), Part(d_two), *shares(part, halves, small), gain_one, Part(unit_one), Part(scale_one), o_a, o_b,
            att_a, att_b, Part(q_b), k_b, v_b, sums_two, sums_three,
        ],
        [full, head_shape, qkv_shape, kept_w, rest_shape, rest_shape], scalars,
        scratch=[pltpu.VMEM((length, width), bf16), pltpu.VMEM((8, width), f32), pltpu.VMEM((2, heads, SPAN, WIDE), bf16)]
        + back_scratch,
        micros=25,
    )
    rest_got = across(rest_b)
    gw_got = across(gw_b)

    early = (0, 4 * each, (0, 1, 2))
    late = ((0, 512, (0, 1, 2)), (512, 384, (1, 2, 0)))

    def hop(name, plans, after=(), micros=2):
        inputs, outputs, kernel_plans, most = [], [], [], 0
        for own, got, chains in plans:
            inputs += [*own, *got]
            kernel_plans.append((len(own), len(got), chains))
            for first, rows, bit in chains:
                most = max(most, first + rows)
                outputs += [((rows, width), bf16, "whole")] if bit is None else [((rows // 2, width), bf16, "whole")] * 2
        return call(
            functools.partial(hop_kernel, plans=kernel_plans, slots=most), name, 1, inputs, outputs, scalars,
            scratch=[pltpu.VMEM((most, width), bf16)], micros=micros, after=after,
        )

    def along(value, bit):
        return lax.ppermute(value, "dp", [(i, i ^ (1 << bit)) for i in range(size)])

    def spread(piece, order):
        pieces = [piece]
        for bit in reversed(order):
            pieces = pieces + [along(p, bit) for p in pieces]
        return pieces

    small_size = size == 8
    if small_size:
        e_order = early[2]
        send, keep_e = hop("sum_cross_a", [([gc_a], [gc_got], [(0, early[1], e_order[0])])])
        got_e = along(send, e_order[0])
    dqkv_a, gw_a = call(
        functools.partial(self_back_second_kernel, heads=heads, blocks=small), "self_back_own", small,
        [Row(tokens, length), Part(q_a), k_a, v_a, Part(do_a)],
        [qkv_shape, kept_w], scalars, scratch=back_scratch, micros=15, after=[keep_e] if small_size else (),
    )
    pinned = ()
    if small_size:
        (f0, n0, o0), (f1, n1, o1) = late
        s0, k0, s1, k1, se, keep_e = hop(
            "sum_self_a",
            [
                ([gw_a, rest_a], [gw_got, rest_got], [(f0, n0, o0[0]), (f1, n1, o1[0])]),
                ([keep_e], [got_e], [(0, early[1] // 2, e_order[1])]),
            ],
            micros=3,
        )
        g0, g1, got_e = along(s0, o0[0]), along(s1, o1[0]), along(se, e_order[1])
        pinned = [k0]
    tokens_send, tokens_keep = call(
        tokens_grad_kernel, "tokens_grad", 2, [Part(d_one), Part(dqkv_a), Part(dqkv_b), w_a, w_b],
        [half_low, ((length // 2, width), f32, "whole")], scalars, micros=5, after=pinned,
    )

    def finish(name, keep, send, after=()):
        mine = call(finish_kernel, name, 2, [Part(keep), Part(sibling(send))], [((length // 2, width), bf16, "rows")], micros=2, after=after)[0]
        return mine, across(mine)

    def placed(name, pieces, shift):
        return call(
            functools.partial(place_kernel, shift=shift), name, 4, pieces, [((2 * length, width), bf16, "rows")], scalars, micros=3
        )[0]

    out_far = across(out_half)
    layer_out = placed("place_layer_out", [out_row, out_far, sibling(out_far)], True)
    mine, far = finish("memory_finish", memory_keep, memory_send)
    memory_grad = placed("place_memory_grad", [mine, sibling(mine), far, sibling(far)], False)
    mine, far = finish("tokens_finish", tokens_keep, tokens_send)
    tokens_grad = placed("place_tokens_grad", [mine, sibling(mine), far, sibling(far)], False)

    shapes = [((each, width), f32, "whole")] * 4
    if small_size:
        s0, k0, s1, k1, se, keep_e = hop(
            "sum_self_b",
            [([k0], [g0], [(0, n0 // 2, o0[1])]), ([k1], [g1], [(0, n1 // 2, o1[1])]), ([keep_e], [got_e], [(0, early[1] // 4, e_order[2])])],
        )
        g0, g1, got_e = along(s0, o0[1]), along(s1, o1[1]), along(se, e_order[2])
        s0, k0, s1, k1, piece_e = hop(
            "sum_self_c",
            [([k0], [g0], [(0, n0 // 4, o0[2])]), ([k1], [g1], [(0, n1 // 4, o1[2])]), ([keep_e], [got_e], [(0, early[1] // 8, None)])],
        )
        g0, g1 = along(s0, o0[2]), along(s1, o1[2])
        pieces_e = spread(piece_e, e_order)
        piece0, piece1 = hop("sum_self_d", [([k0], [g0], [(0, n0 // 8, None)]), ([k1], [g1], [(0, n1 // 8, None)])])
        pieces = spread(piece0, o0) + spread(piece1, o1)
        cross = call(
            functools.partial(gather_kernel, chains=[early], cuts=[(i * each, each) for i in range(4)]), "gather_cross", 1,
            pieces_e, shapes, scalars, scratch=[pltpu.VMEM((early[1], width), bf16)], micros=3,
        )
        self_grads = call(
            functools.partial(gather_kernel, chains=late, cuts=[(i * each, each) for i in range(4)] + [(4 * each, 16)]),
            "gather_self", 1, pieces, shapes + [((16, width), f32, "whole")], scalars,
            scratch=[pltpu.VMEM((896, width), bf16)], micros=3,
        )
        norms = self_grads[4]
    else:
        def add(mine, got):
            return (mine.astype(f32) + got.astype(f32)).astype(bf16)

        cross = jnp.split(lax.psum(add(gc_a, gc_got), "dp").astype(f32), 4)
        self_grads = jnp.split(lax.psum(add(gw_a, gw_got), "dp").astype(f32), 3)
        rest = lax.psum(add(rest_a, rest_got), "dp").astype(f32)
        self_grads = [*self_grads, rest[:each]]
        norms = rest[each:]
    return (
        layer_out, tokens_grad, memory_grad,
        self_grads[0].T, self_grads[1].T, self_grads[2].T, self_grads[3],
        cross[0].T, cross[1].T, cross[2].T, cross[3],
        gu_sum.astype(f32), gd_sum.astype(f32),
        *(norms[i] for i in range(6)),
    )


def solution(mesh):
    rows, columns, down = P("dp", None), P(None, "tp"), P("tp", None)
    return jax.shard_map(
        functools.partial(local, mesh.shape["dp"]),
        mesh=mesh,
        in_specs=(rows, rows, rows, P("dp"), P("dp"))
        + (columns, columns, columns, down) * 2
        + (columns, down)
        + (P(),) * 6,
        out_specs=(rows, rows, rows) + (columns, columns, columns, down) * 2 + (columns, down) + (P(),) * 6,
        check_vma=False,
    )
```

time: 623 us -> 446 us (0.72)
  waiting for transfers between devices: 248 us -> 95.8 us
  Pallas kernels: 168 us -> 242 us
  other arithmetic: 54.1 us -> 5.73 us
  starting transfers between devices: 89.7 us -> 53.8 us
  local copies, waits for them, and re-layouts: 52.4 us -> 27.4 us
  between operations: 2.58 us -> 14.8 us
    ppermute x51 -> x30, waiting for transfers between devices: 136 us -> 49.7 us  [along(): return lax.ppermute(value, 'dp', [(i, i ^ 1 << bit) for i in range(size)])]
    pallas_call x10 -> x22, Pallas kernels: 136 us -> 207 us  [call(): pl.pallas_call(kernel, grid_spec=grid_spec, **settings)(scalars, *arrays)]
    ppermute x17 -> x13, waiting for transfers between devices: 109 us -> 43.6 us  [across(): return lax.ppermute(value, 'tp', ACROSS)]
    ppermute x51 -> x30, starting transfers between devices: 67.6 us -> 33.9 us  [along(): return lax.ppermute(value, 'dp', [(i, i ^ 1 << bit) for i in range(size)])]
    unnamed x210 -> x134, local copies, waits for them, and re-layouts: 42.6 us -> 14 us
    select_n x57 -> x0, other arithmetic: 19.6 us -> none  [the longest x24 6.17 us: sum_over_dp(): jnp.where(take, got, pieces)]
    convert_element_type x39 -> x2, other arithmetic: 18 us -> 4.52 us  [the longest x1 2.94 us: local(): gu_sum.astype(f32)]
    concatenate x23 -> x1, other arithmetic: 10.3 us -> 1.21 us  [local(): w_a = jnp.concatenate([self_query.T, self_key.T, self_value.T], 0)]
  transfers between devices with their start and end apart: 78 -> 61, of which waited for: 43 -> 17; matrix products, arithmetic and copies ran while one was open for 12% -> 4% of each run, Pallas kernels for 17% -> 48%
where the time goes in v2:
time: 446 us; the launch traced here: 439 us
  Pallas kernels  242 us (54%)
  waiting for transfers between devices  95.8 us (21%)
  starting transfers between devices  53.8 us (12%)
  local copies, waits for them, and re-layouts  27.4 us (6%)
  between operations  14.8 us (3%)
  other arithmetic  5.73 us (1%)
    pallas_call x22, Pallas kernels, call(): pl.pallas_call(kernel, grid_spec=grid_spec, **settings)(scalars, *arrays)  207 us
    ppermute x30, waiting for transfers between devices, along(): return lax.ppermute(value, 'dp', [(i, i ^ 1 << bit) for i in range(size)])  49.7 us
    ppermute x13, waiting for transfers between devices, across(): return lax.ppermute(value, 'tp', ACROSS)  43.6 us
    pallas_call x6, Pallas kernels, call(): pl.pallas_call(kernel, grid=(blocks,), in_specs=specs, out_specs=out_spec...  34.7 us
    ppermute x30, starting transfers between devices, along(): return lax.ppermute(value, 'dp', [(i, i ^ 1 << bit) for i in range(size)])  33.9 us
    ppermute x13, starting transfers between devices, across(): return lax.ppermute(value, 'tp', ACROSS)  15.9 us
    unnamed x134, local copies, waits for them, and re-layouts  14 us
  transfers between devices with their start and end apart: 61, of which 17 were waited for; matrix products, arithmetic and copies ran while one was open for 4% of the time, Pallas kernels for 48%

profile of v2, /device:TPU:0, one launch (start us, length us, event | category | flops | bytes accessed | tf_op | source)
XLA Modules:
  0.0 439.5 jit_solution(7016945755499254591)
XLA Ops:
  8.4 3.0 collective-permute-start
  12.1 13.3 %self_forward_own.1 = (bf16[576,768]{1,0:T(8,128)(2,1)}, bf16[384,768]{1,0:T(8,128)(2,1)}, bf16[3,1024,128]{2,1,0:T(8,128)(2,1)}, bf16[3,1024,128]{2,1,0:T(8,128...) custom-call(s32[9]{0:T(128)} %concatenate.6.s_ref.refs_0_, ...), custom_call_target="tpu_custom_call" | custom-call | flops 12999999488 | tf_op jit(solution)/shard_map/self_forward_own/pallas_call | solution.py:630
  27.5 17.1 %collective-permute-done.1.rest_2_.ob_ref = bf16[384,768]{1,0:T(8,128)(2,1)S(1)} collective-permute-done((bf16[384,768]{1,0:T(8,128)(2,1)}, bf16[384,768]{1,0:T(8,128)(2,1)S(1)}, u32[]{:S(2)}, u32[]{:S(2)}) %collective-permute-start.1) | collective-permute-done | bytes 589856 | tf_op jit(solution)/shard_map/ppermute | solution.py:655
  45.7 12.9 %self_forward_other.1 = (bf16[1024,768]{1,0:T(8,128)(2,1)}, bf16[3,1024,128]{2,1,0:T(8,128)(2,1)}, bf16[3,1024,128]{2,1,0:T(8,128)(2,1)}, bf16[3,1024,128]{2,1,0:T(8,128)(2,1)}, bf16[1024,192]{1,0:T(8,128)(2,1)}) custom-call(s32[9]{0:T(128)} %concatenate.6.s_ref.refs_0_, bf16[2048,768]{1,0:T(8,128)(2,1)} %refs_1_.1, bf16[576,768]{1,0:T(8,128)(2,1)} %copy-done.17, ...), custom_call_target="tpu_custom_call" | custom-call | flops 12999999488 | tf_op jit(solution)/shard_map/self_forward_other/pallas_call | solution.py:630
  60.8 2.1 collective-permute-start.7
  65.1 4.4 memory_keys_other.1
  70.4 20.0 %cross_forward.1 = (bf16[1024,768]{1,0:T(8,128)(2,1)}, f32[1024,768]{1,0:T(8,128)}, bf16[1024,768]{1,0:T(8,128)(2,1)}, bf16[1024,768]{1,0:T(8,128)(2,1)}, f32[10...) custom-call(s32[9]{0:T(128)} %concatenate.6.s_ref.refs_0_, ...), custom_call_target="tpu_custom_call" | custom-call | flops 20000000000 | tf_op jit(solution)/shard_map/cross_forward/pallas_call | solution.py:630
  93.6 20.7 %collective-permute-done.8.downb_ref = bf16[768,768]{1,0:T(8,128)(2,1)S(1)} collective-permute-done((bf16[768,768]{1,0:T(8,128)(2,1)S(1)}, bf16[768,768]{1,0:T(8,128)(2,1)S(1)}, u32[]{:S(2)}, u32[]{:S(2)}) %collective-permute-start.8) | collective-permute-done | bytes 1179680 | tf_op jit(solution)/shard_map/ppermute | solution.py:655
  115.9 12.7 %ffn_forward.1 = (bf16[1024,768]{1,0:T(8,128)(2,1)}, f32[1024,768]{1,0:T(8,128)}, bf16[1024,768]{1,0:T(8,128)(2,1)}, bf16[1024,768]{1,0:T(8,128)(2,1)}, f32[1024...) custom-call(f32[1024,768]{1,0:T(8,128)} %get-tuple-element.124.h_in_, ...), custom_call_target="tpu_custom_call" | custom-call | flops 12999999488 | tf_op jit(solution)/shard_map/ffn_forward/pallas_call | solution.py:624
  134.5 15.0 %ffn_back.1 = (bf16[1024,768]{1,0:T(8,128)(2,1)}, bf16[1024,768]{1,0:T(8,128)(2,1)}, bf16[512,768]{1,0:T(8,128)(2,1)}, f32[1024,768]{1,0:T(8,128)}, bf16[1024,76...) custom-call(s32[9]{0:T(128)} %concatenate.6.s_ref.refs_0_, ...), custom_call_target="tpu_custom_call" | custom-call | flops 15000000512 | tf_op jit(solution)/shard_map/ffn_back/pallas_call | solution.py:630
  153.3 6.4 %ffn_grad_other.1 = (bf16[768,768]{1,0:T(8,128)(2,1)}, bf16[768,768]{1,0:T(8,128)(2,1)}) custom-call(bf16[1024,768]{1,0:T(8,128)(2,1)} %get-tuple-element.172.h_ref, bf16[1024,768]{1,0:T(8,128)(2,1)} %get-tuple-element.178.act_ref, bf16[1024,768]{1,0:T(8,128)(2,1)} %get-tuple-element.174.e_ref, bf16[1024,768]{1,0:T(8,128)(2,1)} %get-tuple-element.179.pre_ref), custom_call_target="tpu_custom_call" | custom-call | flops 6000000000 | tf_op jit(solution)/shard_map/ffn_grad_other/pallas_call | solution.py:624
  161.7 6.4 %ffn_grad_own.1 = (bf16[768,768]{1,0:T(8,128)(2,1)}, bf16[768,768]{1,0:T(8,128)(2,1)}) custom-call(bf16[1024,768]{1,0:T(8,128)(2,1)} %get-tuple-element.172.h_ref, bf16[1024,768]{1,0:T(8,128)(2,1)} %get-tuple-element.173.act_ref, bf16[1024,768]{1,0:T(8,128)(2,1)} %get-tuple-element.174.e_ref, bf16[1024,768]{1,0:T(8,128)(2,1)} %get-tuple-element.175.pre_ref), custom_call_target="tpu_custom_call" | custom-call | flops 6000000000 | tf_op jit(solution)/shard_map/ffn_grad_own/pallas_call | solution.py:624
  169.2 36.2 %cross_back.1 = (bf16[1024,768]{1,0:T(8,128)(2,1)}, f32[1024,768]{1,0:T(8,128)}, bf16[1024,768]{1,0:T(8,128)(2,1)}, f32[8,768]{1,0:T(8,128)}, bf16[1024,192]{1,0...) custom-call(s32[9]{0:T(128)} %concatenate.6.s_ref.refs_0_, ...), custom_call_target="tpu_custom_call" | custom-call | flops 35999997952 | tf_op jit(solution)/shard_map/cross_back/pallas_call | solution.py:630
  207.5 7.1 %cross_grad_own.1.refs_0_.refs_4_ = bf16[768,768]{1,0:T(8,128)(2,1)} custom-call(s32[9]{0:T(128)} %concatenate.6.s_ref.refs_0_, bf16[1024,768]{1,0:T(8,128)(2,1)} %get-tuple-element.155.h_ref, bf16[2048,768]{1,0:T(8,128)(2,1)} %m_ref.5, bf16[1024,192]{1,0:T(8,128)(2,1)} %get-tuple-element.136.atta_ref.att_ref, bf16[1024,768]{1,0:T(8,128)(2,1)} %get-tuple-element.156.e_ref, ...), custom_call_target="tpu_custom_call" | custom-call | flops 6000000000 | tf_op jit(solution)/shard_map/cross_grad_own/pallas_call | solution.py:630
  214.6 6.6 %cross_grad_other.1 = bf16[768,768]{1,0:T(8,128)(2,1)} custom-call(s32[9]{0:T(128)} %concatenate.6.s_ref.refs_0_, bf16[1024,768]{1,0:T(8,128)(2,1)} %get-tuple-element.155.h_ref, bf16[2048,768]{1,0:T(8,128)(2,1)} %m_ref.5, bf16[1024,192]{1,0:T(8,128)(2,1)} %get-tuple-element.137.attb_ref.att_ref, bf16[1024,768]{1,0:T(8,128)(2,1)} %get-tuple-element.156.e_ref, ...), custom_call_target="tpu_custom_call" | custom-call | flops 6000000000 | tf_op jit(solution)/shard_map/cross_grad_other/pallas_call | solution.py:630
  222.6 4.5 %ffn_grad_join.1 = (bf16[768,768]{1,0:T(8,128)(2,1)}, bf16[768,768]{1,0:T(8,128)(2,1)}) custom-call(bf16[768,768]{1,0:T(8,128)(2,1)} %get-tuple-element.176.refs_0_, bf16[768,768]{1,0:T(8,128)(2,1)} %get-tuple-element.177.refs_1_, bf16[768,768]{1,0:T(8,128)(2,1)} %copy-done.15, bf16[768,768]{1,0:T(8,128)(2,1)} %copy-done.16, ...), custom_call_target="tpu_custom_call" | custom-call | flops 3000000000 | tf_op jit(solution)/shard_map/ffn_grad_join/pallas_call | solution.py:624
  227.1 5.6 %memory_grad.1 = (bf16[512,768]{1,0:T(8,128)(2,1)}, bf16[512,768]{1,0:T(8,128)(2,1)}) custom-call(s32[9]{0:T(128)} %concatenate.6.s_ref.refs_0_, bf16[1024,384]{1,0:T(8,128)(2,1)} %get-tuple-element.158.dkv_ref.refs_1_, bf16[1024,384]{1,0:T(8,128)(2,1)} %get-tuple-element.160.dkv_ref.refs_2_, bf16[576,768]{1,0:T(8,128)(2,1)} %get-tuple-element.119.cwa_ref.refs_3_, ...), custom_call_target="tpu_custom_call" | custom-call | flops 4000000000 | tf_op jit(solution)/shard_map/memory_grad/pallas_call | solution.py:630
  233.6 25.5 %self_back_other.1 = (f32[1024,768]{1,0:T(8,128)}, bf16[3,1024,128]{2,1,0:T(8,128)(2,1)}, bf16[1024,576]{1,0:T(8,128)(2,1)}, bf16[576,768]{1,0:T(8,128)(2,1)}, b...) custom-call(s32[9]{0:T(128)} %concatenate.6.s_ref.refs_0_, bf16[2048,768]{1,0:T(8,128)(2,1)} %refs_1_.1, ...), custom_call_target="tpu_custom_call" | custom-call | flops 24999999488 | tf_op jit(solution)/shard_map/self_back_other/pallas_call | solution.py:630
  262.2 4.0 sum_cross_a.1
  267.9 14.5 %self_back_own.1 = (bf16[1024,576]{1,0:T(8,128)(2,1)}, bf16[576,768]{1,0:T(8,128)(2,1)}) custom-call(s32[9]{0:T(128)} %concatenate.6.s_ref.refs_0_, bf16[2048,768]{1,0:T(8,128)(2,1)} %refs_1_.1, bf16[3,1024,128]{2,1,0:T(8,128)(2,1)} %get-tuple-element.151.refs_2_, bf16[3,1024,128]{2,1,0:T(8,128)(2,1)} %get-tuple-element.152.refs_3_, ...), custom_call_target="tpu_custom_call" | custom-call | flops 15000000512 | tf_op jit(solution)/shard_map/self_back_own/pallas_call | solution.py:630
  282.5 5.8 %collective-permute-done.18.refs_2_ = bf16[576,768]{1,0:T(8,128)(2,1)S(1)} collective-permute-done((bf16[576,768]{1,0:T(8,128)(2,1)}, bf16[576,768]{1,0:T(8,128)(2,1)S(1)}, u32[]{:S(2)}, u32[]{:S(2)}) %collective-permute-start.18) | collective-permute-done | bytes 884768 | tf_op jit(solution)/shard_map/ppermute | solution.py:655
  289.3 4.5 %sum_self_a.1 = (bf16[256,768]{1,0:T(8,128)(2,1)}, bf16[256,768]{1,0:T(8,128)(2,1)}, bf16[192,768]{1,0:T(8,128)(2,1)}, bf16[192,768]{1,0:T(8,128)(2,1)}, bf16[19...) custom-call(s32[9]{0:T(128)} %concatenate.6.s_ref.refs_0_, bf16[576,768]{1,0:T(8,128)(2,1)} %get-tuple-element.164.refs_0_, ...), custom_call_target="tpu_custom_call" | custom-call | flops 3000000000 | tf_op jit(solution)/shard_map/sum_self_a/pallas_call | solution.py:630
  297.6 7.8 %tokens_grad.1 = (bf16[512,768]{1,0:T(8,128)(2,1)}, f32[512,768]{1,0:T(8,128)}) custom-call(s32[9]{0:T(128)} %concatenate.6.s_ref.refs_0_, f32[1024,768]{1,0:T(8,128)} %get-tuple-element.150.refs_1_, bf16[1024,576]{1,0:T(8,128)(2,1)} %get-tuple-element.162.refs_2_, bf16[1024,576]{1,0:T(8,128)(2,1)} %get-tuple-element.163.refs_3_, ...), custom_call_target="tpu_custom_call" | custom-call | flops 5000000000 | tf_op jit(solution)/shard_map/tokens_grad/pallas_call | solution.py:630
  306.0 8.3 %collective-permute-done.33.refs_5_ = bf16[192,768]{1,0:T(8,128)(2,1)S(1)} collective-permute-done((bf16[192,768]{1,0:T(8,128)(2,1)}, bf16[192,768]{1,0:T(8,128)(2,1)S(1)}, u32[]{:S(2)}, u32[]{:S(2)}) %collective-permute-start.33) | collective-permute-done | bytes 294944 | tf_op jit(solution)/shard_map/ppermute | solution.py:822
  315.2 3.4 sum_self_b.1
  318.5 2.7 collective-permute-start.35
  321.5 2.4 collective-permute-start.34
  323.9 2.4 memory_finish.1.refs_0_
  326.2 8.5 %collective-permute-done.35.refs_3_ = bf16[96,768]{1,0:T(8,128)(2,1)S(1)} collective-permute-done((bf16[96,768]{1,0:T(8,128)(2,1)}, bf16[96,768]{1,0:T(8,128)(2,1)S(1)}, u32[]{:S(2)}, u32[]{:S(2)}) %collective-permute-start.35) | collective-permute-done | bytes 147488 | tf_op jit(solution)/shard_map/ppermute | solution.py:822
  336.6 6.2 %collective-permute-done.36.refs_5_ = bf16[96,768]{1,0:T(8,128)(2,1)S(1)} collective-permute-done((bf16[96,768]{1,0:T(8,128)(2,1)}, bf16[96,768]{1,0:T(8,128)(2,1)S(1)}, u32[]{:S(2)}, u32[]{:S(2)}) %collective-permute-start.36) | collective-permute-done | bytes 147488 | tf_op jit(solution)/shard_map/ppermute | solution.py:822
  343.5 2.8 sum_self_c.1
  346.2 3.7 collective-permute-start.38
  350.8 2.4 tokens_finish.1.refs_0_
  354.8 7.4 %collective-permute-done.37.refs_1_ = bf16[64,768]{1,0:T(8,128)(2,1)S(1)} collective-permute-done((bf16[64,768]{1,0:T(8,128)(2,1)}, bf16[64,768]{1,0:T(8,128)(2,1)S(1)}, u32[]{:S(2)}, u32[]{:S(2)}) %collective-permute-start.37) | collective-permute-done | bytes 98336 | tf_op jit(solution)/shard_map/ppermute | solution.py:822
  362.9 2.4 sum_self_d.1
  365.2 2.8 collective-permute-start.49
  369.9 3.8 collective-permute-done.53.refs_1_
  375.8 2.4 collective-permute-done.46.refs_9_
  380.2 2.5 collective-permute-done.40.refs_2_
  386.1 5.1 %collective-permute-done.48.refs_11_ = bf16[48,768]{1,0:T(8,128)(2,1)S(1)} collective-permute-done((bf16[48,768]{1,0:T(8,128)(2,1)S(1)}, bf16[48,768]{1,0:T(8,128)(2,1)S(1)}, u32[]{:S(2)}, u32[]{:S(2)}) %collective-permute-start.48) | collective-permute-done | bytes 73760 | tf_op jit(solution)/shard_map/ppermute | solution.py:822
  393.7 4.8 %place_layer_out.1 = bf16[2048,768]{1,0:T(8,128)(2,1)} custom-call(s32[9]{0:T(128)} %concatenate.6.s_ref.refs_0_, bf16[1024,768]{1,0:T(8,128)(2,1)} %get-tuple-element.130.refs_0_, bf16[512,768]{1,0:T(8,128)(2,1)} %copy-done.20, bf16[512,768]{1,0:T(8,128)(2,1)} %copy-done.25), custom_call_target="tpu_custom_call" | custom-call | flops 3000000000 | tf_op jit(solution)/shard_map/place_layer_out/pallas_call | solution.py:630
  401.4 3.6 gather_self.1
  406.7 2.9 convert_element_type.6
  414.2 4.7 %place_memory_grad.1 = bf16[2048,768]{1,0:T(8,128)(2,1)} custom-call(s32[9]{0:T(128)} %concatenate.6.s_ref.refs_0_, bf16[512,768]{1,0:T(8,128)(2,1)} %memory_finish.1.refs_0_, bf16[512,768]{1,0:T(8,128)(2,1)} %copy-done.23, bf16[512,768]{1,0:T(8,128)(2,1)} %copy-done.21, bf16[512,768]{1,0:T(8,128)(2,1)} %copy-done.27), custom_call_target="tpu_custom_call" | custom-call | flops 3000000000 | tf_op jit(solution)/shard_map/place_memory_grad/pallas_call | solution.py:630
  418.9 2.5 collective-permute-done.58.refs_6_
  421.3 2.2 collective-permute-done.59.refs_7_
  424.3 3.5 gather_cross.1
  427.8 4.7 %place_tokens_grad.1 = bf16[2048,768]{1,0:T(8,128)(2,1)} custom-call(s32[9]{0:T(128)} %concatenate.6.s_ref.refs_0_, bf16[512,768]{1,0:T(8,128)(2,1)} %tokens_finish.1.refs_0_, bf16[512,768]{1,0:T(8,128)(2,1)} %collective-permute-done.22.refs_1_, bf16[512,768]{1,0:T(8,128)(2,1)} %copy-done.24, bf16[512,768]{1,0:T(8,128)(2,1)} %collective-permute-done.24.refs_3_), custom_call_target="tpu_custom_call" | custom-call | flops 3000000000 | tf_op jit(solution)/shard_map/place_tokens_grad/pallas_call | solution.py:630
  (253 shorter events, 70.8 us)
Async XLA Ops:
  8.4 36.1 %collective-permute-start = (bf16[576,768]{1,0:T(8,128)(2,1)S(1)}, bf16[576,768]{1,0:T(8,128)(2,1)S(1)}, u32[]{:S(2)}, u32[]{:S(2)}) collective-permute-start(bf16[576,768]{1,0:T(8,128)(2,1)S(1)} %pad_maximum_fusion.w_ref.refs_4_), channel_id=1, source_target_pairs={{0,16},{16,0},{8,24},{24,8},{1,17},{17,1},{9,25},{25,9},{2,18},{18... | collective-permute-start | bytes 2654216 | tf_op jit(solution)/shard_map/ppermute | solution.py:655
  25.4 19.2 %collective-permute-start.1 = (bf16[384,768]{1,0:T(8,128)(2,1)}, bf16[384,768]{1,0:T(8,128)(2,1)S(1)}, u32[]{:S(2)}, u32[]{:S(2)}) collective-permute-start(bf16[384,768]{1,0:T(8,128)(2,1)} %get-tuple-element.117.rest_1_.oa_ref), channel_id=1, source_target_pairs={{0,16},{16,0},{8,24},{24,8},{1,17},{17,1},{9,25},{25,9},{2,18},{18... | collective-permute-start | bytes 1769480 | tf_op jit(solution)/shard_map/ppermute | solution.py:655
  25.6 38.5 %collective-permute-start.4 = (bf16[576,768]{1,0:T(8,128)(2,1)}, bf16[576,768]{1,0:T(8,128)(2,1)S(1)}, u32[]{:S(2)}, u32[]{:S(2)}) collective-permute-start(bf16[576,768]{1,0:T(8,128)(2,1)} %get-tuple-element.119.cwa_ref.refs_3_), channel_id=1, source_target_pairs={{0,16},{16,0},{8,24},{24,8},{1,17},{17,1},{9,25},{25,9},{2,18},{18... | collective-permute-start | bytes 2654216 | tf_op jit(solution)/shard_map/ppermute | solution.py:655
  60.2 9.3 %collective-permute-start.3 = (bf16[512,768]{1,0:T(8,128)(2,1)S(1)}, bf16[512,768]{1,0:T(8,128)(2,1)S(1)}, u32[]{:S(2)}, u32[]{:S(2)}) collective-permute-start(bf16[512,768]{1,0:T(8,128)(2,1)S(1)} %get-tuple-element.229), channel_id=1, source_target_pairs={{0,8},{8,0},{16,24},{24,16},{1,9},{9,1},{17,25},{25,17},{2,10},{10... | collective-permute-start | bytes 2359304 | tf_op jit(solution)/shard_map/ppermute | solution.py:658
  60.3 9.2 %collective-permute-start.2 = (bf16[512,768]{1,0:T(8,128)(2,1)S(1)}, bf16[512,768]{1,0:T(8,128)(2,1)}, u32[]{:S(2)}, u32[]{:S(2)}) collective-permute-start(bf16[512,768]{1,0:T(8,128)(2,1)S(1)} %get-tuple-element.230), channel_id=1, source_target_pairs={{0,8},{8,0},{16,24},{24,16},{1,9},{9,1},{17,25},{25,17},{2,10},{10... | collective-permute-start | bytes 2359304 | tf_op jit(solution)/shard_map/ppermute | solution.py:658
  60.8 32.8 %collective-permute-start.7 = (bf16[768,768]{1,0:T(8,128)(2,1)S(1)}, bf16[768,768]{1,0:T(8,128)(2,1)S(1)}, u32[]{:S(2)}, u32[]{:S(2)}) collective-permute-start(bf16[768,768]{1,0:T(8,128)(2,1)S(1)} %copy-done.10), channel_id=1, source_target_pairs={{0,16},{16,0},{8,24},{24,8},{1,17},{17,1},{9,25},{25,9},{2,18},{18... | collective-permute-start | bytes 3538952 | tf_op jit(solution)/shard_map/ppermute | solution.py:655
  62.9 51.5 %collective-permute-start.8 = (bf16[768,768]{1,0:T(8,128)(2,1)S(1)}, bf16[768,768]{1,0:T(8,128)(2,1)S(1)}, u32[]{:S(2)}, u32[]{:S(2)}) collective-permute-start(bf16[768,768]{1,0:T(8,128)(2,1)S(1)} %copy-done.11), channel_id=1, source_target_pairs={{0,16},{16,0},{8,24},{24,8},{1,17},{17,1},{9,25},{25,9},{2,18},{18... | collective-permute-start | bytes 3538952 | tf_op jit(solution)/shard_map/ppermute | solution.py:655
  91.9 22.5 %collective-permute-start.6 = (bf16[512,768]{1,0:T(8,128)(2,1)S(1)}, bf16[512,768]{1,0:T(8,128)(2,1)S(1)}, u32[]{:S(2)}, u32[]{:S(2)}) collective-permute-start(bf16[512,768]{1,0:T(8,128)(2,1)S(1)} %get-tuple-element.227), channel_id=1, source_target_pairs={{0,8},{8,0},{16,24},{24,16},{1,9},{9,1},{17,25},{25,17},{2,10},{10... | collective-permute-start | bytes 2359304 | tf_op jit(solution)/shard_map/ppermute | solution.py:658
  91.9 22.4 %collective-permute-start.5 = (bf16[512,768]{1,0:T(8,128)(2,1)S(1)}, bf16[512,768]{1,0:T(8,128)(2,1)S(1)}, u32[]{:S(2)}, u32[]{:S(2)}) collective-permute-start(bf16[512,768]{1,0:T(8,128)(2,1)S(1)} %get-tuple-element.228), channel_id=1, source_target_pairs={{0,8},{8,0},{16,24},{24,16},{1,9},{9,1},{17,25},{25,17},{2,10},{10... | collective-permute-start | bytes 2359304 | tf_op jit(solution)/shard_map/ppermute | solution.py:658
  149.5 156.0 %collective-permute-start.11 = (bf16[512,768]{1,0:T(8,128)(2,1)}, bf16[512,768]{1,0:T(8,128)(2,1)S(1)}, u32[]{:S(2)}, u32[]{:S(2)}) collective-permute-start(bf16[512,768]{1,0:T(8,128)(2,1)} %get-tuple-element.131), channel_id=1, source_target_pairs={{0,16},{16,0},{8,24},{24,8},{1,17},{17,1},{9,25},{25,9},{2,18},{18... | collective-permute-start | bytes 2359304 | tf_op jit(solution)/shard_map/ppermute | solution.py:655
  152.7 15.4 %collective-permute-start.14 = (bf16[512,768]{1,0:T(8,128)(2,1)S(1)}, bf16[512,768]{1,0:T(8,128)(2,1)S(1)}, u32[]{:S(2)}, u32[]{:S(2)}) collective-permute-start(bf16[512,768]{1,0:T(8,128)(2,1)S(1)} %get-tuple-element.223), channel_id=1, source_target_pairs={{0,8},{8,0},{16,24},{24,16},{1,9},{9,1},{17,25},{25,17},{2,10},{10... | collective-permute-start | bytes 2359304 | tf_op jit(solution)/shard_map/ppermute | solution.py:658
  152.8 15.3 %collective-permute-start.13 = (bf16[512,768]{1,0:T(8,128)(2,1)S(1)}, bf16[512,768]{1,0:T(8,128)(2,1)S(1)}, u32[]{:S(2)}, u32[]{:S(2)}) collective-permute-start(bf16[512,768]{1,0:T(8,128)(2,1)S(1)} %get-tuple-element.224), channel_id=1, source_target_pairs={{0,8},{8,0},{16,24},{24,16},{1,9},{9,1},{17,25},{25,17},{2,10},{10... | collective-permute-start | bytes 2359304 | tf_op jit(solution)/shard_map/ppermute | solution.py:658
  159.7 61.5 %collective-permute-start.25 = (bf16[768,768]{1,0:T(8,128)(2,1)}, bf16[768,768]{1,0:T(8,128)(2,1)S(1)}, u32[]{:S(2)}, u32[]{:S(2)}) collective-permute-start(bf16[768,768]{1,0:T(8,128)(2,1)} %get-tuple-element.180), channel_id=1, source_target_pairs={{0,16},{16,0},{8,24},{24,8},{1,17},{17,1},{9,25},{25,9},{2,18},{18... | collective-permute-start | bytes 3538952 | tf_op jit(solution)/shard_map/ppermute | solution.py:655
  160.0 61.3 %collective-permute-start.26 = (bf16[768,768]{1,0:T(8,128)(2,1)}, bf16[768,768]{1,0:T(8,128)(2,1)S(1)}, u32[]{:S(2)}, u32[]{:S(2)}) collective-permute-start(bf16[768,768]{1,0:T(8,128)(2,1)} %get-tuple-element.181), channel_id=1, source_target_pairs={{0,16},{16,0},{8,24},{24,8},{1,17},{17,1},{9,25},{25,9},{2,18},{18... | collective-permute-start | bytes 3538952 | tf_op jit(solution)/shard_map/ppermute | solution.py:655
  206.9 26.6 %collective-permute-start.16 = (bf16[512,768]{1,0:T(8,128)(2,1)S(1)}, bf16[512,768]{1,0:T(8,128)(2,1)}, u32[]{:S(2)}, u32[]{:S(2)}) collective-permute-start(bf16[512,768]{1,0:T(8,128)(2,1)S(1)} %get-tuple-element.221), channel_id=1, source_target_pairs={{0,8},{8,0},{16,24},{24,16},{1,9},{9,1},{17,25},{25,17},{2,10},{10... | collective-permute-start | bytes 2359304 | tf_op jit(solution)/shard_map/ppermute | solution.py:658
  207.0 26.6 %collective-permute-start.15 = (bf16[512,768]{1,0:T(8,128)(2,1)S(1)}, bf16[512,768]{1,0:T(8,128)(2,1)}, u32[]{:S(2)}, u32[]{:S(2)}) collective-permute-start(bf16[512,768]{1,0:T(8,128)(2,1)S(1)} %get-tuple-element.222), channel_id=1, source_target_pairs={{0,8},{8,0},{16,24},{24,16},{1,9},{9,1},{17,25},{25,17},{2,10},{10... | collective-permute-start | bytes 2359304 | tf_op jit(solution)/shard_map/ppermute | solution.py:658
  221.2 40.0 %collective-permute-start.17 = (bf16[768,768]{1,0:T(8,128)(2,1)}, bf16[768,768]{1,0:T(8,128)(2,1)S(1)}, u32[]{:S(2)}, u32[]{:S(2)}) collective-permute-start(bf16[768,768]{1,0:T(8,128)(2,1)} %cross_grad_other.1), channel_id=1, source_target_pairs={{0,16},{16,0},{8,24},{24,8},{1,17},{17,1},{9,25},{25,9},{2,18},{18... | collective-permute-start | bytes 3538952 | tf_op jit(solution)/shard_map/ppermute | solution.py:655
  232.7 174.0 %all-reduce.3.cloned.1.call-start = ((), (), s32[]{:S(2)}) async-start(), calls=%async_computation | async-start | bytes 4718592 | tf_op jit(solution)/shard_map/psum | solution.py:776
  233.4 88.1 %collective-permute-start.27 = (bf16[512,768]{1,0:T(8,128)(2,1)}, bf16[512,768]{1,0:T(8,128)(2,1)S(1)}, u32[]{:S(2)}, u32[]{:S(2)}) collective-permute-start(bf16[512,768]{1,0:T(8,128)(2,1)} %get-tuple-element.184), channel_id=1, source_target_pairs={{0,8},{8,0},{16,24},{24,16},{1,9},{9,1},{17,25},{25,17},{2,10},{10... | collective-permute-start | bytes 2359304 | tf_op jit(solution)/shard_map/ppermute | solution.py:658
  259.1 23.3 %collective-permute-start.19 = (bf16[208,768]{1,0:T(8,128)(2,1)}, bf16[208,768]{1,0:T(8,128)(2,1)S(1)}, u32[]{:S(2)}, u32[]{:S(2)}) collective-permute-start(bf16[208,768]{1,0:T(8,128)(2,1)} %get-tuple-element.167), channel_id=1, source_target_pairs={{0,16},{16,0},{8,24},{24,8},{1,17},{17,1},{9,25},{25,9},{2,18},{18... | collective-permute-start | bytes 958472 | tf_op jit(solution)/shard_map/ppermute | solution.py:655
  260.9 27.4 %collective-permute-start.18 = (bf16[576,768]{1,0:T(8,128)(2,1)}, bf16[576,768]{1,0:T(8,128)(2,1)S(1)}, u32[]{:S(2)}, u32[]{:S(2)}) collective-permute-start(bf16[576,768]{1,0:T(8,128)(2,1)} %get-tuple-element.166), channel_id=1, source_target_pairs={{0,16},{16,0},{8,24},{24,8},{1,17},{17,1},{9,25},{25,9},{2,18},{18... | collective-permute-start | bytes 2654216 | tf_op jit(solution)/shard_map/ppermute | solution.py:655
  266.2 22.0 %collective-permute-start.20 = (bf16[384,768]{1,0:T(8,128)(2,1)}, bf16[384,768]{1,0:T(8,128)(2,1)S(1)}, u32[]{:S(2)}, u32[]{:S(2)}) collective-permute-start(bf16[384,768]{1,0:T(8,128)(2,1)} %get-tuple-element.168), channel_id=1, source_target_pairs={{0,1},{1,0},{2,3},{3,2},{4,5},{5,4},{6,7},{7,6},{8,9},{9,8},{10,11... | collective-permute-start | bytes 1769480 | tf_op jit(solution)/shard_map/ppermute | solution.py:822
  293.9 11.6 %collective-permute-start.32 = (bf16[192,768]{1,0:T(8,128)(2,1)}, bf16[192,768]{1,0:T(8,128)(2,1)S(1)}, u32[]{:S(2)}, u32[]{:S(2)}) collective-permute-start(bf16[192,768]{1,0:T(8,128)(2,1)} %get-tuple-element.187), channel_id=1, source_target_pairs={{0,2},{1,3},{2,0},{3,1},{4,6},{5,7},{6,4},{7,5},{8,10},{9,11},{10,... | collective-permute-start | bytes 884744 | tf_op jit(solution)/shard_map/ppermute | solution.py:822
  295.5 18.9 %collective-permute-start.33 = (bf16[192,768]{1,0:T(8,128)(2,1)}, bf16[192,768]{1,0:T(8,128)(2,1)S(1)}, u32[]{:S(2)}, u32[]{:S(2)}) collective-permute-start(bf16[192,768]{1,0:T(8,128)(2,1)} %get-tuple-element.189), channel_id=1, source_target_pairs={{0,2},{1,3},{2,0},{3,1},{4,6},{5,7},{6,4},{7,5},{8,10},{9,11},{10,... | collective-permute-start | bytes 884744 | tf_op jit(solution)/shard_map/ppermute | solution.py:822
  295.9 18.4 %collective-permute-start.31 = (bf16[256,768]{1,0:T(8,128)(2,1)}, bf16[256,768]{1,0:T(8,128)(2,1)S(1)}, u32[]{:S(2)}, u32[]{:S(2)}) collective-permute-start(bf16[256,768]{1,0:T(8,128)(2,1)} %get-tuple-element.185), channel_id=1, source_target_pairs={{0,1},{1,0},{2,3},{3,2},{4,5},{5,4},{6,7},{7,6},{8,9},{9,8},{10,11... | collective-permute-start | bytes 1179656 | tf_op jit(solution)/shard_map/ppermute | solution.py:822
  305.4 44.5 %collective-permute-start.21 = (bf16[512,768]{1,0:T(8,128)(2,1)}, bf16[512,768]{1,0:T(8,128)(2,1)S(1)}, u32[]{:S(2)}, u32[]{:S(2)}) collective-permute-start(bf16[512,768]{1,0:T(8,128)(2,1)} %get-tuple-element.171), channel_id=1, source_target_pairs={{0,8},{8,0},{16,24},{24,16},{1,9},{9,1},{17,25},{25,17},{2,10},{10... | collective-permute-start | bytes 2359304 | tf_op jit(solution)/shard_map/ppermute | solution.py:658
  305.6 47.7 %collective-permute-start.12 = (bf16[512,768]{1,0:T(8,128)(2,1)S(1)}, bf16[512,768]{1,0:T(8,128)(2,1)S(1)}, u32[]{:S(2)}, u32[]{:S(2)}) collective-permute-start(bf16[512,768]{1,0:T(8,128)(2,1)S(1)} %collective-permute-done.11.refs_1_), channel_id=1, source_target_pairs={{0,8},{8,0},{16,24},{24,16},{1,9},{9,1},{17,25},{25,17},{2,10},{10... | collective-permute-start | bytes 2359304 | tf_op jit(solution)/shard_map/ppermute | solution.py:658
  318.5 16.2 %collective-permute-start.35 = (bf16[96,768]{1,0:T(8,128)(2,1)}, bf16[96,768]{1,0:T(8,128)(2,1)S(1)}, u32[]{:S(2)}, u32[]{:S(2)}) collective-permute-start(bf16[96,768]{1,0:T(8,128)(2,1)} %get-tuple-element.193), channel_id=1, source_target_pairs={{0,4},{1,5},{2,6},{3,7},{4,0},{5,1},{6,2},{7,3},{8,12},{9,13},{10,... | collective-permute-start | bytes 442376 | tf_op jit(solution)/shard_map/ppermute | solution.py:822
  321.3 21.4 %collective-permute-start.36 = (bf16[96,768]{1,0:T(8,128)(2,1)}, bf16[96,768]{1,0:T(8,128)(2,1)S(1)}, u32[]{:S(2)}, u32[]{:S(2)}) collective-permute-start(bf16[96,768]{1,0:T(8,128)(2,1)} %get-tuple-element.195), channel_id=1, source_target_pairs={{0,4},{1,5},{2,6},{3,7},{4,0},{5,1},{6,2},{7,3},{8,12},{9,13},{10,... | collective-permute-start | bytes 442376 | tf_op jit(solution)/shard_map/ppermute | solution.py:822
  321.5 21.3 %collective-permute-start.34 = (bf16[128,768]{1,0:T(8,128)(2,1)}, bf16[128,768]{1,0:T(8,128)(2,1)S(1)}, u32[]{:S(2)}, u32[]{:S(2)}) collective-permute-start(bf16[128,768]{1,0:T(8,128)(2,1)} %get-tuple-element.191), channel_id=1, source_target_pairs={{0,2},{1,3},{2,0},{3,1},{4,6},{5,7},{6,4},{7,5},{8,10},{9,11},{10,... | collective-permute-start | bytes 589832 | tf_op jit(solution)/shard_map/ppermute | solution.py:822
  334.7 30.5 %collective-permute-start.29 = (bf16[512,768]{1,0:T(8,128)(2,1)}, bf16[512,768]{1,0:T(8,128)(2,1)S(1)}, u32[]{:S(2)}, u32[]{:S(2)}) collective-permute-start(bf16[512,768]{1,0:T(8,128)(2,1)} %memory_finish.1.refs_0_), channel_id=1, source_target_pairs={{0,16},{16,0},{8,24},{24,8},{1,17},{17,1},{9,25},{25,9},{2,18},{18... | collective-permute-start | bytes 2359304 | tf_op jit(solution)/shard_map/ppermute | solution.py:655
  342.7 25.3 %collective-permute-start.28 = (bf16[512,768]{1,0:T(8,128)(2,1)}, bf16[512,768]{1,0:T(8,128)(2,1)S(1)}, u32[]{:S(2)}, u32[]{:S(2)}) collective-permute-start(bf16[512,768]{1,0:T(8,128)(2,1)} %memory_finish.1.refs_0_), channel_id=1, source_target_pairs={{0,8},{8,0},{16,24},{24,16},{1,9},{9,1},{17,25},{25,17},{2,10},{10... | collective-permute-start | bytes 2359304 | tf_op jit(solution)/shard_map/ppermute | solution.py:658
  350.0 12.3 %collective-permute-start.37 = (bf16[64,768]{1,0:T(8,128)(2,1)}, bf16[64,768]{1,0:T(8,128)(2,1)S(1)}, u32[]{:S(2)}, u32[]{:S(2)}) collective-permute-start(bf16[64,768]{1,0:T(8,128)(2,1)} %get-tuple-element.197), channel_id=1, source_target_pairs={{0,4},{1,5},{2,6},{3,7},{4,0},{5,1},{6,2},{7,3},{8,12},{9,13},{10,... | collective-permute-start | bytes 294920 | tf_op jit(solution)/shard_map/ppermute | solution.py:822
  353.3 47.6 %collective-permute-start.23 = (bf16[512,768]{1,0:T(8,128)(2,1)}, bf16[512,768]{1,0:T(8,128)(2,1)S(1)}, u32[]{:S(2)}, u32[]{:S(2)}) collective-permute-start(bf16[512,768]{1,0:T(8,128)(2,1)} %tokens_finish.1.refs_0_), channel_id=1, source_target_pairs={{0,16},{16,0},{8,24},{24,8},{1,17},{17,1},{9,25},{25,9},{2,18},{18... | collective-permute-start | bytes 2359304 | tf_op jit(solution)/shard_map/ppermute | solution.py:655
  354.1 14.5 %collective-permute-start.56 = (bf16[96,768]{1,0:T(8,128)(2,1)S(1)}, bf16[96,768]{1,0:T(8,128)(2,1)S(1)}, u32[]{:S(2)}, u32[]{:S(2)}) collective-permute-start(bf16[96,768]{1,0:T(8,128)(2,1)S(1)} %copy-done.43), channel_id=1, source_target_pairs={{0,1},{1,0},{2,3},{3,2},{4,5},{5,4},{6,7},{7,6},{8,9},{9,8},{10,11... | collective-permute-start | bytes 442376 | tf_op jit(solution)/shard_map/ppermute | solution.py:822
  362.2 11.4 %collective-permute-start.53 = (bf16[96,768]{1,0:T(8,128)(2,1)S(1)}, bf16[96,768]{1,0:T(8,128)(2,1)}, u32[]{:S(2)}, u32[]{:S(2)}) collective-permute-start(bf16[96,768]{1,0:T(8,128)(2,1)S(1)} %copy-done.43), channel_id=1, source_target_pairs={{0,4},{1,5},{2,6},{3,7},{4,0},{5,1},{6,2},{7,3},{8,12},{9,13},{10,... | collective-permute-start | bytes 442376 | tf_op jit(solution)/shard_map/ppermute | solution.py:822
  365.2 9.8 %collective-permute-start.49 = (bf16[48,768]{1,0:T(8,128)(2,1)}, bf16[48,768]{1,0:T(8,128)(2,1)S(1)}, u32[]{:S(2)}, u32[]{:S(2)}) collective-permute-start(bf16[48,768]{1,0:T(8,128)(2,1)} %get-tuple-element.201.refs_8_), channel_id=1, source_target_pairs={{0,2},{1,3},{2,0},{3,1},{4,6},{5,7},{6,4},{7,5},{8,10},{9,11},{10,... | collective-permute-start | bytes 221192 | tf_op jit(solution)/shard_map/ppermute | solution.py:822
  368.6 9.6 %collective-permute-start.42 = (bf16[64,768]{1,0:T(8,128)(2,1)}, bf16[64,768]{1,0:T(8,128)(2,1)S(1)}, u32[]{:S(2)}, u32[]{:S(2)}) collective-permute-start(bf16[64,768]{1,0:T(8,128)(2,1)} %get-tuple-element.200.refs_0_), channel_id=1, source_target_pairs={{0,1},{1,0},{2,3},{3,2},{4,5},{5,4},{6,7},{7,6},{8,9},{9,8},{10,11... | collective-permute-start | bytes 294920 | tf_op jit(solution)/shard_map/ppermute | solution.py:822
  382.7 30.6 %collective-permute-start.30 = (bf16[512,768]{1,0:T(8,128)(2,1)S(1)}, bf16[512,768]{1,0:T(8,128)(2,1)S(1)}, u32[]{:S(2)}, u32[]{:S(2)}) collective-permute-start(bf16[512,768]{1,0:T(8,128)(2,1)S(1)} %collective-permute-done.29.refs_2_), channel_id=1, source_target_pairs={{0,8},{8,0},{16,24},{24,16},{1,9},{9,1},{17,25},{25,17},{2,10},{10... | collective-permute-start | bytes 2359304 | tf_op jit(solution)/shard_map/ppermute | solution.py:658
  382.7 9.6 %collective-permute-start.44 = (bf16[64,768]{1,0:T(8,128)(2,1)S(1)}, bf16[64,768]{1,0:T(8,128)(2,1)S(1)}, u32[]{:S(2)}, u32[]{:S(2)}) collective-permute-start(bf16[64,768]{1,0:T(8,128)(2,1)S(1)} %collective-permute-done.40.refs_2_), channel_id=1, source_target_pairs={{0,1},{1,0},{2,3},{3,2},{4,5},{5,4},{6,7},{7,6},{8,9},{9,8},{10,11... | collective-permute-start | bytes 294920 | tf_op jit(solution)/shard_map/ppermute | solution.py:822
  392.4 8.4 %collective-permute-start.45 = (bf16[64,768]{1,0:T(8,128)(2,1)S(1)}, bf16[64,768]{1,0:T(8,128)(2,1)S(1)}, u32[]{:S(2)}, u32[]{:S(2)}) collective-permute-start(bf16[64,768]{1,0:T(8,128)(2,1)S(1)} %collective-permute-done.41.refs_3_), channel_id=1, source_target_pairs={{0,1},{1,0},{2,3},{3,2},{4,5},{5,4},{6,7},{7,6},{8,9},{9,8},{10,11... | collective-permute-start | bytes 294920 | tf_op jit(solution)/shard_map/ppermute | solution.py:822
  398.6 12.6 %collective-permute-start.54 = (bf16[96,768]{1,0:T(8,128)(2,1)S(1)}, bf16[96,768]{1,0:T(8,128)(2,1)S(1)}, u32[]{:S(2)}, u32[]{:S(2)}) collective-permute-start(bf16[96,768]{1,0:T(8,128)(2,1)S(1)} %copy-done.43), channel_id=1, source_target_pairs={{0,2},{1,3},{2,0},{3,1},{4,6},{5,7},{6,4},{7,5},{8,10},{9,11},{10,... | collective-permute-start | bytes 442376 | tf_op jit(solution)/shard_map/ppermute | solution.py:822
  400.2 11.7 %collective-permute-start.55 = (bf16[96,768]{1,0:T(8,128)(2,1)}, bf16[96,768]{1,0:T(8,128)(2,1)}, u32[]{:S(2)}, u32[]{:S(2)}) collective-permute-start(bf16[96,768]{1,0:T(8,128)(2,1)} %collective-permute-done.53.refs_1_), channel_id=1, source_target_pairs={{0,2},{1,3},{2,0},{3,1},{4,6},{5,7},{6,4},{7,5},{8,10},{9,11},{10,... | collective-permute-start | bytes 442376 | tf_op jit(solution)/shard_map/ppermute | solution.py:822
  400.7 27.0 %collective-permute-start.22 = (bf16[512,768]{1,0:T(8,128)(2,1)S(1)}, bf16[512,768]{1,0:T(8,128)(2,1)}, u32[]{:S(2)}, u32[]{:S(2)}) collective-permute-start(bf16[512,768]{1,0:T(8,128)(2,1)S(1)} %copy-done.22), channel_id=1, source_target_pairs={{0,8},{8,0},{16,24},{24,16},{1,9},{9,1},{17,25},{25,17},{2,10},{10... | collective-permute-start | bytes 2359304 | tf_op jit(solution)/shard_map/ppermute | solution.py:658
  400.8 26.9 %collective-permute-start.24 = (bf16[512,768]{1,0:T(8,128)(2,1)S(1)}, bf16[512,768]{1,0:T(8,128)(2,1)}, u32[]{:S(2)}, u32[]{:S(2)}) collective-permute-start(bf16[512,768]{1,0:T(8,128)(2,1)S(1)} %collective-permute-done.23.refs_2_), channel_id=1, source_target_pairs={{0,8},{8,0},{16,24},{24,16},{1,9},{9,1},{17,25},{25,17},{2,10},{10... | collective-permute-start | bytes 2359304 | tf_op jit(solution)/shard_map/ppermute | solution.py:658
  411.2 10.1 %collective-permute-start.57 = (bf16[96,768]{1,0:T(8,128)(2,1)}, bf16[96,768]{1,0:T(8,128)(2,1)S(1)}, u32[]{:S(2)}, u32[]{:S(2)}) collective-permute-start(bf16[96,768]{1,0:T(8,128)(2,1)} %collective-permute-done.53.refs_1_), channel_id=1, source_target_pairs={{0,1},{1,0},{2,3},{3,2},{4,5},{5,4},{6,7},{7,6},{8,9},{9,8},{10,11... | collective-permute-start | bytes 442376 | tf_op jit(solution)/shard_map/ppermute | solution.py:822
  412.0 9.4 %collective-permute-start.58 = (bf16[96,768]{1,0:T(8,128)(2,1)S(1)}, bf16[96,768]{1,0:T(8,128)(2,1)S(1)}, u32[]{:S(2)}, u32[]{:S(2)}) collective-permute-start(bf16[96,768]{1,0:T(8,128)(2,1)S(1)} %collective-permute-done.54.refs_2_), channel_id=1, source_target_pairs={{0,1},{1,0},{2,3},{3,2},{4,5},{5,4},{6,7},{7,6},{8,9},{9,8},{10,11... | collective-permute-start | bytes 442376 | tf_op jit(solution)/shard_map/ppermute | solution.py:822
  413.3 10.3 %collective-permute-start.59 = (bf16[96,768]{1,0:T(8,128)(2,1)}, bf16[96,768]{1,0:T(8,128)(2,1)S(1)}, u32[]{:S(2)}, u32[]{:S(2)}) collective-permute-start(bf16[96,768]{1,0:T(8,128)(2,1)} %collective-permute-done.55.refs_3_), channel_id=1, source_target_pairs={{0,1},{1,0},{2,3},{3,2},{4,5},{5,4},{6,7},{7,6},{8,9},{9,8},{10,11... | collective-permute-start | bytes 442376 | tf_op jit(solution)/shard_map/ppermute | solution.py:822
  (80 other events, 517.0 us)
Sparse Core Ops, SparseCore 0:
  237.1 125.3 all-reduce.2

commit v3 on v2

v3 whole, which is shorter than its diff:
```python
import functools

import jax
import jax.numpy as jnp
from jax import lax
from jax.experimental import pallas as pl
from jax.experimental.pallas import tpu as pltpu
from jax.sharding import PartitionSpec as P

HEAD_DIM = 64
WIDE = 2 * HEAD_DIM
EPS = 1e-05
MASKED = -1e30
LOG2E = 1.4426950408889634
LN2 = 0.6931471805599453
f32 = jnp.float32
bf16 = jnp.bfloat16

CORE = [(0, 1), (1, 0), (2, 3), (3, 2)]
ACROSS = [(0, 2), (2, 0), (1, 3), (3, 1)]
MIB = 1 << 20
LIMIT = 18


def nn(left, right):
    return lax.dot_general(left, right, (((1,), (0,)), ((), ())), preferred_element_type=f32)


def nt(left, right):
    return lax.dot_general(left, right, (((1,), (1,)), ((), ())), preferred_element_type=f32)


def tn(left, right):
    return lax.dot_general(left, right, (((0,), (0,)), ((), ())), preferred_element_type=f32)


def lanes(rows):
    return lax.broadcasted_iota(jnp.int32, (rows, HEAD_DIM), 1)


def three_parts(value):
    high = value.astype(bf16).astype(f32)
    rest = value - high
    middle = rest.astype(bf16).astype(f32)
    return high, middle, rest - middle


def fill_queries(q_ref, rows, count, acc, heads):
    tail = jnp.where(lanes(count) == 0, 1.0, 0.0)
    for h in range(heads):
        part = acc[:, h * HEAD_DIM : (h + 1) * HEAD_DIM]
        q_ref[h, rows, :] = jnp.concatenate([part, tail], 1).astype(bf16)


def fill_keys(k_ref, v_ref, rows, start, count, acc, heads, limit):
    lane = lanes(count)
    index = start + lax.broadcasted_iota(jnp.int32, (count, HEAD_DIM), 0)
    tail = jnp.where(lane == 0, jnp.where(index < limit, 0.0, MASKED), jnp.where(lane < 4, 1.0, 0.0))
    ones = jnp.ones((count, HEAD_DIM), f32)
    for h in range(heads):
        k = acc[:, h * HEAD_DIM : (h + 1) * HEAD_DIM]
        v = acc[:, (heads + h) * HEAD_DIM : (heads + h + 1) * HEAD_DIM]
        k_ref[h, rows, :] = jnp.concatenate([k, tail], 1).astype(bf16)
        v_ref[h, rows, :] = jnp.concatenate([v, ones], 1).astype(bf16)


def attend_block(q_ref, k_ref, v_ref, att_ref, h, column, rows, count, key_end, causal):
    s = nt(q_ref[h, rows, :], k_ref[h, :key_end, :])
    if causal:
        r = lax.broadcasted_iota(jnp.int32, (count, count), 0)
        c = lax.broadcasted_iota(jnp.int32, (count, count), 1)
        diagonal = jnp.where(c <= r, s[:, key_end - count :], MASKED)
        s = diagonal if key_end == count else jnp.concatenate([s[:, : key_end - count], diagonal], 1)
    peak = jnp.max(s, 1, keepdims=True)
    p = jnp.exp2(s - peak).astype(bf16)
    o = nn(p, v_ref[h, :key_end, :])
    total = o[:, HEAD_DIM : HEAD_DIM + 1]
    att_ref[rows, column : column + HEAD_DIM] = (o[:, :HEAD_DIM] / total).astype(bf16)
    high, middle, low = three_parts(-(peak + jnp.log2(total)))
    lane = lanes(count)
    tail = jnp.where(
        lane == 0, 1.0, jnp.where(lane == 1, high, jnp.where(lane == 2, middle, jnp.where(lane == 3, low, 0.0)))
    )
    q_ref[h, rows, HEAD_DIM:] = tail.astype(bf16)


def fill_grads(do_ref, rows, count, grad, att, heads):
    lane = lanes(count)
    for h in range(heads):
        part = grad[:, h * HEAD_DIM : (h + 1) * HEAD_DIM].astype(bf16)
        mixed = att[:, h * HEAD_DIM : (h + 1) * HEAD_DIM].astype(f32)
        inner = jnp.sum(part.astype(f32) * mixed, 1, keepdims=True)
        high, middle, low = three_parts(-inner)
        tail = jnp.where(lane == 0, high, jnp.where(lane == 1, middle, jnp.where(lane == 2, low, 0.0)))
        do_ref[h, rows, :] = jnp.concatenate([part, tail.astype(bf16)], 1)


def back_block(q_ref, k_ref, v_ref, do_ref, dq_ref, dk_ref, dv_ref, h, rows, count, key_end, causal, first):
    q = q_ref[h, rows, :]
    d = do_ref[h, rows, :]
    k = k_ref[h, :key_end, :]
    v = v_ref[h, :key_end, :]
    p = jnp.exp2(nt(k, q))
    if causal:
        r = lax.broadcasted_iota(jnp.int32, (count, count), 0)
        c = lax.broadcasted_iota(jnp.int32, (count, count), 1)
        diagonal = jnp.where(r <= c, p[key_end - count :], 0.0)
        p = diagonal if key_end == count else jnp.concatenate([p[: key_end - count], diagonal], 0)
    ds = (p * nt(v, d)).astype(bf16)
    dv = nn(p.astype(bf16), d)
    dk = nn(ds, q)
    if first:
        dv_ref[h, :key_end, :] = dv
        dk_ref[h, :key_end, :] = dk
    else:
        dv_ref[h, :key_end, :] += dv
        dk_ref[h, :key_end, :] += dk
    dq_ref[h, rows, :] = tn(k, ds).T


def pack_heads(source, rows, heads, factor):
    return jnp.concatenate([source[h, rows, :HEAD_DIM] * factor for h in range(heads)], 1).astype(bf16)


def norm(resid):
    center = resid - jnp.mean(resid, -1, keepdims=True)
    scale = lax.rsqrt(jnp.mean(center * center, -1, keepdims=True) + EPS)
    return center * scale, scale


def norm_back(grad, gain, unit, scale):
    lifted = grad * gain
    first = jnp.mean(lifted, -1, keepdims=True)
    second = jnp.mean(lifted * unit, -1, keepdims=True)
    return scale * (lifted - first - unit * second)


def gelu_pair(value):
    scaled = value * 0.7071067811865476
    density = jnp.exp(-scaled * scaled) * 0.3989422804014327
    below = 0.5 * (1.0 + lax.erf(scaled))
    return value * below, below + value * density


BLOCK = 512
SPAN = 256
ROW, TGT, SRC, CORE_AT, BIT = 0, 1, 3, 5, 6
FACTOR = HEAD_DIM ** (-0.5) * LOG2E


def vector(ref):
    return ref[...].reshape(1, ref.shape[0])


def branch_of(shares, blocks):
    own0, own1, got0, got1 = shares
    first = pl.program_id(0) < blocks // 2
    own = jnp.where(first, own0[...], own1[...]).astype(f32)
    return own + jnp.where(first, got0[...], got1[...]).astype(f32)


def put_part(first_ref, second_ref, value, blocks):
    at = pl.program_id(0)

    @pl.when(at < blocks // 2)
    def _():
        first_ref[...] = value

    @pl.when(at >= blocks // 2)
    def _():
        second_ref[...] = value


def rows_at(size):
    return pl.ds(pl.multiple_of(pl.program_id(0) * size, size), size)


def project_own_kernel(
    s_ref, x_ref, m_ref, sq_ref, sk_ref, sv_ref, cq_ref, ck_ref, cv_ref, so_ref, co_ref, down_ref,
    q_ref, k_ref, v_ref, mk_ref, mv_ref, wa_ref, cwa_ref, half_out_ref, half_down_ref, *, heads,
):
    each = heads * HEAD_DIM
    at = pl.program_id(0)

    @pl.when(at == 0)
    def _():
        for n, ref in enumerate((sq_ref, sk_ref, sv_ref)):
            wa_ref[n * each : (n + 1) * each, :] = ref[...]
        for n, ref in enumerate((cq_ref, ck_ref, cv_ref)):
            cwa_ref[n * each : (n + 1) * each, :] = ref[...]
        half_out_ref[...] = jnp.where(s_ref[BIT] == 0, so_ref[...], co_ref[...])
        half_down_ref[...] = down_ref[...]

    limit = s_ref[TGT + s_ref[ROW]]
    memory_limit = s_ref[SRC + s_ref[ROW]]
    rows = pl.ds(0, BLOCK)
    acc = nt(x_ref[...], wa_ref[...])
    fill_queries(q_ref, rows, BLOCK, acc[:, :each] * FACTOR, heads)
    fill_keys(k_ref, v_ref, rows, at * BLOCK, BLOCK, acc[:, each:], heads, limit)
    acc = nt(m_ref[...], cwa_ref[each:, :])
    fill_keys(mk_ref, mv_ref, rows, at * BLOCK, BLOCK, acc, heads, memory_limit)


def causal_blocks(q_ref, k_ref, v_ref, att_ref, heads):
    at = pl.program_id(0)
    for block in range(k_ref.shape[1] // BLOCK):

        @pl.when(at == block)
        def _():
            for h in range(heads):
                attend_block(q_ref, k_ref, v_ref, att_ref, h, h * HEAD_DIM, pl.ds(0, BLOCK), BLOCK, (block + 1) * BLOCK, True)


def self_own_kernel(q_in_ref, k_ref, v_ref, q_ref, k_out_ref, v_out_ref, att_ref, *, heads):
    q_ref[...] = q_in_ref[...]
    k_out_ref[...] = k_ref[:, rows_at(BLOCK), :]
    v_out_ref[...] = v_ref[:, rows_at(BLOCK), :]
    causal_blocks(q_ref, k_ref, v_ref, att_ref, heads)


def self_other_kernel(s_ref, x_ref, near_ref, far_ref, w_ref, q_ref, k_out_ref, v_out_ref, att_ref, k_ref, v_ref, *, heads):
    each = heads * HEAD_DIM
    at = pl.program_id(0)
    half = near_ref.shape[0]
    high = s_ref[BIT]

    @pl.when(at == 0)
    def _():
        w_ref[pl.ds(pl.multiple_of(high * half, 16), half), :] = near_ref[...]
        w_ref[pl.ds(pl.multiple_of((1 - high) * half, 16), half), :] = far_ref[...]

    acc = nt(x_ref[...], w_ref[...])
    fill_queries(q_ref, pl.ds(0, BLOCK), BLOCK, acc[:, :each] * FACTOR, heads)
    fill_keys(k_ref, v_ref, rows_at(BLOCK), at * BLOCK, BLOCK, acc[:, each:], heads, s_ref[TGT + s_ref[ROW]])
    k_out_ref[...] = k_ref[:, rows_at(BLOCK), :]
    v_out_ref[...] = v_ref[:, rows_at(BLOCK), :]
    causal_blocks(q_ref, k_ref, v_ref, att_ref, heads)


def self_out_kernel(s_ref, atta_ref, attb_ref, soa_ref, near_ref, far_ref, part0_ref, part1_ref, sob_ref, cob_ref, *, blocks):
    @pl.when(pl.program_id(0) == 0)
    def _():
        low = s_ref[BIT] == 0
        sob_ref[...] = jnp.where(low, near_ref[...], far_ref[...])
        cob_ref[...] = jnp.where(low, far_ref[...], near_ref[...])

    part = nn(atta_ref[...], soa_ref[...]) + nn(attb_ref[...], sob_ref[...])
    put_part(part0_ref, part1_ref, part.astype(bf16), blocks)


def cross_blocks(q_ref, k_ref, v_ref, att_ref, heads, limit):
    step = 256
    live = (limit + step - 1) // step
    for count in range(1, k_ref.shape[1] // step + 1):

        @pl.when(live == count)
        def _():
            for h in range(heads):
                attend_block(q_ref, k_ref, v_ref, att_ref, h, h * HEAD_DIM, pl.ds(0, BLOCK), BLOCK, count * step, False)


def cross_own_kernel(
    s_ref, x_ref, own0, own1, got0, got1, gain_ref, shift_ref, cq_ref, k_ref, v_ref,
    h_ref, hl_ref, unit_ref, scale_ref, q_ref, att_ref, *, heads, blocks,
):
    unit, scale = norm(x_ref[...].astype(f32) + branch_of((own0, own1, got0, got1), blocks))
    h = unit * vector(gain_ref) + vector(shift_ref)
    h_ref[...] = h
    unit_ref[...] = unit.astype(bf16)
    scale_ref[...] = scale
    low = h.astype(bf16)
    hl_ref[...] = low
    fill_queries(q_ref, pl.ds(0, BLOCK), BLOCK, nt(low, cq_ref[...]) * FACTOR, heads)
    cross_blocks(q_ref, k_ref, v_ref, att_ref, heads, s_ref[SRC + s_ref[ROW]])


def cross_other_kernel(
    s_ref, m_ref, hl_ref, cwb_ref, atta_ref, coa_ref, cob_ref, part0_ref, part1_ref, k_ref, v_ref, q_ref, att_ref, *, heads, blocks,
):
    each = heads * HEAD_DIM
    limit = s_ref[SRC + s_ref[ROW]]

    @pl.when(pl.program_id(0) == 0)
    def _():
        @pl.loop(0, m_ref.shape[0], step=BLOCK)
        def _(start):
            rows = pl.ds(pl.multiple_of(start, BLOCK), BLOCK)
            fill_keys(k_ref, v_ref, rows, start, BLOCK, nt(m_ref[rows, :], cwb_ref[each:, :]), heads, limit)

    fill_queries(q_ref, pl.ds(0, BLOCK), BLOCK, nt(hl_ref[...], cwb_ref[:each, :]) * FACTOR, heads)
    cross_blocks(q_ref, k_ref, v_ref, att_ref, heads, limit)
    part = nn(atta_ref[...], coa_ref[...]) + nn(att_ref[...], cob_ref[...])
    put_part(part0_ref, part1_ref, part.astype(bf16), blocks)


def ffn_own_kernel(
    h_in_ref, own0, own1, got0, got1, gain_ref, shift_ref, up_ref, down_ref,
    h_ref, hl_ref, unit_ref, scale_ref, act_ref, slope_ref, term_ref, *, blocks,
):
    unit, scale = norm(h_in_ref[...] + branch_of((own0, own1, got0, got1), blocks))
    h = unit * vector(gain_ref) + vector(shift_ref)
    h_ref[...] = h
    unit_ref[...] = unit.astype(bf16)
    scale_ref[...] = scale
    low = h.astype(bf16)
    hl_ref[...] = low
    act, slope = gelu_pair(nn(low, up_ref[...]))
    act = act.astype(bf16)
    act_ref[...] = act
    slope_ref[...] = slope.astype(bf16)
    term_ref[...] = nn(act, down_ref[...])


def ffn_other_kernel(
    s_ref, hl_ref, term_ref, up_ref, near_ref, far_ref, part0_ref, part1_ref, act_ref, slope_ref, down_ref, *, blocks
):
    half = near_ref.shape[0]
    high = s_ref[BIT + 1]

    @pl.when(pl.program_id(0) == 0)
    def _():
        down_ref[pl.ds(pl.multiple_of(high * half, 16), half), :] = near_ref[...]
        down_ref[pl.ds(pl.multiple_of((1 - high) * half, 16), half), :] = far_ref[...]

    act, slope = gelu_pair(nn(hl_ref[...], up_ref[...]))
    act = act.astype(bf16)
    act_ref[...] = act
    slope_ref[...] = slope.astype(bf16)
    put_part(part0_ref, part1_ref, (term_ref[...] + nn(act, down_ref[...])).astype(bf16), blocks)


def ffn_back_kernel(
    s_ref, h_ref, own0, own1, got0, got1, cot_ref, gain_ref, shift_ref, upa_ref, upb_ref, downa_ref, downb_ref, slopea_ref, slopeb_ref,
    part0_ref, part1_ref, out_ref, d_ref, e_ref, prea_ref, preb_ref, sums_ref, *, blocks,
):
    limit = s_ref[TGT + s_ref[ROW]]
    at = pl.program_id(0)

    @pl.when(at == 0)
    def _():
        sums_ref[...] = jnp.zeros_like(sums_ref)

    gain = vector(gain_ref)
    unit, scale = norm(h_ref[...] + branch_of((own0, own1, got0, got1), blocks))
    out_ref[...] = (unit * gain + vector(shift_ref)).astype(bf16)
    index = at * SPAN + lax.broadcasted_iota(jnp.int32, (SPAN, 1), 0)
    grad = jnp.where(index < limit, cot_ref[...].astype(f32), 0.0)
    sums_ref[0:1, :] += jnp.sum(grad * unit, 0, keepdims=True)
    sums_ref[1:2, :] += jnp.sum(grad, 0, keepdims=True)
    d = norm_back(grad, gain, unit, scale)
    d_ref[...] = d
    e = d.astype(bf16)
    e_ref[...] = e
    part = None
    for up_ref, down_ref, slope_ref, pre_ref in (
        (upa_ref, downa_ref, slopea_ref, prea_ref),
        (upb_ref, downb_ref, slopeb_ref, preb_ref),
    ):
        pre = (nt(e, down_ref[...]) * slope_ref[...].astype(f32)).astype(bf16)
        pre_ref[...] = pre
        term = nt(pre, up_ref[...])
        part = term if part is None else part + term
    put_part(part0_ref, part1_ref, part.astype(bf16), blocks)


def ffn_grad_kernel(h_ref, act_ref, e_ref, pre_ref, up_ref, down_ref):
    up_ref[...] = tn(h_ref[...], pre_ref[...]).astype(bf16)
    down_ref[...] = tn(act_ref[...], e_ref[...]).astype(bf16)


def norm_step(d_in_ref, shares, gain, unit_ref, scale_ref, d_ref, e_ref, sums_ref, blocks):
    @pl.when(pl.program_id(0) == 0)
    def _():
        sums_ref[...] = jnp.zeros_like(sums_ref)

    grad = d_in_ref[...] + branch_of(shares, blocks)
    unit = unit_ref[...].astype(f32)
    sums_ref[0:1, :] += jnp.sum(grad * unit, 0, keepdims=True)
    sums_ref[1:2, :] += jnp.sum(grad, 0, keepdims=True)
    d = norm_back(grad, gain, unit, scale_ref[...])
    d_ref[...] = d
    e = d.astype(bf16)
    e_ref[...] = e
    return e


def cross_back_heads(s_ref, q_ref, k_ref, v_ref, do_ref, dqo_ref, dkv_ref, dq_ref, dk_ref, dv_ref, heads, blocks):
    at = pl.program_id(0)
    source = k_ref.shape[1]

    @pl.when(at == 0)
    def _():
        dk_ref[...] = jnp.zeros_like(dk_ref)
        dv_ref[...] = jnp.zeros_like(dv_ref)

    step = 256
    live = (s_ref[SRC + s_ref[ROW]] + step - 1) // step
    rows = pl.ds(0, BLOCK)
    for count in range(1, source // step + 1):

        @pl.when(live == count)
        def _():
            @pl.loop(0, heads)
            def _(h):
                back_block(q_ref, k_ref, v_ref, do_ref, dq_ref, dk_ref, dv_ref, h, rows, BLOCK, count * step, False, False)

    dqo_ref[...] = pack_heads(dq_ref, rows, heads, HEAD_DIM ** (-0.5))

    @pl.when(at == blocks - 1)
    def _():
        @pl.loop(0, source, step=BLOCK)
        def _(start):
            some = pl.ds(pl.multiple_of(start, BLOCK), BLOCK)
            dkv_ref[some, :] = jnp.concatenate(
                [pack_heads(dk_ref, some, heads, LN2), pack_heads(dv_ref, some, heads, 1.0)], 1
            )


def cross_back_other_kernel(
    s_ref, d_in_ref, own0, own1, got0, got1, gain_ref, unit_ref, scale_ref, coa_ref, cob_ref, atta_ref, attb_ref,
    q_ref, k_ref, v_ref,
    d_ref, e_ref, sums_ref, doa_ref, dqo_ref, dkv_ref, do_ref, dq_ref, dk_ref, dv_ref, *, heads, blocks,
):
    e = norm_step(
        d_in_ref, (own0, own1, got0, got1), vector(gain_ref), unit_ref, scale_ref, d_ref, e_ref, sums_ref, blocks
    )
    fill_grads(doa_ref, pl.ds(0, BLOCK), BLOCK, nt(e, coa_ref[...]), atta_ref[...], heads)
    fill_grads(do_ref, pl.ds(0, BLOCK), BLOCK, nt(e, cob_ref[...]), attb_ref[...], heads)
    cross_back_heads(s_ref, q_ref, k_ref, v_ref, do_ref, dqo_ref, dkv_ref, dq_ref, dk_ref, dv_ref, heads, blocks)


def cross_back_own_kernel(
    s_ref, q_ref, k_ref, v_ref, do_ref, dqb_ref, cqa_ref, cwb_ref,
    part0_ref, part1_ref, dqo_ref, dkv_ref, dq_ref, dk_ref, dv_ref, *, heads, blocks,
):
    cross_back_heads(s_ref, q_ref, k_ref, v_ref, do_ref, dqo_ref, dkv_ref, dq_ref, dk_ref, dv_ref, heads, blocks)
    part = nn(dqo_ref[...], cqa_ref[...]) + nn(dqb_ref[...], cwb_ref[: heads * HEAD_DIM, :])
    put_part(part0_ref, part1_ref, part.astype(bf16), blocks)


def cross_grad_kernel(s_ref, h_ref, m_ref, att_ref, e_ref, dq_ref, dkv_ref, g_ref):
    each = dq_ref.shape[1]
    g_ref[:each, :] = tn(dq_ref[...], h_ref[...]).astype(bf16)
    g_ref[each : 3 * each, :] = tn(dkv_ref[...], m_ref[...]).astype(bf16)
    g_ref[3 * each :, :] = tn(att_ref[...], e_ref[...]).astype(bf16)


def memory_grad_kernel(s_ref, a_ref, b_ref, wa_ref, wb_ref, out_ref, send_ref, keep_ref, half_ref):
    half_ref[...] = out_ref[...]
    each = a_ref.shape[1] // 2
    part = (nn(a_ref[...], wa_ref[each:, :]) + nn(b_ref[...], wb_ref[each:, :])).astype(bf16)
    mine = pl.program_id(0) == s_ref[CORE_AT]

    @pl.when(mine)
    def _():
        keep_ref[...] = part

    @pl.when(jnp.logical_not(mine))
    def _():
        send_ref[...] = part


def norm_one_back_kernel(
    s_ref, d_in_ref, own0, own1, got0, got1, gain_ref, unit_ref, scale_ref, soa_ref, sob_ref, atta_ref, attb_ref,
    sums_two_ref, sums_three_ref, d_ref, doa_ref, dob_ref, ra_ref, rb_ref, e_ref, sums_ref, *, heads, blocks,
):
    each = heads * HEAD_DIM
    rows = rows_at(SPAN)
    e = norm_step(
        d_in_ref, (own0, own1, got0, got1), vector(gain_ref), unit_ref, scale_ref, d_ref, e_ref.at[rows, :], sums_ref, blocks
    )
    fill_grads(doa_ref, pl.ds(0, SPAN), SPAN, nt(e, soa_ref[...]), atta_ref[rows, :], heads)
    fill_grads(dob_ref, pl.ds(0, SPAN), SPAN, nt(e, sob_ref[...]), attb_ref[rows, :], heads)

    @pl.when(pl.program_id(0) == blocks - 1)
    def _():
        norms = jnp.concatenate(
            [sums_ref[:2, :], sums_two_ref[:2, :], sums_three_ref[:2, :], jnp.zeros((10, d_in_ref.shape[1]), f32)], 0
        ).astype(bf16)
        for att_ref, r_ref in ((atta_ref, ra_ref), (attb_ref, rb_ref)):
            r_ref[:each, :] = tn(att_ref[...], e_ref[...]).astype(bf16)
            r_ref[each:, :] = norms


def self_back_kernel(s_ref, x_ref, q_ref, k_ref, v_ref, do_ref, dqkv_ref, gw_ref, dq_ref, dk_ref, dv_ref, *, heads, blocks):
    at = pl.program_id(0)
    each = heads * HEAD_DIM
    length = k_ref.shape[1]

    @pl.when(at == 0)
    def _():
        dk_ref[...] = jnp.zeros_like(dk_ref)
        dv_ref[...] = jnp.zeros_like(dv_ref)

    rows = pl.ds(0, SPAN)
    for block in range(blocks):

        @pl.when(at == block)
        def _():
            @pl.loop(0, heads)
            def _(h):
                back_block(q_ref, k_ref, v_ref, do_ref, dq_ref, dk_ref, dv_ref, h, rows, SPAN, (block + 1) * SPAN, True, False)

    dqkv_ref[rows_at(SPAN), :each] = pack_heads(dq_ref, rows, heads, HEAD_DIM ** (-0.5))

    @pl.when(at == blocks - 1)
    def _():
        @pl.loop(0, length, step=BLOCK)
        def _(start):
            some = pl.ds(pl.multiple_of(start, BLOCK), BLOCK)
            dqkv_ref[some, each:] = jnp.concatenate(
                [pack_heads(dk_ref, some, heads, LN2), pack_heads(dv_ref, some, heads, 1.0)], 1
            )
        gw_ref[...] = tn(dqkv_ref[...], x_ref[...]).astype(bf16)


def tokens_grad_kernel(s_ref, d_ref, a_ref, b_ref, wa_ref, wb_ref, send_ref, keep_ref):
    part = nn(a_ref[...], wa_ref[...]) + nn(b_ref[...], wb_ref[...])
    mine = pl.program_id(0) == s_ref[CORE_AT]

    @pl.when(mine)
    def _():
        keep_ref[...] = d_ref[...] + part

    @pl.when(jnp.logical_not(mine))
    def _():
        send_ref[...] = part.astype(bf16)


def place_kernel(s_ref, *refs, shift):
    out_ref = refs[-1]
    pieces = refs[:-1]
    half = out_ref.shape[0]
    row, core, at = s_ref[ROW], s_ref[CORE_AT], pl.program_id(0)
    if shift:
        sources = [
            (pieces[0].at[:half, :], 2 * row), (pieces[0].at[half:, :], 2 * row + 1),
            (pieces[1], 2 * (1 - row) + core), (pieces[2], 2 * (1 - row) + 1 - core),
        ]
    else:
        sources = [
            (pieces[0], 2 * row + core), (pieces[1], 2 * row + 1 - core),
            (pieces[2], 2 * (1 - row) + core), (pieces[3], 2 * (1 - row) + 1 - core),
        ]
    for ref, place in sources:

        @pl.when(at == place)
        def _():
            out_ref[...] = ref[...]


def step_kernel(s_ref, *refs, plans):
    scratch = refs[-1]
    inputs = sum(plan[1] for plan in plans)
    ins, outs = list(refs[:inputs]), list(refs[inputs:-1])
    for kind, count, rows, bit, cuts in plans:
        mine, ins = ins[:count], ins[count:]
        if kind == "sum":
            at = 0
            for a_ref, b_ref in zip(mine[: count // 2], mine[count // 2 :]):
                size = a_ref.shape[0]
                scratch[at : at + size, :] = (a_ref[...].astype(f32) + b_ref[...].astype(f32)).astype(bf16)
                at += size
            if at < rows:
                scratch[at:rows, :] = jnp.zeros((rows - at, scratch.shape[1]), bf16)
            if bit is None:
                outs.pop(0)[...] = scratch[:rows, :]
            else:
                half, high = rows // 2, s_ref[BIT + bit]
                outs.pop(0)[...] = scratch[pl.ds(pl.multiple_of((1 - high) * half, 16), half), :]
                outs.pop(0)[...] = scratch[pl.ds(pl.multiple_of(high * half, 16), half), :]
        else:
            high, size = s_ref[BIT + bit], mine[0].shape[0]
            target = outs.pop(0) if kind == "pack" else scratch
            target[pl.ds(pl.multiple_of(high * size, 16), size), :] = mine[0][...]
            target[pl.ds(pl.multiple_of((1 - high) * size, 16), size), :] = mine[1][...]
            for first, size in cuts:
                outs.pop(0)[...] = scratch[first : first + size, :].astype(f32)


class Row:
    def __init__(self, array, length, how="whole"):
        self.array, self.length, self.how = array, length, how


class Part:
    def __init__(self, array, how="rows", pick=None):
        self.array, self.how, self.pick = array, how, pick


class Pick:
    def __init__(self, array, scalar, parts):
        self.array, self.scalar, self.parts = array, scalar, parts


class Far:
    def __init__(self, array):
        self.array = array


def block_of(shape, how, blocks, pick=None, once=False):
    rank = len(shape)
    if rank == 1:
        return pl.BlockSpec(shape, lambda *a: (0,))
    if isinstance(how, tuple):
        how, pick = how
    if how == "whole":
        return pl.BlockSpec(shape, lambda *a: (0,) * rank, pipeline_mode=pl.Buffered(1) if once else None)
    pick = pick or (lambda i: i)
    dim = rank - 1 if how == "columns" else rank - 2
    parts = blocks // 2 if how == "half" else blocks
    block = tuple(n // parts if d == dim else n for d, n in enumerate(shape))
    return pl.BlockSpec(block, lambda i, *a: tuple(pick(i) if d == dim else 0 for d in range(rank)))


def row_of(item, blocks):
    width = item.array.shape[1]
    if item.how == "whole":
        return pl.BlockSpec((item.length, width), lambda i, s: (s[0], 0))
    if item.how == "rows":
        return pl.BlockSpec((item.length // blocks, width), lambda i, s: (s[0] * blocks + i, 0))
    if item.how[0] == "part":
        return pl.BlockSpec((item.length // blocks, width), lambda i, s: (s[item.how[1]] * blocks + i, 0))
    return pl.BlockSpec((item.length, width // blocks), lambda i, s: (s[0], i))


class Held:
    def __init__(self, array, how="rows"):
        self.array, self.how = array, how


def view_of(shape, how, blocks):
    rank = len(shape)
    if how == "whole":
        return None
    if how == "rows":
        size = shape[-2] // blocks

        def rows(ref):
            place = pl.ds(pl.multiple_of(pl.program_id(0) * size, size), size)
            return ref.at[place, :] if rank == 2 else ref.at[:, place, :]

        return rows
    size = shape[-1] // blocks
    return lambda ref: ref.at[:, pl.ds(pl.multiple_of(pl.program_id(0) * size, size), size)]


def call(kernel, name, blocks, inputs, outputs, scalars=None, scratch=(), micros=5.0, limit=LIMIT, after=(), scale=1.0):
    specs, arrays, views = [], [], []
    here = pl.BlockSpec(memory_space=pltpu.VMEM)
    for item in inputs:
        view = None
        if isinstance(item, Row):
            specs.append(row_of(item, blocks))
            arrays.append(pltpu.with_memory_space_constraint(item.array, pltpu.HBM))
        elif isinstance(item, Part):
            specs.append(block_of(item.array.shape, item.how, blocks, item.pick))
            arrays.append(item.array)
        elif isinstance(item, Pick):
            rows, width = item.array.shape
            specs.append(pl.BlockSpec((rows // item.parts, width), functools.partial(lambda at, i, s: (s[at], 0), item.scalar)))
            arrays.append(pltpu.with_memory_space_constraint(item.array, pltpu.HBM))
        elif isinstance(item, Far):
            specs.append(block_of(item.array.shape, "whole", blocks, once=True))
            arrays.append(pltpu.with_memory_space_constraint(item.array, pltpu.HBM))
        elif isinstance(item, Held):
            specs.append(here)
            arrays.append(pltpu.with_memory_space_constraint(item.array, pltpu.VMEM))
            view = view_of(item.array.shape, item.how, blocks)
        else:
            specs.append(block_of(item.shape, "whole", blocks, once=True))
            arrays.append(item)
        views.append(view)
    for item in after:
        specs.append(pl.BlockSpec(memory_space=pl.ANY))
        arrays.append(item)
        views.append("skip")
    shapes, out_specs = [], []
    for shape, dtype, how in outputs:
        if how[:4] == "held":
            shapes.append(pltpu.VMEM(shape, dtype))
            out_specs.append(here)
            views.append(view_of(shape, how[5:], blocks))
        else:
            far = how[:3] == "hbm"
            shapes.append(pltpu.HBM(shape, dtype) if far else jax.ShapeDtypeStruct(shape, dtype))
            out_specs.append(block_of(shape, how[4:] if far else how, blocks))
            views.append(None)
    lead = 0 if scalars is None else 1

    def viewed(*refs):
        passed = list(refs[:lead])
        for ref, view in zip(refs[lead : lead + len(views)], views):
            if view == "skip":
                continue
            passed.append(ref if view is None else view(ref))
        return kernel(*passed, *refs[lead + len(views) :])

    settings = dict(
        out_shape=shapes,
        compiler_params=pltpu.CompilerParams(vmem_limit_bytes=limit * MIB, dimension_semantics=("arbitrary",)),
        cost_estimate=pl.CostEstimate(flops=int(micros * scale * 1.0e9), bytes_accessed=0, transcendentals=0),
        name=name,
    )
    if scalars is None:
        return pl.pallas_call(
            viewed, grid=(blocks,), in_specs=specs, out_specs=out_specs, scratch_shapes=list(scratch), **settings
        )(*arrays)
    grid_spec = pltpu.PrefetchScalarGridSpec(
        num_scalar_prefetch=1, grid=(blocks,), in_specs=specs, out_specs=out_specs, scratch_shapes=list(scratch)
    )
    return pl.pallas_call(viewed, grid_spec=grid_spec, **settings)(scalars, *arrays)


def local(
    size, tokens, memory, cotangent, tgt_len, src_len, self_query, self_key, self_value, self_out,
    cross_query, cross_key, cross_value, cross_out, ffn_up, ffn_down,
    gain_one, shift_one, gain_two, shift_two, gain_three, shift_three,
):
    width = tokens.shape[1]
    length = tokens.shape[0] // 2
    source = memory.shape[0] // 2
    each = self_query.shape[1]
    heads = each // HEAD_DIM
    hidden = ffn_up.shape[1]
    place = lax.axis_index("tp").astype(jnp.int32)
    group = lax.axis_index("dp").astype(jnp.int32)
    scalars = jnp.concatenate(
        [jnp.stack([place // 2]), tgt_len, src_len, jnp.stack([place % 2] + [(group >> b) & 1 for b in range(3)])]
    )
    big, small, third = length // BLOCK, length // SPAN, width // SPAN
    short = size == 8

    def across(value):
        return lax.ppermute(value, "tp", ACROSS)

    def sibling(value):
        return lax.ppermute(value, "tp", CORE)

    def along(value, bit):
        return lax.ppermute(value, "dp", [(i, i ^ (1 << bit)) for i in range(size)])

    def shares(part, blocks):
        per = blocks // 2
        first, second = (lambda i: jnp.minimum(i, per - 1)), (lambda i: jnp.maximum(i - per, 0))
        got = [sibling(p) for p in part]
        return [Part(v, "half", pick) for v, pick in zip((*part, *got), (first, second) * 2)]

    def part_shapes(blocks):
        per = blocks // 2
        first, second = (lambda i: jnp.minimum(i, per - 1)), (lambda i: jnp.maximum(i - per, 0))
        return [((length // 2, width), bf16, ("half", pick)) for pick in (first, second)]

    head_rows = ((heads, length, WIDE), bf16, "hbm rows")
    head_held = ((heads, length, WIDE), bf16, "held rows")
    key_held = ((heads, source, WIDE), bf16, "held rows")
    held = ((length, width), f32, "held rows")
    held_low = ((length, width), bf16, "held rows")
    column = ((length, 1), f32, "held rows")
    att_held = ((length, each), bf16, "held rows")
    hid = ((length, hidden), bf16, "held rows")
    sums = ((8, width), f32, "whole")
    low = ((length, width), bf16, "rows")
    square = ((width, hidden), bf16, "rows")
    half_low = ((length // 2, width), bf16, "whole")
    out_shape = ((each, width), bf16, "whole")
    qkv = functools.partial(pltpu.VMEM, (heads, length, WIDE))

    w_parts = (self_query.T, self_key.T, self_value.T)
    c_parts = (cross_query.T, cross_key.T, cross_value.T)
    bit = scalars[BIT]
    w_half = lax.dynamic_slice_in_dim(jnp.concatenate(w_parts, 0), bit * (3 * each // 2), 3 * each // 2, 0)
    w_near = across(w_half)
    q_new, k_new, v_new, ck_a, cv_a, w_a, cw_a, o_half, down_half = call(
        functools.partial(project_own_kernel, heads=heads), "project_own", big,
        [
            Row(tokens, length, "rows"), Row(memory, source, "rows"), *(Far(v) for v in (*w_parts, *c_parts, self_out, cross_out)),
            Pick(ffn_down, BIT + 1, 2),
        ],
        [
            head_held, head_held, head_held, key_held, key_held, ((3 * each, width), bf16, "whole"),
            ((3 * each, width), bf16, "whole"), out_shape, ((hidden // 2, width), bf16, "whole"),
        ],
        scalars, micros=7, scale=0.05,
    )
    o_near = across(o_half)
    cw_b = across(cw_a)
    up_b = across(ffn_up)
    down_near = across(down_half)
    down_far = along(down_near, 1)
    w_far = along(w_near, 0)
    q_a, k_a, v_a, att_a = call(
        functools.partial(self_own_kernel, heads=heads), "self_own", big, [Held(q_new), Held(k_new, "whole"), Held(v_new, "whole")],
        [head_rows, head_rows, head_rows, att_held], micros=6, scale=0.05, after=[w_near],
    )
    o_far = along(o_near, 0)
    w_b, q_b, k_b, v_b, att_b = call(
        functools.partial(self_other_kernel, heads=heads), "self_other", big, [Row(tokens, length, "rows"), w_near, w_far],
        [((3 * each, width), bf16, "whole"), head_rows, head_rows, head_rows, att_held], scalars, scratch=[qkv(bf16), qkv(bf16)],
        micros=9, scale=0.05, after=[o_near],
    )
    part0, part1, so_b, co_b = call(
        functools.partial(self_out_kernel, blocks=big), "self_out", big, [Held(att_a), Held(att_b), self_out, o_near, o_far],
        [*part_shapes(big), out_shape, out_shape], scalars, micros=3, scale=0.05,
    )
    h_one, h_one_low, unit_one, scale_one, cq_a, catt_a = call(
        functools.partial(cross_own_kernel, heads=heads, blocks=big), "cross_own", big,
        [Row(tokens, length, "rows"), *shares((part0, part1), big), gain_one, shift_one, c_parts[0], Held(ck_a, "whole"), Held(cv_a, "whole")],
        [held, held_low, held_low, column, head_held, att_held], scalars, micros=10, scale=0.05,
    )
    part0, part1, ck_b, cv_b, cq_b, catt_b = call(
        functools.partial(cross_other_kernel, heads=heads, blocks=big), "cross_other", big,
        [Row(memory, source), Held(h_one_low), cw_b, Held(catt_a), cross_out, co_b],
        [
            *part_shapes(big), ((heads, source, WIDE), bf16, "held whole"), ((heads, source, WIDE), bf16, "held whole"),
            head_held, att_held,
        ],
        scalars, micros=11, scale=0.05, after=[down_near],
    )
    h_two, h_two_low, unit_two, scale_two, act_a, slope_a, term = call(
        functools.partial(ffn_own_kernel, blocks=small), "ffn_own", small,
        [Held(h_one), *shares((part0, part1), small), gain_two, shift_two, Held(ffn_up, "whole"), Held(ffn_down, "whole")],
        [held, held_low, held_low, column, hid, hid, held], micros=7, scale=0.05,
    )
    part0, part1, act_b, slope_b, down_b = call(
        functools.partial(ffn_other_kernel, blocks=small), "ffn_other", small,
        [Held(h_two_low), Held(term), up_b, down_near, down_far],
        [*part_shapes(small), hid, hid, ((hidden, width), bf16, "held whole")], scalars, micros=5, scale=0.05,
    )

    part0, part1, out_row, d_three, e_three, pre_a, pre_b, sums_three = call(
        functools.partial(ffn_back_kernel, blocks=small), "ffn_back", small,
        [
            Held(h_two), *shares((part0, part1), small), Row(cotangent, length, "rows"), gain_three, shift_three,
            Held(ffn_up, "whole"), up_b, Held(ffn_down, "whole"), Held(down_b, "whole"), Held(slope_a), Held(slope_b),
        ],
        [*part_shapes(small), low, held, held_low, hid, hid, sums], scalars, micros=11,
    )
    part = (part0, part1)
    gu_b, gd_b = call(
        ffn_grad_kernel, "ffn_grad_other", third,
        [Held(h_two_low, "columns"), Held(act_b, "columns"), Held(e_three, "whole"), Held(pre_b, "whole")], [square, square], micros=4,
    )
    gu_got, gd_got = across(gu_b), across(gd_b)
    gu_a, gd_a = call(
        ffn_grad_kernel, "ffn_grad_own", third,
        [Held(h_two_low, "columns"), Held(act_a, "columns"), Held(e_three, "whole"), Held(pre_a, "whole")], [square, square], micros=4,
    )
    back_scratch = [
        pltpu.VMEM((heads, BLOCK, WIDE), f32), pltpu.VMEM((heads, source, WIDE), f32), pltpu.VMEM((heads, source, WIDE), f32),
    ]
    dkv_held = ((source, 2 * each), bf16, "held whole")
    d_two, e_two, sums_two, do_a, dcq_b, dckv_b = call(
        functools.partial(cross_back_other_kernel, heads=heads, blocks=big), "cross_back_other", big,
        [
            Held(d_three), *shares(part, big), gain_two, Held(unit_two), Held(scale_two), cross_out, co_b, Held(catt_a), Held(catt_b),
            Held(cq_b), Held(ck_b, "whole"), Held(cv_b, "whole"),
        ],
        [held, held_low, sums, head_held, att_held, dkv_held], scalars,
        scratch=[pltpu.VMEM((heads, BLOCK, WIDE), bf16)] + back_scratch, micros=18,
    )

    def step(name, plans, after=(), micros=2):
        inputs, outputs, kernel_plans, counts, most = [], [], [], [], 16
        for kind, arrays, rows, bit, cuts in plans:
            inputs += arrays
            if kind == "sum":
                made = [((rows, width), bf16, "whole")] if bit is None else [((rows // 2, width), bf16, "whole")] * 2
            elif kind == "pack":
                made = [((rows, width), bf16, "whole")]
            else:
                made = [((size, width), f32, "hbm whole") for _, size in cuts]
            if kind != "pack":
                most = max(most, rows)
            outputs += made
            counts.append(len(made))
            kernel_plans.append((kind, len(arrays), rows, bit, cuts))
        made = list(
            call(
                functools.partial(step_kernel, plans=kernel_plans), name, 1, inputs, outputs, scalars,
                scratch=[pltpu.VMEM((most, width), bf16)], micros=micros, after=after,
            )
        )
        return [made[sum(counts[:n]) : sum(counts[: n + 1])] for n in range(len(counts))]

    class Chain:
        def __init__(self, mine, got, rows, cuts):
            self.arrays, self.rows, self.cuts, self.stage = [*mine, *got], rows, cuts, 0

        def plan(self):
            stage = self.stage
            if stage <= 3:
                return ("sum", self.arrays, self.rows >> stage, stage if stage < 3 else None, ())
            bit = 6 - stage
            return ("wide" if stage == 6 else "pack", self.arrays, self.rows >> bit, bit, self.cuts if stage == 6 else ())

        def take(self, made):
            stage, self.stage = self.stage, self.stage + 1
            if stage < 3:
                self.arrays = [made[1], along(made[0], stage)]
            elif stage < 6:
                self.arrays = [made[0], along(made[0], 5 - stage)]
            else:
                self.done = made

    def advance(name, chains, plans=(), after=(), micros=2):
        made = step(name, [c.plan() for c in chains] + list(plans), after, micros)
        for chain, one in zip(chains, made):
            chain.take(one)
        return [made[0][-1]], [m[0] for m in made[len(chains) :]]

    everything = [(0, width)]
    thirds = [(n * each, each) for n in range(3)]
    pin = []
    if short:
        up = Chain([gu_a], [gu_got], width, everything)
        pin, _ = advance("step_0", [up], after=[dcq_b])
    part0, part1, dcq_a, dckv_a = call(
        functools.partial(cross_back_own_kernel, heads=heads, blocks=big), "cross_back_own", big,
        [Held(cq_a), Held(ck_a, "whole"), Held(cv_a, "whole"), Held(do_a), Held(dcq_b), c_parts[0], cw_b],
        [*part_shapes(big), att_held, dkv_held], scalars, scratch=back_scratch, micros=16, after=pin,
    )
    part = (part0, part1)

    def cross_grads(name, att, dq, dkv, after=()):
        return call(
            cross_grad_kernel, name, third,
            [
                Held(h_one_low, "columns"), Row(memory, source, "columns"), Held(att, "whole"), Held(e_two, "columns"),
                Held(dq, "whole"), Held(dkv, "whole"),
            ],
            [((4 * each, width), bf16, "columns")], scalars, micros=5, after=after,
        )[0]

    gc_b = cross_grads("cross_grad_other", catt_b, dcq_b, dckv_b, [dcq_a])
    gc_got = across(gc_b)
    if short:
        down = Chain([gd_a], [gd_got], width, everything)
        pin, _ = advance("step_1", [up, down], after=[gc_b])
    gc_a = cross_grads("cross_grad_own", catt_a, dcq_a, dckv_a, pin)
    memory_send, memory_keep, out_half = call(
        memory_grad_kernel, "memory_grad", 2,
        [Held(dckv_a), Held(dckv_b), cw_a, cw_b, Row(out_row, length // 2, ("part", CORE_AT))],
        [half_low, half_low, ((length // 2, width), bf16, "rows")], scalars, micros=5, after=[gc_a],
    )
    out_far = across(out_half)
    memory_got = sibling(memory_send)
    pin = [memory_send]
    if short:
        cross = Chain([gc_a], [gc_got], 4 * each, [(n * each, each) for n in range(4)])
        pin, _ = advance("step_2", [up, down, cross], after=[memory_send])
    rest_shape = ((each + 16, width), bf16, "whole")
    d_one, do_a, do_b, rest_a, rest_b = call(
        functools.partial(norm_one_back_kernel, heads=heads, blocks=small), "norm_one_back", small,
        [
            Held(d_two), *shares(part, small), gain_one, Held(unit_one), Held(scale_one), self_out, so_b,
            Held(att_a, "whole"), Held(att_b, "whole"), sums_two, sums_three,
        ],
        [held, head_held, head_held, rest_shape, rest_shape], scalars,
        scratch=[pltpu.VMEM((length, width), bf16), pltpu.VMEM((8, width), f32)], micros=6, after=pin,
    )
    rest_got = across(rest_b)
    kept_w = ((3 * each, width), bf16, "whole")
    qkv_held = ((length, 3 * each), bf16, "held whole")
    self_scratch = [
        pltpu.VMEM((heads, SPAN, WIDE), f32), pltpu.VMEM((heads, length, WIDE), f32), pltpu.VMEM((heads, length, WIDE), f32),
    ]

    def self_back(name, q, k, v, do, after=()):
        return call(
            functools.partial(self_back_kernel, heads=heads, blocks=small), name, small,
            [Row(tokens, length), Part(q), k, v, Held(do)], [qkv_held, kept_w], scalars, scratch=self_scratch, micros=14, after=after,
        )

    pin = []
    if short:
        pin, _ = advance("step_3", [up, down, cross], after=[do_b])
    dqkv_b, gw_b = self_back("self_back_other", q_b, k_b, v_b, do_b, pin)
    gw_got = across(gw_b)

    pin = []
    if short:
        rest = Chain([rest_a], [rest_got], 256, [(0, each), (each, 16)])
        pin, _ = advance("step_4", [up, down, cross, rest], (), [dqkv_b], 3)
    dqkv_a, gw_a = self_back("self_back_own", q_a, k_a, v_a, do_a, pin)
    memory_plan = ("sum", [memory_keep, memory_got], length // 2, None, ())
    if short:
        own = Chain([gw_a], [gw_got], 640, thirds)
        pin, (mine,) = advance("step_5", [own, up, down, cross, rest], [memory_plan], (), 4)
    else:
        ((mine,),) = step("memory_finish", [memory_plan], [gw_a])
        pin = []
    far = across(mine)
    memory_pieces = [mine, sibling(mine), far, sibling(far)]
    tokens_send, tokens_keep = call(
        tokens_grad_kernel, "tokens_grad", 2, [Held(d_one), Held(dqkv_a), Held(dqkv_b), w_a, w_b],
        [half_low, ((length // 2, width), f32, "whole")], scalars, micros=6, after=pin,
    )
    tokens_plan = ("sum", [tokens_keep, sibling(tokens_send)], length // 2, None, ())

    def placed(name, pieces, shift, after=()):
        return call(
            functools.partial(place_kernel, shift=shift), name, 4, pieces, [((2 * length, width), bf16, "hbm rows")], scalars,
            micros=4, after=after,
        )[0]

    if short:
        pin, (mine,) = advance("step_6", [own, up, down, cross, rest], [tokens_plan], [tokens_send], 3)
    else:
        ((mine,),) = step("tokens_finish", [tokens_plan])
        pin = []
    far = across(mine)
    tokens_pieces = [mine, sibling(mine), far, sibling(far)]
    layer_out = placed("place_layer_out", [out_row, out_far, sibling(out_far)], True, pin)
    if short:
        pin, _ = advance("step_7", [own, down, cross, rest], (), [layer_out])
        memory_grad = placed("place_memory_grad", memory_pieces, False, pin)
        pin, _ = advance("step_8", [own, cross, rest], (), [memory_grad])
        pin, _ = advance("step_9", [own, rest], (), pin)
        tokens_grad = placed("place_tokens_grad", tokens_pieces, False, pin)
        pin, _ = advance("step_10", [own, rest], (), [tokens_grad])
        advance("step_11", [own], (), pin)
        (gu_wide,), (gd_wide,), cross, own = up.done, down.done, cross.done, own.done
        rest, norms = rest.done
    else:
        memory_grad = placed("place_memory_grad", memory_pieces, False)
        tokens_grad = placed("place_tokens_grad", tokens_pieces, False)

        def total(mine, got):
            return lax.psum((mine.astype(f32) + got.astype(f32)).astype(bf16), "dp").astype(f32)

        gu_wide, gd_wide = total(gu_a, gu_got), total(gd_a, gd_got)
        cross = jnp.split(total(gc_a, gc_got), 4)
        own = jnp.split(total(gw_a, gw_got), 3)
        rest = total(rest_a, rest_got)
        rest, norms = rest[:each], rest[each:]
    return (
        layer_out, tokens_grad, memory_grad,
        own[0].T, own[1].T, own[2].T, rest,
        cross[0].T, cross[1].T, cross[2].T, cross[3],
        gu_wide, gd_wide, *(norms[i] for i in range(6)),
    )


def solution(mesh):
    rows, columns, down = P("dp", None), P(None, "tp"), P("tp", None)
    return jax.shard_map(
        functools.partial(local, mesh.shape["dp"]),
        mesh=mesh,
        in_specs=(rows, rows, rows, P("dp"), P("dp"))
        + (columns, columns, columns, down) * 2
        + (columns, down)
        + (P(),) * 6,
        out_specs=(rows, rows, rows) + (columns, columns, columns, down) * 2 + (columns, down) + (P(),) * 6,
        check_vma=False,
    )
```

time: 446 us -> 376 us (0.84)
  Pallas kernels: 242 us -> 184 us
  waiting for transfers between devices: 95.8 us -> 110 us
  between operations: 14.8 us -> 1.6 us
  local copies, waits for them, and re-layouts: 27.4 us -> 20.2 us
    pallas_call x28 -> x35, Pallas kernels: 242 us -> 184 us  [the longest x31 165 us: call(): pl.pallas_call(viewed, grid_spec=grid_spec, **settings)(scalars, *arrays)]
    slice x5 -> x0, local copies, waits for them, and re-layouts: 7.54 us -> none  [exchange(): return (sibling(part[:half]), sibling(part[half:]))]
    ppermute x30 -> x33, waiting for transfers between devices: 49.7 us -> 55.8 us  [along(): return lax.ppermute(value, 'dp', [(i, i ^ 1 << bit) for i in range(size)])]
    ppermute x13, waiting for transfers between devices: 43.6 us -> 49.1 us  [across(): return lax.ppermute(value, 'tp', ACROSS)]
    convert_element_type x2 -> x0, other arithmetic: 4.52 us -> none  [the longest x1 2.94 us: local(): gu_sum.astype(f32)]
    unnamed x134 -> x94, local copies, waits for them, and re-layouts: 14 us -> 17.8 us
    ppermute x30 -> x33, starting transfers between devices: 33.9 us -> 35.8 us  [along(): return lax.ppermute(value, 'dp', [(i, i ^ 1 << bit) for i in range(size)])]
  transfers between devices with their start and end apart: 61 -> 63, of which waited for: 17 -> 28; matrix products, arithmetic and copies ran while one was open for 4% -> 1% of each run, Pallas kernels for 48% -> 44%
where the time goes in v3:
time: 376 us; the launch traced here: 370 us
  Pallas kernels  184 us (49%)
  waiting for transfers between devices  110 us (29%)
  starting transfers between devices  52.9 us (14%)
  local copies, waits for them, and re-layouts  20.2 us (5%)
    pallas_call x31, Pallas kernels, call(): pl.pallas_call(viewed, grid_spec=grid_spec, **settings)(scalars, *arrays)  165 us
    ppermute x33, waiting for transfers between devices, along(): return lax.ppermute(value, 'dp', [(i, i ^ 1 << bit) for i in range(size)])  55.8 us
    ppermute x13, waiting for transfers between devices, across(): return lax.ppermute(value, 'tp', ACROSS)  49.1 us
    ppermute x33, starting transfers between devices, along(): return lax.ppermute(value, 'dp', [(i, i ^ 1 << bit) for i in range(size)])  35.8 us
    pallas_call x4, Pallas kernels, call(): pl.pallas_call(viewed, grid=(blocks,), in_specs=specs, out_specs=out_spec...  19.1 us
    unnamed x94, local copies, waits for them, and re-layouts  17.8 us
    ppermute x13, starting transfers between devices, across(): return lax.ppermute(value, 'tp', ACROSS)  14.2 us
  transfers between devices with their start and end apart: 63, of which 28 were waited for; matrix products, arithmetic and copies ran while one was open for 1% of the time, Pallas kernels for 44%

profile of v3, /device:TPU:0, one launch (start us, length us, event | category | flops | bytes accessed | tf_op | source)
XLA Modules:
  0.0 370.2 jit_solution(6469654706541219066)
XLA Ops:
  2.0 3.0 collective-permute-start
  5.8 5.7 %project_own.1 = (bf16[3,1024,128]{2,1,0:T(8,128)(2,1)S(1)}, bf16[3,1024,128]{2,1,0:T(8,128)(2,1)S(1)}, bf16[3,1024,128]{2,1,0:T(8,128)(2,1)S(1)}, bf16[3,1024,1...) custom-call(s32[9]{0:T(128)S(1)} %concatenate.6.refs_0_, ...), custom_call_target="tpu_custom_call" | custom-call | flops 350000000 | tf_op jit(solution)/shard_map/project_own/pallas_call | solution.py:712
  11.7 4.4 %collective-permute-done.refs_3_.refs_2_ = bf16[288,768]{1,0:T(8,128)(2,1)S(1)} collective-permute-done((bf16[288,768]{1,0:T(8,128)(2,1)S(1)}, bf16[288,768]{1,0:T(8,128)(2,1)S(1)}, u32[]{:S(2)}, u32[]{:S(2)}) %collective-permute-start) | collective-permute-done | bytes 442400 | tf_op jit(solution)/shard_map/ppermute | solution.py:735
  16.0 2.1 collective-permute-start.1
  18.2 3.4 collective-permute-done.2.refs_4_
  24.8 6.8 %self_own.1 = (bf16[3,1024,128]{2,1,0:T(8,128)(2,1)}, bf16[3,1024,128]{2,1,0:T(8,128)(2,1)}, bf16[3,1024,128]{2,1,0:T(8,128)(2,1)}, bf16[1024,192]{1,0:T(8,128)(2,1)S(1)}) custom-call(bf16[3,1024,128]{2,1,0:T(8,128)(2,1)S(1)} %get-tuple-element.159.refs_0_, bf16[3,1024,128]{2,1,0:T(8,128)(2,1)S(1)} %get-tuple-element.160.refs_1_, ...), custom_call_target="tpu_custom_call" | custom-call | flops 300000000 | tf_op jit(solution)/shard_map/self_own/pallas_call | solution.py:706
  31.6 10.9 %self_other.1 = (bf16[576,768]{1,0:T(8,128)(2,1)S(1)}, bf16[3,1024,128]{2,1,0:T(8,128)(2,1)}, bf16[3,1024,128]{2,1,0:T(8,128)(2,1)}, bf16[3,1024,128]{2,1,0:T(8,128)(2,1)}, bf16[1024,192]{1,0:T(8,128)(2,1)S(1)}) custom-call(s32[9]{0:T(128)S(1)} %concatenate.6.refs_0_, bf16[2048,768]{1,0:T(8,128)(2,1)} %refs_1_.11, ...), custom_call_target="tpu_custom_call" | custom-call | flops 450000000 | tf_op jit(solution)/shard_map/self_other/pallas_call | solution.py:712
  48.0 9.8 %cross_own.1 = (f32[1024,768]{1,0:T(8,128)S(1)}, bf16[1024,768]{1,0:T(8,128)(2,1)S(1)}, bf16[1024,768]{1,0:T(8,128)(2,1)S(1)}, f32[1024,1]{1,0:T(8,128)S(1)}, bf...) custom-call(s32[9]{0:T(128)S(1)} %concatenate.6.refs_0_, bf16[2048,768]{1,0:T(8,128)(2,1)} %refs_1_.11, ...), custom_call_target="tpu_custom_call" | custom-call | flops 500000000 | tf_op jit(solution)/shard_map/cross_own/pallas_call | solution.py:712
  58.6 2.7 collective-permute-done.7.refs_7_.refs_4_
  61.3 11.5 %cross_other.1 = (bf16[512,768]{1,0:T(8,128)(2,1)S(1)}, bf16[512,768]{1,0:T(8,128)(2,1)S(1)}, bf16[3,1024,128]{2,1,0:T(8,128)(2,1)S(1)}, bf16[3,1024,128]{2,1,0:...) custom-call(s32[9]{0:T(128)S(1)} %concatenate.6.refs_0_, bf16[2048,768]{1,0:T(8,128)(2,1)} %refs_2_.5, ...), custom_call_target="tpu_custom_call" | custom-call | flops 550000000 | tf_op jit(solution)/shard_map/cross_other/pallas_call | solution.py:712
  79.8 6.1 %ffn_own.1 = (f32[1024,768]{1,0:T(8,128)S(1)}, bf16[1024,768]{1,0:T(8,128)(2,1)S(1)}, bf16[1024,768]{1,0:T(8,128)(2,1)S(1)}, f32[1024,1]{1,0:T(8,128)S(1)}, bf16...) custom-call(f32[1024,768]{1,0:T(8,128)S(1)} %get-tuple-element.169.refs_0_, ...), custom_call_target="tpu_custom_call" | custom-call | flops 350000000 | tf_op jit(solution)/shard_map/ffn_own/pallas_call | solution.py:706
  86.7 5.4 %collective-permute-done.11.refs_5_ = bf16[384,768]{1,0:T(8,128)(2,1)S(1)} collective-permute-done((bf16[384,768]{1,0:T(8,128)(2,1)S(1)}, bf16[384,768]{1,0:T(8,128)(2,1)S(1)}, u32[]{:S(2)}, u32[]{:S(2)}) %collective-permute-start.11) | collective-permute-done | bytes 589856 | tf_op jit(solution)/shard_map/ppermute | solution.py:741
  92.1 5.1 %ffn_other.1 = (bf16[512,768]{1,0:T(8,128)(2,1)S(1)}, bf16[512,768]{1,0:T(8,128)(2,1)S(1)}, bf16[1024,768]{1,0:T(8,128)(2,1)S(1)}, bf16[1024,768]{1,0:T(8,128)(2,1)S(1)}, bf16[768,768]{1,0:T(8,128)(2,1)S(1)}) custom-call(s32[9]{0:T(128)S(1)} %concatenate.6.refs_0_, bf16[1024,768]{1,0:T(8,128)(2,1)S(1)} %get-tuple-element.178.refs_1_.refs_0_, ...), custom_call_target="tpu_custom_call" | custom-call | flops 250000000 | tf_op jit(solution)/shard_map/ffn_other/pallas_call | solution.py:712
  100.6 11.6 %ffn_back.1 = (bf16[512,768]{1,0:T(8,128)(2,1)S(1)}, bf16[512,768]{1,0:T(8,128)(2,1)S(1)}, bf16[1024,768]{1,0:T(8,128)(2,1)S(1)}, f32[1024,768]{1,0:T(8,128)S(1)...) custom-call(s32[9]{0:T(128)S(1)} %concatenate.6.refs_0_, ...), custom_call_target="tpu_custom_call" | custom-call | flops 11000000512 | tf_op jit(solution)/shard_map/ffn_back/pallas_call | solution.py:712
  115.6 2.5 copy-done.41
  118.1 3.1 ffn_grad_other.1
  124.8 3.1 ffn_grad_own.1
  128.2 18.3 %cross_back_other.1 = (f32[1024,768]{1,0:T(8,128)S(1)}, bf16[1024,768]{1,0:T(8,128)(2,1)S(1)}, f32[8,768]{1,0:T(8,128)S(1)}, bf16[3,1024,128]{2,1,0:T(8,128)(2,1...) custom-call(s32[9]{0:T(128)S(1)} %concatenate.6.refs_0_, f32[1024,768]{1,0:T(8,128)S(1)} %copy-done.46, ...), custom_call_target="tpu_custom_call" | custom-call | flops 17999998976 | tf_op jit(solution)/shard_map/cross_back_other/pallas_call | solution.py:712
  146.5 3.7 collective-permute-done.16.refs_2_
  151.9 12.0 %cross_back_own.1 = (bf16[512,768]{1,0:T(8,128)(2,1)S(1)}, bf16[512,768]{1,0:T(8,128)(2,1)S(1)}, bf16[1024,192]{1,0:T(8,128)(2,1)S(1)}, bf16[1024,384]{1,0:T(8,128)(2,1)S(1)}) custom-call(s32[9]{0:T(128)S(1)} %concatenate.6.refs_0_, bf16[3,1024,128]{2,1,0:T(8,128)(2,1)S(1)} %copy-done.16, bf16[3,1024,128]{2,1,0:T(8,128)(2,1)S(1)} %get-tuple-element.167.refs_9_.refs_2_, ...), custom_call_target="tpu_custom_call" | custom-call | flops 16000000000 | tf_op jit(solution)/shard_map/cross_back_own/pallas_call | solution.py:712
  163.9 4.2 %cross_grad_other.1.refs_5_ = bf16[768,768]{1,0:T(8,128)(2,1)S(1)} custom-call(s32[9]{0:T(128)S(1)} %concatenate.6.refs_0_, bf16[1024,768]{1,0:T(8,128)(2,1)S(1)} %get-tuple-element.170.refs_2_.refs_1_, bf16[2048,768]{1,0:T(8,128)(2,1)} %refs_2_.5, bf16[1024,192]{1,0:T(8,128)(2,1)S(1)} %copy-done.30, bf16[1024,768]{1,0:T(8,128)(2,1)S(1)} %get-tuple-element.208.refs_4_, ...), custom_call_target="tpu_custom_call" | custom-call | flops 5000000000 | tf_op jit(solution)/shard_map/cross_grad_other/pallas_call | solution.py:712
  168.8 6.6 %collective-permute-done.18.refs_4_ = bf16[768,768]{1,0:T(8,128)(2,1)S(1)} collective-permute-done((bf16[768,768]{1,0:T(8,128)(2,1)S(1)}, bf16[768,768]{1,0:T(8,128)(2,1)S(1)}, u32[]{:S(2)}, u32[]{:S(2)}) %collective-permute-start.18) | collective-permute-done | bytes 1179680 | tf_op jit(solution)/shard_map/ppermute | solution.py:735
  179.1 4.2 %cross_grad_own.1.refs_6_.refs_5_ = bf16[768,768]{1,0:T(8,128)(2,1)S(1)} custom-call(s32[9]{0:T(128)S(1)} %concatenate.6.refs_0_, bf16[1024,768]{1,0:T(8,128)(2,1)S(1)} %get-tuple-element.170.refs_2_.refs_1_, bf16[2048,768]{1,0:T(8,128)(2,1)} %refs_2_.5, bf16[1024,192]{1,0:T(8,128)(2,1)S(1)} %get-tuple-element.172.refs_4_.refs_11_.refs_3_, ...), custom_call_target="tpu_custom_call" | custom-call | flops 5000000000 | tf_op jit(solution)/shard_map/cross_grad_own/pallas_call | solution.py:712
  183.3 3.7 %memory_grad.1 = (bf16[512,768]{1,0:T(8,128)(2,1)S(1)}, bf16[512,768]{1,0:T(8,128)(2,1)S(1)}, bf16[512,768]{1,0:T(8,128)(2,1)S(1)}) custom-call(s32[9]{0:T(128)S(1)} %concatenate.6.refs_0_, bf16[1024,384]{1,0:T(8,128)(2,1)S(1)} %get-tuple-element.206.refs_6_.refs_1_, bf16[1024,384]{1,0:T(8,128)(2,1)S(1)} %get-tuple-element.207.refs_6_.refs_2_, ...), custom_call_target="tpu_custom_call" | custom-call | flops 5000000000 | tf_op jit(solution)/shard_map/memory_grad/pallas_call | solution.py:712
  187.0 5.1 %collective-permute-done.24.refs_4_ = bf16[384,768]{1,0:T(8,128)(2,1)S(1)} collective-permute-done((bf16[384,768]{1,0:T(8,128)(2,1)S(1)}, bf16[384,768]{1,0:T(8,128)(2,1)S(1)}, u32[]{:S(2)}, u32[]{:S(2)}) %collective-permute-start.24) | collective-permute-done | bytes 589856 | tf_op jit(solution)/shard_map/ppermute | solution.py:741
  192.1 7.8 %collective-permute-done.25.refs_6_ = bf16[768,768]{1,0:T(8,128)(2,1)S(1)} collective-permute-done((bf16[768,768]{1,0:T(8,128)(2,1)S(1)}, bf16[768,768]{1,0:T(8,128)(2,1)S(1)}, u32[]{:S(2)}, u32[]{:S(2)}) %collective-permute-start.25) | collective-permute-done | bytes 1179680 | tf_op jit(solution)/shard_map/ppermute | solution.py:735
  202.2 2.4 collective-permute-start.26
  206.3 10.2 %norm_one_back.1 = (f32[1024,768]{1,0:T(8,128)S(1)}, bf16[3,1024,128]{2,1,0:T(8,128)(2,1)S(1)}, bf16[3,1024,128]{2,1,0:T(8,128)(2,1)S(1)}, bf16[208,768]{1,0:T(8,128)(2,1)S(1)}, bf16[208,768]{1,0:T(8,128)(2,1)S(1)}) custom-call(s32[9]{0:T(128)S(1)} %concatenate.6.refs_0_, f32[1024,768]{1,0:T(8,128)S(1)} %get-tuple-element.218.refs_1_, ...), custom_call_target="tpu_custom_call" | custom-call | flops 6000000000 | tf_op jit(solution)/shard_map/norm_one_back/pallas_call | solution.py:712
  221.9 12.4 %self_back_other.1 = (bf16[1024,576]{1,0:T(8,128)(2,1)S(1)}, bf16[576,768]{1,0:T(8,128)(2,1)S(1)}) custom-call(s32[9]{0:T(128)S(1)} %concatenate.6.refs_0_, bf16[2048,768]{1,0:T(8,128)(2,1)} %refs_1_.11, bf16[3,1024,128]{2,1,0:T(8,128)(2,1)S(1)} %copy-done.12, bf16[3,1024,128]{2,1,0:T(8,128)(2,1)S(1)} %copy-done.13, bf16[3,1024,128]{2,1,0:T(8,128)(2,1)S(1)} %copy-done.14, ...), custom_call_target="tpu_custom_call" | custom-call | flops 14000000000 | tf_op jit(solution)/shard_map/self_back_other/pallas_call | solution.py:712
  242.8 12.4 %self_back_own.1 = (bf16[1024,576]{1,0:T(8,128)(2,1)S(1)}, bf16[576,768]{1,0:T(8,128)(2,1)S(1)}) custom-call(s32[9]{0:T(128)S(1)} %concatenate.6.refs_0_, bf16[2048,768]{1,0:T(8,128)(2,1)} %refs_1_.11, bf16[3,1024,128]{2,1,0:T(8,128)(2,1)S(1)} %copy-done.9, bf16[3,1024,128]{2,1,0:T(8,128)(2,1)S(1)} %copy-done.10, bf16[3,1024,128]{2,1,0:T(8,128)(2,1)S(1)} %copy-done.11, ...), custom_call_target="tpu_custom_call" | custom-call | flops 14000000000 | tf_op jit(solution)/shard_map/self_back_own/pallas_call | solution.py:712
  257.6 3.8 %tokens_grad.1 = (bf16[512,768]{1,0:T(8,128)(2,1)S(1)}, f32[512,768]{1,0:T(8,128)S(1)}) custom-call(s32[9]{0:T(128)S(1)} %concatenate.6.refs_0_, f32[1024,768]{1,0:T(8,128)S(1)} %get-tuple-element.265.refs_1_, bf16[1024,576]{1,0:T(8,128)(2,1)S(1)} %get-tuple-element.266.refs_2_, bf16[1024,576]{1,0:T(8,128)(2,1)S(1)} %get-tuple-element.248.refs_9_.refs_3_, ...), custom_call_target="tpu_custom_call" | custom-call | flops 6000000000 | tf_op jit(solution)/shard_map/tokens_grad/pallas_call | solution.py:712
  262.2 2.7 collective-permute-start.41
  265.0 7.2 %collective-permute-done.19.refs_2_ = bf16[512,768]{1,0:T(8,128)(2,1)S(1)} collective-permute-done((bf16[512,768]{1,0:T(8,128)(2,1)S(1)}, bf16[512,768]{1,0:T(8,128)(2,1)S(1)}, u32[]{:S(2)}, u32[]{:S(2)}) %collective-permute-start.19) | collective-permute-done | bytes 786464 | tf_op jit(solution)/shard_map/ppermute | solution.py:735
  275.2 8.7 %collective-permute-done.42.refs_8_ = bf16[96,768]{1,0:T(8,128)(2,1)S(1)} collective-permute-done((bf16[96,768]{1,0:T(8,128)(2,1)S(1)}, bf16[96,768]{1,0:T(8,128)(2,1)S(1)}, u32[]{:S(2)}, u32[]{:S(2)}) %collective-permute-start.42) | collective-permute-done | bytes 147488 | tf_op jit(solution)/shard_map/ppermute | solution.py:741
  285.5 2.2 collective-permute-done.39.refs_2_
  287.8 2.6 step_6.1
  294.1 9.8 %collective-permute-done.56.refs_3_ = bf16[512,768]{1,0:T(8,128)(2,1)S(1)} collective-permute-done((bf16[512,768]{1,0:T(8,128)(2,1)S(1)}, bf16[512,768]{1,0:T(8,128)(2,1)S(1)}, u32[]{:S(2)}, u32[]{:S(2)}) %collective-permute-start.56) | collective-permute-done | bytes 786464 | tf_op jit(solution)/shard_map/ppermute | solution.py:735
  305.6 2.7 place_layer_out.1.refs_9_
  308.3 6.6 %collective-permute-done.50.refs_6_ = bf16[192,768]{1,0:T(8,128)(2,1)S(1)} collective-permute-done((bf16[192,768]{1,0:T(8,128)(2,1)S(1)}, bf16[192,768]{1,0:T(8,128)(2,1)S(1)}, u32[]{:S(2)}, u32[]{:S(2)}) %collective-permute-start.50) | collective-permute-done | bytes 294944 | tf_op jit(solution)/shard_map/ppermute | solution.py:741
  316.8 2.4 step_7.1
  319.4 3.6 collective-permute-done.46.refs_3_
  323.0 2.7 place_memory_grad.1.refs_7_
  327.9 2.6 collective-permute-done.52.refs_2_
  330.5 3.6 collective-permute-done.53.refs_4_
  339.9 4.2 %collective-permute-done.59.refs_4_ = bf16[64,768]{1,0:T(8,128)(2,1)S(1)} collective-permute-done((bf16[64,768]{1,0:T(8,128)(2,1)S(1)}, bf16[64,768]{1,0:T(8,128)(2,1)S(1)}, u32[]{:S(2)}, u32[]{:S(2)}) %collective-permute-start.59) | collective-permute-done | bytes 98336 | tf_op jit(solution)/shard_map/ppermute | solution.py:741
  346.7 2.7 place_tokens_grad.1.refs_5_
  349.4 2.8 collective-permute-done.61.refs_4_
  360.0 8.1 %collective-permute-done.62.refs_2_ = bf16[320,768]{1,0:T(8,128)(2,1)S(1)} collective-permute-done((bf16[320,768]{1,0:T(8,128)(2,1)S(1)}, bf16[320,768]{1,0:T(8,128)(2,1)S(1)}, u32[]{:S(2)}, u32[]{:S(2)}) %collective-permute-start.62) | collective-permute-done | bytes 491552 | tf_op jit(solution)/shard_map/ppermute | solution.py:741
  (210 shorter events, 89.4 us)
Async XLA Ops:
  2.0 14.0 %collective-permute-start = (bf16[288,768]{1,0:T(8,128)(2,1)S(1)}, bf16[288,768]{1,0:T(8,128)(2,1)S(1)}, u32[]{:S(2)}, u32[]{:S(2)}) collective-permute-start(bf16[288,768]{1,0:T(8,128)(2,1)S(1)} %fusion.1), channel_id=1, source_target_pairs={{0,16},{16,0},{8,24},{24,8},{1,17},{17,1},{9,25},{25,9},{2,18},{18... | collective-permute-start | bytes 1327112 | tf_op jit(solution)/shard_map/ppermute | solution.py:735
  11.5 10.0 %collective-permute-start.2 = (bf16[192,768]{1,0:T(8,128)(2,1)S(1)}, bf16[192,768]{1,0:T(8,128)(2,1)S(1)}, u32[]{:S(2)}, u32[]{:S(2)}) collective-permute-start(bf16[192,768]{1,0:T(8,128)(2,1)S(1)} %get-tuple-element.163), channel_id=1, source_target_pairs={{0,16},{16,0},{8,24},{24,8},{1,17},{17,1},{9,25},{25,9},{2,18},{18... | collective-permute-start | bytes 884744 | tf_op jit(solution)/shard_map/ppermute | solution.py:735
  16.0 15.6 %collective-permute-start.1 = (bf16[288,768]{1,0:T(8,128)(2,1)S(1)}, bf16[288,768]{1,0:T(8,128)(2,1)S(1)}, u32[]{:S(2)}, u32[]{:S(2)}) collective-permute-start(bf16[288,768]{1,0:T(8,128)(2,1)S(1)} %collective-permute-done.refs_3_.refs_2_), channel_id=1, source_target_pairs={{0,1},{1,0},{2,3},{3,2},{4,5},{5,4},{6,7},{7,6},{8,9},{9,8},{10,11... | collective-permute-start | bytes 1327112 | tf_op jit(solution)/shard_map/ppermute | solution.py:741
  21.5 21.1 %collective-permute-start.3 = (bf16[192,768]{1,0:T(8,128)(2,1)S(1)}, bf16[192,768]{1,0:T(8,128)(2,1)S(1)}, u32[]{:S(2)}, u32[]{:S(2)}) collective-permute-start(bf16[192,768]{1,0:T(8,128)(2,1)S(1)} %collective-permute-done.2.refs_4_), channel_id=1, source_target_pairs={{0,1},{1,0},{2,3},{3,2},{4,5},{5,4},{6,7},{7,6},{8,9},{9,8},{10,11... | collective-permute-start | bytes 884744 | tf_op jit(solution)/shard_map/ppermute | solution.py:741
  23.4 37.9 %collective-permute-start.6 = (bf16[576,768]{1,0:T(8,128)(2,1)S(1)}, bf16[576,768]{1,0:T(8,128)(2,1)S(1)}, u32[]{:S(2)}, u32[]{:S(2)}) collective-permute-start(bf16[576,768]{1,0:T(8,128)(2,1)S(1)} %get-tuple-element.171.refs_3_), channel_id=1, source_target_pairs={{0,16},{16,0},{8,24},{24,8},{1,17},{17,1},{9,25},{25,9},{2,18},{18... | collective-permute-start | bytes 2654216 | tf_op jit(solution)/shard_map/ppermute | solution.py:735
  45.1 16.2 %collective-permute-start.7 = (bf16[384,768]{1,0:T(8,128)(2,1)S(1)}, bf16[384,768]{1,0:T(8,128)(2,1)S(1)}, u32[]{:S(2)}, u32[]{:S(2)}) collective-permute-start(bf16[384,768]{1,0:T(8,128)(2,1)S(1)} %get-tuple-element.174), channel_id=1, source_target_pairs={{0,16},{16,0},{8,24},{24,8},{1,17},{17,1},{9,25},{25,9},{2,18},{18... | collective-permute-start | bytes 1769480 | tf_op jit(solution)/shard_map/ppermute | solution.py:735
  45.6 41.1 %collective-permute-start.10 = (bf16[768,768]{1,0:T(8,128)(2,1)S(1)}, bf16[768,768]{1,0:T(8,128)(2,1)S(1)}, u32[]{:S(2)}, u32[]{:S(2)}) collective-permute-start(bf16[768,768]{1,0:T(8,128)(2,1)S(1)} %copy-done.1), channel_id=1, source_target_pairs={{0,16},{16,0},{8,24},{24,8},{1,17},{17,1},{9,25},{25,9},{2,18},{18... | collective-permute-start | bytes 3538952 | tf_op jit(solution)/shard_map/ppermute | solution.py:735
  76.9 15.2 %collective-permute-start.11 = (bf16[384,768]{1,0:T(8,128)(2,1)S(1)}, bf16[384,768]{1,0:T(8,128)(2,1)S(1)}, u32[]{:S(2)}, u32[]{:S(2)}) collective-permute-start(bf16[384,768]{1,0:T(8,128)(2,1)S(1)} %collective-permute-done.7.refs_7_.refs_4_), channel_id=1, source_target_pairs={{0,2},{1,3},{2,0},{3,1},{4,6},{5,7},{6,4},{7,5},{8,10},{9,11},{10,... | collective-permute-start | bytes 1769480 | tf_op jit(solution)/shard_map/ppermute | solution.py:741
  115.0 12.9 %collective-permute-start.14 = (bf16[512,768]{1,0:T(8,128)(2,1)S(1)}, bf16[512,768]{1,0:T(8,128)(2,1)S(1)}, u32[]{:S(2)}, u32[]{:S(2)}) collective-permute-start(bf16[512,768]{1,0:T(8,128)(2,1)S(1)} %get-tuple-element.188.refs_2_), channel_id=1, source_target_pairs={{0,8},{8,0},{16,24},{24,16},{1,9},{9,1},{17,25},{25,17},{2,10},{10... | collective-permute-start | bytes 2359304 | tf_op jit(solution)/shard_map/ppermute | solution.py:738
  115.2 12.7 %collective-permute-start.15 = (bf16[512,768]{1,0:T(8,128)(2,1)S(1)}, bf16[512,768]{1,0:T(8,128)(2,1)S(1)}, u32[]{:S(2)}, u32[]{:S(2)}) collective-permute-start(bf16[512,768]{1,0:T(8,128)(2,1)S(1)} %get-tuple-element.189.refs_3_), channel_id=1, source_target_pairs={{0,8},{8,0},{16,24},{24,16},{1,9},{9,1},{17,25},{25,17},{2,10},{10... | collective-permute-start | bytes 2359304 | tf_op jit(solution)/shard_map/ppermute | solution.py:738
  121.3 28.9 %collective-permute-start.16 = (bf16[768,768]{1,0:T(8,128)(2,1)S(1)}, bf16[768,768]{1,0:T(8,128)(2,1)S(1)}, u32[]{:S(2)}, u32[]{:S(2)}) collective-permute-start(bf16[768,768]{1,0:T(8,128)(2,1)S(1)} %get-tuple-element.204), channel_id=1, source_target_pairs={{0,16},{16,0},{8,24},{24,8},{1,17},{17,1},{9,25},{25,9},{2,18},{18... | collective-permute-start | bytes 3538952 | tf_op jit(solution)/shard_map/ppermute | solution.py:735
  121.4 54.1 %collective-permute-start.18 = (bf16[768,768]{1,0:T(8,128)(2,1)S(1)}, bf16[768,768]{1,0:T(8,128)(2,1)S(1)}, u32[]{:S(2)}, u32[]{:S(2)}) collective-permute-start(bf16[768,768]{1,0:T(8,128)(2,1)S(1)} %get-tuple-element.212), channel_id=1, source_target_pairs={{0,16},{16,0},{8,24},{24,8},{1,17},{17,1},{9,25},{25,9},{2,18},{18... | collective-permute-start | bytes 3538952 | tf_op jit(solution)/shard_map/ppermute | solution.py:735
  151.4 24.0 %collective-permute-start.17 = (bf16[384,768]{1,0:T(8,128)(2,1)S(1)}, bf16[384,768]{1,0:T(8,128)(2,1)S(1)}, u32[]{:S(2)}, u32[]{:S(2)}) collective-permute-start(bf16[384,768]{1,0:T(8,128)(2,1)S(1)} %get-tuple-element.210), channel_id=1, source_target_pairs={{0,1},{1,0},{2,3},{3,2},{4,5},{5,4},{6,7},{7,6},{8,9},{9,8},{10,11... | collective-permute-start | bytes 1769480 | tf_op jit(solution)/shard_map/ppermute | solution.py:741
  168.1 31.8 %collective-permute-start.25 = (bf16[768,768]{1,0:T(8,128)(2,1)S(1)}, bf16[768,768]{1,0:T(8,128)(2,1)S(1)}, u32[]{:S(2)}, u32[]{:S(2)}) collective-permute-start(bf16[768,768]{1,0:T(8,128)(2,1)S(1)} %cross_grad_other.1.refs_5_), channel_id=1, source_target_pairs={{0,16},{16,0},{8,24},{24,8},{1,17},{17,1},{9,25},{25,9},{2,18},{18... | collective-permute-start | bytes 3538952 | tf_op jit(solution)/shard_map/ppermute | solution.py:735
  168.2 36.4 %collective-permute-start.21 = (bf16[512,768]{1,0:T(8,128)(2,1)S(1)}, bf16[512,768]{1,0:T(8,128)(2,1)S(1)}, u32[]{:S(2)}, u32[]{:S(2)}) collective-permute-start(bf16[512,768]{1,0:T(8,128)(2,1)S(1)} %get-tuple-element.219.refs_2_), channel_id=1, source_target_pairs={{0,8},{8,0},{16,24},{24,16},{1,9},{9,1},{17,25},{25,17},{2,10},{10... | collective-permute-start | bytes 2359304 | tf_op jit(solution)/shard_map/ppermute | solution.py:738
  168.3 38.0 %collective-permute-start.22 = (bf16[512,768]{1,0:T(8,128)(2,1)S(1)}, bf16[512,768]{1,0:T(8,128)(2,1)S(1)}, u32[]{:S(2)}, u32[]{:S(2)}) collective-permute-start(bf16[512,768]{1,0:T(8,128)(2,1)S(1)} %get-tuple-element.220.refs_3_), channel_id=1, source_target_pairs={{0,8},{8,0},{16,24},{24,16},{1,9},{9,1},{17,25},{25,17},{2,10},{10... | collective-permute-start | bytes 2359304 | tf_op jit(solution)/shard_map/ppermute | solution.py:738
  177.0 10.0 %collective-permute-start.23 = (bf16[192,768]{1,0:T(8,128)(2,1)S(1)}, bf16[192,768]{1,0:T(8,128)(2,1)S(1)}, u32[]{:S(2)}, u32[]{:S(2)}) collective-permute-start(bf16[192,768]{1,0:T(8,128)(2,1)S(1)} %get-tuple-element.226), channel_id=1, source_target_pairs={{0,2},{1,3},{2,0},{3,1},{4,6},{5,7},{6,4},{7,5},{8,10},{9,11},{10,... | collective-permute-start | bytes 884744 | tf_op jit(solution)/shard_map/ppermute | solution.py:741
  178.6 13.4 %collective-permute-start.24 = (bf16[384,768]{1,0:T(8,128)(2,1)S(1)}, bf16[384,768]{1,0:T(8,128)(2,1)S(1)}, u32[]{:S(2)}, u32[]{:S(2)}) collective-permute-start(bf16[384,768]{1,0:T(8,128)(2,1)S(1)} %get-tuple-element.228), channel_id=1, source_target_pairs={{0,1},{1,0},{2,3},{3,2},{4,5},{5,4},{6,7},{7,6},{8,9},{9,8},{10,11... | collective-permute-start | bytes 1769480 | tf_op jit(solution)/shard_map/ppermute | solution.py:741
  201.6 15.2 %collective-permute-start.28 = (bf16[384,768]{1,0:T(8,128)(2,1)S(1)}, bf16[384,768]{1,0:T(8,128)(2,1)S(1)}, u32[]{:S(2)}, u32[]{:S(2)}) collective-permute-start(bf16[384,768]{1,0:T(8,128)(2,1)S(1)} %get-tuple-element.236), channel_id=1, source_target_pairs={{0,1},{1,0},{2,3},{3,2},{4,5},{5,4},{6,7},{7,6},{8,9},{9,8},{10,11... | collective-permute-start | bytes 1769480 | tf_op jit(solution)/shard_map/ppermute | solution.py:741
  202.2 39.1 %collective-permute-start.38 = (bf16[512,768]{1,0:T(8,128)(2,1)S(1)}, bf16[512,768]{1,0:T(8,128)(2,1)S(1)}, u32[]{:S(2)}, u32[]{:S(2)}) collective-permute-start(bf16[512,768]{1,0:T(8,128)(2,1)S(1)} %get-tuple-element.229.refs_7_), channel_id=1, source_target_pairs={{0,8},{8,0},{16,24},{24,16},{1,9},{9,1},{17,25},{25,17},{2,10},{10... | collective-permute-start | bytes 2359304 | tf_op jit(solution)/shard_map/ppermute | solution.py:738
  202.2 14.7 %collective-permute-start.26 = (bf16[96,768]{1,0:T(8,128)(2,1)S(1)}, bf16[96,768]{1,0:T(8,128)(2,1)S(1)}, u32[]{:S(2)}, u32[]{:S(2)}) collective-permute-start(bf16[96,768]{1,0:T(8,128)(2,1)S(1)} %get-tuple-element.232), channel_id=1, source_target_pairs={{0,4},{1,5},{2,6},{3,7},{4,0},{5,1},{6,2},{7,3},{8,12},{9,13},{10,... | collective-permute-start | bytes 442376 | tf_op jit(solution)/shard_map/ppermute | solution.py:741
  204.6 12.3 %collective-permute-start.27 = (bf16[192,768]{1,0:T(8,128)(2,1)S(1)}, bf16[192,768]{1,0:T(8,128)(2,1)S(1)}, u32[]{:S(2)}, u32[]{:S(2)}) collective-permute-start(bf16[192,768]{1,0:T(8,128)(2,1)S(1)} %get-tuple-element.234), channel_id=1, source_target_pairs={{0,2},{1,3},{2,0},{3,1},{4,6},{5,7},{6,4},{7,5},{8,10},{9,11},{10,... | collective-permute-start | bytes 884744 | tf_op jit(solution)/shard_map/ppermute | solution.py:741
  216.5 17.9 %collective-permute-start.32 = (bf16[208,768]{1,0:T(8,128)(2,1)S(1)}, bf16[208,768]{1,0:T(8,128)(2,1)S(1)}, u32[]{:S(2)}, u32[]{:S(2)}) collective-permute-start(bf16[208,768]{1,0:T(8,128)(2,1)S(1)} %get-tuple-element.244), channel_id=1, source_target_pairs={{0,16},{16,0},{8,24},{24,8},{1,17},{17,1},{9,25},{25,9},{2,18},{18... | collective-permute-start | bytes 958472 | tf_op jit(solution)/shard_map/ppermute | solution.py:735
  218.0 17.5 %collective-permute-start.30 = (bf16[96,768]{1,0:T(8,128)(2,1)S(1)}, bf16[96,768]{1,0:T(8,128)(2,1)S(1)}, u32[]{:S(2)}, u32[]{:S(2)}) collective-permute-start(bf16[96,768]{1,0:T(8,128)(2,1)S(1)} %get-tuple-element.240), channel_id=1, source_target_pairs={{0,4},{1,5},{2,6},{3,7},{4,0},{5,1},{6,2},{7,3},{8,12},{9,13},{10,... | collective-permute-start | bytes 442376 | tf_op jit(solution)/shard_map/ppermute | solution.py:741
  220.0 15.5 %collective-permute-start.29 = (bf16[96,768]{1,0:T(8,128)(2,1)S(1)}, bf16[96,768]{1,0:T(8,128)(2,1)S(1)}, u32[]{:S(2)}, u32[]{:S(2)}) collective-permute-start(bf16[96,768]{1,0:T(8,128)(2,1)S(1)} %get-tuple-element.238.refs_6_.refs_1_), channel_id=1, source_target_pairs={{0,4},{1,5},{2,6},{3,7},{4,0},{5,1},{6,2},{7,3},{8,12},{9,13},{10,... | collective-permute-start | bytes 442376 | tf_op jit(solution)/shard_map/ppermute | solution.py:741
  221.0 14.6 %collective-permute-start.31 = (bf16[192,768]{1,0:T(8,128)(2,1)S(1)}, bf16[192,768]{1,0:T(8,128)(2,1)S(1)}, u32[]{:S(2)}, u32[]{:S(2)}) collective-permute-start(bf16[192,768]{1,0:T(8,128)(2,1)S(1)} %get-tuple-element.242), channel_id=1, source_target_pairs={{0,2},{1,3},{2,0},{3,1},{4,6},{5,7},{6,4},{7,5},{8,10},{9,11},{10,... | collective-permute-start | bytes 884744 | tf_op jit(solution)/shard_map/ppermute | solution.py:741
  234.4 21.5 %collective-permute-start.33 = (bf16[576,768]{1,0:T(8,128)(2,1)S(1)}, bf16[576,768]{1,0:T(8,128)(2,1)S(1)}, u32[]{:S(2)}, u32[]{:S(2)}) collective-permute-start(bf16[576,768]{1,0:T(8,128)(2,1)S(1)} %get-tuple-element.251), channel_id=1, source_target_pairs={{0,16},{16,0},{8,24},{24,8},{1,17},{17,1},{9,25},{25,9},{2,18},{18... | collective-permute-start | bytes 2654216 | tf_op jit(solution)/shard_map/ppermute | solution.py:735
  236.5 18.7 %collective-permute-start.36 = (bf16[96,768]{1,0:T(8,128)(2,1)S(1)}, bf16[96,768]{1,0:T(8,128)(2,1)S(1)}, u32[]{:S(2)}, u32[]{:S(2)}) collective-permute-start(bf16[96,768]{1,0:T(8,128)(2,1)S(1)} %get-tuple-element.254), channel_id=1, source_target_pairs={{0,4},{1,5},{2,6},{3,7},{4,0},{5,1},{6,2},{7,3},{8,12},{9,13},{10,... | collective-permute-start | bytes 442376 | tf_op jit(solution)/shard_map/ppermute | solution.py:741
  238.6 17.2 %collective-permute-start.35 = (bf16[96,768]{1,0:T(8,128)(2,1)S(1)}, bf16[96,768]{1,0:T(8,128)(2,1)S(1)}, u32[]{:S(2)}, u32[]{:S(2)}) collective-permute-start(bf16[96,768]{1,0:T(8,128)(2,1)S(1)} %get-tuple-element.252.refs_5_), channel_id=1, source_target_pairs={{0,4},{1,5},{2,6},{3,7},{4,0},{5,1},{6,2},{7,3},{8,12},{9,13},{10,... | collective-permute-start | bytes 442376 | tf_op jit(solution)/shard_map/ppermute | solution.py:741
  239.5 16.3 %collective-permute-start.37 = (bf16[128,768]{1,0:T(8,128)(2,1)S(1)}, bf16[128,768]{1,0:T(8,128)(2,1)S(1)}, u32[]{:S(2)}, u32[]{:S(2)}) collective-permute-start(bf16[128,768]{1,0:T(8,128)(2,1)S(1)} %get-tuple-element.256), channel_id=1, source_target_pairs={{0,1},{1,0},{2,3},{3,2},{4,5},{5,4},{6,7},{7,6},{8,9},{9,8},{10,11... | collective-permute-start | bytes 589832 | tf_op jit(solution)/shard_map/ppermute | solution.py:741
  241.2 14.6 %collective-permute-start.34 = (bf16[192,768]{1,0:T(8,128)(2,1)S(1)}, bf16[192,768]{1,0:T(8,128)(2,1)S(1)}, u32[]{:S(2)}, u32[]{:S(2)}) collective-permute-start(bf16[192,768]{1,0:T(8,128)(2,1)S(1)} %get-tuple-element.249.refs_6_.refs_3_), channel_id=1, source_target_pairs={{0,2},{1,3},{2,0},{3,1},{4,6},{5,7},{6,4},{7,5},{8,10},{9,11},{10,... | collective-permute-start | bytes 884744 | tf_op jit(solution)/shard_map/ppermute | solution.py:741
  255.2 16.9 %collective-permute-start.19 = (bf16[512,768]{1,0:T(8,128)(2,1)S(1)}, bf16[512,768]{1,0:T(8,128)(2,1)S(1)}, u32[]{:S(2)}, u32[]{:S(2)}) collective-permute-start(bf16[512,768]{1,0:T(8,128)(2,1)S(1)} %get-tuple-element.214), channel_id=1, source_target_pairs={{0,16},{16,0},{8,24},{24,8},{1,17},{17,1},{9,25},{25,9},{2,18},{18... | collective-permute-start | bytes 2359304 | tf_op jit(solution)/shard_map/ppermute | solution.py:735
  261.4 26.4 %collective-permute-start.44 = (bf16[512,768]{1,0:T(8,128)(2,1)S(1)}, bf16[512,768]{1,0:T(8,128)(2,1)S(1)}, u32[]{:S(2)}, u32[]{:S(2)}) collective-permute-start(bf16[512,768]{1,0:T(8,128)(2,1)S(1)} %get-tuple-element.270.refs_13_), channel_id=1, source_target_pairs={{0,8},{8,0},{16,24},{24,16},{1,9},{9,1},{17,25},{25,17},{2,10},{10... | collective-permute-start | bytes 2359304 | tf_op jit(solution)/shard_map/ppermute | solution.py:738
  261.5 26.3 %collective-permute-start.40 = (bf16[384,768]{1,0:T(8,128)(2,1)S(1)}, bf16[384,768]{1,0:T(8,128)(2,1)S(1)}, u32[]{:S(2)}, u32[]{:S(2)}) collective-permute-start(bf16[384,768]{1,0:T(8,128)(2,1)S(1)} %get-tuple-element.260.refs_3_), channel_id=1, source_target_pairs={{0,1},{1,0},{2,3},{3,2},{4,5},{5,4},{6,7},{7,6},{8,9},{9,8},{10,11... | collective-permute-start | bytes 1769480 | tf_op jit(solution)/shard_map/ppermute | solution.py:741
  262.2 21.7 %collective-permute-start.41 = (bf16[192,768]{1,0:T(8,128)(2,1)S(1)}, bf16[192,768]{1,0:T(8,128)(2,1)S(1)}, u32[]{:S(2)}, u32[]{:S(2)}) collective-permute-start(bf16[192,768]{1,0:T(8,128)(2,1)S(1)} %get-tuple-element.261.refs_5_), channel_id=1, source_target_pairs={{0,2},{1,3},{2,0},{3,1},{4,6},{5,7},{6,4},{7,5},{8,10},{9,11},{10,... | collective-permute-start | bytes 884744 | tf_op jit(solution)/shard_map/ppermute | solution.py:741
  272.2 15.6 %collective-permute-start.39 = (bf16[320,768]{1,0:T(8,128)(2,1)S(1)}, bf16[320,768]{1,0:T(8,128)(2,1)S(1)}, u32[]{:S(2)}, u32[]{:S(2)}) collective-permute-start(bf16[320,768]{1,0:T(8,128)(2,1)S(1)} %get-tuple-element.259), channel_id=1, source_target_pairs={{0,1},{1,0},{2,3},{3,2},{4,5},{5,4},{6,7},{7,6},{8,9},{9,8},{10,11... | collective-permute-start | bytes 1474568 | tf_op jit(solution)/shard_map/ppermute | solution.py:741
  283.9 10.2 %collective-permute-start.20 = (bf16[512,768]{1,0:T(8,128)(2,1)S(1)}, bf16[512,768]{1,0:T(8,128)(2,1)S(1)}, u32[]{:S(2)}, u32[]{:S(2)}) collective-permute-start(bf16[512,768]{1,0:T(8,128)(2,1)S(1)} %collective-permute-done.19.refs_2_), channel_id=1, source_target_pairs={{0,8},{8,0},{16,24},{24,16},{1,9},{9,1},{17,25},{25,17},{2,10},{10... | collective-permute-start | bytes 2359304 | tf_op jit(solution)/shard_map/ppermute | solution.py:738
  283.9 20.0 %collective-permute-start.56 = (bf16[512,768]{1,0:T(8,128)(2,1)S(1)}, bf16[512,768]{1,0:T(8,128)(2,1)S(1)}, u32[]{:S(2)}, u32[]{:S(2)}) collective-permute-start(bf16[512,768]{1,0:T(8,128)(2,1)S(1)} %get-tuple-element.282.refs_1_), channel_id=1, source_target_pairs={{0,16},{16,0},{8,24},{24,8},{1,17},{17,1},{9,25},{25,9},{2,18},{18... | collective-permute-start | bytes 2359304 | tf_op jit(solution)/shard_map/ppermute | solution.py:735
  290.4 15.1 %collective-permute-start.48 = (bf16[160,768]{1,0:T(8,128)(2,1)S(1)}, bf16[160,768]{1,0:T(8,128)(2,1)S(1)}, u32[]{:S(2)}, u32[]{:S(2)}) collective-permute-start(bf16[160,768]{1,0:T(8,128)(2,1)S(1)} %get-tuple-element.273), channel_id=1, source_target_pairs={{0,2},{1,3},{2,0},{3,1},{4,6},{5,7},{6,4},{7,5},{8,10},{9,11},{10,... | collective-permute-start | bytes 737288 | tf_op jit(solution)/shard_map/ppermute | solution.py:741
  292.0 22.9 %collective-permute-start.49 = (bf16[384,768]{1,0:T(8,128)(2,1)S(1)}, bf16[384,768]{1,0:T(8,128)(2,1)S(1)}, u32[]{:S(2)}, u32[]{:S(2)}) collective-permute-start(bf16[384,768]{1,0:T(8,128)(2,1)S(1)} %get-tuple-element.274.refs_3_), channel_id=1, source_target_pairs={{0,1},{1,0},{2,3},{3,2},{4,5},{5,4},{6,7},{7,6},{8,9},{9,8},{10,11... | collective-permute-start | bytes 1769480 | tf_op jit(solution)/shard_map/ppermute | solution.py:741
  293.8 11.7 %collective-permute-start.51 = (bf16[32,768]{1,0:T(8,128)(2,1)S(1)}, bf16[32,768]{1,0:T(8,128)(2,1)S(1)}, u32[]{:S(2)}, u32[]{:S(2)}) collective-permute-start(bf16[32,768]{1,0:T(8,128)(2,1)S(1)} %get-tuple-element.277), channel_id=1, source_target_pairs={{0,4},{1,5},{2,6},{3,7},{4,0},{5,1},{6,2},{7,3},{8,12},{9,13},{10,... | collective-permute-start | bytes 147464 | tf_op jit(solution)/shard_map/ppermute | solution.py:741
  294.1 25.3 %collective-permute-start.55 = (bf16[512,768]{1,0:T(8,128)(2,1)S(1)}, bf16[512,768]{1,0:T(8,128)(2,1)S(1)}, u32[]{:S(2)}, u32[]{:S(2)}) collective-permute-start(bf16[512,768]{1,0:T(8,128)(2,1)S(1)} %get-tuple-element.282.refs_1_), channel_id=1, source_target_pairs={{0,8},{8,0},{16,24},{24,16},{1,9},{9,1},{17,25},{25,17},{2,10},{10... | collective-permute-start | bytes 2359304 | tf_op jit(solution)/shard_map/ppermute | solution.py:738
  303.9 19.2 %collective-permute-start.46 = (bf16[512,768]{1,0:T(8,128)(2,1)S(1)}, bf16[512,768]{1,0:T(8,128)(2,1)S(1)}, u32[]{:S(2)}, u32[]{:S(2)}) collective-permute-start(bf16[512,768]{1,0:T(8,128)(2,1)S(1)} %get-tuple-element.272.refs_1_), channel_id=1, source_target_pairs={{0,16},{16,0},{8,24},{24,8},{1,17},{17,1},{9,25},{25,9},{2,18},{18... | collective-permute-start | bytes 2359304 | tf_op jit(solution)/shard_map/ppermute | solution.py:735
  305.5 17.5 %collective-permute-start.57 = (bf16[512,768]{1,0:T(8,128)(2,1)S(1)}, bf16[512,768]{1,0:T(8,128)(2,1)S(1)}, u32[]{:S(2)}, u32[]{:S(2)}) collective-permute-start(bf16[512,768]{1,0:T(8,128)(2,1)S(1)} %collective-permute-done.56.refs_3_), channel_id=1, source_target_pairs={{0,8},{8,0},{16,24},{24,16},{1,9},{9,1},{17,25},{25,17},{2,10},{10... | collective-permute-start | bytes 2359304 | tf_op jit(solution)/shard_map/ppermute | solution.py:738
  319.2 14.9 %collective-permute-start.53 = (bf16[384,768]{1,0:T(8,128)(2,1)S(1)}, bf16[384,768]{1,0:T(8,128)(2,1)S(1)}, u32[]{:S(2)}, u32[]{:S(2)}) collective-permute-start(bf16[384,768]{1,0:T(8,128)(2,1)S(1)} %get-tuple-element.280.refs_3_), channel_id=1, source_target_pairs={{0,1},{1,0},{2,3},{3,2},{4,5},{5,4},{6,7},{7,6},{8,9},{9,8},{10,11... | collective-permute-start | bytes 1769480 | tf_op jit(solution)/shard_map/ppermute | solution.py:741
  319.4 27.3 %collective-permute-start.45 = (bf16[512,768]{1,0:T(8,128)(2,1)S(1)}, bf16[512,768]{1,0:T(8,128)(2,1)S(1)}, u32[]{:S(2)}, u32[]{:S(2)}) collective-permute-start(bf16[512,768]{1,0:T(8,128)(2,1)S(1)} %get-tuple-element.272.refs_1_), channel_id=1, source_target_pairs={{0,8},{8,0},{16,24},{24,16},{1,9},{9,1},{17,25},{25,17},{2,10},{10... | collective-permute-start | bytes 2359304 | tf_op jit(solution)/shard_map/ppermute | solution.py:738
  323.0 23.7 %collective-permute-start.47 = (bf16[512,768]{1,0:T(8,128)(2,1)S(1)}, bf16[512,768]{1,0:T(8,128)(2,1)S(1)}, u32[]{:S(2)}, u32[]{:S(2)}) collective-permute-start(bf16[512,768]{1,0:T(8,128)(2,1)S(1)} %collective-permute-done.46.refs_3_), channel_id=1, source_target_pairs={{0,8},{8,0},{16,24},{24,16},{1,9},{9,1},{17,25},{25,17},{2,10},{10... | collective-permute-start | bytes 2359304 | tf_op jit(solution)/shard_map/ppermute | solution.py:738
  356.9 11.2 %collective-permute-start.62 = (bf16[320,768]{1,0:T(8,128)(2,1)S(1)}, bf16[320,768]{1,0:T(8,128)(2,1)S(1)}, u32[]{:S(2)}, u32[]{:S(2)}) collective-permute-start(bf16[320,768]{1,0:T(8,128)(2,1)S(1)} %get-tuple-element.287.refs_1_.refs_3_), channel_id=1, source_target_pairs={{0,1},{1,0},{2,3},{3,2},{4,5},{5,4},{6,7},{7,6},{8,9},{9,8},{10,11... | collective-permute-start | bytes 1474568 | tf_op jit(solution)/shard_map/ppermute | solution.py:741
  (62 other events, 354.5 us)

commit v4 on v3

--- a/solution.py
+++ b/solution.py
@@ -19,7 +19,11 @@
 CORE = [(0, 1), (1, 0), (2, 3), (3, 2)]
 ACROSS = [(0, 2), (2, 0), (1, 3), (3, 1)]
 MIB = 1 << 20
-LIMIT = 18
+LIMIT = 16
+
+ROWS, WHOLE, COLUMNS, HALF, PART, SKIP, ARBITRARY = "rows", "whole", "columns", "half", "part", "skip", "arbitrary"
+HELD_ROWS, HELD_WHOLE, FAR_ROWS, FAR_WHOLE = "held rows", "held whole", "hbm rows", "hbm whole"
+SUM, PACK, WIDEN, STACK, LAST = "sum", "pack", "wide", "stack", "last"
 
 
 def nn(left, right):
@@ -176,8 +180,8 @@
 
 
 def project_own_kernel(
-    s_ref, x_ref, m_ref, sq_ref, sk_ref, sv_ref, cq_ref, ck_ref, cv_ref, so_ref, co_ref, down_ref,
-    q_ref, k_ref, v_ref, mk_ref, mv_ref, wa_ref, cwa_ref, half_out_ref, half_down_ref, *, heads,
+    s_ref, x_ref, m_ref, sq_ref, sk_ref, sv_ref, cq_ref, ck_ref, cv_ref, so_ref, co_ref,
+    q_ref, k_ref, v_ref, mk_ref, mv_ref, wa_ref, cwa_ref, half_out_ref, half_cw_ref, *, heads,
 ):
     each = heads * HEAD_DIM
     at = pl.program_id(0)
@@ -189,7 +193,8 @@
         for n, ref in enumerate((cq_ref, ck_ref, cv_ref)):
             cwa_ref[n * each : (n + 1) * each, :] = ref[...]
         half_out_ref[...] = jnp.where(s_ref[BIT] == 0, so_ref[...], co_ref[...])
-        half_down_ref[...] = down_ref[...]
+        half = half_cw_ref.shape[0]
+        half_cw_ref[...] = cwa_ref[pl.ds(pl.multiple_of(s_ref[BIT + 1] * half, 16), half), :]
 
     limit = s_ref[TGT + s_ref[ROW]]
     memory_limit = s_ref[SRC + s_ref[ROW]]
@@ -211,7 +216,12 @@
                 attend_block(q_ref, k_ref, v_ref, att_ref, h, h * HEAD_DIM, pl.ds(0, BLOCK), BLOCK, (block + 1) * BLOCK, True)
 
 
-def self_own_kernel(q_in_ref, k_ref, v_ref, q_ref, k_out_ref, v_out_ref, att_ref, *, heads):
+def self_own_kernel(
+    s_ref, q_in_ref, k_ref, v_ref, up_ref, down_ref, q_ref, k_out_ref, v_out_ref, att_ref, halves_ref, *, heads
+):
+    half = up_ref.shape[0]
+    halves_ref[:half, :] = up_ref[...]
+    halves_ref[half:, :] = down_ref[...]
     q_ref[...] = q_in_ref[...]
     k_out_ref[...] = k_ref[:, rows_at(BLOCK), :]
     v_out_ref[...] = v_ref[:, rows_at(BLOCK), :]
@@ -221,13 +231,10 @@
 def self_other_kernel(s_ref, x_ref, near_ref, far_ref, w_ref, q_ref, k_out_ref, v_out_ref, att_ref, k_ref, v_ref, *, heads):
     each = heads * HEAD_DIM
     at = pl.program_id(0)
-    half = near_ref.shape[0]
-    high = s_ref[BIT]
 
     @pl.when(at == 0)
     def _():
-        w_ref[pl.ds(pl.multiple_of(high * half, 16), half), :] = near_ref[...]
-        w_ref[pl.ds(pl.multiple_of((1 - high) * half, 16), half), :] = far_ref[...]
+        put_halves(w_ref, near_ref, far_ref, s_ref[BIT])
 
     acc = nt(x_ref[...], w_ref[...])
     fill_queries(q_ref, pl.ds(0, BLOCK), BLOCK, acc[:, :each] * FACTOR, heads)
@@ -274,14 +281,20 @@
     cross_blocks(q_ref, k_ref, v_ref, att_ref, heads, s_ref[SRC + s_ref[ROW]])
 
 
-def cross_other_kernel(
-    s_ref, m_ref, hl_ref, cwb_ref, atta_ref, coa_ref, cob_ref, part0_ref, part1_ref, k_ref, v_ref, q_ref, att_ref, *, heads, blocks,
-):
+def put_halves(target_ref, near_ref, far_ref, high):
+    half = near_ref.shape[0]
+    target_ref[pl.ds(pl.multiple_of(high * half, 16), half), :] = near_ref[...]
+    target_ref[pl.ds(pl.multiple_of((1 - high) * half, 16), half), :] = far_ref[...]
+
+
+def cross_other_kernel(s_ref, m_ref, hl_ref, near_ref, far_ref, cwb_ref, k_ref, v_ref, q_ref, att_ref, *, heads):
     each = heads * HEAD_DIM
     limit = s_ref[SRC + s_ref[ROW]]
 
     @pl.when(pl.program_id(0) == 0)
     def _():
+        put_halves(cwb_ref, near_ref, far_ref, s_ref[BIT + 1])
+
         @pl.loop(0, m_ref.shape[0], step=BLOCK)
         def _(start):
             rows = pl.ds(pl.multiple_of(start, BLOCK), BLOCK)
@@ -289,7 +302,10 @@
 
     fill_queries(q_ref, pl.ds(0, BLOCK), BLOCK, nt(hl_ref[...], cwb_ref[:each, :]) * FACTOR, heads)
     cross_blocks(q_ref, k_ref, v_ref, att_ref, heads, limit)
-    part = nn(atta_ref[...], coa_ref[...]) + nn(att_ref[...], cob_ref[...])
+
+
+def cross_out_kernel(atta_ref, attb_ref, coa_ref, cob_ref, part0_ref, part1_ref, *, blocks):
+    part = nn(atta_ref[...], coa_ref[...]) + nn(attb_ref[...], cob_ref[...])
     put_part(part0_ref, part1_ref, part.astype(bf16), blocks)
 
 
@@ -312,15 +328,13 @@
 
 
 def ffn_other_kernel(
-    s_ref, hl_ref, term_ref, up_ref, near_ref, far_ref, part0_ref, part1_ref, act_ref, slope_ref, down_ref, *, blocks
+    s_ref, hl_ref, term_ref, up_near_ref, up_far_ref, down_near_ref, down_far_ref,
+    part0_ref, part1_ref, act_ref, slope_ref, up_ref, down_ref, *, blocks,
 ):
-    half = near_ref.shape[0]
-    high = s_ref[BIT + 1]
-
     @pl.when(pl.program_id(0) == 0)
     def _():
-        down_ref[pl.ds(pl.multiple_of(high * half, 16), half), :] = near_ref[...]
-        down_ref[pl.ds(pl.multiple_of((1 - high) * half, 16), half), :] = far_ref[...]
+        put_halves(up_ref, up_near_ref, up_far_ref, s_ref[BIT])
+        put_halves(down_ref, down_near_ref, down_far_ref, s_ref[BIT + 1])
 
     act, slope = gelu_pair(nn(hl_ref[...], up_ref[...]))
     act = act.astype(bf16)
@@ -363,9 +377,18 @@
     put_part(part0_ref, part1_ref, part.astype(bf16), blocks)
 
 
-def ffn_grad_kernel(h_ref, act_ref, e_ref, pre_ref, up_ref, down_ref):
+def ffn_grad_kernel(s_ref, h_ref, act_ref, e_ref, pre_ref, up_ref, send_ref, keep_ref):
     up_ref[...] = tn(h_ref[...], pre_ref[...]).astype(bf16)
-    down_ref[...] = tn(act_ref[...], e_ref[...]).astype(bf16)
+    down = tn(act_ref[...], e_ref[...]).astype(bf16)
+    mine = pl.program_id(0) == s_ref[BIT]
+
+    @pl.when(mine)
+    def _():
+        keep_ref[...] = down
+
+    @pl.when(jnp.logical_not(mine))
+    def _():
+        send_ref[...] = down
 
 
 def norm_step(d_in_ref, shares, gain, unit_ref, scale_ref, d_ref, e_ref, sums_ref, blocks):
@@ -445,6 +468,12 @@
     g_ref[3 * each :, :] = tn(att_ref[...], e_ref[...]).astype(bf16)
 
 
+def relay_kernel(s_ref, in_ref, first_ref, second_ref):
+    half = first_ref.shape[0]
+    first_ref[...] = in_ref[:half, :]
+    second_ref[...] = in_ref[half:, :]
+
+
 def memory_grad_kernel(s_ref, a_ref, b_ref, wa_ref, wb_ref, out_ref, send_ref, keep_ref, half_ref):
     half_ref[...] = out_ref[...]
     each = a_ref.shape[1] // 2
@@ -528,10 +557,10 @@
 
 
 def place_kernel(s_ref, *refs, shift):
-    out_ref = refs[-1]
-    pieces = refs[:-1]
+    pieces, out_ref, mark_ref = refs[:-2], refs[-2], refs[-1]
     half = out_ref.shape[0]
     row, core, at = s_ref[ROW], s_ref[CORE_AT], pl.program_id(0)
+    mark_ref[...] = jnp.zeros_like(mark_ref)
     if shift:
         sources = [
             (pieces[0].at[:half, :], 2 * row), (pieces[0].at[half:, :], 2 * row + 1),
@@ -539,8 +568,8 @@
         ]
     else:
         sources = [
-            (pieces[0], 2 * row + core), (pieces[1], 2 * row + 1 - core),
-            (pieces[2], 2 * (1 - row) + core), (pieces[3], 2 * (1 - row) + 1 - core),
+            (pieces[0].at[:half, :], 2 * row + core), (pieces[1].at[:half, :], 2 * row + 1 - core),
+            (pieces[0].at[half:, :], 2 * (1 - row) + core), (pieces[1].at[half:, :], 2 * (1 - row) + 1 - core),
         ]
     for ref, place in sources:
 
@@ -553,13 +582,13 @@
     scratch = refs[-1]
     inputs = sum(plan[1] for plan in plans)
     ins, outs = list(refs[:inputs]), list(refs[inputs:-1])
-    for kind, count, rows, bit, cuts in plans:
+    for kind, count, rows, bit, cuts, parts in plans:
         mine, ins = ins[:count], ins[count:]
-        if kind == "sum":
+        if kind == SUM:
             at = 0
             for a_ref, b_ref in zip(mine[: count // 2], mine[count // 2 :]):
-                size = a_ref.shape[0]
-                scratch[at : at + size, :] = (a_ref[...].astype(f32) + b_ref[...].astype(f32)).astype(bf16)
+                size = min(a_ref.shape[0], rows - at)
+                scratch[at : at + size, :] = (a_ref[:size, :].astype(f32) + b_ref[:size, :].astype(f32)).astype(bf16)
                 at += size
             if at < rows:
                 scratch[at:rows, :] = jnp.zeros((rows - at, scratch.shape[1]), bf16)
@@ -569,22 +598,30 @@
                 half, high = rows // 2, s_ref[BIT + bit]
                 outs.pop(0)[...] = scratch[pl.ds(pl.multiple_of((1 - high) * half, 16), half), :]
                 outs.pop(0)[...] = scratch[pl.ds(pl.multiple_of(high * half, 16), half), :]
+        elif kind == LAST:
+            outs.pop(0)[...] = mine[0][-rows:, :].astype(f32) + mine[1][-rows:, :].astype(f32)
+        elif kind == STACK:
+            size, target = mine[0].shape[0], outs.pop(0)
+            target[:size, :] = mine[0][...]
+            target[size:, :] = mine[1][...]
         else:
-            high, size = s_ref[BIT + bit], mine[0].shape[0]
-            target = outs.pop(0) if kind == "pack" else scratch
-            target[pl.ds(pl.multiple_of(high * size, 16), size), :] = mine[0][...]
-            target[pl.ds(pl.multiple_of((1 - high) * size, 16), size), :] = mine[1][...]
+            high, size = s_ref[BIT + bit], mine[0].shape[0] // parts
+            target = outs.pop(0) if kind == PACK else scratch
+            for part in range(parts):
+                some, first = slice(part * size, (part + 1) * size), 2 * part * size
+                target[pl.ds(pl.multiple_of(first + high * size, 16), size), :] = mine[0][some, :]
+                target[pl.ds(pl.multiple_of(first + (1 - high) * size, 16), size), :] = mine[1][some, :]
             for first, size in cuts:
                 outs.pop(0)[...] = scratch[first : first + size, :].astype(f32)
 
 
 class Row:
-    def __init__(self, array, length, how="whole"):
+    def __init__(self, array, length, how=WHOLE):
         self.array, self.length, self.how = array, length, how
 
 
 class Part:
-    def __init__(self, array, how="rows", pick=None):
+    def __init__(self, array, how=ROWS, pick=None):
         self.array, self.how, self.pick = array, how, pick
 
 
@@ -604,36 +641,36 @@
         return pl.BlockSpec(shape, lambda *a: (0,))
     if isinstance(how, tuple):
         how, pick = how
-    if how == "whole":
+    if how == WHOLE:
         return pl.BlockSpec(shape, lambda *a: (0,) * rank, pipeline_mode=pl.Buffered(1) if once else None)
     pick = pick or (lambda i: i)
-    dim = rank - 1 if how == "columns" else rank - 2
-    parts = blocks // 2 if how == "half" else blocks
+    dim = rank - 1 if how == COLUMNS else rank - 2
+    parts = blocks // 2 if how == HALF else blocks
     block = tuple(n // parts if d == dim else n for d, n in enumerate(shape))
     return pl.BlockSpec(block, lambda i, *a: tuple(pick(i) if d == dim else 0 for d in range(rank)))
 
 
 def row_of(item, blocks):
     width = item.array.shape[1]
-    if item.how == "whole":
+    if item.how == WHOLE:
         return pl.BlockSpec((item.length, width), lambda i, s: (s[0], 0))
-    if item.how == "rows":
+    if item.how == ROWS:
         return pl.BlockSpec((item.length // blocks, width), lambda i, s: (s[0] * blocks + i, 0))
-    if item.how[0] == "part":
+    if item.how[0] == PART:
         return pl.BlockSpec((item.length // blocks, width), lambda i, s: (s[item.how[1]] * blocks + i, 0))
     return pl.BlockSpec((item.length, width // blocks), lambda i, s: (s[0], i))
 
 
 class Held:
-    def __init__(self, array, how="rows"):
+    def __init__(self, array, how=ROWS):
         self.array, self.how = array, how
 
 
 def view_of(shape, how, blocks):
     rank = len(shape)
-    if how == "whole":
+    if how == WHOLE:
         return None
-    if how == "rows":
+    if how == ROWS:
         size = shape[-2] // blocks
 
         def rows(ref):
@@ -645,7 +682,7 @@
     return lambda ref: ref.at[:, pl.ds(pl.multiple_of(pl.program_id(0) * size, size), size)]
 
 
-def call(kernel, name, blocks, inputs, outputs, scalars=None, scratch=(), micros=5.0, limit=LIMIT, after=(), scale=1.0):
+def call(kernel, blocks, inputs, outputs, scalars=None, scratch=(), micros=5.0, limit=LIMIT, after=(), scale=0.4):
     specs, arrays, views = [], [], []
     here = pl.BlockSpec(memory_space=pltpu.VMEM)
     for item in inputs:
@@ -661,20 +698,20 @@
             specs.append(pl.BlockSpec((rows // item.parts, width), functools.partial(lambda at, i, s: (s[at], 0), item.scalar)))
             arrays.append(pltpu.with_memory_space_constraint(item.array, pltpu.HBM))
         elif isinstance(item, Far):
-            specs.append(block_of(item.array.shape, "whole", blocks, once=True))
+            specs.append(block_of(item.array.shape, WHOLE, blocks, once=True))
             arrays.append(pltpu.with_memory_space_constraint(item.array, pltpu.HBM))
         elif isinstance(item, Held):
             specs.append(here)
             arrays.append(pltpu.with_memory_space_constraint(item.array, pltpu.VMEM))
             view = view_of(item.array.shape, item.how, blocks)
         else:
-            specs.append(block_of(item.shape, "whole", blocks, once=True))
+            specs.append(block_of(item.shape, WHOLE, blocks, once=True))
             arrays.append(item)
         views.append(view)
     for item in after:
         specs.append(pl.BlockSpec(memory_space=pl.ANY))
         arrays.append(item)
-        views.append("skip")
+        views.append(SKIP)
     shapes, out_specs = [], []
     for shape, dtype, how in outputs:
         if how[:4] == "held":
@@ -691,16 +728,16 @@
     def viewed(*refs):
         passed = list(refs[:lead])
         for ref, view in zip(refs[lead : lead + len(views)], views):
-            if view == "skip":
+            if view == SKIP:
                 continue
             passed.append(ref if view is None else view(ref))
         return kernel(*passed, *refs[lead + len(views) :])
 
     settings = dict(
         out_shape=shapes,
-        compiler_params=pltpu.CompilerParams(vmem_limit_bytes=limit * MIB, dimension_semantics=("arbitrary",)),
+        compiler_params=pltpu.CompilerParams(vmem_limit_bytes=limit * MIB, dimension_semantics=(ARBITRARY,)),
         cost_estimate=pl.CostEstimate(flops=int(micros * scale * 1.0e9), bytes_accessed=0, transcendentals=0),
-        name=name,
+        name=getattr(kernel, "func", kernel).__name__,
     )
     if scalars is None:
         return pl.pallas_call(
@@ -744,26 +781,26 @@
         per = blocks // 2
         first, second = (lambda i: jnp.minimum(i, per - 1)), (lambda i: jnp.maximum(i - per, 0))
         got = [sibling(p) for p in part]
-        return [Part(v, "half", pick) for v, pick in zip((*part, *got), (first, second) * 2)]
+        return [Part(v, HALF, pick) for v, pick in zip((*part, *got), (first, second) * 2)]
 
     def part_shapes(blocks):
         per = blocks // 2
         first, second = (lambda i: jnp.minimum(i, per - 1)), (lambda i: jnp.maximum(i - per, 0))
-        return [((length // 2, width), bf16, ("half", pick)) for pick in (first, second)]
-
-    head_rows = ((heads, length, WIDE), bf16, "hbm rows")
-    head_held = ((heads, length, WIDE), bf16, "held rows")
-    key_held = ((heads, source, WIDE), bf16, "held rows")
-    held = ((length, width), f32, "held rows")
-    held_low = ((length, width), bf16, "held rows")
-    column = ((length, 1), f32, "held rows")
-    att_held = ((length, each), bf16, "held rows")
-    hid = ((length, hidden), bf16, "held rows")
-    sums = ((8, width), f32, "whole")
-    low = ((length, width), bf16, "rows")
-    square = ((width, hidden), bf16, "rows")
-    half_low = ((length // 2, width), bf16, "whole")
-    out_shape = ((each, width), bf16, "whole")
+        return [((length // 2, width), bf16, (HALF, pick)) for pick in (first, second)]
+
+    head_rows = ((heads, length, WIDE), bf16, FAR_ROWS)
+    head_held = ((heads, length, WIDE), bf16, HELD_ROWS)
+    key_held = ((heads, source, WIDE), bf16, HELD_ROWS)
+    held = ((length, width), f32, HELD_ROWS)
+    held_low = ((length, width), bf16, HELD_ROWS)
+    column = ((length, 1), f32, HELD_ROWS)
+    att_held = ((length, each), bf16, HELD_ROWS)
+    hid = ((length, hidden), bf16, HELD_ROWS)
+    sums = ((8, width), f32, WHOLE)
+    low = ((length, width), bf16, ROWS)
+    square = ((width, hidden), bf16, ROWS)
+    half_low = ((length // 2, width), bf16, WHOLE)
+    out_shape = ((each, width), bf16, WHOLE)
     qkv = functools.partial(pltpu.VMEM, (heads, length, WIDE))
 
     w_parts = (self_query.T, self_key.T, self_value.T)
@@ -771,265 +808,295 @@
     bit = scalars[BIT]
     w_half = lax.dynamic_slice_in_dim(jnp.concatenate(w_parts, 0), bit * (3 * each // 2), 3 * each // 2, 0)
     w_near = across(w_half)
-    q_new, k_new, v_new, ck_a, cv_a, w_a, cw_a, o_half, down_half = call(
-        functools.partial(project_own_kernel, heads=heads), "project_own", big,
+    q_new, k_new, v_new, ck_a, cv_a, w_a, cw_a, o_half, cw_half = call(
+        functools.partial(project_own_kernel, heads=heads), big,
         [
-            Row(tokens, length, "rows"), Row(memory, source, "rows"), *(Far(v) for v in (*w_parts, *c_parts, self_out, cross_out)),
-            Pick(ffn_down, BIT + 1, 2),
+            Row(tokens, length, ROWS), Row(memory, source, ROWS), *(Far(v) for v in (*w_parts, *c_parts, self_out, cross_out)),
         ],
         [
-            head_held, head_held, head_held, key_held, key_held, ((3 * each, width), bf16, "whole"),
-            ((3 * each, width), bf16, "whole"), out_shape, ((hidden // 2, width), bf16, "whole"),
+            head_held, head_held, head_held, key_held, key_held, ((3 * each, width), bf16, WHOLE),
+            ((3 * each, width), bf16, WHOLE), out_shape, ((3 * each // 2, width), bf16, WHOLE),
         ],
-        scalars, micros=7, scale=0.05,
+        scalars, micros=7, scale=0.4,
     )
     o_near = across(o_half)
-    cw_b = across(cw_a)
-    up_b = across(ffn_up)
-    down_near = across(down_half)
-    down_far = along(down_near, 1)
+    cw_near = across(cw_half)
     w_far = along(w_near, 0)
-    q_a, k_a, v_a, att_a = call(
-        functools.partial(self_own_kernel, heads=heads), "self_own", big, [Held(q_new), Held(k_new, "whole"), Held(v_new, "whole")],
-        [head_rows, head_rows, head_rows, att_held], micros=6, scale=0.05, after=[w_near],
-    )
+    quarter = ((hidden // 2, width), bf16, WHOLE)
+    q_a, k_a, v_a, att_a, ffn_half = call(
+        functools.partial(self_own_kernel, heads=heads), big,
+        [Held(q_new), Held(k_new, WHOLE), Held(v_new, WHOLE), Pick(ffn_up, BIT, 2), Pick(ffn_down, BIT + 1, 2)],
+        [head_rows, head_rows, head_rows, att_held, ((width, width), bf16, WHOLE)], scalars, micros=6, scale=0.4, after=[w_near],
+    )
+    ffn_near = across(ffn_half)
+    cw_far = along(cw_near, 1)
     o_far = along(o_near, 0)
     w_b, q_b, k_b, v_b, att_b = call(
-        functools.partial(self_other_kernel, heads=heads), "self_other", big, [Row(tokens, length, "rows"), w_near, w_far],
-        [((3 * each, width), bf16, "whole"), head_rows, head_rows, head_rows, att_held], scalars, scratch=[qkv(bf16), qkv(bf16)],
-        micros=9, scale=0.05, after=[o_near],
+        functools.partial(self_other_kernel, heads=heads), big, [Row(tokens, length, ROWS), w_near, w_far],
+        [((3 * each, width), bf16, WHOLE), head_rows, head_rows, head_rows, att_held], scalars, scratch=[qkv(bf16), qkv(bf16)],
+        micros=9, scale=0.4, after=[o_near],
     )
     part0, part1, so_b, co_b = call(
-        functools.partial(self_out_kernel, blocks=big), "self_out", big, [Held(att_a), Held(att_b), self_out, o_near, o_far],
-        [*part_shapes(big), out_shape, out_shape], scalars, micros=3, scale=0.05,
+        functools.partial(self_out_kernel, blocks=big), big, [Held(att_a), Held(att_b), self_out, o_near, o_far],
+        [*part_shapes(big), out_shape, out_shape], scalars, micros=3, scale=0.4, after=[cw_near],
     )
     h_one, h_one_low, unit_one, scale_one, cq_a, catt_a = call(
-        functools.partial(cross_own_kernel, heads=heads, blocks=big), "cross_own", big,
-        [Row(tokens, length, "rows"), *shares((part0, part1), big), gain_one, shift_one, c_parts[0], Held(ck_a, "whole"), Held(cv_a, "whole")],
-        [held, held_low, held_low, column, head_held, att_held], scalars, micros=10, scale=0.05,
-    )
-    part0, part1, ck_b, cv_b, cq_b, catt_b = call(
-        functools.partial(cross_other_kernel, heads=heads, blocks=big), "cross_other", big,
-        [Row(memory, source), Held(h_one_low), cw_b, Held(catt_a), cross_out, co_b],
+        functools.partial(cross_own_kernel, heads=heads, blocks=big), big,
+        [Row(tokens, length, ROWS), *shares((part0, part1), big), gain_one, shift_one, c_parts[0], Held(ck_a, WHOLE), Held(cv_a, WHOLE)],
+        [held, held_low, held_low, column, head_held, att_held], scalars, micros=10, scale=0.4,
+    )
+    up_near, down_near = call(
+        relay_kernel, 1, [ffn_near], [quarter, quarter], scalars, micros=1, after=[scale_one]
+    )
+    up_far, down_far = along(up_near, 0), along(down_near, 1)
+    cw_b, ck_b, cv_b, cq_b, catt_b = call(
+        functools.partial(cross_other_kernel, heads=heads), big,
+        [Row(memory, source), Held(h_one_low), cw_near, cw_far],
+        [((3 * each, width), bf16, WHOLE), ((heads, source, WIDE), bf16, HELD_WHOLE), ((heads, source, WIDE), bf16, HELD_WHOLE), head_held, att_held],
+        scalars, micros=100, scale=1.0, after=[up_near, down_near],
+    )
+    part0, part1 = call(
+        functools.partial(cross_out_kernel, blocks=big), big, [Held(catt_a), Held(catt_b), cross_out, co_b],
+        part_shapes(big), micros=2, scale=0.4, after=[up_far, down_far],
+    )
+    h_two, h_two_low, unit_two, scale_two, act_a, slope_a, term = call(
+        functools.partial(ffn_own_kernel, blocks=small), small,
+        [Held(h_one), *shares((part0, part1), small), gain_two, shift_two, Held(ffn_up, WHOLE), Held(ffn_down, WHOLE)],
+        [held, held_low, held_low, column, hid, hid, held], micros=7, scale=0.4,
+    )
+    part0, part1, act_b, slope_b, up_b, down_b = call(
+        functools.partial(ffn_other_kernel, blocks=small), small,
+        [Held(h_two_low), Held(term), up_near, up_far, down_near, down_far],
+        [*part_shapes(small), hid, hid, ((width, hidden), bf16, HELD_WHOLE), ((hidden, width), bf16, HELD_WHOLE)], scalars, micros=5, scale=0.4,
+    )
+
+    part0, part1, out_row, d_three, e_three, pre_a, pre_b, sums_three = call(
+        functools.partial(ffn_back_kernel, blocks=small), small,
         [
-            *part_shapes(big), ((heads, source, WIDE), bf16, "held whole"), ((heads, source, WIDE), bf16, "held whole"),
-            head_held, att_held,
+            Held(h_two), *shares((part0, part1), small), Row(cotangent, length, ROWS), gain_three, shift_three,
+            Held(ffn_up, WHOLE), Held(up_b, WHOLE), Held(ffn_down, WHOLE), Held(down_b, WHOLE), Held(slope_a), Held(slope_b),
         ],
-        scalars, micros=11, scale=0.05, after=[down_near],
-    )
-    h_two, h_two_low, unit_two, scale_two, act_a, slope_a, term = call(
-        functools.partial(ffn_own_kernel, blocks=small), "ffn_own", small,
-        [Held(h_one), *shares((part0, part1), small), gain_two, shift_two, Held(ffn_up, "whole"), Held(ffn_down, "whole")],
-        [held, held_low, held_low, column, hid, hid, held], micros=7, scale=0.05,
-    )
-    part0, part1, act_b, slope_b, down_b = call(
-        functools.partial(ffn_other_kernel, blocks=small), "ffn_other", small,
-        [Held(h_two_low), Held(term), up_b, down_near, down_far],
-        [*part_shapes(small), hid, hid, ((hidden, width), bf16, "held whole")], scalars, micros=5, scale=0.05,
-    )
-
-    part0, part1, out_row, d_three, e_three, pre_a, pre_b, sums_three = call(
-        functools.partial(ffn_back_kernel, blocks=small), "ffn_back", small,
-        [
-            Held(h_two), *shares((part0, part1), small), Row(cotangent, length, "rows"), gain_three, shift_three,
-            Held(ffn_up, "whole"), up_b, Held(ffn_down, "whole"), Held(down_b, "whole"), Held(slope_a), Held(slope_b),
-        ],
-        [*part_shapes(small), low, held, held_low, hid, hid, sums], scalars, micros=11,
+        [*part_shapes(small), ((length, width), bf16, FAR_ROWS), held, held_low, hid, hid, sums], scalars, micros=11,
     )
     part = (part0, part1)
-    gu_b, gd_b = call(
-        ffn_grad_kernel, "ffn_grad_other", third,
-        [Held(h_two_low, "columns"), Held(act_b, "columns"), Held(e_three, "whole"), Held(pre_b, "whole")], [square, square], micros=4,
-    )
-    gu_got, gd_got = across(gu_b), across(gd_b)
-    gu_a, gd_a = call(
-        ffn_grad_kernel, "ffn_grad_own", third,
-        [Held(h_two_low, "columns"), Held(act_a, "columns"), Held(e_three, "whole"), Held(pre_a, "whole")], [square, square], micros=4,
-    )
+    quarter = ((width // 2, hidden), bf16, WHOLE)
+
+    def ffn_grads(act, pre, after=()):
+        return call(
+            ffn_grad_kernel, 2,
+            [Held(h_two_low, COLUMNS), Held(act, COLUMNS), Held(e_three, WHOLE), Held(pre, WHOLE)],
+            [square, quarter, quarter], scalars, micros=4, after=after,
+        )
+
+    gu_b, send_b, keep_b = ffn_grads(act_b, pre_b)
+    gu_got, got_b = across(gu_b), along(send_b, 0)
+    gu_a, send_a, keep_a = ffn_grads(act_a, pre_a, [send_b])
+    got_a = along(send_a, 0)
     back_scratch = [
         pltpu.VMEM((heads, BLOCK, WIDE), f32), pltpu.VMEM((heads, source, WIDE), f32), pltpu.VMEM((heads, source, WIDE), f32),
     ]
-    dkv_held = ((source, 2 * each), bf16, "held whole")
+    dkv_held = ((source, 2 * each), bf16, HELD_WHOLE)
     d_two, e_two, sums_two, do_a, dcq_b, dckv_b = call(
-        functools.partial(cross_back_other_kernel, heads=heads, blocks=big), "cross_back_other", big,
+        functools.partial(cross_back_other_kernel, heads=heads, blocks=big), big,
         [
             Held(d_three), *shares(part, big), gain_two, Held(unit_two), Held(scale_two), cross_out, co_b, Held(catt_a), Held(catt_b),
-            Held(cq_b), Held(ck_b, "whole"), Held(cv_b, "whole"),
+            Held(cq_b), Held(ck_b, WHOLE), Held(cv_b, WHOLE),
         ],
         [held, held_low, sums, head_held, att_held, dkv_held], scalars,
         scratch=[pltpu.VMEM((heads, BLOCK, WIDE), bf16)] + back_scratch, micros=18,
     )
 
-    def step(name, plans, after=(), micros=2):
+    def cross_grads(att, dq, dkv, after=()):
+        return call(
+            cross_grad_kernel, third,
+            [
+                Held(h_one_low, COLUMNS), Row(memory, source, COLUMNS), Held(att, WHOLE), Held(e_two, COLUMNS),
+                Held(dq, WHOLE), Held(dkv, WHOLE),
+            ],
+            [((4 * each, width), bf16, COLUMNS)], scalars, micros=5, after=after,
+        )[0]
+
+    def step(plans, after=(), micros=2):
         inputs, outputs, kernel_plans, counts, most = [], [], [], [], 16
-        for kind, arrays, rows, bit, cuts in plans:
+        for kind, arrays, rows, bit, cuts, parts in plans:
             inputs += arrays
-            if kind == "sum":
-                made = [((rows, width), bf16, "whole")] if bit is None else [((rows // 2, width), bf16, "whole")] * 2
-            elif kind == "pack":
-                made = [((rows, width), bf16, "whole")]
+            if kind == SUM:
+                made = [((rows, width), bf16, WHOLE)] if bit is None else [((rows // 2, width), bf16, WHOLE)] * 2
+            elif kind == LAST:
+                made = [((rows, width), f32, WHOLE)]
+            elif kind in (PACK, STACK):
+                made = [((rows, width), bf16, WHOLE)]
             else:
-                made = [((size, width), f32, "hbm whole") for _, size in cuts]
-            if kind != "pack":
+                made = [((size, width), f32, FAR_WHOLE) for _, size in cuts]
+            if kind not in (PACK, STACK, LAST):
                 most = max(most, rows)
             outputs += made
             counts.append(len(made))
-            kernel_plans.append((kind, len(arrays), rows, bit, cuts))
+            kernel_plans.append((kind, len(arrays), rows, bit, cuts, parts))
         made = list(
             call(
-                functools.partial(step_kernel, plans=kernel_plans), name, 1, inputs, outputs, scalars,
+                functools.partial(step_kernel, plans=kernel_plans), 1, inputs, outputs, scalars,
                 scratch=[pltpu.VMEM((most, width), bf16)], micros=micros, after=after,
             )
         )
         return [made[sum(counts[:n]) : sum(counts[: n + 1])] for n in range(len(counts))]
 
     class Chain:
-        def __init__(self, mine, got, rows, cuts):
+        def __init__(self, mine, got, rows, cuts, bits=(0, 1, 2), back=(2, 1, 0), parts=1):
             self.arrays, self.rows, self.cuts, self.stage = [*mine, *got], rows, cuts, 0
+            self.bits, self.back, self.parts = bits, back, parts
 
         def plan(self):
-            stage = self.stage
-            if stage <= 3:
-                return ("sum", self.arrays, self.rows >> stage, stage if stage < 3 else None, ())
-            bit = 6 - stage
-            return ("wide" if stage == 6 else "pack", self.arrays, self.rows >> bit, bit, self.cuts if stage == 6 else ())
+            count = len(self.bits)
+            if self.stage <= count:
+                bit = self.bits[self.stage] if self.stage < count else None
+                return (SUM, self.arrays, self.rows >> self.stage, bit, (), 1)
+            at = self.stage - count
+            rows, last = self.rows >> count << at, at == len(self.back)
+            return (WIDEN if last else PACK, self.arrays, rows, self.back[at - 1], self.cuts if last else (), self.parts if last else 1)
 
         def take(self, made):
-            stage, self.stage = self.stage, self.stage + 1
-            if stage < 3:
-                self.arrays = [made[1], along(made[0], stage)]
-            elif stage < 6:
-                self.arrays = [made[0], along(made[0], 5 - stage)]
+            stage, count, self.stage = self.stage, len(self.bits), self.stage + 1
+            if stage < count:
+                self.arrays = [made[1], along(made[0], self.bits[stage])]
+            elif stage < count + len(self.back):
+                self.arrays = [made[0], along(made[0], self.back[stage - count])]
             else:
                 self.done = made
 
-    def advance(name, chains, plans=(), after=(), micros=2):
-        made = step(name, [c.plan() for c in chains] + list(plans), after, micros)
+    def advance(chains, plans=(), after=(), micros=2):
+        made = step([c.plan() for c in chains] + list(plans), after, micros)
         for chain, one in zip(chains, made):
             chain.take(one)
         return [made[0][-1]], [m[0] for m in made[len(chains) :]]
 
-    everything = [(0, width)]
-    thirds = [(n * each, each) for n in range(3)]
+    def plain(arrays, rows):
+        return (SUM, arrays, rows, None, (), 1)
+
+    def last(mine, got):
+        return (LAST, [mine, got], 16, None, (), 1)
+
     pin = []
     if short:
-        up = Chain([gu_a], [gu_got], width, everything)
-        pin, _ = advance("step_0", [up], after=[dcq_b])
+        (send_u, keep_u), (down_a,), (down_b,) = step(
+            [
+                (SUM, [gu_a, gu_got], width, 0, (), 1), plain([keep_a, got_a], width // 2), plain([keep_b, got_b], width // 2),
+            ],
+            [dcq_b],
+        )
+        got_u, got_d = along(send_u, 0), across(down_b)
+        pin = [keep_u]
+    gc_b = cross_grads(catt_b, dcq_b, dckv_b, pin)
     part0, part1, dcq_a, dckv_a = call(
-        functools.partial(cross_back_own_kernel, heads=heads, blocks=big), "cross_back_own", big,
-        [Held(cq_a), Held(ck_a, "whole"), Held(cv_a, "whole"), Held(do_a), Held(dcq_b), c_parts[0], cw_b],
-        [*part_shapes(big), att_held, dkv_held], scalars, scratch=back_scratch, micros=16, after=pin,
+        functools.partial(cross_back_own_kernel, heads=heads, blocks=big), big,
+        [Held(cq_a), Held(ck_a, WHOLE), Held(cv_a, WHOLE), Held(do_a), Held(dcq_b), c_parts[0], cw_b],
+        [*part_shapes(big), att_held, dkv_held], scalars, scratch=back_scratch, micros=16, after=[gc_b],
     )
     part = (part0, part1)
 
-    def cross_grads(name, att, dq, dkv, after=()):
-        return call(
-            cross_grad_kernel, name, third,
-            [
-                Held(h_one_low, "columns"), Row(memory, source, "columns"), Held(att, "whole"), Held(e_two, "columns"),
-                Held(dq, "whole"), Held(dkv, "whole"),
-            ],
-            [((4 * each, width), bf16, "columns")], scalars, micros=5, after=after,
-        )[0]
-
-    gc_b = cross_grads("cross_grad_other", catt_b, dcq_b, dckv_b, [dcq_a])
     gc_got = across(gc_b)
     if short:
-        down = Chain([gd_a], [gd_got], width, everything)
-        pin, _ = advance("step_1", [up, down], after=[gc_b])
-    gc_a = cross_grads("cross_grad_own", catt_a, dcq_a, dckv_a, pin)
+        ffn = Chain([keep_u, down_a], [got_u, got_d], width, [(0, width), (width, width)], (1, 2), (2, 1, 0), 2)
+        pin, _ = advance([ffn], after=[dcq_a])
     memory_send, memory_keep, out_half = call(
-        memory_grad_kernel, "memory_grad", 2,
-        [Held(dckv_a), Held(dckv_b), cw_a, cw_b, Row(out_row, length // 2, ("part", CORE_AT))],
-        [half_low, half_low, ((length // 2, width), bf16, "rows")], scalars, micros=5, after=[gc_a],
+        memory_grad_kernel, 2,
+        [Held(dckv_a), Held(dckv_b), cw_a, cw_b, Row(out_row, length // 2, (PART, CORE_AT))],
+        [half_low, half_low, ((length // 2, width), bf16, ROWS)], scalars, micros=5, after=pin,
     )
     out_far = across(out_half)
     memory_got = sibling(memory_send)
-    pin = [memory_send]
-    if short:
-        cross = Chain([gc_a], [gc_got], 4 * each, [(n * each, each) for n in range(4)])
-        pin, _ = advance("step_2", [up, down, cross], after=[memory_send])
-    rest_shape = ((each + 16, width), bf16, "whole")
+    gc_a = cross_grads(catt_a, dcq_a, dckv_a, [memory_send])
+    memory_plan = plain([memory_keep, memory_got], length // 2)
+    pin = [gc_a]
+    rest_shape = ((each + 16, width), bf16, WHOLE)
     d_one, do_a, do_b, rest_a, rest_b = call(
-        functools.partial(norm_one_back_kernel, heads=heads, blocks=small), "norm_one_back", small,
+        functools.partial(norm_one_back_kernel, heads=heads, blocks=small), small,
         [
             Held(d_two), *shares(part, small), gain_one, Held(unit_one), Held(scale_one), self_out, so_b,
-            Held(att_a, "whole"), Held(att_b, "whole"), sums_two, sums_three,
+            Held(att_a, WHOLE), Held(att_b, WHOLE), sums_two, sums_three,
         ],
         [held, head_held, head_held, rest_shape, rest_shape], scalars,
         scratch=[pltpu.VMEM((length, width), bf16), pltpu.VMEM((8, width), f32)], micros=6, after=pin,
     )
     rest_got = across(rest_b)
-    kept_w = ((3 * each, width), bf16, "whole")
-    qkv_held = ((length, 3 * each), bf16, "held whole")
+    kept_w = ((3 * each, width), bf16, WHOLE)
+    qkv_held = ((length, 3 * each), bf16, HELD_WHOLE)
     self_scratch = [
         pltpu.VMEM((heads, SPAN, WIDE), f32), pltpu.VMEM((heads, length, WIDE), f32), pltpu.VMEM((heads, length, WIDE), f32),
     ]
 
-    def self_back(name, q, k, v, do, after=()):
+    def self_back(q, k, v, do, after=()):
         return call(
-            functools.partial(self_back_kernel, heads=heads, blocks=small), name, small,
+            functools.partial(self_back_kernel, heads=heads, blocks=small), small,
             [Row(tokens, length), Part(q), k, v, Held(do)], [qkv_held, kept_w], scalars, scratch=self_scratch, micros=14, after=after,
         )
 
     pin = []
     if short:
-        pin, _ = advance("step_3", [up, down, cross], after=[do_b])
-    dqkv_b, gw_b = self_back("self_back_other", q_b, k_b, v_b, do_b, pin)
+        cross = Chain([gc_a], [gc_got], 4 * each, [(n * each, each) for n in range(4)])
+        pin, _ = advance([ffn, cross], after=[do_b])
+    dqkv_b, gw_b = self_back(q_b, k_b, v_b, do_b, pin)
     gw_got = across(gw_b)
 
     pin = []
     if short:
-        rest = Chain([rest_a], [rest_got], 256, [(0, each), (each, 16)])
-        pin, _ = advance("step_4", [up, down, cross, rest], (), [dqkv_b], 3)
-    dqkv_a, gw_a = self_back("self_back_own", q_a, k_a, v_a, do_a, pin)
-    memory_plan = ("sum", [memory_keep, memory_got], length // 2, None, ())
+        pin, (norms,) = advance([ffn, cross], [last(rest_a, rest_got)], [dqkv_b])
+        norms = last(norms, along(norms, 0))
+    dqkv_a, gw_a = self_back(q_a, k_a, v_a, do_a, pin)
+    pin = []
     if short:
-        own = Chain([gw_a], [gw_got], 640, thirds)
-        pin, (mine,) = advance("step_5", [own, up, down, cross, rest], [memory_plan], (), 4)
+        own = Chain([gw_a, rest_a], [gw_got, rest_got], 4 * each, [(n * each, each) for n in range(4)])
+        pin, (memory_mine, norms) = advance([own, ffn, cross], [memory_plan, norms])
+        norms = last(norms, along(norms, 1))
     else:
-        ((mine,),) = step("memory_finish", [memory_plan], [gw_a])
-        pin = []
-    far = across(mine)
-    memory_pieces = [mine, sibling(mine), far, sibling(far)]
+        ((memory_mine,),) = step([memory_plan], [gw_a])
+    memory_far = across(memory_mine)
     tokens_send, tokens_keep = call(
-        tokens_grad_kernel, "tokens_grad", 2, [Held(d_one), Held(dqkv_a), Held(dqkv_b), w_a, w_b],
-        [half_low, ((length // 2, width), f32, "whole")], scalars, micros=6, after=pin,
-    )
-    tokens_plan = ("sum", [tokens_keep, sibling(tokens_send)], length // 2, None, ())
-
-    def placed(name, pieces, shift, after=()):
+        tokens_grad_kernel, 2, [Held(d_one), Held(dqkv_a), Held(dqkv_b), w_a, w_b],
+        [half_low, ((length // 2, width), f32, WHOLE)], scalars, micros=6, after=pin,
+    )
+    def placed(pieces, shift, after=()):
         return call(
-            functools.partial(place_kernel, shift=shift), name, 4, pieces, [((2 * length, width), bf16, "hbm rows")], scalars,
-            micros=4, after=after,
-        )[0]
+            functools.partial(place_kernel, shift=shift), 4, pieces,
+            [((2 * length, width), bf16, FAR_ROWS), ((8, WIDE), f32, WHOLE)], scalars, micros=4, after=after,
+        )
+
+    def pair(mine, far):
+        return (STACK, [mine, far], length, None, (), 1)
 
     if short:
-        pin, (mine,) = advance("step_6", [own, up, down, cross, rest], [tokens_plan], [tokens_send], 3)
+        out_sibling = sibling(out_far)
+        pin, _ = advance([own, ffn, cross], (), [tokens_send, out_sibling])
+        tokens_plan = plain([tokens_keep, sibling(tokens_send)], length // 2)
+        pin, _ = advance([own, cross], (), pin)
+        layer_out, mark = placed([out_row, out_far, out_sibling], True, pin)
+        pin, (tokens_mine, memory_pair) = advance([own, ffn, cross], [tokens_plan, pair(memory_mine, memory_far)], [mark], 3)
+        tokens_far, memory_sibling = across(tokens_mine), sibling(memory_pair)
+        pin, (norms,) = advance([own], [norms], [*pin, memory_sibling])
+        norms = last(norms, along(norms, 2))
+        memory_grad, mark = placed([memory_pair, memory_sibling], False, pin)
+        pin, (tokens_pair, norms) = advance([own, cross], [pair(tokens_mine, tokens_far), norms], [mark])
+        tokens_grad, mark = placed([tokens_pair, sibling(tokens_pair)], False, pin)
+        advance([own], (), [mark])
+        (gu_wide, gd_wide), cross, own = ffn.done, cross.done, own.done
+        rest = own[3]
     else:
-        ((mine,),) = step("tokens_finish", [tokens_plan])
-        pin = []
-    far = across(mine)
-    tokens_pieces = [mine, sibling(mine), far, sibling(far)]
-    layer_out = placed("place_layer_out", [out_row, out_far, sibling(out_far)], True, pin)
-    if short:
-        pin, _ = advance("step_7", [own, down, cross, rest], (), [layer_out])
-        memory_grad = placed("place_memory_grad", memory_pieces, False, pin)
-        pin, _ = advance("step_8", [own, cross, rest], (), [memory_grad])
-        pin, _ = advance("step_9", [own, rest], (), pin)
-        tokens_grad = placed("place_tokens_grad", tokens_pieces, False, pin)
-        pin, _ = advance("step_10", [own, rest], (), [tokens_grad])
-        advance("step_11", [own], (), pin)
-        (gu_wide,), (gd_wide,), cross, own = up.done, down.done, cross.done, own.done
-        rest, norms = rest.done
-    else:
-        memory_grad = placed("place_memory_grad", memory_pieces, False)
-        tokens_grad = placed("place_tokens_grad", tokens_pieces, False)
+        tokens_plan = plain([tokens_keep, sibling(tokens_send)], length // 2)
+        (tokens_mine,), (memory_pair,) = step([tokens_plan, pair(memory_mine, memory_far)])
+        ((tokens_pair,),) = step([pair(tokens_mine, across(tokens_mine))])
+        layer_out, _ = placed([out_row, out_far, sibling(out_far)], True)
+        memory_grad, _ = placed([memory_pair, sibling(memory_pair)], False)
+        tokens_grad, _ = placed([tokens_pair, sibling(tokens_pair)], False)
 
         def total(mine, got):
             return lax.psum((mine.astype(f32) + got.astype(f32)).astype(bf16), "dp").astype(f32)
 
-        gu_wide, gd_wide = total(gu_a, gu_got), total(gd_a, gd_got)
+        high = scalars[BIT] == 1
+        down_a, down_b = (
+            jnp.where(high, jnp.concatenate([send, keep]), jnp.concatenate([keep, send]))
+            for send, keep in ((send_a, keep_a), (send_b, keep_b))
+        )
+        gu_wide, gd_wide = total(gu_a, gu_got), total(down_a, across(down_b))
         cross = jnp.split(total(gc_a, gc_got), 4)
         own = jnp.split(total(gw_a, gw_got), 3)
         rest = total(rest_a, rest_got)

time: 376 us -> 330 us (0.88)
  waiting for transfers between devices: 110 us -> 68.5 us
  local copies, waits for them, and re-layouts: 20.2 us -> 5.61 us
  starting transfers between devices: 52.9 us -> 59.7 us
    ppermute x13 -> x12, waiting for transfers between devices: 49.1 us -> 11.5 us  [across(): return lax.ppermute(value, 'tp', ACROSS)]
    pallas_call x31 -> x34, Pallas kernels: 165 us -> 179 us  [call(): pl.pallas_call(viewed, grid_spec=grid_spec, **settings)(scalars, *arrays)]
    unnamed x94 -> x72, local copies, waits for them, and re-layouts: 17.8 us -> 4.22 us
    pallas_call x4 -> x2, Pallas kernels: 19.1 us -> 7.09 us  [call(): pl.pallas_call(viewed, grid=(blocks,), in_specs=specs, out_specs=out_spec...]
    ppermute x33 -> x28, waiting for transfers between devices: 55.8 us -> 47.6 us  [along(): return lax.ppermute(value, 'dp', [(i, i ^ 1 << bit) for i in range(size)])]
    ppermute x33 -> x28, starting transfers between devices: 35.8 us -> 42 us  [along(): return lax.ppermute(value, 'dp', [(i, i ^ 1 << bit) for i in range(size)])]
    ppermute x17 -> x15, waiting for transfers between devices: 5.12 us -> 9.43 us  [sibling(): return lax.ppermute(value, 'tp', CORE)]
    ppermute x13 -> x12, starting transfers between devices: 14.2 us -> 14.7 us  [across(): return lax.ppermute(value, 'tp', ACROSS)]
  transfers between devices with their start and end apart: 63 -> 55, of which waited for: 28 -> 26; matrix products, arithmetic and copies ran while one was open for 1% -> 0% of each run, Pallas kernels for 44% -> 47%
where the time goes in v4:
time: 330 us; the launch traced here: 324 us
  Pallas kernels  186 us (56%)
  waiting for transfers between devices  68.5 us (21%)
  starting transfers between devices  59.7 us (18%)
  local copies, waits for them, and re-layouts  5.61 us (2%)
    pallas_call x34, Pallas kernels, call(): pl.pallas_call(viewed, grid_spec=grid_spec, **settings)(scalars, *arrays)  179 us
    ppermute x28, waiting for transfers between devices, along(): return lax.ppermute(value, 'dp', [(i, i ^ 1 << bit) for i in range(size)])  47.6 us
    ppermute x28, starting transfers between devices, along(): return lax.ppermute(value, 'dp', [(i, i ^ 1 << bit) for i in range(size)])  42 us
    ppermute x12, starting transfers between devices, across(): return lax.ppermute(value, 'tp', ACROSS)  14.7 us
    ppermute x12, waiting for transfers between devices, across(): return lax.ppermute(value, 'tp', ACROSS)  11.5 us
    ppermute x15, waiting for transfers between devices, sibling(): return lax.ppermute(value, 'tp', CORE)  9.43 us
    pallas_call x2, Pallas kernels, call(): pl.pallas_call(viewed, grid=(blocks,), in_specs=specs, out_specs=out_spec...  7.09 us
  transfers between devices with their start and end apart: 55, of which 26 were waited for; matrix products, arithmetic and copies ran while one was open for 0% of the time, Pallas kernels for 47%

profile of v4, /device:TPU:0, one launch (start us, length us, event | category | flops | bytes accessed | tf_op | source)
XLA Modules:
  0.0 323.7 jit_solution(2466148686793678291)
XLA Ops:
  0.7 2.1 fusion.1
  2.8 2.9 collective-permute-start
  6.5 5.5 %project_own_kernel.1 = (bf16[3,1024,128]{2,1,0:T(8,128)(2,1)S(1)}, bf16[3,1024,128]{2,1,0:T(8,128)(2,1)S(1)}, bf16[3,1024,128]{2,1,0:T(8,128)(2,1)S(1)}, bf16[3...) custom-call(s32[9]{0:T(128)S(1)} %concatenate.6.refs_0_, ...), custom_call_target="tpu_custom_call" | custom-call | flops 2800000000 | tf_op jit(solution)/shard_map/project_own_kernel/pallas_call | solution.py:749
  12.1 4.8 %collective-permute-done.refs_6_.refs_2_ = bf16[288,768]{1,0:T(8,128)(2,1)S(1)} collective-permute-done((bf16[288,768]{1,0:T(8,128)(2,1)}, bf16[288,768]{1,0:T(8,128)(2,1)S(1)}, u32[]{:S(2)}, u32[]{:S(2)}) %collective-permute-start) | collective-permute-done | bytes 442400 | tf_op jit(solution)/shard_map/ppermute | solution.py:772
  16.9 2.1 collective-permute-start.1
  20.6 2.7 collective-permute-done.2.refs_4_
  23.3 2.1 collective-permute-start.3
  25.4 8.8 %self_own_kernel.1 = (bf16[3,1024,128]{2,1,0:T(8,128)(2,1)}, bf16[3,1024,128]{2,1,0:T(8,128)(2,1)}, bf16[3,1024,128]{2,1,0:T(8,128)(2,1)}, bf16[1024,192]{1,0:T(8,128)(2,1)S(1)}, bf16[768,768]{1,0:T(8,128)(2,1)S(1)}) custom-call(s32[9]{0:T(128)S(1)} %concatenate.6.refs_0_, bf16[3,1024,128]{2,1,0:T(8,128)(2,1)S(1)} %get-tuple-element.161.refs_1_, ...), custom_call_target="tpu_custom_call" | custom-call | flops 2400000000 | tf_op jit(solution)/shard_map/self_own_kernel/pallas_call | solution.py:749
  35.7 10.9 %self_other_kernel.1 = (bf16[576,768]{1,0:T(8,128)(2,1)S(1)}, bf16[3,1024,128]{2,1,0:T(8,128)(2,1)}, bf16[3,1024,128]{2,1,0:T(8,128)(2,1)}, bf16[3,1024,128]{2,1,0:T(8,128)(2,1)}, bf16[1024,192]{1,0:T(8,128)(2,1)S(1)}) custom-call(s32[9]{0:T(128)S(1)} %concatenate.6.refs_0_, bf16[2048,768]{1,0:T(8,128)(2,1)} %refs_1_.11, ...), custom_call_target="tpu_custom_call" | custom-call | flops 3600000000 | tf_op jit(solution)/shard_map/self_other_kernel/pallas_call | solution.py:749
  46.7 1.9 self_out_kernel.1
  52.1 9.8 %cross_own_kernel.1 = (f32[1024,768]{1,0:T(8,128)S(1)}, bf16[1024,768]{1,0:T(8,128)(2,1)S(1)}, bf16[1024,768]{1,0:T(8,128)(2,1)S(1)}, f32[1024,1]{1,0:T(8,128)S(...) custom-call(s32[9]{0:T(128)S(1)} %concatenate.6.refs_0_, bf16[2048,768]{1,0:T(8,128)(2,1)} %refs_1_.11, ...), custom_call_target="tpu_custom_call" | custom-call | flops 4000000000 | tf_op jit(solution)/shard_map/cross_own_kernel/pallas_call | solution.py:749
  64.8 10.4 %cross_other_kernel.1 = (bf16[576,768]{1,0:T(8,128)(2,1)S(1)}, bf16[3,1024,128]{2,1,0:T(8,128)(2,1)S(1)}, bf16[3,1024,128]{2,1,0:T(8,128)(2,1)S(1)}, bf16[3,1024...) custom-call(s32[9]{0:T(128)S(1)} %concatenate.6.refs_0_, bf16[2048,768]{1,0:T(8,128)(2,1)} %refs_2_.7, ...), custom_call_target="tpu_custom_call" | custom-call | flops 99999997952 | tf_op jit(solution)/shard_map/cross_other_kernel/pallas_call | solution.py:749
  83.1 5.8 %ffn_own_kernel.1 = (f32[1024,768]{1,0:T(8,128)S(1)}, bf16[1024,768]{1,0:T(8,128)(2,1)S(1)}, bf16[1024,768]{1,0:T(8,128)(2,1)S(1)}, f32[1024,1]{1,0:T(8,128)S(1)...) custom-call(f32[1024,768]{1,0:T(8,128)S(1)} %get-tuple-element.172.refs_0_, ...), custom_call_target="tpu_custom_call" | custom-call | flops 2800000000 | tf_op jit(solution)/shard_map/ffn_own_kernel/pallas_call | solution.py:743
  90.9 5.1 %ffn_other_kernel.1 = (bf16[512,768]{1,0:T(8,128)(2,1)S(1)}, bf16[512,768]{1,0:T(8,128)(2,1)S(1)}, bf16[1024,768]{1,0:T(8,128)(2,1)S(1)}, bf16[1024,768]{1,0:T(8...) custom-call(s32[9]{0:T(128)S(1)} %concatenate.6.refs_0_, ...), custom_call_target="tpu_custom_call" | custom-call | flops 2000000000 | tf_op jit(solution)/shard_map/ffn_other_kernel/pallas_call | solution.py:749
  99.5 12.3 %ffn_back_kernel.1 = (bf16[512,768]{1,0:T(8,128)(2,1)S(1)}, bf16[512,768]{1,0:T(8,128)(2,1)S(1)}, bf16[1024,768]{1,0:T(8,128)(2,1)}, f32[1024,768]{1,0:T(8,128)S...) custom-call(s32[9]{0:T(128)S(1)} %concatenate.6.refs_0_, ...), custom_call_target="tpu_custom_call" | custom-call | flops 4400000000 | tf_op jit(solution)/shard_map/ffn_back_kernel/pallas_call | solution.py:749
  112.3 3.5 %ffn_grad_kernel.2 = (bf16[768,768]{1,0:T(8,128)(2,1)S(1)}, bf16[384,768]{1,0:T(8,128)(2,1)S(1)}, bf16[384,768]{1,0:T(8,128)(2,1)S(1)}) custom-call(s32[9]{0:T(128)S(1)} %concatenate.6.refs_0_, bf16[1024,768]{1,0:T(8,128)(2,1)S(1)} %get-tuple-element.184.refs_1_, bf16[1024,768]{1,0:T(8,128)(2,1)S(1)} %get-tuple-element.210.refs_2_, ...), custom_call_target="tpu_custom_call" | custom-call | flops 1600000000 | tf_op jit(solution)/shard_map/ffn_grad_kernel/pallas_call | solution.py:749
  118.1 3.5 %ffn_grad_kernel.3 = (bf16[768,768]{1,0:T(8,128)(2,1)S(1)}, bf16[384,768]{1,0:T(8,128)(2,1)S(1)}, bf16[384,768]{1,0:T(8,128)(2,1)S(1)}) custom-call(s32[9]{0:T(128)S(1)} %concatenate.6.refs_0_, bf16[1024,768]{1,0:T(8,128)(2,1)S(1)} %get-tuple-element.184.refs_1_, bf16[1024,768]{1,0:T(8,128)(2,1)S(1)} %get-tuple-element.207.refs_2_, ...), custom_call_target="tpu_custom_call" | custom-call | flops 1600000000 | tf_op jit(solution)/shard_map/ffn_grad_kernel/pallas_call | solution.py:749
  122.0 18.4 %cross_back_other_kernel.1 = (f32[1024,768]{1,0:T(8,128)S(1)}, bf16[1024,768]{1,0:T(8,128)(2,1)S(1)}, f32[8,768]{1,0:T(8,128)S(1)}, bf16[3,1024,128]{2,1,0:T(8,1...) custom-call(s32[9]{0:T(128)S(1)} %concatenate.6.refs_0_, ...), custom_call_target="tpu_custom_call" | custom-call | flops 7200000000 | tf_op jit(solution)/shard_map/cross_back_other_kernel/pallas_call | solution.py:749
  140.5 3.6 %collective-permute-done.18.refs_4_ = bf16[384,768]{1,0:T(8,128)(2,1)S(1)} collective-permute-done((bf16[384,768]{1,0:T(8,128)(2,1)S(1)}, bf16[384,768]{1,0:T(8,128)(2,1)S(1)}, u32[]{:S(2)}, u32[]{:S(2)}) %collective-permute-start.18) | collective-permute-done | bytes 589856 | tf_op jit(solution)/shard_map/ppermute | solution.py:778
  149.2 4.5 %cross_grad_kernel.2.refs_8_ = bf16[768,768]{1,0:T(8,128)(2,1)S(1)} custom-call(s32[9]{0:T(128)S(1)} %concatenate.6.refs_0_, bf16[1024,768]{1,0:T(8,128)(2,1)S(1)} %get-tuple-element.174.refs_2_.refs_1_, bf16[2048,768]{1,0:T(8,128)(2,1)} %refs_2_.7, bf16[1024,192]{1,0:T(8,128)(2,1)S(1)} %get-tuple-element.179.refs_1_.refs_12_.refs_3_, ...), custom_call_target="tpu_custom_call" | custom-call | flops 2000000000 | tf_op jit(solution)/shard_map/cross_grad_kernel/pallas_call | solution.py:749
  154.3 12.2 %cross_back_own_kernel.1 = (bf16[512,768]{1,0:T(8,128)(2,1)S(1)}, bf16[512,768]{1,0:T(8,128)(2,1)S(1)}, bf16[1024,192]{1,0:T(8,128)(2,1)S(1)}, bf16[1024,384]{1,0:T(8,128)(2,1)S(1)}) custom-call(s32[9]{0:T(128)S(1)} %concatenate.6.refs_0_, bf16[3,1024,128]{2,1,0:T(8,128)(2,1)S(1)} %copy-done.26, bf16[3,1024,128]{2,1,0:T(8,128)(2,1)S(1)} %copy-done.15, ...), custom_call_target="tpu_custom_call" | custom-call | flops 6400000000 | tf_op jit(solution)/shard_map/cross_back_own_kernel/pallas_call | solution.py:749
  168.4 3.7 %memory_grad_kernel.1 = (bf16[512,768]{1,0:T(8,128)(2,1)S(1)}, bf16[512,768]{1,0:T(8,128)(2,1)S(1)}, bf16[512,768]{1,0:T(8,128)(2,1)S(1)}) custom-call(s32[9]{0:T(128)S(1)} %concatenate.6.refs_0_, bf16[1024,384]{1,0:T(8,128)(2,1)S(1)} %get-tuple-element.219.refs_1_.refs_6_, bf16[1024,384]{1,0:T(8,128)(2,1)S(1)} %get-tuple-element.206.refs_6_.refs_2_, ...), custom_call_target="tpu_custom_call" | custom-call | flops 2000000000 | tf_op jit(solution)/shard_map/memory_grad_kernel/pallas_call | solution.py:749
  172.3 4.2 %cross_grad_kernel.3.refs_15_.refs_3_ = bf16[768,768]{1,0:T(8,128)(2,1)S(1)} custom-call(s32[9]{0:T(128)S(1)} %concatenate.6.refs_0_, bf16[1024,768]{1,0:T(8,128)(2,1)S(1)} %get-tuple-element.174.refs_2_.refs_1_, bf16[2048,768]{1,0:T(8,128)(2,1)} %refs_2_.7, bf16[1024,192]{1,0:T(8,128)(2,1)S(1)} %get-tuple-element.173.refs_0_.refs_11_.refs_3_, ...), custom_call_target="tpu_custom_call" | custom-call | flops 2000000000 | tf_op jit(solution)/shard_map/cross_grad_kernel/pallas_call | solution.py:749
  176.6 2.6 collective-permute-start.22
  179.1 9.9 %norm_one_back_kernel.1 = (f32[1024,768]{1,0:T(8,128)S(1)}, bf16[3,1024,128]{2,1,0:T(8,128)(2,1)S(1)}, bf16[3,1024,128]{2,1,0:T(8,128)(2,1)S(1)}, bf16[208,768]{1,0:T(8,128)(2,1)S(1)}, bf16[208,768]{1,0:T(8,128)(2,1)S(1)}) custom-call(s32[9]{0:T(128)S(1)} %concatenate.6.refs_0_, f32[1024,768]{1,0:T(8,128)S(1)} %get-tuple-element.230.refs_1_, ...), custom_call_target="tpu_custom_call" | custom-call | flops 2400000000 | tf_op jit(solution)/shard_map/norm_one_back_kernel/pallas_call | solution.py:749
  190.9 2.8 collective-permute-start.28
  195.0 12.6 %self_back_kernel.2 = (bf16[1024,576]{1,0:T(8,128)(2,1)S(1)}, bf16[576,768]{1,0:T(8,128)(2,1)S(1)}) custom-call(s32[9]{0:T(128)S(1)} %concatenate.6.refs_0_, bf16[2048,768]{1,0:T(8,128)(2,1)} %refs_1_.11, bf16[3,1024,128]{2,1,0:T(8,128)(2,1)S(1)} %copy-done.27, bf16[3,1024,128]{2,1,0:T(8,128)(2,1)S(1)} %copy-done.28, bf16[3,1024,128]{2,1,0:T(8,128)(2,1)S(1)} %copy-done.29, ...), custom_call_target="tpu_custom_call" | custom-call | flops 5600000000 | tf_op jit(solution)/shard_map/self_back_kernel/pallas_call | solution.py:749
  207.6 3.1 collective-permute-done.30.refs_6_.refs_4_
  215.3 2.6 collective-permute-start.32
  217.9 12.4 %self_back_kernel.3 = (bf16[1024,576]{1,0:T(8,128)(2,1)S(1)}, bf16[576,768]{1,0:T(8,128)(2,1)S(1)}) custom-call(s32[9]{0:T(128)S(1)} %concatenate.6.refs_0_, bf16[2048,768]{1,0:T(8,128)(2,1)} %refs_1_.11, bf16[3,1024,128]{2,1,0:T(8,128)(2,1)S(1)} %copy-done.22, bf16[3,1024,128]{2,1,0:T(8,128)(2,1)S(1)} %copy-done.23, bf16[3,1024,128]{2,1,0:T(8,128)(2,1)S(1)} %copy-done.24, ...), custom_call_target="tpu_custom_call" | custom-call | flops 5600000000 | tf_op jit(solution)/shard_map/self_back_kernel/pallas_call | solution.py:749
  235.2 2.7 collective-permute-start.38
  237.9 3.6 %tokens_grad_kernel.1 = (bf16[512,768]{1,0:T(8,128)(2,1)S(1)}, f32[512,768]{1,0:T(8,128)S(1)}) custom-call(s32[9]{0:T(128)S(1)} %concatenate.6.refs_0_, f32[1024,768]{1,0:T(8,128)S(1)} %get-tuple-element.263.refs_1_, bf16[1024,576]{1,0:T(8,128)(2,1)S(1)} %get-tuple-element.264.refs_2_, bf16[1024,576]{1,0:T(8,128)(2,1)S(1)} %get-tuple-element.250.refs_7_.refs_3_, ...), custom_call_target="tpu_custom_call" | custom-call | flops 2400000000 | tf_op jit(solution)/shard_map/tokens_grad_kernel/pallas_call | solution.py:749
  241.6 8.7 %collective-permute-done.38.refs_6_ = bf16[96,768]{1,0:T(8,128)(2,1)S(1)} collective-permute-done((bf16[96,768]{1,0:T(8,128)(2,1)S(1)}, bf16[96,768]{1,0:T(8,128)(2,1)S(1)}, u32[]{:S(2)}, u32[]{:S(2)}) %collective-permute-start.38) | collective-permute-done | bytes 147488 | tf_op jit(solution)/shard_map/ppermute | solution.py:778
  257.5 8.1 %collective-permute-done.40.refs_4_ = bf16[96,768]{1,0:T(8,128)(2,1)S(1)} collective-permute-done((bf16[96,768]{1,0:T(8,128)(2,1)S(1)}, bf16[96,768]{1,0:T(8,128)(2,1)S(1)}, u32[]{:S(2)}, u32[]{:S(2)}) %collective-permute-start.40) | collective-permute-done | bytes 147488 | tf_op jit(solution)/shard_map/ppermute | solution.py:778
  267.0 1.9 collective-permute-start.43
  270.6 2.9 place_kernel.3
  273.5 4.5 %collective-permute-done.41.refs_2_ = bf16[96,768]{1,0:T(8,128)(2,1)S(1)} collective-permute-done((bf16[96,768]{1,0:T(8,128)(2,1)S(1)}, bf16[96,768]{1,0:T(8,128)(2,1)S(1)}, u32[]{:S(2)}, u32[]{:S(2)}) %collective-permute-start.41) | collective-permute-done | bytes 147488 | tf_op jit(solution)/shard_map/ppermute | solution.py:778
  278.7 3.1 step_kernel.18
  284.8 2.6 collective-permute-start.46
  288.0 3.7 %collective-permute-done.47.refs_4_ = f32[16,768]{1,0:T(8,128)S(1)} collective-permute-done((f32[16,768]{1,0:T(8,128)S(1)}, f32[16,768]{1,0:T(8,128)S(1)}, u32[]{:S(2)}, u32[]{:S(2)}) %collective-permute-start.47) | collective-permute-done | bytes 49184 | tf_op jit(solution)/shard_map/ppermute | solution.py:778
  291.7 2.9 collective-permute-done.46.refs_2_
  295.2 3.1 collective-permute-start.52
  298.4 2.7 place_kernel.4
  303.6 2.1 step_kernel.20
  306.8 2.3 collective-permute-done.53.refs_2_
  309.1 2.7 place_kernel.5
  311.8 9.6 %collective-permute-done.54.refs_2_ = bf16[384,768]{1,0:T(8,128)(2,1)S(1)} collective-permute-done((bf16[384,768]{1,0:T(8,128)(2,1)S(1)}, bf16[384,768]{1,0:T(8,128)(2,1)S(1)}, u32[]{:S(2)}, u32[]{:S(2)}) %collective-permute-start.54) | collective-permute-done | bytes 589856 | tf_op jit(solution)/shard_map/ppermute | solution.py:778
  321.5 2.1 step_kernel.21
  (173 shorter events, 65.9 us)
Async XLA Ops:
  2.8 14.1 %collective-permute-start = (bf16[288,768]{1,0:T(8,128)(2,1)}, bf16[288,768]{1,0:T(8,128)(2,1)S(1)}, u32[]{:S(2)}, u32[]{:S(2)}) collective-permute-start(bf16[288,768]{1,0:T(8,128)(2,1)} %fusion.1), channel_id=1, source_target_pairs={{0,16},{16,0},{8,24},{24,8},{1,17},{17,1},{9,25},{25,9},{2,18},{18... | collective-permute-start | bytes 1327112 | tf_op jit(solution)/shard_map/ppermute | solution.py:772
  12.0 11.2 %collective-permute-start.2 = (bf16[192,768]{1,0:T(8,128)(2,1)S(1)}, bf16[192,768]{1,0:T(8,128)(2,1)S(1)}, u32[]{:S(2)}, u32[]{:S(2)}) collective-permute-start(bf16[192,768]{1,0:T(8,128)(2,1)S(1)} %get-tuple-element.165), channel_id=1, source_target_pairs={{0,16},{16,0},{8,24},{24,8},{1,17},{17,1},{9,25},{25,9},{2,18},{18... | collective-permute-start | bytes 884744 | tf_op jit(solution)/shard_map/ppermute | solution.py:772
  16.9 18.7 %collective-permute-start.1 = (bf16[288,768]{1,0:T(8,128)(2,1)S(1)}, bf16[288,768]{1,0:T(8,128)(2,1)S(1)}, u32[]{:S(2)}, u32[]{:S(2)}) collective-permute-start(bf16[288,768]{1,0:T(8,128)(2,1)S(1)} %collective-permute-done.refs_6_.refs_2_), channel_id=1, source_target_pairs={{0,1},{1,0},{2,3},{3,2},{4,5},{5,4},{6,7},{7,6},{8,9},{9,8},{10,11... | collective-permute-start | bytes 1327112 | tf_op jit(solution)/shard_map/ppermute | solution.py:778
  19.1 27.5 %collective-permute-start.4 = (bf16[288,768]{1,0:T(8,128)(2,1)S(1)}, bf16[288,768]{1,0:T(8,128)(2,1)S(1)}, u32[]{:S(2)}, u32[]{:S(2)}) collective-permute-start(bf16[288,768]{1,0:T(8,128)(2,1)S(1)} %get-tuple-element.167), channel_id=1, source_target_pairs={{0,16},{16,0},{8,24},{24,8},{1,17},{17,1},{9,25},{25,9},{2,18},{18... | collective-permute-start | bytes 1327112 | tf_op jit(solution)/shard_map/ppermute | solution.py:772
  23.3 23.4 %collective-permute-start.3 = (bf16[192,768]{1,0:T(8,128)(2,1)S(1)}, bf16[192,768]{1,0:T(8,128)(2,1)S(1)}, u32[]{:S(2)}, u32[]{:S(2)}) collective-permute-start(bf16[192,768]{1,0:T(8,128)(2,1)S(1)} %collective-permute-done.2.refs_4_), channel_id=1, source_target_pairs={{0,1},{1,0},{2,3},{3,2},{4,5},{5,4},{6,7},{7,6},{8,9},{9,8},{10,11... | collective-permute-start | bytes 884744 | tf_op jit(solution)/shard_map/ppermute | solution.py:778
  34.2 27.7 %collective-permute-start.8 = (bf16[768,768]{1,0:T(8,128)(2,1)S(1)}, bf16[768,768]{1,0:T(8,128)(2,1)S(1)}, u32[]{:S(2)}, u32[]{:S(2)}) collective-permute-start(bf16[768,768]{1,0:T(8,128)(2,1)S(1)} %get-tuple-element.175), channel_id=1, source_target_pairs={{0,16},{16,0},{8,24},{24,8},{1,17},{17,1},{9,25},{25,9},{2,18},{18... | collective-permute-start | bytes 3538952 | tf_op jit(solution)/shard_map/ppermute | solution.py:772
  49.1 15.6 %collective-permute-start.7 = (bf16[288,768]{1,0:T(8,128)(2,1)S(1)}, bf16[288,768]{1,0:T(8,128)(2,1)S(1)}, u32[]{:S(2)}, u32[]{:S(2)}) collective-permute-start(bf16[288,768]{1,0:T(8,128)(2,1)S(1)} %collective-permute-done.4.refs_6_.refs_3_), channel_id=1, source_target_pairs={{0,2},{1,3},{2,0},{3,1},{4,6},{5,7},{6,4},{7,5},{8,10},{9,11},{10,... | collective-permute-start | bytes 1327112 | tf_op jit(solution)/shard_map/ppermute | solution.py:778
  62.8 15.4 %collective-permute-start.9 = (bf16[384,768]{1,0:T(8,128)(2,1)S(1)}, bf16[384,768]{1,0:T(8,128)(2,1)S(1)}, u32[]{:S(2)}, u32[]{:S(2)}) collective-permute-start(bf16[384,768]{1,0:T(8,128)(2,1)S(1)} %get-tuple-element.177.refs_5_.refs_3_), channel_id=1, source_target_pairs={{0,1},{1,0},{2,3},{3,2},{4,5},{5,4},{6,7},{7,6},{8,9},{9,8},{10,11... | collective-permute-start | bytes 1769480 | tf_op jit(solution)/shard_map/ppermute | solution.py:778
  63.2 15.1 %collective-permute-start.10 = (bf16[384,768]{1,0:T(8,128)(2,1)S(1)}, bf16[384,768]{1,0:T(8,128)(2,1)S(1)}, u32[]{:S(2)}, u32[]{:S(2)}) collective-permute-start(bf16[384,768]{1,0:T(8,128)(2,1)S(1)} %get-tuple-element.178.refs_6_.refs_5_), channel_id=1, source_target_pairs={{0,2},{1,3},{2,0},{3,1},{4,6},{5,7},{6,4},{7,5},{8,10},{9,11},{10,... | collective-permute-start | bytes 1769480 | tf_op jit(solution)/shard_map/ppermute | solution.py:778
  111.8 10.2 %collective-permute-start.15 = (bf16[512,768]{1,0:T(8,128)(2,1)S(1)}, bf16[512,768]{1,0:T(8,128)(2,1)S(1)}, u32[]{:S(2)}, u32[]{:S(2)}) collective-permute-start(bf16[512,768]{1,0:T(8,128)(2,1)S(1)} %get-tuple-element.195.refs_2_), channel_id=1, source_target_pairs={{0,8},{8,0},{16,24},{24,16},{1,9},{9,1},{17,25},{25,17},{2,10},{10... | collective-permute-start | bytes 2359304 | tf_op jit(solution)/shard_map/ppermute | solution.py:775
  112.0 10.0 %collective-permute-start.16 = (bf16[512,768]{1,0:T(8,128)(2,1)S(1)}, bf16[512,768]{1,0:T(8,128)(2,1)S(1)}, u32[]{:S(2)}, u32[]{:S(2)}) collective-permute-start(bf16[512,768]{1,0:T(8,128)(2,1)S(1)} %get-tuple-element.196.refs_3_), channel_id=1, source_target_pairs={{0,8},{8,0},{16,24},{24,16},{1,9},{9,1},{17,25},{25,17},{2,10},{10... | collective-permute-start | bytes 2359304 | tf_op jit(solution)/shard_map/ppermute | solution.py:775
  115.9 28.2 %collective-permute-start.17 = (bf16[768,768]{1,0:T(8,128)(2,1)S(1)}, bf16[768,768]{1,0:T(8,128)(2,1)S(1)}, u32[]{:S(2)}, u32[]{:S(2)}) collective-permute-start(bf16[768,768]{1,0:T(8,128)(2,1)S(1)} %get-tuple-element.214), channel_id=1, source_target_pairs={{0,16},{16,0},{8,24},{24,8},{1,17},{17,1},{9,25},{25,9},{2,18},{18... | collective-permute-start | bytes 3538952 | tf_op jit(solution)/shard_map/ppermute | solution.py:772
  116.3 27.7 %collective-permute-start.19 = (bf16[384,768]{1,0:T(8,128)(2,1)S(1)}, bf16[384,768]{1,0:T(8,128)(2,1)S(1)}, u32[]{:S(2)}, u32[]{:S(2)}) collective-permute-start(bf16[384,768]{1,0:T(8,128)(2,1)S(1)} %get-tuple-element.212.refs_5_), channel_id=1, source_target_pairs={{0,1},{1,0},{2,3},{3,2},{4,5},{5,4},{6,7},{7,6},{8,9},{9,8},{10,11... | collective-permute-start | bytes 1769480 | tf_op jit(solution)/shard_map/ppermute | solution.py:778
  121.6 22.4 %collective-permute-start.18 = (bf16[384,768]{1,0:T(8,128)(2,1)S(1)}, bf16[384,768]{1,0:T(8,128)(2,1)S(1)}, u32[]{:S(2)}, u32[]{:S(2)}) collective-permute-start(bf16[384,768]{1,0:T(8,128)(2,1)S(1)} %get-tuple-element.216), channel_id=1, source_target_pairs={{0,1},{1,0},{2,3},{3,2},{4,5},{5,4},{6,7},{7,6},{8,9},{9,8},{10,11... | collective-permute-start | bytes 1769480 | tf_op jit(solution)/shard_map/ppermute | solution.py:778
  145.9 21.2 %collective-permute-start.20 = (bf16[384,768]{1,0:T(8,128)(2,1)S(1)}, bf16[384,768]{1,0:T(8,128)(2,1)S(1)}, u32[]{:S(2)}, u32[]{:S(2)}) collective-permute-start(bf16[384,768]{1,0:T(8,128)(2,1)S(1)} %get-tuple-element.222), channel_id=1, source_target_pairs={{0,1},{1,0},{2,3},{3,2},{4,5},{5,4},{6,7},{7,6},{8,9},{9,8},{10,11... | collective-permute-start | bytes 1769480 | tf_op jit(solution)/shard_map/ppermute | solution.py:778
  147.7 19.4 %collective-permute-start.21 = (bf16[384,768]{1,0:T(8,128)(2,1)S(1)}, bf16[384,768]{1,0:T(8,128)(2,1)S(1)}, u32[]{:S(2)}, u32[]{:S(2)}) collective-permute-start(bf16[384,768]{1,0:T(8,128)(2,1)S(1)} %get-tuple-element.223), channel_id=1, source_target_pairs={{0,16},{16,0},{8,24},{24,8},{1,17},{17,1},{9,25},{25,9},{2,18},{18... | collective-permute-start | bytes 1769480 | tf_op jit(solution)/shard_map/ppermute | solution.py:772
  153.7 35.6 %collective-permute-start.27 = (bf16[768,768]{1,0:T(8,128)(2,1)S(1)}, bf16[768,768]{1,0:T(8,128)(2,1)S(1)}, u32[]{:S(2)}, u32[]{:S(2)}) collective-permute-start(bf16[768,768]{1,0:T(8,128)(2,1)S(1)} %cross_grad_kernel.2.refs_8_), channel_id=1, source_target_pairs={{0,16},{16,0},{8,24},{24,8},{1,17},{17,1},{9,25},{25,9},{2,18},{18... | collective-permute-start | bytes 3538952 | tf_op jit(solution)/shard_map/ppermute | solution.py:772
  166.6 10.0 %collective-permute-start.24 = (bf16[512,768]{1,0:T(8,128)(2,1)S(1)}, bf16[512,768]{1,0:T(8,128)(2,1)S(1)}, u32[]{:S(2)}, u32[]{:S(2)}) collective-permute-start(bf16[512,768]{1,0:T(8,128)(2,1)S(1)} %get-tuple-element.231.refs_2_), channel_id=1, source_target_pairs={{0,8},{8,0},{16,24},{24,16},{1,9},{9,1},{17,25},{25,17},{2,10},{10... | collective-permute-start | bytes 2359304 | tf_op jit(solution)/shard_map/ppermute | solution.py:775
  166.6 12.5 %collective-permute-start.25 = (bf16[512,768]{1,0:T(8,128)(2,1)S(1)}, bf16[512,768]{1,0:T(8,128)(2,1)S(1)}, u32[]{:S(2)}, u32[]{:S(2)}) collective-permute-start(bf16[512,768]{1,0:T(8,128)(2,1)S(1)} %get-tuple-element.232.refs_3_), channel_id=1, source_target_pairs={{0,8},{8,0},{16,24},{24,16},{1,9},{9,1},{17,25},{25,17},{2,10},{10... | collective-permute-start | bytes 2359304 | tf_op jit(solution)/shard_map/ppermute | solution.py:775
  168.4 20.8 %collective-permute-start.26 = (bf16[384,768]{1,0:T(8,128)(2,1)S(1)}, bf16[384,768]{1,0:T(8,128)(2,1)S(1)}, u32[]{:S(2)}, u32[]{:S(2)}) collective-permute-start(bf16[384,768]{1,0:T(8,128)(2,1)S(1)} %get-tuple-element.239), channel_id=1, source_target_pairs={{0,2},{1,3},{2,0},{3,1},{4,6},{5,7},{6,4},{7,5},{8,10},{9,11},{10,... | collective-permute-start | bytes 1769480 | tf_op jit(solution)/shard_map/ppermute | solution.py:778
  172.2 43.1 %collective-permute-start.34 = (bf16[512,768]{1,0:T(8,128)(2,1)S(1)}, bf16[512,768]{1,0:T(8,128)(2,1)S(1)}, u32[]{:S(2)}, u32[]{:S(2)}) collective-permute-start(bf16[512,768]{1,0:T(8,128)(2,1)S(1)} %get-tuple-element.237.refs_7_), channel_id=1, source_target_pairs={{0,8},{8,0},{16,24},{24,16},{1,9},{9,1},{17,25},{25,17},{2,10},{10... | collective-permute-start | bytes 2359304 | tf_op jit(solution)/shard_map/ppermute | solution.py:775
  176.6 35.6 %collective-permute-start.22 = (bf16[512,768]{1,0:T(8,128)(2,1)S(1)}, bf16[512,768]{1,0:T(8,128)(2,1)S(1)}, u32[]{:S(2)}, u32[]{:S(2)}) collective-permute-start(bf16[512,768]{1,0:T(8,128)(2,1)S(1)} %get-tuple-element.226), channel_id=1, source_target_pairs={{0,16},{16,0},{8,24},{24,8},{1,17},{17,1},{9,25},{25,9},{2,18},{18... | collective-permute-start | bytes 2359304 | tf_op jit(solution)/shard_map/ppermute | solution.py:772
  189.0 21.7 %collective-permute-start.30 = (bf16[208,768]{1,0:T(8,128)(2,1)S(1)}, bf16[208,768]{1,0:T(8,128)(2,1)S(1)}, u32[]{:S(2)}, u32[]{:S(2)}) collective-permute-start(bf16[208,768]{1,0:T(8,128)(2,1)S(1)} %get-tuple-element.246), channel_id=1, source_target_pairs={{0,16},{16,0},{8,24},{24,8},{1,17},{17,1},{9,25},{25,9},{2,18},{18... | collective-permute-start | bytes 958472 | tf_op jit(solution)/shard_map/ppermute | solution.py:772
  190.9 21.3 %collective-permute-start.28 = (bf16[192,768]{1,0:T(8,128)(2,1)S(1)}, bf16[192,768]{1,0:T(8,128)(2,1)S(1)}, u32[]{:S(2)}, u32[]{:S(2)}) collective-permute-start(bf16[192,768]{1,0:T(8,128)(2,1)S(1)} %get-tuple-element.242), channel_id=1, source_target_pairs={{0,4},{1,5},{2,6},{3,7},{4,0},{5,1},{6,2},{7,3},{8,12},{9,13},{10,... | collective-permute-start | bytes 884744 | tf_op jit(solution)/shard_map/ppermute | solution.py:778
  193.7 18.5 %collective-permute-start.29 = (bf16[384,768]{1,0:T(8,128)(2,1)S(1)}, bf16[384,768]{1,0:T(8,128)(2,1)S(1)}, u32[]{:S(2)}, u32[]{:S(2)}) collective-permute-start(bf16[384,768]{1,0:T(8,128)(2,1)S(1)} %get-tuple-element.244), channel_id=1, source_target_pairs={{0,1},{1,0},{2,3},{3,2},{4,5},{5,4},{6,7},{7,6},{8,9},{9,8},{10,11... | collective-permute-start | bytes 1769480 | tf_op jit(solution)/shard_map/ppermute | solution.py:778
  210.7 20.7 %collective-permute-start.31 = (bf16[576,768]{1,0:T(8,128)(2,1)S(1)}, bf16[576,768]{1,0:T(8,128)(2,1)S(1)}, u32[]{:S(2)}, u32[]{:S(2)}) collective-permute-start(bf16[576,768]{1,0:T(8,128)(2,1)S(1)} %get-tuple-element.253), channel_id=1, source_target_pairs={{0,16},{16,0},{8,24},{24,8},{1,17},{17,1},{9,25},{25,9},{2,18},{18... | collective-permute-start | bytes 2654216 | tf_op jit(solution)/shard_map/ppermute | solution.py:772
  212.1 29.4 %collective-permute-start.23 = (bf16[512,768]{1,0:T(8,128)(2,1)S(1)}, bf16[512,768]{1,0:T(8,128)(2,1)S(1)}, u32[]{:S(2)}, u32[]{:S(2)}) collective-permute-start(bf16[512,768]{1,0:T(8,128)(2,1)S(1)} %collective-permute-done.22.refs_2_), channel_id=1, source_target_pairs={{0,8},{8,0},{16,24},{24,16},{1,9},{9,1},{17,25},{25,17},{2,10},{10... | collective-permute-start | bytes 2359304 | tf_op jit(solution)/shard_map/ppermute | solution.py:775
  213.2 17.1 %collective-permute-start.35 = (f32[16,768]{1,0:T(8,128)S(1)}, f32[16,768]{1,0:T(8,128)S(1)}, u32[]{:S(2)}, u32[]{:S(2)}) collective-permute-start(f32[16,768]{1,0:T(8,128)S(1)} %get-tuple-element.257.refs_11_), channel_id=1, source_target_pairs={{0,1},{1,0},{2,3},{3,2},{4,5},{5,4},{6,7},{7,6},{8,9},{9,8},{10,11... | collective-permute-start | bytes 147464 | tf_op jit(solution)/shard_map/ppermute | solution.py:778
  213.8 16.6 %collective-permute-start.33 = (bf16[192,768]{1,0:T(8,128)(2,1)S(1)}, bf16[192,768]{1,0:T(8,128)(2,1)S(1)}, u32[]{:S(2)}, u32[]{:S(2)}) collective-permute-start(bf16[192,768]{1,0:T(8,128)(2,1)S(1)} %get-tuple-element.255), channel_id=1, source_target_pairs={{0,2},{1,3},{2,0},{3,1},{4,6},{5,7},{6,4},{7,5},{8,10},{9,11},{10,... | collective-permute-start | bytes 884744 | tf_op jit(solution)/shard_map/ppermute | solution.py:778
  215.3 16.1 %collective-permute-start.32 = (bf16[192,768]{1,0:T(8,128)(2,1)S(1)}, bf16[192,768]{1,0:T(8,128)(2,1)S(1)}, u32[]{:S(2)}, u32[]{:S(2)}) collective-permute-start(bf16[192,768]{1,0:T(8,128)(2,1)S(1)} %get-tuple-element.251.refs_6_.refs_5_), channel_id=1, source_target_pairs={{0,4},{1,5},{2,6},{3,7},{4,0},{5,1},{6,2},{7,3},{8,12},{9,13},{10,... | collective-permute-start | bytes 884744 | tf_op jit(solution)/shard_map/ppermute | solution.py:778
  233.3 17.0 %collective-permute-start.36 = (bf16[384,768]{1,0:T(8,128)(2,1)S(1)}, bf16[384,768]{1,0:T(8,128)(2,1)S(1)}, u32[]{:S(2)}, u32[]{:S(2)}) collective-permute-start(bf16[384,768]{1,0:T(8,128)(2,1)S(1)} %get-tuple-element.259), channel_id=1, source_target_pairs={{0,1},{1,0},{2,3},{3,2},{4,5},{5,4},{6,7},{7,6},{8,9},{9,8},{10,11... | collective-permute-start | bytes 1769480 | tf_op jit(solution)/shard_map/ppermute | solution.py:778
  233.3 17.8 %collective-permute-start.37 = (bf16[384,768]{1,0:T(8,128)(2,1)S(1)}, bf16[384,768]{1,0:T(8,128)(2,1)S(1)}, u32[]{:S(2)}, u32[]{:S(2)}) collective-permute-start(bf16[384,768]{1,0:T(8,128)(2,1)S(1)} %get-tuple-element.260.refs_3_), channel_id=1, source_target_pairs={{0,2},{1,3},{2,0},{3,1},{4,6},{5,7},{6,4},{7,5},{8,10},{9,11},{10,... | collective-permute-start | bytes 1769480 | tf_op jit(solution)/shard_map/ppermute | solution.py:778
  235.2 15.0 %collective-permute-start.38 = (bf16[96,768]{1,0:T(8,128)(2,1)S(1)}, bf16[96,768]{1,0:T(8,128)(2,1)S(1)}, u32[]{:S(2)}, u32[]{:S(2)}) collective-permute-start(bf16[96,768]{1,0:T(8,128)(2,1)S(1)} %get-tuple-element.262), channel_id=1, source_target_pairs={{0,4},{1,5},{2,6},{3,7},{4,0},{5,1},{6,2},{7,3},{8,12},{9,13},{10,... | collective-permute-start | bytes 442376 | tf_op jit(solution)/shard_map/ppermute | solution.py:778
  252.1 26.6 %collective-permute-start.42 = (bf16[768,768]{1,0:T(8,128)(2,1)S(1)}, bf16[768,768]{1,0:T(8,128)(2,1)S(1)}, u32[]{:S(2)}, u32[]{:S(2)}) collective-permute-start(bf16[768,768]{1,0:T(8,128)(2,1)S(1)} %get-tuple-element.274.refs_3_), channel_id=1, source_target_pairs={{0,1},{1,0},{2,3},{3,2},{4,5},{5,4},{6,7},{7,6},{8,9},{9,8},{10,11... | collective-permute-start | bytes 3538952 | tf_op jit(solution)/shard_map/ppermute | solution.py:778
  253.1 20.4 %collective-permute-start.44 = (bf16[512,768]{1,0:T(8,128)(2,1)S(1)}, bf16[512,768]{1,0:T(8,128)(2,1)S(1)}, u32[]{:S(2)}, u32[]{:S(2)}) collective-permute-start(bf16[512,768]{1,0:T(8,128)(2,1)S(1)} %get-tuple-element.267.refs_7_), channel_id=1, source_target_pairs={{0,8},{8,0},{16,24},{24,16},{1,9},{9,1},{17,25},{25,17},{2,10},{10... | collective-permute-start | bytes 2359304 | tf_op jit(solution)/shard_map/ppermute | solution.py:775
  253.1 20.4 %collective-permute-start.45 = (bf16[512,768]{1,0:T(8,128)(2,1)S(1)}, bf16[512,768]{1,0:T(8,128)(2,1)S(1)}, u32[]{:S(2)}, u32[]{:S(2)}) collective-permute-start(bf16[512,768]{1,0:T(8,128)(2,1)S(1)} %get-tuple-element.277.refs_9_), channel_id=1, source_target_pairs={{0,16},{16,0},{8,24},{24,8},{1,17},{17,1},{9,25},{25,9},{2,18},{18... | collective-permute-start | bytes 2359304 | tf_op jit(solution)/shard_map/ppermute | solution.py:772
  253.9 12.4 %collective-permute-start.39 = (bf16[192,768]{1,0:T(8,128)(2,1)S(1)}, bf16[192,768]{1,0:T(8,128)(2,1)S(1)}, u32[]{:S(2)}, u32[]{:S(2)}) collective-permute-start(bf16[192,768]{1,0:T(8,128)(2,1)S(1)} %get-tuple-element.269), channel_id=1, source_target_pairs={{0,2},{1,3},{2,0},{3,1},{4,6},{5,7},{6,4},{7,5},{8,10},{9,11},{10,... | collective-permute-start | bytes 884744 | tf_op jit(solution)/shard_map/ppermute | solution.py:778
  255.7 9.8 %collective-permute-start.40 = (bf16[96,768]{1,0:T(8,128)(2,1)S(1)}, bf16[96,768]{1,0:T(8,128)(2,1)S(1)}, u32[]{:S(2)}, u32[]{:S(2)}) collective-permute-start(bf16[96,768]{1,0:T(8,128)(2,1)S(1)} %get-tuple-element.270.refs_3_), channel_id=1, source_target_pairs={{0,4},{1,5},{2,6},{3,7},{4,0},{5,1},{6,2},{7,3},{8,12},{9,13},{10,... | collective-permute-start | bytes 442376 | tf_op jit(solution)/shard_map/ppermute | solution.py:778
  267.0 11.7 %collective-permute-start.43 = (bf16[192,768]{1,0:T(8,128)(2,1)S(1)}, bf16[192,768]{1,0:T(8,128)(2,1)S(1)}, u32[]{:S(2)}, u32[]{:S(2)}) collective-permute-start(bf16[192,768]{1,0:T(8,128)(2,1)S(1)} %get-tuple-element.275.refs_5_), channel_id=1, source_target_pairs={{0,2},{1,3},{2,0},{3,1},{4,6},{5,7},{6,4},{7,5},{8,10},{9,11},{10,... | collective-permute-start | bytes 884744 | tf_op jit(solution)/shard_map/ppermute | solution.py:778
  269.0 9.0 %collective-permute-start.41 = (bf16[96,768]{1,0:T(8,128)(2,1)S(1)}, bf16[96,768]{1,0:T(8,128)(2,1)S(1)}, u32[]{:S(2)}, u32[]{:S(2)}) collective-permute-start(bf16[96,768]{1,0:T(8,128)(2,1)S(1)} %get-tuple-element.273), channel_id=1, source_target_pairs={{0,4},{1,5},{2,6},{3,7},{4,0},{5,1},{6,2},{7,3},{8,12},{9,13},{10,... | collective-permute-start | bytes 442376 | tf_op jit(solution)/shard_map/ppermute | solution.py:778
  281.8 12.8 %collective-permute-start.48 = (bf16[1024,768]{1,0:T(8,128)(2,1)S(1)}, bf16[1024,768]{1,0:T(8,128)(2,1)S(1)}, u32[]{:S(2)}, u32[]{:S(2)}) collective-permute-start(bf16[1024,768]{1,0:T(8,128)(2,1)S(1)} %get-tuple-element.281.refs_1_), channel_id=1, source_target_pairs={{0,8},{8,0},{16,24},{24,16},{1,9},{9,1},{17,25},{25,17},{2,10},{10... | collective-permute-start | bytes 4718600 | tf_op jit(solution)/shard_map/ppermute | solution.py:775
  281.8 20.0 %collective-permute-start.51 = (bf16[512,768]{1,0:T(8,128)(2,1)S(1)}, bf16[512,768]{1,0:T(8,128)(2,1)S(1)}, u32[]{:S(2)}, u32[]{:S(2)}) collective-permute-start(bf16[512,768]{1,0:T(8,128)(2,1)S(1)} %get-tuple-element.284.refs_5_), channel_id=1, source_target_pairs={{0,16},{16,0},{8,24},{24,8},{1,17},{17,1},{9,25},{25,9},{2,18},{18... | collective-permute-start | bytes 2359304 | tf_op jit(solution)/shard_map/ppermute | solution.py:772
  283.1 18.0 %collective-permute-start.50 = (bf16[384,768]{1,0:T(8,128)(2,1)S(1)}, bf16[384,768]{1,0:T(8,128)(2,1)S(1)}, u32[]{:S(2)}, u32[]{:S(2)}) collective-permute-start(bf16[384,768]{1,0:T(8,128)(2,1)S(1)} %get-tuple-element.283.refs_3_), channel_id=1, source_target_pairs={{0,1},{1,0},{2,3},{3,2},{4,5},{5,4},{6,7},{7,6},{8,9},{9,8},{10,11... | collective-permute-start | bytes 1769480 | tf_op jit(solution)/shard_map/ppermute | solution.py:778
  284.8 9.8 %collective-permute-start.46 = (bf16[96,768]{1,0:T(8,128)(2,1)S(1)}, bf16[96,768]{1,0:T(8,128)(2,1)S(1)}, u32[]{:S(2)}, u32[]{:S(2)}) collective-permute-start(bf16[96,768]{1,0:T(8,128)(2,1)S(1)} %get-tuple-element.279.refs_1_.refs_5_), channel_id=1, source_target_pairs={{0,4},{1,5},{2,6},{3,7},{4,0},{5,1},{6,2},{7,3},{8,12},{9,13},{10,... | collective-permute-start | bytes 442376 | tf_op jit(solution)/shard_map/ppermute | solution.py:778
  287.4 4.3 %collective-permute-start.47 = (f32[16,768]{1,0:T(8,128)S(1)}, f32[16,768]{1,0:T(8,128)S(1)}, u32[]{:S(2)}, u32[]{:S(2)}) collective-permute-start(f32[16,768]{1,0:T(8,128)S(1)} %get-tuple-element.280.refs_3_), channel_id=1, source_target_pairs={{0,2},{1,3},{2,0},{3,1},{4,6},{5,7},{6,4},{7,5},{8,10},{9,11},{10,... | collective-permute-start | bytes 147464 | tf_op jit(solution)/shard_map/ppermute | solution.py:778
  295.2 8.5 %collective-permute-start.49 = (bf16[192,768]{1,0:T(8,128)(2,1)S(1)}, bf16[192,768]{1,0:T(8,128)(2,1)S(1)}, u32[]{:S(2)}, u32[]{:S(2)}) collective-permute-start(bf16[192,768]{1,0:T(8,128)(2,1)S(1)} %get-tuple-element.282.refs_3_.refs_1_), channel_id=1, source_target_pairs={{0,2},{1,3},{2,0},{3,1},{4,6},{5,7},{6,4},{7,5},{8,10},{9,11},{10,... | collective-permute-start | bytes 884744 | tf_op jit(solution)/shard_map/ppermute | solution.py:778
  295.2 6.5 %collective-permute-start.52 = (f32[16,768]{1,0:T(8,128)S(1)}, f32[16,768]{1,0:T(8,128)S(1)}, u32[]{:S(2)}, u32[]{:S(2)}) collective-permute-start(f32[16,768]{1,0:T(8,128)S(1)} %get-tuple-element.285.refs_7_), channel_id=1, source_target_pairs={{0,4},{1,5},{2,6},{3,7},{4,0},{5,1},{6,2},{7,3},{8,12},{9,13},{10,... | collective-permute-start | bytes 147464 | tf_op jit(solution)/shard_map/ppermute | solution.py:778
  305.7 15.7 %collective-permute-start.54 = (bf16[384,768]{1,0:T(8,128)(2,1)S(1)}, bf16[384,768]{1,0:T(8,128)(2,1)S(1)}, u32[]{:S(2)}, u32[]{:S(2)}) collective-permute-start(bf16[384,768]{1,0:T(8,128)(2,1)S(1)} %get-tuple-element.288.refs_3_.refs_1_), channel_id=1, source_target_pairs={{0,1},{1,0},{2,3},{3,2},{4,5},{5,4},{6,7},{7,6},{8,9},{9,8},{10,11... | collective-permute-start | bytes 1769480 | tf_op jit(solution)/shard_map/ppermute | solution.py:778
  (43 other events, 290.4 us)

commit v5 on v4

--- a/solution.py
+++ b/solution.py
@@ -23,7 +23,7 @@
 
 ROWS, WHOLE, COLUMNS, HALF, PART, SKIP, ARBITRARY = "rows", "whole", "columns", "half", "part", "skip", "arbitrary"
 HELD_ROWS, HELD_WHOLE, FAR_ROWS, FAR_WHOLE = "held rows", "held whole", "hbm rows", "hbm whole"
-SUM, PACK, WIDEN, STACK, LAST = "sum", "pack", "wide", "stack", "last"
+SUM, PACK, WIDEN, STACK, LAST, PASS = "sum", "pack", "wide", "stack", "last", "pass"
 
 
 def nn(left, right):
@@ -68,7 +68,7 @@
         v_ref[h, rows, :] = jnp.concatenate([v, ones], 1).astype(bf16)
 
 
-def attend_block(q_ref, k_ref, v_ref, att_ref, h, column, rows, count, key_end, causal):
+def attend_block(q_ref, k_ref, v_ref, att_ref, h, rows, count, key_end, causal):
     s = nt(q_ref[h, rows, :], k_ref[h, :key_end, :])
     if causal:
         r = lax.broadcasted_iota(jnp.int32, (count, count), 0)
@@ -79,7 +79,8 @@
     p = jnp.exp2(s - peak).astype(bf16)
     o = nn(p, v_ref[h, :key_end, :])
     total = o[:, HEAD_DIM : HEAD_DIM + 1]
-    att_ref[rows, column : column + HEAD_DIM] = (o[:, :HEAD_DIM] / total).astype(bf16)
+    mixed = (o / total).astype(bf16)
+    att_ref[rows, h * WIDE : (h + 1) * WIDE] = mixed
     high, middle, low = three_parts(-(peak + jnp.log2(total)))
     lane = lanes(count)
     tail = jnp.where(
@@ -88,18 +89,29 @@
     q_ref[h, rows, HEAD_DIM:] = tail.astype(bf16)
 
 
-def fill_grads(do_ref, rows, count, grad, att, heads):
-    lane = lanes(count)
+def widen_out(wide_ref, out_ref, heads):
+    wide_ref[...] = jnp.zeros_like(wide_ref)
     for h in range(heads):
-        part = grad[:, h * HEAD_DIM : (h + 1) * HEAD_DIM].astype(bf16)
-        mixed = att[:, h * HEAD_DIM : (h + 1) * HEAD_DIM].astype(f32)
-        inner = jnp.sum(part.astype(f32) * mixed, 1, keepdims=True)
-        high, middle, low = three_parts(-inner)
-        tail = jnp.where(lane == 0, high, jnp.where(lane == 1, middle, jnp.where(lane == 2, low, 0.0)))
-        do_ref[h, rows, :] = jnp.concatenate([part, tail.astype(bf16)], 1)
-
-
-def back_block(q_ref, k_ref, v_ref, do_ref, dq_ref, dk_ref, dv_ref, h, rows, count, key_end, causal, first):
+        wide_ref[h * WIDE : h * WIDE + HEAD_DIM, :] = out_ref[h * HEAD_DIM : (h + 1) * HEAD_DIM, :]
+
+
+def narrow_out(out_ref, wide, first, heads):
+    for h in range(heads):
+        out_ref[first + h * HEAD_DIM : first + (h + 1) * HEAD_DIM, :] = wide[h * WIDE : h * WIDE + HEAD_DIM, :]
+
+
+def fill_grads(do_ref, inner_ref, rows, places, e, wide_ref, att, heads):
+    grad = nt(e, wide_ref[...]).astype(bf16)
+    ones = jnp.ones((8, WIDE), bf16)
+    for h in range(heads):
+        part = grad[:, h * WIDE : (h + 1) * WIDE]
+        do_ref[h, rows, :] = part
+        product = part.astype(f32) * att[:, h * WIDE : (h + 1) * WIDE].astype(f32)
+        high = product.astype(bf16)
+        inner_ref[h, :, places] = nt(ones, high) + nt(ones, (product - high.astype(f32)).astype(bf16))
+
+
+def back_block(q_ref, k_ref, v_ref, do_ref, inner_ref, dq_ref, dk_ref, dv_ref, h, rows, places, count, key_end, causal):
     q = q_ref[h, rows, :]
     d = do_ref[h, rows, :]
     k = k_ref[h, :key_end, :]
@@ -110,15 +122,11 @@
         c = lax.broadcasted_iota(jnp.int32, (count, count), 1)
         diagonal = jnp.where(r <= c, p[key_end - count :], 0.0)
         p = diagonal if key_end == count else jnp.concatenate([p[: key_end - count], diagonal], 0)
-    ds = (p * nt(v, d)).astype(bf16)
+    ds = (p * (nt(v, d) - inner_ref[h, 0:1, places])).astype(bf16)
     dv = nn(p.astype(bf16), d)
     dk = nn(ds, q)
-    if first:
-        dv_ref[h, :key_end, :] = dv
-        dk_ref[h, :key_end, :] = dk
-    else:
-        dv_ref[h, :key_end, :] += dv
-        dk_ref[h, :key_end, :] += dk
+    dv_ref[h, :key_end, :] += dv
+    dk_ref[h, :key_end, :] += dk
     dq_ref[h, rows, :] = tn(k, ds).T
 
 
@@ -181,7 +189,7 @@
 
 def project_own_kernel(
     s_ref, x_ref, m_ref, sq_ref, sk_ref, sv_ref, cq_ref, ck_ref, cv_ref, so_ref, co_ref,
-    q_ref, k_ref, v_ref, mk_ref, mv_ref, wa_ref, cwa_ref, half_out_ref, half_cw_ref, *, heads,
+    q_ref, k_ref, v_ref, k_out_ref, v_out_ref, mk_ref, mv_ref, wa_ref, cwa_ref, half_out_ref, half_cw_ref, *, heads,
 ):
     each = heads * HEAD_DIM
     at = pl.program_id(0)
@@ -202,6 +210,8 @@
     acc = nt(x_ref[...], wa_ref[...])
     fill_queries(q_ref, rows, BLOCK, acc[:, :each] * FACTOR, heads)
     fill_keys(k_ref, v_ref, rows, at * BLOCK, BLOCK, acc[:, each:], heads, limit)
+    k_out_ref[...] = k_ref[...]
+    v_out_ref[...] = v_ref[...]
     acc = nt(m_ref[...], cwa_ref[each:, :])
     fill_keys(mk_ref, mv_ref, rows, at * BLOCK, BLOCK, acc, heads, memory_limit)
 
@@ -213,18 +223,15 @@
         @pl.when(at == block)
         def _():
             for h in range(heads):
-                attend_block(q_ref, k_ref, v_ref, att_ref, h, h * HEAD_DIM, pl.ds(0, BLOCK), BLOCK, (block + 1) * BLOCK, True)
-
-
-def self_own_kernel(
-    s_ref, q_in_ref, k_ref, v_ref, up_ref, down_ref, q_ref, k_out_ref, v_out_ref, att_ref, halves_ref, *, heads
-):
+                attend_block(q_ref, k_ref, v_ref, att_ref, h, pl.ds(0, BLOCK), BLOCK, (block + 1) * BLOCK, True)
+
+
+def self_own_kernel(s_ref, q_in_ref, k_ref, v_ref, up_ref, down_ref, q_ref, att_ref, halves_ref, mark_ref, *, heads):
     half = up_ref.shape[0]
     halves_ref[:half, :] = up_ref[...]
     halves_ref[half:, :] = down_ref[...]
+    mark_ref[...] = jnp.zeros_like(mark_ref)
     q_ref[...] = q_in_ref[...]
-    k_out_ref[...] = k_ref[:, rows_at(BLOCK), :]
-    v_out_ref[...] = v_ref[:, rows_at(BLOCK), :]
     causal_blocks(q_ref, k_ref, v_ref, att_ref, heads)
 
 
@@ -244,14 +251,18 @@
     causal_blocks(q_ref, k_ref, v_ref, att_ref, heads)
 
 
-def self_out_kernel(s_ref, atta_ref, attb_ref, soa_ref, near_ref, far_ref, part0_ref, part1_ref, sob_ref, cob_ref, *, blocks):
+def self_out_kernel(
+    s_ref, atta_ref, attb_ref, soa_ref, near_ref, far_ref, part0_ref, part1_ref, sob_ref, cob_ref, wide_ref, *, heads, blocks
+):
     @pl.when(pl.program_id(0) == 0)
     def _():
         low = s_ref[BIT] == 0
         sob_ref[...] = jnp.where(low, near_ref[...], far_ref[...])
         cob_ref[...] = jnp.where(low, far_ref[...], near_ref[...])
-
-    part = nn(atta_ref[...], soa_ref[...]) + nn(attb_ref[...], sob_ref[...])
+        widen_out(wide_ref.at[0], soa_ref, heads)
+        widen_out(wide_ref.at[1], sob_ref, heads)
+
+    part = nn(atta_ref[...], wide_ref[0]) + nn(attb_ref[...], wide_ref[1])
     put_part(part0_ref, part1_ref, part.astype(bf16), blocks)
 
 
@@ -263,7 +274,7 @@
         @pl.when(live == count)
         def _():
             for h in range(heads):
-                attend_block(q_ref, k_ref, v_ref, att_ref, h, h * HEAD_DIM, pl.ds(0, BLOCK), BLOCK, count * step, False)
+                attend_block(q_ref, k_ref, v_ref, att_ref, h, pl.ds(0, BLOCK), BLOCK, count * step, False)
 
 
 def cross_own_kernel(
@@ -304,8 +315,13 @@
     cross_blocks(q_ref, k_ref, v_ref, att_ref, heads, limit)
 
 
-def cross_out_kernel(atta_ref, attb_ref, coa_ref, cob_ref, part0_ref, part1_ref, *, blocks):
-    part = nn(atta_ref[...], coa_ref[...]) + nn(attb_ref[...], cob_ref[...])
+def cross_out_kernel(atta_ref, attb_ref, coa_ref, cob_ref, part0_ref, part1_ref, wide_ref, *, heads, blocks):
+    @pl.when(pl.program_id(0) == 0)
+    def _():
+        widen_out(wide_ref.at[0], coa_ref, heads)
+        widen_out(wide_ref.at[1], cob_ref, heads)
+
+    part = nn(atta_ref[...], wide_ref[0]) + nn(attb_ref[...], wide_ref[1])
     put_part(part0_ref, part1_ref, part.astype(bf16), blocks)
 
 
@@ -407,7 +423,7 @@
     return e
 
 
-def cross_back_heads(s_ref, q_ref, k_ref, v_ref, do_ref, dqo_ref, dkv_ref, dq_ref, dk_ref, dv_ref, heads, blocks):
+def cross_back_heads(s_ref, q_ref, k_ref, v_ref, do_ref, inner_ref, dqo_ref, dkv_ref, dq_ref, dk_ref, dv_ref, heads, blocks):
     at = pl.program_id(0)
     source = k_ref.shape[1]
 
@@ -425,7 +441,9 @@
         def _():
             @pl.loop(0, heads)
             def _(h):
-                back_block(q_ref, k_ref, v_ref, do_ref, dq_ref, dk_ref, dv_ref, h, rows, BLOCK, count * step, False, False)
+                back_block(
+                    q_ref, k_ref, v_ref, do_ref, inner_ref, dq_ref, dk_ref, dv_ref, h, rows, rows_at(BLOCK), BLOCK, count * step, False
+                )
 
     dqo_ref[...] = pack_heads(dq_ref, rows, heads, HEAD_DIM ** (-0.5))
 
@@ -442,21 +460,27 @@
 def cross_back_other_kernel(
     s_ref, d_in_ref, own0, own1, got0, got1, gain_ref, unit_ref, scale_ref, coa_ref, cob_ref, atta_ref, attb_ref,
     q_ref, k_ref, v_ref,
-    d_ref, e_ref, sums_ref, doa_ref, dqo_ref, dkv_ref, do_ref, dq_ref, dk_ref, dv_ref, *, heads, blocks,
+    d_ref, e_ref, sums_ref, doa_ref, innera_ref, dqo_ref, dkv_ref, wide_ref, do_ref, inner_ref, dq_ref, dk_ref, dv_ref, *, heads, blocks,
 ):
+    @pl.when(pl.program_id(0) == 0)
+    def _():
+        widen_out(wide_ref.at[0], coa_ref, heads)
+        widen_out(wide_ref.at[1], cob_ref, heads)
+
     e = norm_step(
         d_in_ref, (own0, own1, got0, got1), vector(gain_ref), unit_ref, scale_ref, d_ref, e_ref, sums_ref, blocks
     )
-    fill_grads(doa_ref, pl.ds(0, BLOCK), BLOCK, nt(e, coa_ref[...]), atta_ref[...], heads)
-    fill_grads(do_ref, pl.ds(0, BLOCK), BLOCK, nt(e, cob_ref[...]), attb_ref[...], heads)
-    cross_back_heads(s_ref, q_ref, k_ref, v_ref, do_ref, dqo_ref, dkv_ref, dq_ref, dk_ref, dv_ref, heads, blocks)
+    rows, places = pl.ds(0, BLOCK), rows_at(BLOCK)
+    fill_grads(doa_ref, innera_ref, rows, places, e, wide_ref.at[0], atta_ref[...], heads)
+    fill_grads(do_ref, inner_ref, rows, places, e, wide_ref.at[1], attb_ref[...], heads)
+    cross_back_heads(s_ref, q_ref, k_ref, v_ref, do_ref, inner_ref, dqo_ref, dkv_ref, dq_ref, dk_ref, dv_ref, heads, blocks)
 
 
 def cross_back_own_kernel(
-    s_ref, q_ref, k_ref, v_ref, do_ref, dqb_ref, cqa_ref, cwb_ref,
+    s_ref, q_ref, k_ref, v_ref, do_ref, inner_ref, dqb_ref, cqa_ref, cwb_ref,
     part0_ref, part1_ref, dqo_ref, dkv_ref, dq_ref, dk_ref, dv_ref, *, heads, blocks,
 ):
-    cross_back_heads(s_ref, q_ref, k_ref, v_ref, do_ref, dqo_ref, dkv_ref, dq_ref, dk_ref, dv_ref, heads, blocks)
+    cross_back_heads(s_ref, q_ref, k_ref, v_ref, do_ref, inner_ref, dqo_ref, dkv_ref, dq_ref, dk_ref, dv_ref, heads, blocks)
     part = nn(dqo_ref[...], cqa_ref[...]) + nn(dqb_ref[...], cwb_ref[: heads * HEAD_DIM, :])
     put_part(part0_ref, part1_ref, part.astype(bf16), blocks)
 
@@ -465,7 +489,11 @@
     each = dq_ref.shape[1]
     g_ref[:each, :] = tn(dq_ref[...], h_ref[...]).astype(bf16)
     g_ref[each : 3 * each, :] = tn(dkv_ref[...], m_ref[...]).astype(bf16)
-    g_ref[3 * each :, :] = tn(att_ref[...], e_ref[...]).astype(bf16)
+    narrow_out(g_ref, tn(att_ref[...], e_ref[...]).astype(bf16), 3 * each, each // HEAD_DIM)
+
+
+def pass_kernel(s_ref, in_ref, out_ref):
+    out_ref[...] = in_ref[...]
 
 
 def relay_kernel(s_ref, in_ref, first_ref, second_ref):
@@ -474,8 +502,7 @@
     second_ref[...] = in_ref[half:, :]
 
 
-def memory_grad_kernel(s_ref, a_ref, b_ref, wa_ref, wb_ref, out_ref, send_ref, keep_ref, half_ref):
-    half_ref[...] = out_ref[...]
+def memory_grad_kernel(s_ref, a_ref, b_ref, wa_ref, wb_ref, send_ref, keep_ref):
     each = a_ref.shape[1] // 2
     part = (nn(a_ref[...], wa_ref[each:, :]) + nn(b_ref[...], wb_ref[each:, :])).astype(bf16)
     mine = pl.program_id(0) == s_ref[CORE_AT]
@@ -491,15 +518,20 @@
 
 def norm_one_back_kernel(
     s_ref, d_in_ref, own0, own1, got0, got1, gain_ref, unit_ref, scale_ref, soa_ref, sob_ref, atta_ref, attb_ref,
-    sums_two_ref, sums_three_ref, d_ref, doa_ref, dob_ref, ra_ref, rb_ref, e_ref, sums_ref, *, heads, blocks,
+    sums_two_ref, sums_three_ref, d_ref, doa_ref, dob_ref, innera_ref, innerb_ref, ra_ref, rb_ref, e_ref, sums_ref, wide_ref, *, heads, blocks,
 ):
+    @pl.when(pl.program_id(0) == 0)
+    def _():
+        widen_out(wide_ref.at[0], soa_ref, heads)
+        widen_out(wide_ref.at[1], sob_ref, heads)
+
     each = heads * HEAD_DIM
     rows = rows_at(SPAN)
     e = norm_step(
         d_in_ref, (own0, own1, got0, got1), vector(gain_ref), unit_ref, scale_ref, d_ref, e_ref.at[rows, :], sums_ref, blocks
     )
-    fill_grads(doa_ref, pl.ds(0, SPAN), SPAN, nt(e, soa_ref[...]), atta_ref[rows, :], heads)
-    fill_grads(dob_ref, pl.ds(0, SPAN), SPAN, nt(e, sob_ref[...]), attb_ref[rows, :], heads)
+    fill_grads(doa_ref, innera_ref, pl.ds(0, SPAN), rows, e, wide_ref.at[0], atta_ref[rows, :], heads)
+    fill_grads(dob_ref, innerb_ref, pl.ds(0, SPAN), rows, e, wide_ref.at[1], attb_ref[rows, :], heads)
 
     @pl.when(pl.program_id(0) == blocks - 1)
     def _():
@@ -507,11 +539,11 @@
             [sums_ref[:2, :], sums_two_ref[:2, :], sums_three_ref[:2, :], jnp.zeros((10, d_in_ref.shape[1]), f32)], 0
         ).astype(bf16)
         for att_ref, r_ref in ((atta_ref, ra_ref), (attb_ref, rb_ref)):
-            r_ref[:each, :] = tn(att_ref[...], e_ref[...]).astype(bf16)
+            narrow_out(r_ref, tn(att_ref[...], e_ref[...]).astype(bf16), 0, heads)
             r_ref[each:, :] = norms
 
 
-def self_back_kernel(s_ref, x_ref, q_ref, k_ref, v_ref, do_ref, dqkv_ref, gw_ref, dq_ref, dk_ref, dv_ref, *, heads, blocks):
+def self_back_kernel(s_ref, x_ref, q_ref, k_ref, v_ref, do_ref, inner_ref, dqkv_ref, gw_ref, dq_ref, dk_ref, dv_ref, *, heads, blocks):
     at = pl.program_id(0)
     each = heads * HEAD_DIM
     length = k_ref.shape[1]
@@ -528,7 +560,10 @@
         def _():
             @pl.loop(0, heads)
             def _(h):
-                back_block(q_ref, k_ref, v_ref, do_ref, dq_ref, dk_ref, dv_ref, h, rows, SPAN, (block + 1) * SPAN, True, False)
+                back_block(
+                    q_ref, k_ref, v_ref, do_ref, inner_ref, dq_ref, dk_ref, dv_ref, h, rows, pl.ds(block * SPAN, SPAN), SPAN,
+                    (block + 1) * SPAN, True,
+                )
 
     dqkv_ref[rows_at(SPAN), :each] = pack_heads(dq_ref, rows, heads, HEAD_DIM ** (-0.5))
 
@@ -600,6 +635,8 @@
                 outs.pop(0)[...] = scratch[pl.ds(pl.multiple_of(high * half, 16), half), :]
         elif kind == LAST:
             outs.pop(0)[...] = mine[0][-rows:, :].astype(f32) + mine[1][-rows:, :].astype(f32)
+        elif kind == PASS:
+            outs.pop(0)[...] = mine[0][...]
         elif kind == STACK:
             size, target = mine[0].shape[0], outs.pop(0)
             target[:size, :] = mine[0][...]
@@ -710,7 +747,7 @@
         views.append(view)
     for item in after:
         specs.append(pl.BlockSpec(memory_space=pl.ANY))
-        arrays.append(item)
+        arrays.append(pltpu.with_memory_space_constraint(item.array, pltpu.HBM) if isinstance(item, Far) else item)
         views.append(SKIP)
     shapes, out_specs = [], []
     for shape, dtype, how in outputs:
@@ -794,7 +831,8 @@
     held = ((length, width), f32, HELD_ROWS)
     held_low = ((length, width), bf16, HELD_ROWS)
     column = ((length, 1), f32, HELD_ROWS)
-    att_held = ((length, each), bf16, HELD_ROWS)
+    att_held = ((length, heads * WIDE), bf16, HELD_ROWS)
+    dq_held = ((length, each), bf16, HELD_ROWS)
     hid = ((length, hidden), bf16, HELD_ROWS)
     sums = ((8, width), f32, WHOLE)
     low = ((length, width), bf16, ROWS)
@@ -802,43 +840,49 @@
     half_low = ((length // 2, width), bf16, WHOLE)
     out_shape = ((each, width), bf16, WHOLE)
     qkv = functools.partial(pltpu.VMEM, (heads, length, WIDE))
+    wide_out = pltpu.VMEM((2, heads * WIDE, width), bf16)
+    inner_held = ((heads, 8, length), f32, HELD_WHOLE)
 
     w_parts = (self_query.T, self_key.T, self_value.T)
     c_parts = (cross_query.T, cross_key.T, cross_value.T)
     bit = scalars[BIT]
     w_half = lax.dynamic_slice_in_dim(jnp.concatenate(w_parts, 0), bit * (3 * each // 2), 3 * each // 2, 0)
     w_near = across(w_half)
-    q_new, k_new, v_new, ck_a, cv_a, w_a, cw_a, o_half, cw_half = call(
+    q_new, k_new, v_new, k_a, v_a, ck_a, cv_a, w_a, cw_a, o_half, cw_half = call(
         functools.partial(project_own_kernel, heads=heads), big,
         [
             Row(tokens, length, ROWS), Row(memory, source, ROWS), *(Far(v) for v in (*w_parts, *c_parts, self_out, cross_out)),
         ],
         [
-            head_held, head_held, head_held, key_held, key_held, ((3 * each, width), bf16, WHOLE),
+            head_held, head_held, head_held, head_rows, head_rows, key_held, key_held, ((3 * each, width), bf16, WHOLE),
             ((3 * each, width), bf16, WHOLE), out_shape, ((3 * each // 2, width), bf16, WHOLE),
         ],
         scalars, micros=7, scale=0.4,
     )
     o_near = across(o_half)
     cw_near = across(cw_half)
+    (w_near,) = call(
+        pass_kernel, 1, [w_near], [((3 * each // 2, width), bf16, WHOLE)], scalars, micros=1, scale=0.4, after=[o_half]
+    )
     w_far = along(w_near, 0)
     quarter = ((hidden // 2, width), bf16, WHOLE)
-    q_a, k_a, v_a, att_a, ffn_half = call(
+    q_a, att_a, ffn_half, mark = call(
         functools.partial(self_own_kernel, heads=heads), big,
         [Held(q_new), Held(k_new, WHOLE), Held(v_new, WHOLE), Pick(ffn_up, BIT, 2), Pick(ffn_down, BIT + 1, 2)],
-        [head_rows, head_rows, head_rows, att_held, ((width, width), bf16, WHOLE)], scalars, micros=6, scale=0.4, after=[w_near],
+        [head_rows, att_held, ((width, width), bf16, WHOLE), ((8, WIDE), f32, WHOLE)], scalars, micros=6, scale=0.4, after=[w_near],
     )
     ffn_near = across(ffn_half)
     cw_far = along(cw_near, 1)
+    (o_near,) = call(pass_kernel, 1, [o_near], [out_shape], scalars, micros=1, scale=0.4, after=[mark])
     o_far = along(o_near, 0)
     w_b, q_b, k_b, v_b, att_b = call(
         functools.partial(self_other_kernel, heads=heads), big, [Row(tokens, length, ROWS), w_near, w_far],
         [((3 * each, width), bf16, WHOLE), head_rows, head_rows, head_rows, att_held], scalars, scratch=[qkv(bf16), qkv(bf16)],
-        micros=9, scale=0.4, after=[o_near],
+        micros=9, scale=0.4,
     )
     part0, part1, so_b, co_b = call(
-        functools.partial(self_out_kernel, blocks=big), big, [Held(att_a), Held(att_b), self_out, o_near, o_far],
-        [*part_shapes(big), out_shape, out_shape], scalars, micros=3, scale=0.4, after=[cw_near],
+        functools.partial(self_out_kernel, heads=heads, blocks=big), big, [Held(att_a), Held(att_b), self_out, o_near, o_far],
+        [*part_shapes(big), out_shape, out_shape], scalars, scratch=[wide_out], micros=3, scale=0.4, after=[cw_near],
     )
     h_one, h_one_low, unit_one, scale_one, cq_a, catt_a = call(
         functools.partial(cross_own_kernel, heads=heads, blocks=big), big,
@@ -856,8 +900,8 @@
         scalars, micros=100, scale=1.0, after=[up_near, down_near],
     )
     part0, part1 = call(
-        functools.partial(cross_out_kernel, blocks=big), big, [Held(catt_a), Held(catt_b), cross_out, co_b],
-        part_shapes(big), micros=2, scale=0.4, after=[up_far, down_far],
+        functools.partial(cross_out_kernel, heads=heads, blocks=big), big, [Held(catt_a), Held(catt_b), cross_out, co_b],
+        part_shapes(big), scratch=[wide_out], micros=2, scale=0.4, after=[up_far, down_far],
     )
     h_two, h_two_low, unit_two, scale_two, act_a, slope_a, term = call(
         functools.partial(ffn_own_kernel, blocks=small), small,
@@ -896,14 +940,13 @@
         pltpu.VMEM((heads, BLOCK, WIDE), f32), pltpu.VMEM((heads, source, WIDE), f32), pltpu.VMEM((heads, source, WIDE), f32),
     ]
     dkv_held = ((source, 2 * each), bf16, HELD_WHOLE)
-    d_two, e_two, sums_two, do_a, dcq_b, dckv_b = call(
+    d_two, e_two, sums_two, do_a, inner_a, dcq_b, dckv_b = call(
         functools.partial(cross_back_other_kernel, heads=heads, blocks=big), big,
         [
-            Held(d_three), *shares(part, big), gain_two, Held(unit_two), Held(scale_two), cross_out, co_b, Held(catt_a), Held(catt_b),
-            Held(cq_b), Held(ck_b, WHOLE), Held(cv_b, WHOLE),
+            Held(d_three), *shares(part, big), gain_two, Held(unit_two), Held(scale_two), cross_out, co_b, Held(catt_a), Held(catt_b), Held(cq_b), Held(ck_b, WHOLE), Held(cv_b, WHOLE),
         ],
-        [held, held_low, sums, head_held, att_held, dkv_held], scalars,
-        scratch=[pltpu.VMEM((heads, BLOCK, WIDE), bf16)] + back_scratch, micros=18,
+        [held, held_low, sums, head_held, inner_held, dq_held, dkv_held], scalars,
+        scratch=[wide_out, pltpu.VMEM((heads, BLOCK, WIDE), bf16), pltpu.VMEM((heads, 8, length), f32)] + back_scratch, micros=18,
     )
 
     def cross_grads(att, dq, dkv, after=()):
@@ -924,11 +967,11 @@
                 made = [((rows, width), bf16, WHOLE)] if bit is None else [((rows // 2, width), bf16, WHOLE)] * 2
             elif kind == LAST:
                 made = [((rows, width), f32, WHOLE)]
-            elif kind in (PACK, STACK):
-                made = [((rows, width), bf16, WHOLE)]
+            elif kind in (PACK, STACK, PASS):
+                made = [((rows, width), bit if kind == PASS else bf16, WHOLE)]
             else:
                 made = [((size, width), f32, FAR_WHOLE) for _, size in cuts]
-            if kind not in (PACK, STACK, LAST):
+            if kind not in (PACK, STACK, LAST, PASS):
                 most = max(most, rows)
             outputs += made
             counts.append(len(made))
@@ -976,47 +1019,44 @@
     def last(mine, got):
         return (LAST, [mine, got], 16, None, (), 1)
 
-    pin = []
+    gc_b = cross_grads(catt_b, dcq_b, dckv_b)
     if short:
-        (send_u, keep_u), (down_a,), (down_b,) = step(
+        (send_u, keep_u), (down_a,), (down_b,), (gc_b,) = step(
             [
                 (SUM, [gu_a, gu_got], width, 0, (), 1), plain([keep_a, got_a], width // 2), plain([keep_b, got_b], width // 2),
+                (PASS, [gc_b], 4 * each, bf16, (), 1),
             ],
-            [dcq_b],
+            [gc_b],
         )
         got_u, got_d = along(send_u, 0), across(down_b)
-        pin = [keep_u]
-    gc_b = cross_grads(catt_b, dcq_b, dckv_b, pin)
     part0, part1, dcq_a, dckv_a = call(
         functools.partial(cross_back_own_kernel, heads=heads, blocks=big), big,
-        [Held(cq_a), Held(ck_a, WHOLE), Held(cv_a, WHOLE), Held(do_a), Held(dcq_b), c_parts[0], cw_b],
-        [*part_shapes(big), att_held, dkv_held], scalars, scratch=back_scratch, micros=16, after=[gc_b],
+        [Held(cq_a), Held(ck_a, WHOLE), Held(cv_a, WHOLE), Held(do_a), Held(inner_a, WHOLE), Held(dcq_b), c_parts[0], cw_b],
+        [*part_shapes(big), dq_held, dkv_held], scalars, scratch=back_scratch, micros=16, after=[gc_b],
     )
     part = (part0, part1)
 
     gc_got = across(gc_b)
+    pin = []
     if short:
         ffn = Chain([keep_u, down_a], [got_u, got_d], width, [(0, width), (width, width)], (1, 2), (2, 1, 0), 2)
         pin, _ = advance([ffn], after=[dcq_a])
-    memory_send, memory_keep, out_half = call(
-        memory_grad_kernel, 2,
-        [Held(dckv_a), Held(dckv_b), cw_a, cw_b, Row(out_row, length // 2, (PART, CORE_AT))],
-        [half_low, half_low, ((length // 2, width), bf16, ROWS)], scalars, micros=5, after=pin,
-    )
-    out_far = across(out_half)
+    memory_send, memory_keep = call(
+        memory_grad_kernel, 2, [Held(dckv_a), Held(dckv_b), cw_a, cw_b], [half_low, half_low], scalars, micros=5, after=pin,
+    )
     memory_got = sibling(memory_send)
     gc_a = cross_grads(catt_a, dcq_a, dckv_a, [memory_send])
     memory_plan = plain([memory_keep, memory_got], length // 2)
     pin = [gc_a]
     rest_shape = ((each + 16, width), bf16, WHOLE)
-    d_one, do_a, do_b, rest_a, rest_b = call(
+    d_one, do_a, do_b, inner_a, inner_b, rest_a, rest_b = call(
         functools.partial(norm_one_back_kernel, heads=heads, blocks=small), small,
         [
             Held(d_two), *shares(part, small), gain_one, Held(unit_one), Held(scale_one), self_out, so_b,
             Held(att_a, WHOLE), Held(att_b, WHOLE), sums_two, sums_three,
         ],
-        [held, head_held, head_held, rest_shape, rest_shape], scalars,
-        scratch=[pltpu.VMEM((length, width), bf16), pltpu.VMEM((8, width), f32)], micros=6, after=pin,
+        [held, head_held, head_held, inner_held, inner_held, rest_shape, rest_shape], scalars,
+        scratch=[pltpu.VMEM((length, width), bf16), pltpu.VMEM((8, width), f32), wide_out], micros=6, after=pin,
     )
     rest_got = across(rest_b)
     kept_w = ((3 * each, width), bf16, WHOLE)
@@ -1025,62 +1065,74 @@
         pltpu.VMEM((heads, SPAN, WIDE), f32), pltpu.VMEM((heads, length, WIDE), f32), pltpu.VMEM((heads, length, WIDE), f32),
     ]
 
-    def self_back(q, k, v, do, after=()):
+    def self_back(q, k, v, do, inner, after=()):
         return call(
             functools.partial(self_back_kernel, heads=heads, blocks=small), small,
-            [Row(tokens, length), Part(q), k, v, Held(do)], [qkv_held, kept_w], scalars, scratch=self_scratch, micros=14, after=after,
+            [Row(tokens, length), Part(q), k, v, Held(do), Held(inner, WHOLE)], [qkv_held, kept_w], scalars, scratch=self_scratch, micros=14, after=after,
         )
 
     pin = []
     if short:
         cross = Chain([gc_a], [gc_got], 4 * each, [(n * each, each) for n in range(4)])
         pin, _ = advance([ffn, cross], after=[do_b])
-    dqkv_b, gw_b = self_back(q_b, k_b, v_b, do_b, pin)
+    dqkv_b, gw_b = self_back(q_b, k_b, v_b, do_b, inner_b, pin)
     gw_got = across(gw_b)
 
     pin = []
     if short:
         pin, (norms,) = advance([ffn, cross], [last(rest_a, rest_got)], [dqkv_b])
         norms = last(norms, along(norms, 0))
-    dqkv_a, gw_a = self_back(q_a, k_a, v_a, do_a, pin)
+    dqkv_a, gw_a = self_back(q_a, k_a, v_a, do_a, inner_a, pin)
     pin = []
     if short:
         own = Chain([gw_a, rest_a], [gw_got, rest_got], 4 * each, [(n * each, each) for n in range(4)])
         pin, (memory_mine, norms) = advance([own, ffn, cross], [memory_plan, norms])
-        norms = last(norms, along(norms, 1))
     else:
         ((memory_mine,),) = step([memory_plan], [gw_a])
-    memory_far = across(memory_mine)
     tokens_send, tokens_keep = call(
         tokens_grad_kernel, 2, [Held(d_one), Held(dqkv_a), Held(dqkv_b), w_a, w_b],
         [half_low, ((length // 2, width), f32, WHOLE)], scalars, micros=6, after=pin,
     )
+    (out_half,) = call(
+        pass_kernel, 1, [Row(out_row, length // 2, (PART, CORE_AT))], [half_low], scalars, micros=1, after=[tokens_send]
+    )
+    out_far = across(out_half)
+
     def placed(pieces, shift, after=()):
         return call(
             functools.partial(place_kernel, shift=shift), 4, pieces,
             [((2 * length, width), bf16, FAR_ROWS), ((8, WIDE), f32, WHOLE)], scalars, micros=4, after=after,
         )
 
+    def passed(value, rows=length // 2, dtype=bf16):
+        return (PASS, [value], rows, dtype, (), 1)
+
     def pair(mine, far):
         return (STACK, [mine, far], length, None, (), 1)
 
     if short:
-        out_sibling = sibling(out_far)
-        pin, _ = advance([own, ffn, cross], (), [tokens_send, out_sibling])
+        pin, (memory_mine,) = advance([own, ffn, cross], [passed(memory_mine)], [out_half])
+        memory_far = across(memory_mine)
+        pin, (tokens_send,) = advance([own, cross], [passed(tokens_send)], [*pin, out_far])
         tokens_plan = plain([tokens_keep, sibling(tokens_send)], length // 2)
-        pin, _ = advance([own, cross], (), pin)
-        layer_out, mark = placed([out_row, out_far, out_sibling], True, pin)
-        pin, (tokens_mine, memory_pair) = advance([own, ffn, cross], [tokens_plan, pair(memory_mine, memory_far)], [mark], 3)
-        tokens_far, memory_sibling = across(tokens_mine), sibling(memory_pair)
-        pin, (norms,) = advance([own], [norms], [*pin, memory_sibling])
+        pin, (tokens_mine, memory_pair, out_far) = advance(
+            [own, cross], [tokens_plan, pair(memory_mine, memory_far), passed(out_far)], [*pin, ffn.arrays[1]]
+        )
+        tokens_far, memory_sibling, out_sibling = across(tokens_mine), sibling(memory_pair), sibling(out_far)
+        ((gu_wide, gd_wide),) = step([ffn.plan()], pin, 4)
+        pin, (norms,) = advance([own], [passed(norms, 16, f32)], [Far(gu_wide), memory_sibling, out_sibling])
         norms = last(norms, along(norms, 2))
         memory_grad, mark = placed([memory_pair, memory_sibling], False, pin)
-        pin, (tokens_pair, norms) = advance([own, cross], [pair(tokens_mine, tokens_far), norms], [mark])
-        tokens_grad, mark = placed([tokens_pair, sibling(tokens_pair)], False, pin)
-        advance([own], (), [mark])
-        (gu_wide, gd_wide), cross, own = ffn.done, cross.done, own.done
+        pin, (tokens_pair, norms) = advance([own], [pair(tokens_mine, tokens_far), norms], [mark, cross.arrays[1]])
+        norms = last(norms, along(norms, 1))
+        (cross,) = step([cross.plan()], pin, 3)
+        layer_out, mark = placed([out_row, out_far, out_sibling], True, [Far(cross[0])])
+        tokens_grad, mark = placed([tokens_pair, sibling(tokens_pair)], False, [mark])
+        _, (norms,) = advance([own], [norms], [mark])
+        own = own.done
         rest = own[3]
     else:
+        memory_far = across(memory_mine)
         tokens_plan = plain([tokens_keep, sibling(tokens_send)], length // 2)
         (tokens_mine,), (memory_pair,) = step([tokens_plan, pair(memory_mine, memory_far)])
         ((tokens_pair,),) = step([pair(tokens_mine, across(tokens_mine))])

time: 330 us -> 320 us (0.970)
  starting transfers between devices: 59.7 us -> 44 us
  waiting for transfers between devices: 68.5 us -> 76.1 us
    ppermute x28, starting transfers between devices: 42 us -> 26.5 us  [along(): return lax.ppermute(value, 'dp', [(i, i ^ 1 << bit) for i in range(size)])]
    ppermute x12, waiting for transfers between devices: 11.5 us -> 16.6 us  [across(): return lax.ppermute(value, 'tp', ACROSS)]
    ppermute x28, waiting for transfers between devices: 47.6 us -> 52.4 us  [along(): return lax.ppermute(value, 'dp', [(i, i ^ 1 << bit) for i in range(size)])]
    pallas_call x34 -> x39, Pallas kernels: 179 us -> 180 us  [call(): pl.pallas_call(viewed, grid_spec=grid_spec, **settings)(scalars, *arrays)]
  transfers between devices with their start and end apart: 55 -> 55, of which waited for: 26 -> 25; matrix products, arithmetic and copies ran while one was open for 0% -> 0% of each run, Pallas kernels for 47% -> 49%
where the time goes in v5:
time: 320 us; the launch traced here: 314 us
  Pallas kernels  188 us (59%)
  waiting for transfers between devices  76.1 us (24%)
  starting transfers between devices  44 us (14%)
    pallas_call x39, Pallas kernels, call(): pl.pallas_call(viewed, grid_spec=grid_spec, **settings)(scalars, *arrays)  180 us
    ppermute x28, waiting for transfers between devices, along(): return lax.ppermute(value, 'dp', [(i, i ^ 1 << bit) for i in range(size)])  52.4 us
    ppermute x28, starting transfers between devices, along(): return lax.ppermute(value, 'dp', [(i, i ^ 1 << bit) for i in range(size)])  26.5 us
    ppermute x12, waiting for transfers between devices, across(): return lax.ppermute(value, 'tp', ACROSS)  16.6 us
    ppermute x12, starting transfers between devices, across(): return lax.ppermute(value, 'tp', ACROSS)  13.9 us
    pallas_call x2, Pallas kernels, call(): pl.pallas_call(viewed, grid=(blocks,), in_specs=specs, out_specs=out_spec...  8.02 us
    ppermute x15, waiting for transfers between devices, sibling(): return lax.ppermute(value, 'tp', CORE)  7.14 us
  transfers between devices with their start and end apart: 55, of which 25 were waited for; matrix products, arithmetic and copies ran while one was open for 0% of the time, Pallas kernels for 49%

profile of v5, /device:TPU:0, one launch (start us, length us, event | category | flops | bytes accessed | tf_op | source)
XLA Modules:
  0.0 313.7 jit_solution(4776870659785078158)
XLA Ops:
  2.0 3.0 collective-permute-start
  5.8 6.7 %project_own_kernel.1 = (bf16[3,1024,128]{2,1,0:T(8,128)(2,1)S(1)}, bf16[3,1024,128]{2,1,0:T(8,128)(2,1)S(1)}, bf16[3,1024,128]{2,1,0:T(8,128)(2,1)S(1)}, bf16[3...) custom-call(s32[9]{0:T(128)S(1)} %concatenate.6.refs_0_, ...), custom_call_target="tpu_custom_call" | custom-call | flops 2800000000 | tf_op jit(solution)/shard_map/project_own_kernel/pallas_call | solution.py:786
  12.5 2.7 collective-permute-done.refs_1_
  15.8 1.9 collective-permute-start.1
  19.7 8.4 %self_own_kernel.1 = (bf16[3,1024,128]{2,1,0:T(8,128)(2,1)}, bf16[1024,384]{1,0:T(8,128)(2,1)S(1)}, bf16[768,768]{1,0:T(8,128)(2,1)S(1)}, f32[8,128]{1,0:T(8,128)S(1)}) custom-call(s32[9]{0:T(128)S(1)} %concatenate.6.refs_0_, bf16[3,1024,128]{2,1,0:T(8,128)(2,1)S(1)} %get-tuple-element.169.refs_1_, bf16[3,1024,128]{2,1,0:T(8,128)(2,1)S(1)} %get-tuple-element.170.refs_2_, ...), custom_call_target="tpu_custom_call" | custom-call | flops 2400000000 | tf_op jit(solution)/shard_map/self_own_kernel/pallas_call | solution.py:786
  30.7 10.6 %self_other_kernel.1 = (bf16[576,768]{1,0:T(8,128)(2,1)S(1)}, bf16[3,1024,128]{2,1,0:T(8,128)(2,1)}, bf16[3,1024,128]{2,1,0:T(8,128)(2,1)}, bf16[3,1024,128]{2,1,0:T(8,128)(2,1)}, bf16[1024,384]{1,0:T(8,128)(2,1)S(1)}) custom-call(s32[9]{0:T(128)S(1)} %concatenate.6.refs_0_, bf16[2048,768]{1,0:T(8,128)(2,1)} %refs_1_.11, ...), custom_call_target="tpu_custom_call" | custom-call | flops 3600000000 | tf_op jit(solution)/shard_map/self_other_kernel/pallas_call | solution.py:786
  41.3 2.8 self_out_kernel.1
  47.7 10.0 %cross_own_kernel.1 = (f32[1024,768]{1,0:T(8,128)S(1)}, bf16[1024,768]{1,0:T(8,128)(2,1)S(1)}, bf16[1024,768]{1,0:T(8,128)(2,1)S(1)}, f32[1024,1]{1,0:T(8,128)S(...) custom-call(s32[9]{0:T(128)S(1)} %concatenate.6.refs_0_, bf16[2048,768]{1,0:T(8,128)(2,1)} %refs_1_.11, ...), custom_call_target="tpu_custom_call" | custom-call | flops 4000000000 | tf_op jit(solution)/shard_map/cross_own_kernel/pallas_call | solution.py:786
  57.7 2.3 collective-permute-done.8.refs_1_
  62.8 10.1 %cross_other_kernel.1 = (bf16[576,768]{1,0:T(8,128)(2,1)S(1)}, bf16[3,1024,128]{2,1,0:T(8,128)(2,1)S(1)}, bf16[3,1024,128]{2,1,0:T(8,128)(2,1)S(1)}, bf16[3,1024...) custom-call(s32[9]{0:T(128)S(1)} %concatenate.6.refs_0_, bf16[2048,768]{1,0:T(8,128)(2,1)} %refs_2_.7, ...), custom_call_target="tpu_custom_call" | custom-call | flops 99999997952 | tf_op jit(solution)/shard_map/cross_other_kernel/pallas_call | solution.py:786
  75.1 2.2 cross_out_kernel.1
  77.9 1.8 collective-permute-done.11.refs_3_
  80.8 5.8 %ffn_own_kernel.1 = (f32[1024,768]{1,0:T(8,128)S(1)}, bf16[1024,768]{1,0:T(8,128)(2,1)S(1)}, bf16[1024,768]{1,0:T(8,128)(2,1)S(1)}, f32[1024,1]{1,0:T(8,128)S(1)...) custom-call(f32[1024,768]{1,0:T(8,128)S(1)} %get-tuple-element.181.refs_0_, ...), custom_call_target="tpu_custom_call" | custom-call | flops 2800000000 | tf_op jit(solution)/shard_map/ffn_own_kernel/pallas_call | solution.py:780
  86.7 5.1 %ffn_other_kernel.1 = (bf16[512,768]{1,0:T(8,128)(2,1)S(1)}, bf16[512,768]{1,0:T(8,128)(2,1)S(1)}, bf16[1024,768]{1,0:T(8,128)(2,1)S(1)}, bf16[1024,768]{1,0:T(8...) custom-call(s32[9]{0:T(128)S(1)} %concatenate.6.refs_0_, ...), custom_call_target="tpu_custom_call" | custom-call | flops 2000000000 | tf_op jit(solution)/shard_map/ffn_other_kernel/pallas_call | solution.py:786
  92.4 1.8 collective-permute-done.13.refs_4_
  95.3 12.3 %ffn_back_kernel.1 = (bf16[512,768]{1,0:T(8,128)(2,1)S(1)}, bf16[512,768]{1,0:T(8,128)(2,1)S(1)}, bf16[1024,768]{1,0:T(8,128)(2,1)}, f32[1024,768]{1,0:T(8,128)S...) custom-call(s32[9]{0:T(128)S(1)} %concatenate.6.refs_0_, ...), custom_call_target="tpu_custom_call" | custom-call | flops 4400000000 | tf_op jit(solution)/shard_map/ffn_back_kernel/pallas_call | solution.py:786
  108.2 3.5 %ffn_grad_kernel.2 = (bf16[768,768]{1,0:T(8,128)(2,1)S(1)}, bf16[384,768]{1,0:T(8,128)(2,1)S(1)}, bf16[384,768]{1,0:T(8,128)(2,1)S(1)}) custom-call(s32[9]{0:T(128)S(1)} %concatenate.6.refs_0_, bf16[1024,768]{1,0:T(8,128)(2,1)S(1)} %get-tuple-element.193.refs_1_, bf16[1024,768]{1,0:T(8,128)(2,1)S(1)} %get-tuple-element.222.refs_2_, ...), custom_call_target="tpu_custom_call" | custom-call | flops 1600000000 | tf_op jit(solution)/shard_map/ffn_grad_kernel/pallas_call | solution.py:786
  113.7 3.6 %ffn_grad_kernel.3 = (bf16[768,768]{1,0:T(8,128)(2,1)S(1)}, bf16[384,768]{1,0:T(8,128)(2,1)S(1)}, bf16[384,768]{1,0:T(8,128)(2,1)S(1)}) custom-call(s32[9]{0:T(128)S(1)} %concatenate.6.refs_0_, bf16[1024,768]{1,0:T(8,128)(2,1)S(1)} %get-tuple-element.193.refs_1_, bf16[1024,768]{1,0:T(8,128)(2,1)S(1)} %get-tuple-element.219.refs_2_, ...), custom_call_target="tpu_custom_call" | custom-call | flops 1600000000 | tf_op jit(solution)/shard_map/ffn_grad_kernel/pallas_call | solution.py:786
  118.1 16.2 %cross_back_other_kernel.1 = (f32[1024,768]{1,0:T(8,128)S(1)}, bf16[1024,768]{1,0:T(8,128)(2,1)S(1)}, f32[8,768]{1,0:T(8,128)S(1)}, bf16[3,1024,128]{2,1,0:T(8,1...) custom-call(s32[9]{0:T(128)S(1)} %concatenate.6.refs_0_, ...), custom_call_target="tpu_custom_call" | custom-call | flops 7200000000 | tf_op jit(solution)/shard_map/cross_back_other_kernel/pallas_call | solution.py:786
  134.3 4.3 %cross_grad_kernel.2.refs_7_.refs_8_ = bf16[768,768]{1,0:T(8,128)(2,1)S(1)} custom-call(s32[9]{0:T(128)S(1)} %concatenate.6.refs_0_, bf16[1024,768]{1,0:T(8,128)(2,1)S(1)} %get-tuple-element.183.refs_2_.refs_1_, bf16[2048,768]{1,0:T(8,128)(2,1)} %refs_2_.7, bf16[1024,384]{1,0:T(8,128)(2,1)S(1)} %get-tuple-element.188.refs_1_.refs_12_.refs_3_, ...), custom_call_target="tpu_custom_call" | custom-call | flops 2000000000 | tf_op jit(solution)/shard_map/cross_grad_kernel/pallas_call | solution.py:786
  140.2 1.9 step_kernel.13
  145.5 12.1 %cross_back_own_kernel.1 = (bf16[512,768]{1,0:T(8,128)(2,1)S(1)}, bf16[512,768]{1,0:T(8,128)(2,1)S(1)}, bf16[1024,192]{1,0:T(8,128)(2,1)S(1)}, bf16[1024,384]{1,0:T(8,128)(2,1)S(1)}) custom-call(s32[9]{0:T(128)S(1)} %concatenate.6.refs_0_, bf16[3,1024,128]{2,1,0:T(8,128)(2,1)S(1)} %copy-done.26, bf16[3,1024,128]{2,1,0:T(8,128)(2,1)S(1)} %copy-done.19, ...), custom_call_target="tpu_custom_call" | custom-call | flops 6400000000 | tf_op jit(solution)/shard_map/cross_back_own_kernel/pallas_call | solution.py:786
  162.6 2.7 memory_grad_kernel.1
  165.3 4.3 %cross_grad_kernel.3.refs_15_.refs_3_ = bf16[768,768]{1,0:T(8,128)(2,1)S(1)} custom-call(s32[9]{0:T(128)S(1)} %concatenate.6.refs_0_, bf16[1024,768]{1,0:T(8,128)(2,1)S(1)} %get-tuple-element.183.refs_2_.refs_1_, bf16[2048,768]{1,0:T(8,128)(2,1)} %refs_2_.7, bf16[1024,384]{1,0:T(8,128)(2,1)S(1)} %get-tuple-element.182.refs_0_.refs_11_.refs_3_, ...), custom_call_target="tpu_custom_call" | custom-call | flops 2000000000 | tf_op jit(solution)/shard_map/cross_grad_kernel/pallas_call | solution.py:786
  169.6 8.4 %norm_one_back_kernel.1 = (f32[1024,768]{1,0:T(8,128)S(1)}, bf16[3,1024,128]{2,1,0:T(8,128)(2,1)S(1)}, bf16[3,1024,128]{2,1,0:T(8,128)(2,1)S(1)}, f32[3,8,1024]{...) custom-call(s32[9]{0:T(128)S(1)} %concatenate.6.refs_0_, ...), custom_call_target="tpu_custom_call" | custom-call | flops 2400000000 | tf_op jit(solution)/shard_map/norm_one_back_kernel/pallas_call | solution.py:786
  178.6 6.4 %collective-permute-done.25.refs_4_ = bf16[768,768]{1,0:T(8,128)(2,1)S(1)} collective-permute-done((bf16[768,768]{1,0:T(8,128)(2,1)S(1)}, bf16[768,768]{1,0:T(8,128)(2,1)S(1)}, u32[]{:S(2)}, u32[]{:S(2)}) %collective-permute-start.25) | collective-permute-done | bytes 1179680 | tf_op jit(solution)/shard_map/ppermute | solution.py:809
  186.6 2.7 collective-permute-start.26
  189.9 12.6 %self_back_kernel.2 = (bf16[1024,576]{1,0:T(8,128)(2,1)S(1)}, bf16[576,768]{1,0:T(8,128)(2,1)S(1)}) custom-call(s32[9]{0:T(128)S(1)} %concatenate.6.refs_0_, bf16[2048,768]{1,0:T(8,128)(2,1)} %refs_1_.11, bf16[3,1024,128]{2,1,0:T(8,128)(2,1)S(1)} %copy-done.27, bf16[3,1024,128]{2,1,0:T(8,128)(2,1)S(1)} %copy-done.28, bf16[3,1024,128]{2,1,0:T(8,128)(2,1)S(1)} %copy-done.29, ...), custom_call_target="tpu_custom_call" | custom-call | flops 5600000000 | tf_op jit(solution)/shard_map/self_back_kernel/pallas_call | solution.py:786
  207.6 12.4 %self_back_kernel.3 = (bf16[1024,576]{1,0:T(8,128)(2,1)S(1)}, bf16[576,768]{1,0:T(8,128)(2,1)S(1)}) custom-call(s32[9]{0:T(128)S(1)} %concatenate.6.refs_0_, bf16[2048,768]{1,0:T(8,128)(2,1)} %refs_1_.11, bf16[3,1024,128]{2,1,0:T(8,128)(2,1)S(1)} %copy-done.24, bf16[3,1024,128]{2,1,0:T(8,128)(2,1)S(1)} %copy-done.16, bf16[3,1024,128]{2,1,0:T(8,128)(2,1)S(1)} %copy-done.17, ...), custom_call_target="tpu_custom_call" | custom-call | flops 5600000000 | tf_op jit(solution)/shard_map/self_back_kernel/pallas_call | solution.py:786
  220.0 3.3 %collective-permute-done.30.refs_6_ = bf16[192,768]{1,0:T(8,128)(2,1)S(1)} collective-permute-done((bf16[192,768]{1,0:T(8,128)(2,1)S(1)}, bf16[192,768]{1,0:T(8,128)(2,1)S(1)}, u32[]{:S(2)}, u32[]{:S(2)}) %collective-permute-start.30) | collective-permute-done | bytes 294944 | tf_op jit(solution)/shard_map/ppermute | solution.py:815
  223.3 1.8 step_kernel.17
  226.8 3.8 %tokens_grad_kernel.1 = (bf16[512,768]{1,0:T(8,128)(2,1)S(1)}, f32[512,768]{1,0:T(8,128)S(1)}) custom-call(s32[9]{0:T(128)S(1)} %concatenate.6.refs_0_, f32[1024,768]{1,0:T(8,128)S(1)} %get-tuple-element.276.refs_1_, bf16[1024,576]{1,0:T(8,128)(2,1)S(1)} %get-tuple-element.277.refs_2_, bf16[1024,576]{1,0:T(8,128)(2,1)S(1)} %get-tuple-element.262.refs_7_.refs_3_, ...), custom_call_target="tpu_custom_call" | custom-call | flops 2400000000 | tf_op jit(solution)/shard_map/tokens_grad_kernel/pallas_call | solution.py:786
  233.1 8.8 %collective-permute-done.36.refs_6_ = bf16[96,768]{1,0:T(8,128)(2,1)S(1)} collective-permute-done((bf16[96,768]{1,0:T(8,128)(2,1)S(1)}, bf16[96,768]{1,0:T(8,128)(2,1)S(1)}, u32[]{:S(2)}, u32[]{:S(2)}) %collective-permute-start.36) | collective-permute-done | bytes 147488 | tf_op jit(solution)/shard_map/ppermute | solution.py:815
  241.9 2.2 collective-permute-done.35.refs_4_
  248.3 5.1 %collective-permute-done.38.refs_4_ = bf16[96,768]{1,0:T(8,128)(2,1)S(1)} collective-permute-done((bf16[96,768]{1,0:T(8,128)(2,1)S(1)}, bf16[96,768]{1,0:T(8,128)(2,1)S(1)}, u32[]{:S(2)}, u32[]{:S(2)}) %collective-permute-start.38) | collective-permute-done | bytes 147488 | tf_op jit(solution)/shard_map/ppermute | solution.py:815
  253.4 2.0 collective-permute-done.37.refs_2_
  257.7 9.7 %collective-permute-done.40.refs_2_ = bf16[96,768]{1,0:T(8,128)(2,1)S(1)} collective-permute-done((bf16[96,768]{1,0:T(8,128)(2,1)S(1)}, bf16[96,768]{1,0:T(8,128)(2,1)S(1)}, u32[]{:S(2)}, u32[]{:S(2)}) %collective-permute-start.40) | collective-permute-done | bytes 147488 | tf_op jit(solution)/shard_map/ppermute | solution.py:815
  268.8 2.2 collective-permute-done.44.refs_11_.refs_2_
  275.5 3.0 step_kernel.21
  278.6 5.1 %collective-permute-done.47.refs_2_ = bf16[96,768]{1,0:T(8,128)(2,1)S(1)} collective-permute-done((bf16[96,768]{1,0:T(8,128)(2,1)S(1)}, bf16[96,768]{1,0:T(8,128)(2,1)S(1)}, u32[]{:S(2)}, u32[]{:S(2)}) %collective-permute-start.47) | collective-permute-done | bytes 147488 | tf_op jit(solution)/shard_map/ppermute | solution.py:815
  285.7 2.7 place_kernel.3
  288.4 3.6 %collective-permute-done.50.refs_4_ = bf16[512,768]{1,0:T(8,128)(2,1)S(1)} collective-permute-done((bf16[512,768]{1,0:T(8,128)(2,1)S(1)}, bf16[512,768]{1,0:T(8,128)(2,1)S(1)}, u32[]{:S(2)}, u32[]{:S(2)}) %collective-permute-start.50) | collective-permute-done | bytes 786464 | tf_op jit(solution)/shard_map/ppermute | solution.py:809
  292.0 2.2 collective-permute-done.49.refs_2_
  295.5 2.1 step_kernel.24
  297.6 2.7 place_kernel.4
  300.3 2.7 place_kernel.5
  303.0 7.7 %collective-permute-done.53.refs_2_ = bf16[384,768]{1,0:T(8,128)(2,1)S(1)} collective-permute-done((bf16[384,768]{1,0:T(8,128)(2,1)S(1)}, bf16[384,768]{1,0:T(8,128)(2,1)S(1)}, u32[]{:S(2)}, u32[]{:S(2)}) %collective-permute-start.53) | collective-permute-done | bytes 589856 | tf_op jit(solution)/shard_map/ppermute | solution.py:815
  310.8 2.1 step_kernel.25
  (178 shorter events, 60.7 us)
Async XLA Ops:
  2.0 13.2 %collective-permute-start = (bf16[288,768]{1,0:T(8,128)(2,1)S(1)}, bf16[288,768]{1,0:T(8,128)(2,1)S(1)}, u32[]{:S(2)}, u32[]{:S(2)}) collective-permute-start(bf16[288,768]{1,0:T(8,128)(2,1)S(1)} %fusion.1), channel_id=1, source_target_pairs={{0,16},{16,0},{8,24},{24,8},{1,17},{17,1},{9,25},{25,9},{2,18},{18... | collective-permute-start | bytes 1327112 | tf_op jit(solution)/shard_map/ppermute | solution.py:809
  15.8 14.8 %collective-permute-start.1 = (bf16[288,768]{1,0:T(8,128)(2,1)S(1)}, bf16[288,768]{1,0:T(8,128)(2,1)S(1)}, u32[]{:S(2)}, u32[]{:S(2)}) collective-permute-start(bf16[288,768]{1,0:T(8,128)(2,1)S(1)} %pass_kernel.3.refs_6_.refs_2_), channel_id=1, source_target_pairs={{0,1},{1,0},{2,3},{3,2},{4,5},{5,4},{6,7},{7,6},{8,9},{9,8},{10,11... | collective-permute-start | bytes 1327112 | tf_op jit(solution)/shard_map/ppermute | solution.py:815
  17.7 10.4 %collective-permute-start.2 = (bf16[192,768]{1,0:T(8,128)(2,1)S(1)}, bf16[192,768]{1,0:T(8,128)(2,1)S(1)}, u32[]{:S(2)}, u32[]{:S(2)}) collective-permute-start(bf16[192,768]{1,0:T(8,128)(2,1)S(1)} %get-tuple-element.172.refs_2_), channel_id=1, source_target_pairs={{0,16},{16,0},{8,24},{24,8},{1,17},{17,1},{9,25},{25,9},{2,18},{18... | collective-permute-start | bytes 884744 | tf_op jit(solution)/shard_map/ppermute | solution.py:809
  19.2 22.1 %collective-permute-start.4 = (bf16[288,768]{1,0:T(8,128)(2,1)S(1)}, bf16[288,768]{1,0:T(8,128)(2,1)S(1)}, u32[]{:S(2)}, u32[]{:S(2)}) collective-permute-start(bf16[288,768]{1,0:T(8,128)(2,1)S(1)} %get-tuple-element.176), channel_id=1, source_target_pairs={{0,16},{16,0},{8,24},{24,8},{1,17},{17,1},{9,25},{25,9},{2,18},{18... | collective-permute-start | bytes 1327112 | tf_op jit(solution)/shard_map/ppermute | solution.py:809
  28.6 12.6 %collective-permute-start.3 = (bf16[192,768]{1,0:T(8,128)(2,1)S(1)}, bf16[192,768]{1,0:T(8,128)(2,1)S(1)}, u32[]{:S(2)}, u32[]{:S(2)}) collective-permute-start(bf16[192,768]{1,0:T(8,128)(2,1)S(1)} %pass_kernel.4.refs_4_), channel_id=1, source_target_pairs={{0,1},{1,0},{2,3},{3,2},{4,5},{5,4},{6,7},{7,6},{8,9},{9,8},{10,11... | collective-permute-start | bytes 884744 | tf_op jit(solution)/shard_map/ppermute | solution.py:815
  28.9 31.1 %collective-permute-start.8 = (bf16[768,768]{1,0:T(8,128)(2,1)S(1)}, bf16[768,768]{1,0:T(8,128)(2,1)S(1)}, u32[]{:S(2)}, u32[]{:S(2)}) collective-permute-start(bf16[768,768]{1,0:T(8,128)(2,1)S(1)} %get-tuple-element.184), channel_id=1, source_target_pairs={{0,16},{16,0},{8,24},{24,8},{1,17},{17,1},{9,25},{25,9},{2,18},{18... | collective-permute-start | bytes 3538952 | tf_op jit(solution)/shard_map/ppermute | solution.py:809
  44.7 18.0 %collective-permute-start.7 = (bf16[288,768]{1,0:T(8,128)(2,1)S(1)}, bf16[288,768]{1,0:T(8,128)(2,1)S(1)}, u32[]{:S(2)}, u32[]{:S(2)}) collective-permute-start(bf16[288,768]{1,0:T(8,128)(2,1)S(1)} %collective-permute-done.4.refs_6_.refs_3_), channel_id=1, source_target_pairs={{0,2},{1,3},{2,0},{3,1},{4,6},{5,7},{6,4},{7,5},{8,10},{9,11},{10,... | collective-permute-start | bytes 1327112 | tf_op jit(solution)/shard_map/ppermute | solution.py:815
  60.7 13.2 %collective-permute-start.9 = (bf16[384,768]{1,0:T(8,128)(2,1)S(1)}, bf16[384,768]{1,0:T(8,128)(2,1)S(1)}, u32[]{:S(2)}, u32[]{:S(2)}) collective-permute-start(bf16[384,768]{1,0:T(8,128)(2,1)S(1)} %get-tuple-element.186.refs_5_.refs_3_), channel_id=1, source_target_pairs={{0,1},{1,0},{2,3},{3,2},{4,5},{5,4},{6,7},{7,6},{8,9},{9,8},{10,11... | collective-permute-start | bytes 1769480 | tf_op jit(solution)/shard_map/ppermute | solution.py:815
  61.3 13.8 %collective-permute-start.10 = (bf16[384,768]{1,0:T(8,128)(2,1)S(1)}, bf16[384,768]{1,0:T(8,128)(2,1)S(1)}, u32[]{:S(2)}, u32[]{:S(2)}) collective-permute-start(bf16[384,768]{1,0:T(8,128)(2,1)S(1)} %get-tuple-element.187.refs_6_.refs_5_), channel_id=1, source_target_pairs={{0,2},{1,3},{2,0},{3,1},{4,6},{5,7},{6,4},{7,5},{8,10},{9,11},{10,... | collective-permute-start | bytes 1769480 | tf_op jit(solution)/shard_map/ppermute | solution.py:815
  107.6 10.4 %collective-permute-start.15 = (bf16[512,768]{1,0:T(8,128)(2,1)S(1)}, bf16[512,768]{1,0:T(8,128)(2,1)S(1)}, u32[]{:S(2)}, u32[]{:S(2)}) collective-permute-start(bf16[512,768]{1,0:T(8,128)(2,1)S(1)} %get-tuple-element.206.refs_2_), channel_id=1, source_target_pairs={{0,8},{8,0},{16,24},{24,16},{1,9},{9,1},{17,25},{25,17},{2,10},{10... | collective-permute-start | bytes 2359304 | tf_op jit(solution)/shard_map/ppermute | solution.py:812
  107.8 10.3 %collective-permute-start.16 = (bf16[512,768]{1,0:T(8,128)(2,1)S(1)}, bf16[512,768]{1,0:T(8,128)(2,1)S(1)}, u32[]{:S(2)}, u32[]{:S(2)}) collective-permute-start(bf16[512,768]{1,0:T(8,128)(2,1)S(1)} %get-tuple-element.207.refs_3_), channel_id=1, source_target_pairs={{0,8},{8,0},{16,24},{24,16},{1,9},{9,1},{17,25},{25,17},{2,10},{10... | collective-permute-start | bytes 2359304 | tf_op jit(solution)/shard_map/ppermute | solution.py:812
  111.7 28.4 %collective-permute-start.17 = (bf16[768,768]{1,0:T(8,128)(2,1)S(1)}, bf16[768,768]{1,0:T(8,128)(2,1)S(1)}, u32[]{:S(2)}, u32[]{:S(2)}) collective-permute-start(bf16[768,768]{1,0:T(8,128)(2,1)S(1)} %get-tuple-element.226), channel_id=1, source_target_pairs={{0,16},{16,0},{8,24},{24,8},{1,17},{17,1},{9,25},{25,9},{2,18},{18... | collective-permute-start | bytes 3538952 | tf_op jit(solution)/shard_map/ppermute | solution.py:809
  112.4 27.7 %collective-permute-start.19 = (bf16[384,768]{1,0:T(8,128)(2,1)S(1)}, bf16[384,768]{1,0:T(8,128)(2,1)S(1)}, u32[]{:S(2)}, u32[]{:S(2)}) collective-permute-start(bf16[384,768]{1,0:T(8,128)(2,1)S(1)} %get-tuple-element.224.refs_5_), channel_id=1, source_target_pairs={{0,1},{1,0},{2,3},{3,2},{4,5},{5,4},{6,7},{7,6},{8,9},{9,8},{10,11... | collective-permute-start | bytes 1769480 | tf_op jit(solution)/shard_map/ppermute | solution.py:815
  117.3 22.8 %collective-permute-start.18 = (bf16[384,768]{1,0:T(8,128)(2,1)S(1)}, bf16[384,768]{1,0:T(8,128)(2,1)S(1)}, u32[]{:S(2)}, u32[]{:S(2)}) collective-permute-start(bf16[384,768]{1,0:T(8,128)(2,1)S(1)} %get-tuple-element.228), channel_id=1, source_target_pairs={{0,1},{1,0},{2,3},{3,2},{4,5},{5,4},{6,7},{7,6},{8,9},{9,8},{10,11... | collective-permute-start | bytes 1769480 | tf_op jit(solution)/shard_map/ppermute | solution.py:815
  142.1 16.2 %collective-permute-start.22 = (bf16[384,768]{1,0:T(8,128)(2,1)S(1)}, bf16[384,768]{1,0:T(8,128)(2,1)S(1)}, u32[]{:S(2)}, u32[]{:S(2)}) collective-permute-start(bf16[384,768]{1,0:T(8,128)(2,1)S(1)} %get-tuple-element.244), channel_id=1, source_target_pairs={{0,1},{1,0},{2,3},{3,2},{4,5},{5,4},{6,7},{7,6},{8,9},{9,8},{10,11... | collective-permute-start | bytes 1769480 | tf_op jit(solution)/shard_map/ppermute | solution.py:815
  143.5 16.3 %collective-permute-start.23 = (bf16[384,768]{1,0:T(8,128)(2,1)S(1)}, bf16[384,768]{1,0:T(8,128)(2,1)S(1)}, u32[]{:S(2)}, u32[]{:S(2)}) collective-permute-start(bf16[384,768]{1,0:T(8,128)(2,1)S(1)} %get-tuple-element.245), channel_id=1, source_target_pairs={{0,16},{16,0},{8,24},{24,8},{1,17},{17,1},{9,25},{25,9},{2,18},{18... | collective-permute-start | bytes 1769480 | tf_op jit(solution)/shard_map/ppermute | solution.py:809
  144.0 41.0 %collective-permute-start.25 = (bf16[768,768]{1,0:T(8,128)(2,1)S(1)}, bf16[768,768]{1,0:T(8,128)(2,1)S(1)}, u32[]{:S(2)}, u32[]{:S(2)}) collective-permute-start(bf16[768,768]{1,0:T(8,128)(2,1)S(1)} %get-tuple-element.232.refs_9_), channel_id=1, source_target_pairs={{0,16},{16,0},{8,24},{24,8},{1,17},{17,1},{9,25},{25,9},{2,18},{18... | collective-permute-start | bytes 3538952 | tf_op jit(solution)/shard_map/ppermute | solution.py:809
  157.6 11.9 %collective-permute-start.20 = (bf16[512,768]{1,0:T(8,128)(2,1)S(1)}, bf16[512,768]{1,0:T(8,128)(2,1)S(1)}, u32[]{:S(2)}, u32[]{:S(2)}) collective-permute-start(bf16[512,768]{1,0:T(8,128)(2,1)S(1)} %get-tuple-element.233.refs_2_), channel_id=1, source_target_pairs={{0,8},{8,0},{16,24},{24,16},{1,9},{9,1},{17,25},{25,17},{2,10},{10... | collective-permute-start | bytes 2359304 | tf_op jit(solution)/shard_map/ppermute | solution.py:812
  157.7 11.8 %collective-permute-start.21 = (bf16[512,768]{1,0:T(8,128)(2,1)S(1)}, bf16[512,768]{1,0:T(8,128)(2,1)S(1)}, u32[]{:S(2)}, u32[]{:S(2)}) collective-permute-start(bf16[512,768]{1,0:T(8,128)(2,1)S(1)} %get-tuple-element.234.refs_3_), channel_id=1, source_target_pairs={{0,8},{8,0},{16,24},{24,16},{1,9},{9,1},{17,25},{25,17},{2,10},{10... | collective-permute-start | bytes 2359304 | tf_op jit(solution)/shard_map/ppermute | solution.py:812
  161.0 17.6 %collective-permute-start.24 = (bf16[384,768]{1,0:T(8,128)(2,1)S(1)}, bf16[384,768]{1,0:T(8,128)(2,1)S(1)}, u32[]{:S(2)}, u32[]{:S(2)}) collective-permute-start(bf16[384,768]{1,0:T(8,128)(2,1)S(1)} %get-tuple-element.250), channel_id=1, source_target_pairs={{0,2},{1,3},{2,0},{3,1},{4,6},{5,7},{6,4},{7,5},{8,10},{9,11},{10,... | collective-permute-start | bytes 1769480 | tf_op jit(solution)/shard_map/ppermute | solution.py:815
  178.0 26.1 %collective-permute-start.28 = (bf16[208,768]{1,0:T(8,128)(2,1)S(1)}, bf16[208,768]{1,0:T(8,128)(2,1)S(1)}, u32[]{:S(2)}, u32[]{:S(2)}) collective-permute-start(bf16[208,768]{1,0:T(8,128)(2,1)S(1)} %get-tuple-element.257), channel_id=1, source_target_pairs={{0,16},{16,0},{8,24},{24,8},{1,17},{17,1},{9,25},{25,9},{2,18},{18... | collective-permute-start | bytes 958472 | tf_op jit(solution)/shard_map/ppermute | solution.py:809
  186.6 17.4 %collective-permute-start.26 = (bf16[192,768]{1,0:T(8,128)(2,1)S(1)}, bf16[192,768]{1,0:T(8,128)(2,1)S(1)}, u32[]{:S(2)}, u32[]{:S(2)}) collective-permute-start(bf16[192,768]{1,0:T(8,128)(2,1)S(1)} %get-tuple-element.253), channel_id=1, source_target_pairs={{0,4},{1,5},{2,6},{3,7},{4,0},{5,1},{6,2},{7,3},{8,12},{9,13},{10,... | collective-permute-start | bytes 884744 | tf_op jit(solution)/shard_map/ppermute | solution.py:815
  189.3 14.8 %collective-permute-start.27 = (bf16[384,768]{1,0:T(8,128)(2,1)S(1)}, bf16[384,768]{1,0:T(8,128)(2,1)S(1)}, u32[]{:S(2)}, u32[]{:S(2)}) collective-permute-start(bf16[384,768]{1,0:T(8,128)(2,1)S(1)} %get-tuple-element.255), channel_id=1, source_target_pairs={{0,1},{1,0},{2,3},{3,2},{4,5},{5,4},{6,7},{7,6},{8,9},{9,8},{10,11... | collective-permute-start | bytes 1769480 | tf_op jit(solution)/shard_map/ppermute | solution.py:815
  202.5 20.9 %collective-permute-start.29 = (bf16[576,768]{1,0:T(8,128)(2,1)S(1)}, bf16[576,768]{1,0:T(8,128)(2,1)S(1)}, u32[]{:S(2)}, u32[]{:S(2)}) collective-permute-start(bf16[576,768]{1,0:T(8,128)(2,1)S(1)} %get-tuple-element.265), channel_id=1, source_target_pairs={{0,16},{16,0},{8,24},{24,8},{1,17},{17,1},{9,25},{25,9},{2,18},{18... | collective-permute-start | bytes 2654216 | tf_op jit(solution)/shard_map/ppermute | solution.py:809
  204.0 15.9 %collective-permute-start.32 = (bf16[512,768]{1,0:T(8,128)(2,1)S(1)}, bf16[512,768]{1,0:T(8,128)(2,1)S(1)}, u32[]{:S(2)}, u32[]{:S(2)}) collective-permute-start(bf16[512,768]{1,0:T(8,128)(2,1)S(1)} %get-tuple-element.247.refs_7_), channel_id=1, source_target_pairs={{0,8},{8,0},{16,24},{24,16},{1,9},{9,1},{17,25},{25,17},{2,10},{10... | collective-permute-start | bytes 2359304 | tf_op jit(solution)/shard_map/ppermute | solution.py:812
  205.1 14.9 %collective-permute-start.33 = (f32[16,768]{1,0:T(8,128)S(1)}, f32[16,768]{1,0:T(8,128)S(1)}, u32[]{:S(2)}, u32[]{:S(2)}) collective-permute-start(f32[16,768]{1,0:T(8,128)S(1)} %get-tuple-element.269.refs_11_), channel_id=1, source_target_pairs={{0,1},{1,0},{2,3},{3,2},{4,5},{5,4},{6,7},{7,6},{8,9},{9,8},{10,11... | collective-permute-start | bytes 147464 | tf_op jit(solution)/shard_map/ppermute | solution.py:815
  205.7 14.3 %collective-permute-start.31 = (bf16[192,768]{1,0:T(8,128)(2,1)S(1)}, bf16[192,768]{1,0:T(8,128)(2,1)S(1)}, u32[]{:S(2)}, u32[]{:S(2)}) collective-permute-start(bf16[192,768]{1,0:T(8,128)(2,1)S(1)} %get-tuple-element.267), channel_id=1, source_target_pairs={{0,2},{1,3},{2,0},{3,1},{4,6},{5,7},{6,4},{7,5},{8,10},{9,11},{10,... | collective-permute-start | bytes 884744 | tf_op jit(solution)/shard_map/ppermute | solution.py:815
  207.2 16.1 %collective-permute-start.30 = (bf16[192,768]{1,0:T(8,128)(2,1)S(1)}, bf16[192,768]{1,0:T(8,128)(2,1)S(1)}, u32[]{:S(2)}, u32[]{:S(2)}) collective-permute-start(bf16[192,768]{1,0:T(8,128)(2,1)S(1)} %get-tuple-element.263.refs_7_.refs_5_), channel_id=1, source_target_pairs={{0,4},{1,5},{2,6},{3,7},{4,0},{5,1},{6,2},{7,3},{8,12},{9,13},{10,... | collective-permute-start | bytes 884744 | tf_op jit(solution)/shard_map/ppermute | solution.py:815
  225.2 16.7 %collective-permute-start.34 = (bf16[384,768]{1,0:T(8,128)(2,1)S(1)}, bf16[384,768]{1,0:T(8,128)(2,1)S(1)}, u32[]{:S(2)}, u32[]{:S(2)}) collective-permute-start(bf16[384,768]{1,0:T(8,128)(2,1)S(1)} %get-tuple-element.271), channel_id=1, source_target_pairs={{0,1},{1,0},{2,3},{3,2},{4,5},{5,4},{6,7},{7,6},{8,9},{9,8},{10,11... | collective-permute-start | bytes 1769480 | tf_op jit(solution)/shard_map/ppermute | solution.py:815
  226.8 17.2 %collective-permute-start.35 = (bf16[384,768]{1,0:T(8,128)(2,1)S(1)}, bf16[384,768]{1,0:T(8,128)(2,1)S(1)}, u32[]{:S(2)}, u32[]{:S(2)}) collective-permute-start(bf16[384,768]{1,0:T(8,128)(2,1)S(1)} %get-tuple-element.272.refs_3_), channel_id=1, source_target_pairs={{0,2},{1,3},{2,0},{3,1},{4,6},{5,7},{6,4},{7,5},{8,10},{9,11},{10,... | collective-permute-start | bytes 1769480 | tf_op jit(solution)/shard_map/ppermute | solution.py:815
  232.4 21.0 %collective-permute-start.39 = (bf16[512,768]{1,0:T(8,128)(2,1)S(1)}, bf16[512,768]{1,0:T(8,128)(2,1)S(1)}, u32[]{:S(2)}, u32[]{:S(2)}) collective-permute-start(bf16[512,768]{1,0:T(8,128)(2,1)S(1)} %pass_kernel.5.refs_8_), channel_id=1, source_target_pairs={{0,16},{16,0},{8,24},{24,8},{1,17},{17,1},{9,25},{25,9},{2,18},{18... | collective-permute-start | bytes 2359304 | tf_op jit(solution)/shard_map/ppermute | solution.py:809
  232.8 9.0 %collective-permute-start.36 = (bf16[96,768]{1,0:T(8,128)(2,1)S(1)}, bf16[96,768]{1,0:T(8,128)(2,1)S(1)}, u32[]{:S(2)}, u32[]{:S(2)}) collective-permute-start(bf16[96,768]{1,0:T(8,128)(2,1)S(1)} %get-tuple-element.274), channel_id=1, source_target_pairs={{0,4},{1,5},{2,6},{3,7},{4,0},{5,1},{6,2},{7,3},{8,12},{9,13},{10,... | collective-permute-start | bytes 442376 | tf_op jit(solution)/shard_map/ppermute | solution.py:815
  245.1 25.9 %collective-permute-start.44 = (bf16[768,768]{1,0:T(8,128)(2,1)S(1)}, bf16[768,768]{1,0:T(8,128)(2,1)S(1)}, u32[]{:S(2)}, u32[]{:S(2)}) collective-permute-start(bf16[768,768]{1,0:T(8,128)(2,1)S(1)} %get-tuple-element.290.refs_1_), channel_id=1, source_target_pairs={{0,1},{1,0},{2,3},{3,2},{4,5},{5,4},{6,7},{7,6},{8,9},{9,8},{10,11... | collective-permute-start | bytes 3538952 | tf_op jit(solution)/shard_map/ppermute | solution.py:815
  245.6 9.7 %collective-permute-start.37 = (bf16[192,768]{1,0:T(8,128)(2,1)S(1)}, bf16[192,768]{1,0:T(8,128)(2,1)S(1)}, u32[]{:S(2)}, u32[]{:S(2)}) collective-permute-start(bf16[192,768]{1,0:T(8,128)(2,1)S(1)} %get-tuple-element.282), channel_id=1, source_target_pairs={{0,2},{1,3},{2,0},{3,1},{4,6},{5,7},{6,4},{7,5},{8,10},{9,11},{10,... | collective-permute-start | bytes 884744 | tf_op jit(solution)/shard_map/ppermute | solution.py:815
  246.1 7.2 %collective-permute-start.38 = (bf16[96,768]{1,0:T(8,128)(2,1)S(1)}, bf16[96,768]{1,0:T(8,128)(2,1)S(1)}, u32[]{:S(2)}, u32[]{:S(2)}) collective-permute-start(bf16[96,768]{1,0:T(8,128)(2,1)S(1)} %get-tuple-element.283.refs_3_), channel_id=1, source_target_pairs={{0,4},{1,5},{2,6},{3,7},{4,0},{5,1},{6,2},{7,3},{8,12},{9,13},{10,... | collective-permute-start | bytes 442376 | tf_op jit(solution)/shard_map/ppermute | solution.py:815
  246.8 21.9 %collective-permute-start.43 = (bf16[512,768]{1,0:T(8,128)(2,1)S(1)}, bf16[512,768]{1,0:T(8,128)(2,1)S(1)}, u32[]{:S(2)}, u32[]{:S(2)}) collective-permute-start(bf16[512,768]{1,0:T(8,128)(2,1)S(1)} %get-tuple-element.289.refs_7_), channel_id=1, source_target_pairs={{0,16},{16,0},{8,24},{24,8},{1,17},{17,1},{9,25},{25,9},{2,18},{18... | collective-permute-start | bytes 2359304 | tf_op jit(solution)/shard_map/ppermute | solution.py:809
  256.1 12.7 %collective-permute-start.42 = (bf16[512,768]{1,0:T(8,128)(2,1)S(1)}, bf16[512,768]{1,0:T(8,128)(2,1)S(1)}, u32[]{:S(2)}, u32[]{:S(2)}) collective-permute-start(bf16[512,768]{1,0:T(8,128)(2,1)S(1)} %get-tuple-element.288), channel_id=1, source_target_pairs={{0,8},{8,0},{16,24},{24,16},{1,9},{9,1},{17,25},{25,17},{2,10},{10... | collective-permute-start | bytes 2359304 | tf_op jit(solution)/shard_map/ppermute | solution.py:812
  256.2 12.6 %collective-permute-start.41 = (bf16[192,768]{1,0:T(8,128)(2,1)S(1)}, bf16[192,768]{1,0:T(8,128)(2,1)S(1)}, u32[]{:S(2)}, u32[]{:S(2)}) collective-permute-start(bf16[192,768]{1,0:T(8,128)(2,1)S(1)} %get-tuple-element.286.refs_3_), channel_id=1, source_target_pairs={{0,2},{1,3},{2,0},{3,1},{4,6},{5,7},{6,4},{7,5},{8,10},{9,11},{10,... | collective-permute-start | bytes 884744 | tf_op jit(solution)/shard_map/ppermute | solution.py:815
  257.4 10.0 %collective-permute-start.40 = (bf16[96,768]{1,0:T(8,128)(2,1)S(1)}, bf16[96,768]{1,0:T(8,128)(2,1)S(1)}, u32[]{:S(2)}, u32[]{:S(2)}) collective-permute-start(bf16[96,768]{1,0:T(8,128)(2,1)S(1)} %get-tuple-element.285), channel_id=1, source_target_pairs={{0,4},{1,5},{2,6},{3,7},{4,0},{5,1},{6,2},{7,3},{8,12},{9,13},{10,... | collective-permute-start | bytes 442376 | tf_op jit(solution)/shard_map/ppermute | solution.py:815
  271.8 11.8 %collective-permute-start.48 = (bf16[1024,768]{1,0:T(8,128)(2,1)S(1)}, bf16[1024,768]{1,0:T(8,128)(2,1)S(1)}, u32[]{:S(2)}, u32[]{:S(2)}) collective-permute-start(bf16[1024,768]{1,0:T(8,128)(2,1)S(1)} %get-tuple-element.296.refs_1_), channel_id=1, source_target_pairs={{0,8},{8,0},{16,24},{24,16},{1,9},{9,1},{17,25},{25,17},{2,10},{10... | collective-permute-start | bytes 4718600 | tf_op jit(solution)/shard_map/ppermute | solution.py:812
  271.9 11.7 %collective-permute-start.45 = (bf16[512,768]{1,0:T(8,128)(2,1)S(1)}, bf16[512,768]{1,0:T(8,128)(2,1)S(1)}, u32[]{:S(2)}, u32[]{:S(2)}) collective-permute-start(bf16[512,768]{1,0:T(8,128)(2,1)S(1)} %get-tuple-element.291.refs_2_), channel_id=1, source_target_pairs={{0,8},{8,0},{16,24},{24,16},{1,9},{9,1},{17,25},{25,17},{2,10},{10... | collective-permute-start | bytes 2359304 | tf_op jit(solution)/shard_map/ppermute | solution.py:812
  272.4 19.5 %collective-permute-start.50 = (bf16[512,768]{1,0:T(8,128)(2,1)S(1)}, bf16[512,768]{1,0:T(8,128)(2,1)S(1)}, u32[]{:S(2)}, u32[]{:S(2)}) collective-permute-start(bf16[512,768]{1,0:T(8,128)(2,1)S(1)} %get-tuple-element.298.refs_3_), channel_id=1, source_target_pairs={{0,16},{16,0},{8,24},{24,8},{1,17},{17,1},{9,25},{25,9},{2,18},{18... | collective-permute-start | bytes 2359304 | tf_op jit(solution)/shard_map/ppermute | solution.py:809
  272.8 15.6 %collective-permute-start.46 = (bf16[384,768]{1,0:T(8,128)(2,1)S(1)}, bf16[384,768]{1,0:T(8,128)(2,1)S(1)}, u32[]{:S(2)}, u32[]{:S(2)}) collective-permute-start(bf16[384,768]{1,0:T(8,128)(2,1)S(1)} %get-tuple-element.292.refs_1_), channel_id=1, source_target_pairs={{0,1},{1,0},{2,3},{3,2},{4,5},{5,4},{6,7},{7,6},{8,9},{9,8},{10,11... | collective-permute-start | bytes 1769480 | tf_op jit(solution)/shard_map/ppermute | solution.py:815
  274.3 9.3 %collective-permute-start.47 = (bf16[96,768]{1,0:T(8,128)(2,1)S(1)}, bf16[96,768]{1,0:T(8,128)(2,1)S(1)}, u32[]{:S(2)}, u32[]{:S(2)}) collective-permute-start(bf16[96,768]{1,0:T(8,128)(2,1)S(1)} %get-tuple-element.293.refs_3_.refs_1_), channel_id=1, source_target_pairs={{0,4},{1,5},{2,6},{3,7},{4,0},{5,1},{6,2},{7,3},{8,12},{9,13},{10,... | collective-permute-start | bytes 442376 | tf_op jit(solution)/shard_map/ppermute | solution.py:815
  284.2 10.0 %collective-permute-start.49 = (bf16[192,768]{1,0:T(8,128)(2,1)S(1)}, bf16[192,768]{1,0:T(8,128)(2,1)S(1)}, u32[]{:S(2)}, u32[]{:S(2)}) collective-permute-start(bf16[192,768]{1,0:T(8,128)(2,1)S(1)} %get-tuple-element.297.refs_3_.refs_1_), channel_id=1, source_target_pairs={{0,2},{1,3},{2,0},{3,1},{4,6},{5,7},{6,4},{7,5},{8,10},{9,11},{10,... | collective-permute-start | bytes 884744 | tf_op jit(solution)/shard_map/ppermute | solution.py:815
  284.3 7.8 %collective-permute-start.51 = (f32[16,768]{1,0:T(8,128)S(1)}, f32[16,768]{1,0:T(8,128)S(1)}, u32[]{:S(2)}, u32[]{:S(2)}) collective-permute-start(f32[16,768]{1,0:T(8,128)S(1)} %get-tuple-element.299.refs_5_), channel_id=1, source_target_pairs={{0,4},{1,5},{2,6},{3,7},{4,0},{5,1},{6,2},{7,3},{8,12},{9,13},{10,... | collective-permute-start | bytes 147464 | tf_op jit(solution)/shard_map/ppermute | solution.py:815
  295.0 15.7 %collective-permute-start.53 = (bf16[384,768]{1,0:T(8,128)(2,1)S(1)}, bf16[384,768]{1,0:T(8,128)(2,1)S(1)}, u32[]{:S(2)}, u32[]{:S(2)}) collective-permute-start(bf16[384,768]{1,0:T(8,128)(2,1)S(1)} %get-tuple-element.301.refs_3_.refs_1_), channel_id=1, source_target_pairs={{0,1},{1,0},{2,3},{3,2},{4,5},{5,4},{6,7},{7,6},{8,9},{9,8},{10,11... | collective-permute-start | bytes 1769480 | tf_op jit(solution)/shard_map/ppermute | solution.py:815
  295.5 7.5 %collective-permute-start.54 = (f32[16,768]{1,0:T(8,128)S(1)}, f32[16,768]{1,0:T(8,128)S(1)}, u32[]{:S(2)}, u32[]{:S(2)}) collective-permute-start(f32[16,768]{1,0:T(8,128)S(1)} %get-tuple-element.308.refs_3_), channel_id=1, source_target_pairs={{0,2},{1,3},{2,0},{3,1},{4,6},{5,7},{6,4},{7,5},{8,10},{9,11},{10,... | collective-permute-start | bytes 147464 | tf_op jit(solution)/shard_map/ppermute | solution.py:815
  (43 other events, 282.6 us)
